TPU v7x, 32 devices: a whole 2x2x4 slice. The times are simulated.
32 devices in a mesh: tile: 8 (over z, x), layer: 4 (over y, core).
Axes of the slice: x: 2, y: 2, z: 4, core: 2. Of those that a mesh axis runs over, the one named last changes fastest.
Arguments:
- head_start: float32 [8, 512, 512], P('layer', 'tile'), may hold values from -2 to 0.5
- soil_class: int32 [8, 512, 512], P('layer', 'tile'), may hold values from 0 to 11
- land_mask: int32 [512, 512], P('tile'), may hold values 0 or 1
- ks_table: float32 [12], replicated, may hold values from 0.2 to 5
- alpha_table: float32 [12], replicated, may hold values from 0.5 to 2
- store_table: float32 [12], replicated, may hold values from 0.5 to 2
- section: float32 [128, 128], P('tile'), may hold values from -6 to 6
- cross_owner: int32 [8, 256], P('tile'), may hold values from 0 to 7, as said below
- cross_local: int32 [8, 256], P('tile'), may hold values from 0 to 15
- node_cell: int32 [8, 256, 128], P('tile'), may hold values from -1 to 32767, as said below
- bed_cond: float32 [8, 256, 128], P('tile'), may hold values from 0.5 to 4
Outputs:
- head: float32 [8, 512, 512], P('layer', 'tile')
- inflow: float32 [128, 128], P('tile', 'layer')
Inputs may be any that keep to these rules, and one draw needn't show every extreme that they name: `cross_owner`: no strip's row names one owner in more than 32 slots, and in every row some owner is named in exactly 32 slots. `node_cell`: -1 marks a node outside the strip; other values index the strip's top-layer cells row-major over 64 x 512. In each strip the slots with nodes come first, the rest are padding with every node -1.
All inputs are finite; a program needn't handle non-finite values. No bound on the sum of `land_mask` on one device may be relied on, other than what follows from the above.
Results may differ from a plain program's by a relative error of at most 0.00002.
Values sent between devices are 32-bit elements; how exact they have to be, the bound alone decides.
No kernel may reach another device: no remote copies, remote signals or barrier semaphores. Data moves between devices by JAX's collectives and lax.ppermute only.
A program may use at most 64 MiB of HBM per device.

v0:
```python
import jax
import jax.numpy as jnp
from jax import lax
from jax.sharding import PartitionSpec as P

ITERS = 2
SWEEPS = 3


LATERAL = 1.0
VERTICAL = 2.0
GRAVITY = 1.0
NEIGHBOURS = (
    (0, -1, VERTICAL),
    (0, 1, VERTICAL),
    (1, -1, LATERAL),
    (1, 1, LATERAL),
    (2, -1, LATERAL),
    (2, 1, LATERAL),
)


def with_halo(block, sides, width):
    for axis, dim in sides:
        count = lax.axis_size(axis)
        forward = [(i, i + 1) for i in range(count - 1)]
        backward = [(target, source) for source, target in forward]
        low = lax.ppermute(
            lax.slice_in_dim(block, block.shape[dim] - width, None, axis=dim), axis, forward
        )
        high = lax.ppermute(lax.slice_in_dim(block, 0, width, axis=dim), axis, backward)
        block = jnp.concatenate([low, block, high], axis=dim)
    return block


def from_root(value, axis, source):
    kept = jnp.where(lax.axis_index(axis) == source, value, 0).astype(value.dtype)
    return lax.psum(kept, axis)


def beside(padded, axis_id, step):
    spans = [slice(1, -1), slice(1, -1), slice(1, -1)]
    spans[axis_id] = slice(1 + step, padded.shape[axis_id] - 1 + step)
    return padded[tuple(spans)]


def neighbor_weights(cond_pad, open_pad):
    centre = cond_pad[1:-1, 1:-1, 1:-1]
    centre_open = open_pad[1:-1, 1:-1, 1:-1]
    result = []
    for axis_id, step, factor in NEIGHBOURS:
        far = beside(cond_pad, axis_id, step)
        far_open = beside(open_pad, axis_id, step)
        result.append(factor * 2.0 * centre_open * far_open / (centre + far))
    return result


def relax(head_pad, weights, store, head_old, riv_diag, riv_rhs):
    total = store * head_old
    diagonal_sum = store
    for weight, (axis_id, step, factor) in zip(weights, NEIGHBOURS):
        total = total + weight * beside(head_pad, axis_id, step)
        diagonal_sum = diagonal_sum + weight
    total = total + GRAVITY * (weights[0] - weights[1]) + riv_rhs
    return total / (diagonal_sum + riv_diag)


def lookup(values_table, classes):
    result = jnp.zeros(classes.shape, jnp.float32)
    for class_id in range(values_table.shape[0]):
        result = jnp.where(classes == class_id, values_table[class_id], result)
    return result


def pad_dims(field, chosen_dims):
    widths = [(1, 1) if place in chosen_dims else (0, 0) for place in range(field.ndim)]
    return jnp.pad(field, widths)


def pick_heads(top_head, cells):
    breadth = top_head.shape[1]
    slots, width = cells.shape
    group = 16
    grouped = cells.reshape(slots // group, group * width)
    columns = jnp.arange(breadth, dtype=jnp.int32)[None, :]

    def one_group(flat_cells):
        picked_rows = jnp.take(top_head, flat_cells // breadth, axis=0)
        hit = columns == (flat_cells % breadth)[:, None]
        return jnp.sum(jnp.where(hit, picked_rows, 0.0), axis=1)

    return lax.map(one_group, grouped).reshape(slots, width)


def on_device(
    head_start,
    soil_class,
    land_mask,
    ks_table,
    alpha_table,
    store_table,
    section,
    cross_owner,
    cross_local,
    node_cell,
    bed_cond,
):
    layers, across, breadth = head_start.shape
    reach_rows = section.shape[0]
    node_count = section.shape[1]
    tile_count = lax.axis_size("tile")
    quarter = node_count // lax.axis_size("layer")
    node_first = lax.axis_index("layer") * quarter
    ks = lookup(ks_table, soil_class)
    alpha = lookup(alpha_table, soil_class)
    store = lookup(store_table, soil_class)
    landf = land_mask.astype(jnp.float32)[None]
    owners = cross_owner[0]
    positions = cross_local[0]
    node_cells = node_cell[0]
    bed_given = bed_cond[0]
    whole_section = lax.all_gather(section, "tile", axis=0, tiled=True)
    slot_section = jnp.take(whole_section, owners * reach_rows + positions, axis=0)
    in_tile = node_cells >= 0
    flat_index = jnp.where(in_tile, node_cells, across * breadth)
    bed_terms = jnp.where(in_tile, bed_given, 0.0)
    diag_top = (
        jnp.zeros((across * breadth,), jnp.float32)
        .at[flat_index.reshape(-1)]
        .add(bed_terms.reshape(-1), mode="drop")
    )
    rhs_top = (
        jnp.zeros((across * breadth,), jnp.float32)
        .at[flat_index.reshape(-1)]
        .add((bed_terms * slot_section).reshape(-1), mode="drop")
    )
    top_diag = diag_top.reshape(across, breadth)
    top_rhs = rhs_top.reshape(across, breadth)
    head_old, ks_here, alpha_here, store_here, land_here = (head_start, ks, alpha, store, landf)
    on_top = (lax.axis_index("layer") == 0).astype(jnp.float32)
    riv_diag = jnp.zeros((layers, across, breadth), jnp.float32).at[0].set(top_diag * on_top)
    riv_rhs = jnp.zeros((layers, across, breadth), jnp.float32).at[0].set(top_rhs * on_top)

    def head_halo(field):
        return pad_dims(with_halo(field, (("tile", 1), ("layer", 0)), 1), (2,))

    head = head_old
    for picard in range(ITERS):
        head_pad = head_halo(head)
        conduct = ks_here * jnp.exp(alpha_here * jnp.minimum(head, 0.0))
        both_pad = pad_dims(
            with_halo(jnp.stack([conduct, conduct * land_here]), (("tile", 2), ("layer", 1)), 1),
            (3,),
        )
        cond_pad = both_pad[0]
        open_pad = both_pad[1]
        weights = neighbor_weights(cond_pad, open_pad)
        for sweep in range(SWEEPS):
            if sweep > 0:
                head_pad = head_halo(head)
            head = relax(head_pad, weights, store_here, head_old, riv_diag, riv_rhs)
    top_head = from_root(head[0], "layer", 0)
    my_cells = lax.dynamic_slice_in_dim(node_cells, node_first, quarter, 1)
    my_bed = lax.dynamic_slice_in_dim(bed_given, node_first, quarter, 1)
    my_section = lax.dynamic_slice_in_dim(slot_section, node_first, quarter, 1)
    my_inside = my_cells >= 0
    node_head = pick_heads(top_head, jnp.where(my_inside, my_cells, 0))
    slot_in = jnp.where(my_inside, my_bed * (node_head - my_section), 0.0)
    dense = (
        jnp.zeros((reach_rows * tile_count, quarter), jnp.float32)
        .at[owners * reach_rows + positions]
        .add(slot_in)
    )
    inflow = lax.psum_scatter(dense, "tile", scatter_dimension=0, tiled=True)
    return (head, inflow)


def solution(mesh):
    placed = (
        P("layer", "tile", None),
        P("layer", "tile", None),
        P("tile", None),
        P(),
        P(),
        P(),
        P("tile", None),
        P("tile", None),
        P("tile", None),
        P("tile", None, None),
        P("tile", None, None),
    )
    return jax.shard_map(
        on_device,
        mesh=mesh,
        in_specs=placed,
        out_specs=(P("layer", "tile", None), P("tile", "layer")),
        check_vma=False,
    )
```

profile of v0, /device:TPU:0, one launch (start us, length us, event | category | flops | bytes accessed | tf_op | source)
XLA Modules:
  0.0 708.3 jit_solution(17409297109078487553)
XLA Ops:
  11.7 17.5 %fusion.107 = (f32[1,2,64,512]{3,2,1,0:T(8,128)S(1)}, f32[2,64,512]{2,1,0:T(8,128)S(1)}, f32[2,64,512]{2,1,0:T(8,128)S(1)}, pred[2,64,512]{2,1,0:T(8,128)(4,1)S(...) fusion(f32[2,64,512]{2,1,0:T(8,128)} %param.17, ...), kind=kLoop, calls=%fused_computation.316 | loop fusion | flops 2555904 | bytes 2097248 | tf_op jit(solution)/shard_map/stack | solution.py:152
  30.7 5.5 collective-permute-start
  37.5 5.4 collective-permute-start.4
  43.2 30.7 %all_gather.3 = f32[128,128]{1,0:T(8,128)S(1)} all-gather(f32[16,128]{1,0:T(8,128)S(1)} %copy-done.12), channel_id=1, replica_groups=mesh['tile'=8,'layer'=4] {'tile'}, dimensions={0}, use_global_device_ids=true | all-gather | bytes 73728 | tf_op jit(solution)/shard_map/all_gather | solution.py:122
  75.4 171.1 %scatter_custom_fusion.1 = f32[32768]{0:T(1024)S(1)} fusion(s32[32768]{0:T(1024)S(1)} %bitcast.101, f32[32768]{0:T(1024)S(1)} %get-tuple-element.136, f32[]{:T(128)} %constant.189.clone.1), kind=kCustom, calls=%fused_computation.301 | custom fusion | flops 32768 | bytes 131076 | tf_op jit(solution)/shard_map/scatter-add | solution.py:130
  246.5 171.1 %scatter_custom_fusion = f32[32768]{0:T(1024)S(1)} fusion(s32[32768]{0:T(1024)S(1)} %bitcast.102, f32[32768]{0:T(1024)S(1)} %get-tuple-element.134, f32[]{:T(128)} %constant.189.clone.1), kind=kCustom, calls=%fused_computation.303 | custom fusion | flops 32768 | bytes 131076 | tf_op jit(solution)/shard_map/scatter-add | solution.py:135
  419.7 3.0 collective-permute-start.6
  425.1 3.7 collective-permute-start.2
  431.6 8.5 %add_add_fusion.1 = (f32[2,64,512]{2,1,0:T(8,128)S(1)}, f32[2,64,512]{2,1,0:T(8,128)S(1)}, f32[2,64,512]{2,1,0:T(8,128)S(1)}, f32[2,64,512]{2,1,0:T(8,128)S(1)},...) fusion(pred[2,64,512]{2,1,0:T(8,128)(4,1)S(1)} %copy-done.10, ...), kind=kLoop, calls=%fused_computation.245 | loop fusion | flops 2490368 | bytes 6553648 | tf_op jit(solution)/shard_map/add | solution.py:63
  442.0 4.5 collective-permute-start.8
  449.2 5.7 collective-permute-start.10
  458.0 4.5 collective-permute-start.12
  465.2 6.6 collective-permute-start.14
  475.0 5.2 collective-permute-start.20
  481.5 5.4 collective-permute-start.16
  489.7 6.4 collective-permute-start.18
  497.4 6.3 collective-permute-start.22
  508.2 5.4 collective-permute-start.24
  516.3 4.5 collective-permute-start.26
  523.9 5.7 collective-permute-start.28
  533.0 6.1 collective-permute-start.30
  541.8 41.5 %all-reduce.10.cloned.1.call-done = f32[64,512]{1,0:T(8,128)} async-done(((f32[64,512]{1,0:T(8,128)}), f32[64,512]{1,0:T(8,128)}) %all-reduce.10.cloned.1.call-update) | async-done | bytes 131088 | tf_op jit(solution)/shard_map/psum | solution.py:38
  583.3 54.5 %while.15 = (s32[]{:T(128)}, f32[16,512]{1,0:T(8,128)S(1)}, s32[16,512]{1,0:T(8,128)S(1)}, f32[64,512]{1,0:T(8,128)}, s32[]{:T(128)}, /*index=5*/s32[]{:T(128)}) while((s32[]{:T(128)}, f32[16,512]{1,0:T(8,128)S(1)}, s32[16,512]{1,0:T(8,128)S(1)}, f32[64,512]{1,0:T(8,128)}, s32[]{:T(128)}, /*index=5*/s32[]{:T(128)}) %tuple.130), condition=%wide.region_5.6_spmd.clone, body=%wide.region_3.5_spmd.clone.sunk | while | flops 1074690 | bytes 3175509 | solution.py:92
  640.1 61.4 %reduce-scatter.2.cloned.1.call-done = f32[16,32]{1,0:T(8,128)} async-done(((f32[128,32]{1,0:T(8,128)}), f32[16,32]{1,0:T(8,128)}) %reduce-scatter.2.cloned.1.call-update) | async-done | bytes 2064 | tf_op jit(solution)/shard_map/reduce_scatter | solution.py:174
  (271 shorter events, 106.5 us)
Async XLA Ops:
  7.2 576.1 %all-reduce.10.cloned.1.call-start = ((), (), s32[]{:S(2)}) async-start(), calls=%async_computation.1 | async-start | bytes 262144 | tf_op jit(solution)/shard_map/psum | solution.py:38
  29.4 393.4 %collective-permute-start.1 = (f32[2,2,1,512]{3,2,1,0:T(1,128)S(1)}, f32[2,2,1,512]{3,2,1,0:T(1,128)S(1)}, u32[]{:S(2)}, u32[]{:S(2)}) collective-permute-start(f32[2,2,1,512]{3,2,1,0:T(1,128)S(1)} %get-tuple-element.168), channel_id=1, source_target_pairs={{4,0},{8,4},{12,8},{16,12},{20,16},{24,20},{28,24},{5,1},{9,5},{13... | collective-permute-start | bytes 24584 | tf_op jit(solution)/shard_map/ppermute | solution.py:31
  30.7 392.1 %collective-permute-start = (f32[2,2,1,512]{3,2,1,0:T(1,128)S(1)}, f32[2,2,1,512]{3,2,1,0:T(1,128)S(1)}, u32[]{:S(2)}, u32[]{:S(2)}) collective-permute-start(f32[2,2,1,512]{3,2,1,0:T(1,128)S(1)} %get-tuple-element.167), channel_id=1, source_target_pairs={{0,4},{4,8},{8,12},{12,16},{16,20},{20,24},{24,28},{1,5},{5,9},{9,... | collective-permute-start | bytes 24584 | tf_op jit(solution)/shard_map/ppermute | solution.py:28
  36.2 381.5 %collective-permute-start.5 = (f32[2,1,512]{2,1,0:T(1,128)S(1)}, f32[2,1,512]{2,1,0:T(1,128)S(1)}, u32[]{:S(2)}, u32[]{:S(2)}) collective-permute-start(f32[2,1,512]{2,1,0:T(1,128)S(1)} %get-tuple-element.192), channel_id=1, source_target_pairs={{4,0},{8,4},{12,8},{16,12},{20,16},{24,20},{28,24},{5,1},{9,5},{13... | collective-permute-start | bytes 12296 | tf_op jit(solution)/shard_map/ppermute | solution.py:31
  37.5 380.2 %collective-permute-start.4 = (f32[2,1,512]{2,1,0:T(1,128)S(1)}, f32[2,1,512]{2,1,0:T(1,128)S(1)}, u32[]{:S(2)}, u32[]{:S(2)}) collective-permute-start(f32[2,1,512]{2,1,0:T(1,128)S(1)} %get-tuple-element.191), channel_id=1, source_target_pairs={{0,4},{4,8},{8,12},{12,16},{16,20},{20,24},{24,28},{1,5},{5,9},{9,... | collective-permute-start | bytes 12296 | tf_op jit(solution)/shard_map/ppermute | solution.py:28
  418.4 11.1 %collective-permute-start.7 = (f32[1,66,512]{2,1,0:T(8,128)}, f32[1,66,512]{2,1,0:T(8,128)S(1)}, u32[]{:S(2)}, u32[]{:S(2)}) collective-permute-start(f32[1,66,512]{2,1,0:T(8,128)} %get-tuple-element.180), channel_id=1, source_target_pairs={{1,0},{2,1},{3,2},{5,4},{6,5},{7,6},{9,8},{10,9},{11,10},{13,12},{... | collective-permute-start | bytes 405512 | tf_op jit(solution)/shard_map/ppermute | solution.py:31
  419.7 9.8 %collective-permute-start.6 = (f32[1,66,512]{2,1,0:T(8,128)}, f32[1,66,512]{2,1,0:T(8,128)S(1)}, u32[]{:S(2)}, u32[]{:S(2)}) collective-permute-start(f32[1,66,512]{2,1,0:T(8,128)} %get-tuple-element.179), channel_id=1, source_target_pairs={{0,1},{1,2},{2,3},{4,5},{5,6},{6,7},{8,9},{9,10},{10,11},{12,13},{... | collective-permute-start | bytes 405512 | tf_op jit(solution)/shard_map/ppermute | solution.py:28
  447.9 7.0 collective-permute-start.11
  463.9 7.9 %collective-permute-start.15 = (f32[1,66,512]{2,1,0:T(8,128)S(1)}, f32[1,66,512]{2,1,0:T(8,128)S(1)}, u32[]{:S(2)}, u32[]{:S(2)}) collective-permute-start(f32[1,66,512]{2,1,0:T(8,128)S(1)} %get-tuple-element.176), channel_id=1, source_target_pairs={{1,0},{2,1},{3,2},{5,4},{6,5},{7,6},{9,8},{10,9},{11,10},{13,12},{... | collective-permute-start | bytes 405512 | tf_op jit(solution)/shard_map/ppermute | solution.py:31
  465.2 7.5 %collective-permute-start.14 = (f32[1,66,512]{2,1,0:T(8,128)S(1)}, f32[1,66,512]{2,1,0:T(8,128)S(1)}, u32[]{:S(2)}, u32[]{:S(2)}) collective-permute-start(f32[1,66,512]{2,1,0:T(8,128)S(1)} %get-tuple-element.175), channel_id=1, source_target_pairs={{0,1},{1,2},{2,3},{4,5},{5,6},{6,7},{8,9},{9,10},{10,11},{12,13},{... | collective-permute-start | bytes 405512 | tf_op jit(solution)/shard_map/ppermute | solution.py:28
  473.7 13.3 %collective-permute-start.21 = (f32[2,1,512]{2,1,0:T(1,128)S(1)}, f32[2,1,512]{2,1,0:T(1,128)S(1)}, u32[]{:S(2)}, u32[]{:S(2)}) collective-permute-start(f32[2,1,512]{2,1,0:T(1,128)S(1)} %get-tuple-element.186), channel_id=1, source_target_pairs={{4,0},{8,4},{12,8},{16,12},{20,16},{24,20},{28,24},{5,1},{9,5},{13... | collective-permute-start | bytes 12296 | tf_op jit(solution)/shard_map/ppermute | solution.py:31
  475.0 12.0 %collective-permute-start.20 = (f32[2,1,512]{2,1,0:T(1,128)S(1)}, f32[2,1,512]{2,1,0:T(1,128)S(1)}, u32[]{:S(2)}, u32[]{:S(2)}) collective-permute-start(f32[2,1,512]{2,1,0:T(1,128)S(1)} %get-tuple-element.185), channel_id=1, source_target_pairs={{0,4},{4,8},{8,12},{12,16},{16,20},{20,24},{24,28},{1,5},{5,9},{9,... | collective-permute-start | bytes 12296 | tf_op jit(solution)/shard_map/ppermute | solution.py:28
  480.2 6.8 collective-permute-start.17
  481.5 6.8 collective-permute-start.16
  488.4 16.4 %collective-permute-start.19 = (f32[2,1,66,512]{3,2,1,0:T(8,128)S(1)}, f32[2,1,66,512]{3,2,1,0:T(8,128)S(1)}, u32[]{:S(2)}, u32[]{:S(2)}) collective-permute-start(f32[2,1,66,512]{3,2,1,0:T(8,128)S(1)} %get-tuple-element.162), channel_id=1, source_target_pairs={{1,0},{2,1},{3,2},{5,4},{6,5},{7,6},{9,8},{10,9},{11,10},{13,12},{... | collective-permute-start | bytes 811016 | tf_op jit(solution)/shard_map/ppermute | solution.py:31
  489.7 15.1 %collective-permute-start.18 = (f32[2,1,66,512]{3,2,1,0:T(8,128)S(1)}, f32[2,1,66,512]{3,2,1,0:T(8,128)S(1)}, u32[]{:S(2)}, u32[]{:S(2)}) collective-permute-start(f32[2,1,66,512]{3,2,1,0:T(8,128)S(1)} %get-tuple-element.161), channel_id=1, source_target_pairs={{0,1},{1,2},{2,3},{4,5},{5,6},{6,7},{8,9},{9,10},{10,11},{12,13},{... | collective-permute-start | bytes 811016 | tf_op jit(solution)/shard_map/ppermute | solution.py:28
  496.1 7.6 %collective-permute-start.23 = (f32[1,66,512]{2,1,0:T(8,128)S(1)}, f32[1,66,512]{2,1,0:T(8,128)S(1)}, u32[]{:S(2)}, u32[]{:S(2)}) collective-permute-start(f32[1,66,512]{2,1,0:T(8,128)S(1)} %get-tuple-element.174), channel_id=1, source_target_pairs={{1,0},{2,1},{3,2},{5,4},{6,5},{7,6},{9,8},{10,9},{11,10},{13,12},{... | collective-permute-start | bytes 405512 | tf_op jit(solution)/shard_map/ppermute | solution.py:31
  497.4 7.1 %collective-permute-start.22 = (f32[1,66,512]{2,1,0:T(8,128)S(1)}, f32[1,66,512]{2,1,0:T(8,128)S(1)}, u32[]{:S(2)}, u32[]{:S(2)}) collective-permute-start(f32[1,66,512]{2,1,0:T(8,128)S(1)} %get-tuple-element.173), channel_id=1, source_target_pairs={{0,1},{1,2},{2,3},{4,5},{5,6},{6,7},{8,9},{9,10},{10,11},{12,13},{... | collective-permute-start | bytes 405512 | tf_op jit(solution)/shard_map/ppermute | solution.py:28
  508.2 6.8 collective-permute-start.24
  522.6 7.0 collective-permute-start.29
  523.9 7.0 collective-permute-start.28
  531.7 7.6 %collective-permute-start.31 = (f32[1,66,512]{2,1,0:T(8,128)}, f32[1,66,512]{2,1,0:T(8,128)S(1)}, u32[]{:S(2)}, u32[]{:S(2)}) collective-permute-start(f32[1,66,512]{2,1,0:T(8,128)} %get-tuple-element.170), channel_id=1, source_target_pairs={{1,0},{2,1},{3,2},{5,4},{6,5},{7,6},{9,8},{10,9},{11,10},{13,12},{... | collective-permute-start | bytes 405512 | tf_op jit(solution)/shard_map/ppermute | solution.py:31
  533.0 7.3 %collective-permute-start.30 = (f32[1,66,512]{2,1,0:T(8,128)}, f32[1,66,512]{2,1,0:T(8,128)S(1)}, u32[]{:S(2)}, u32[]{:S(2)}) collective-permute-start(f32[1,66,512]{2,1,0:T(8,128)} %get-tuple-element.169), channel_id=1, source_target_pairs={{0,1},{1,2},{2,3},{4,5},{5,6},{6,7},{8,9},{9,10},{10,11},{12,13},{... | collective-permute-start | bytes 405512 | tf_op jit(solution)/shard_map/ppermute | solution.py:28
  541.8 159.7 %reduce-scatter.2.cloned.1.call-start = ((), (), s32[]{:S(2)}) async-start(), calls=%async_computation.2 | async-start | bytes 73728 | tf_op jit(solution)/shard_map/reduce_scatter | solution.py:174
  (25 other events, 372.7 us)
Sparse Core Ops, SparseCore 0:
  541.9 41.3 all-reduce.9
  640.2 61.2 reduce-scatter.1
where the time goes:
time: 710 us; the launch traced here: 708 us
  other arithmetic  386 us (54%)
  waiting for transfers between devices  114 us (16%)
  starting transfers between devices  105 us (15%)
  local copies, waits for them, and re-layouts  56.9 us (8%)
  blocking collectives  30.7 us (4%)
  between operations  15.1 us (2%)
    scatter-add x1, other arithmetic, on_device(): rhs_top = jnp.zeros((across * breadth,), jnp.float32).at[flat_index.resha...  171 us
    scatter-add x1, other arithmetic, on_device(): diag_top = jnp.zeros((across * breadth,), jnp.float32).at[flat_index.resh...  171 us
    ppermute x16, starting transfers between devices, with_halo(): lax.ppermute(lax.slice_in_dim(block, block.shape[dim] - width, None, axis...  84.1 us
    reduce_scatter x1, waiting for transfers between devices, on_device(): inflow = lax.psum_scatter(dense, 'tile', scatter_dimension=0, tiled=True)  61.4 us
    gather x16, local copies, waits for them, and re-layouts, one_group(): picked_rows = jnp.take(top_head, flat_cells // breadth, axis=0)  46.9 us
    psum x1, waiting for transfers between devices, from_root(): return lax.psum(kept, axis)  41.5 us
    all_gather x1, blocking collectives, on_device(): whole_section = lax.all_gather(section, 'tile', axis=0, tiled=True)  30.7 us
    ppermute x16, starting transfers between devices, with_halo(): lax.ppermute(lax.slice_in_dim(block, 0, width, axis=dim), axis, backward)  20.6 us
  transfers between devices with their start and end apart: 34, of which 13 were waited for; matrix products, arithmetic and copies ran while one was open for 49% of the time, Pallas kernels for 0%

commit v1 on v0

v1 whole, which is shorter than its diff:
```python
import functools

import jax
import jax.numpy as jnp
from jax import lax
from jax.experimental import pallas as pl
from jax.experimental.pallas import tpu as pltpu
from jax.sharding import PartitionSpec as P

ITERS = 2
SWEEPS = 3

LATERAL = 1.0
VERTICAL = 2.0
GRAVITY = 1.0

PAD = 8
HALO = ITERS * SWEEPS
LANES = 128
VMEM_LIMIT = 48 * 1024 * 1024
FLAT = ("tile", "layer")

in_vmem = pl.BlockSpec(memory_space=pltpu.VMEM)
in_smem = pl.BlockSpec(memory_space=pltpu.SMEM)


def bf16_pieces(value, count):
    pieces = []
    for _ in range(count):
        piece = value.astype(jnp.bfloat16)
        pieces.append(piece)
        value = value - piece.astype(jnp.float32)
    return pieces


def one_hot(row, size, on):
    index = lax.broadcasted_iota(jnp.int32, (16, LANES), 0)
    zero = jnp.zeros((16, LANES), jnp.bfloat16)
    tiles = []
    for start in range(0, size, 16):
        here = (index + start).astype(jnp.float32).astype(jnp.bfloat16)
        tiles.append(jnp.where(row == here, on, zero))
    return jnp.concatenate(tiles, axis=0)


def row_copies(ref, slot):
    return jnp.broadcast_to(ref[pl.ds(slot, 1), :], (16, LANES)).astype(jnp.bfloat16)


def split_cells(cells, first_row, breadth):
    local = cells - first_row * breadth
    block = jnp.where(cells < 0, -1, local >> 7)
    return block.astype(jnp.float32), (local & (LANES - 1)).astype(jnp.float32)


def scatter_into(out_ref, value, cells, first_row, breadth, blocks, block_sc, lane_sc, high_sc, low_sc):
    block, lane = split_cells(cells, first_row, breadth)
    block_sc[...] = block
    lane_sc[...] = lane
    high, low = bf16_pieces(value, 2)
    high_sc[...] = high.astype(jnp.float32)
    low_sc[...] = low.astype(jnp.float32)
    slots = value.shape[0]
    group = 8
    one = jnp.ones((16, LANES), jnp.bfloat16)

    def step(number, total):
        left, right = [], []
        for place in range(group):
            slot = number * group + place
            lanes = row_copies(lane_sc, slot)
            left.append(one_hot(row_copies(block_sc, slot), blocks, one))
            right.append(
                jnp.concatenate(
                    [
                        one_hot(lanes, LANES, row_copies(high_sc, slot)),
                        one_hot(lanes, LANES, row_copies(low_sc, slot)),
                    ],
                    axis=0,
                )
            )
        return total + lax.dot_general(
            jnp.concatenate(left, axis=1),
            jnp.concatenate(right, axis=1),
            (((1,), (1,)), ((), ())),
            preferred_element_type=jnp.float32,
        )

    total = lax.fori_loop(0, slots // group, step, jnp.zeros((blocks, 2 * LANES), jnp.float32))
    out_ref[...] = total[:, :LANES] + total[:, LANES:]


def diag_kernel(breadth, blocks, place_ref, cells_ref, bed_ref, diag_ref, *scratch):
    first_row = place_ref[0] - HALO
    scatter_into(diag_ref, bed_ref[...], cells_ref[...], first_row, breadth, blocks, *scratch)


def rhs_kernel(
    breadth, blocks, place_ref, cells_ref, bed_ref, section_ref, row_ref, rhs_ref, slot_section_ref, *scratch
):
    first_row = place_ref[0] - HALO
    rows = section_ref.shape[0]
    slots = row_ref.shape[1]
    index = lax.broadcasted_iota(jnp.int32, (rows, slots), 0)
    pick = jnp.where(index == row_ref[...], 1.0, 0.0).astype(jnp.bfloat16)
    picked = jnp.zeros(slot_section_ref.shape, jnp.float32)
    for piece in bf16_pieces(section_ref[...], 3):
        picked = picked + lax.dot_general(
            pick, piece, (((0,), (0,)), ((), ())), preferred_element_type=jnp.float32
        )
    slot_section_ref[...] = picked
    scatter_into(
        rhs_ref, bed_ref[...] * picked, cells_ref[...], first_row, breadth, blocks, *scratch
    )


def flow_kernel(
    place_ref, ks_ref, alpha_ref, store_ref, block_ref, land_ref, halo_ref, land_halo_ref,
    diag_ref, rhs_ref, riv_halo_ref, head_ref,
    soil_sc, first_sc, ks_sc, alpha_sc, diag_sc, rhs_sc, wx_sc, wy_sc, wz_sc, base_sc, inv_sc,
    ping_sc, pong_sc, land_sc, dtop_sc, rtop_sc,
):
    sources, _, held, window, breadth = block_ref.shape
    layers = sources * held
    span = window - 2 * PAD
    low, high = PAD - HALO, PAD + span
    is_first = place_ref[1] == 1
    is_last = place_ref[2] == 1
    per_row = breadth // LANES

    def put_rows(ref, layer, row, value):
        for part in range(per_row):
            spot = pl.ds(row * layers + layer, value.shape[0], stride=layers)
            ref[part, spot, :] = value[:, part * LANES:(part + 1) * LANES]

    for source in range(sources):
        for held_layer in range(held):
            layer = source * held + held_layer
            put_rows(first_sc, layer, 0, block_ref[source, 0, held_layer])
            put_rows(soil_sc, layer, 0, block_ref[source, 1, held_layer])
    land_sc[...] = land_ref[...]
    dtop_sc[...] = diag_ref[...]
    rtop_sc[...] = rhs_ref[...]
    side = riv_halo_ref.shape[1]
    for chosen, row, block in ((is_first, low, 0), (is_last, high, diag_ref.shape[0] - side)):
        @pl.when(chosen)
        def _(row=row, block=block):
            for layer in range(layers):
                put_rows(first_sc, layer, row, halo_ref[layer])
                put_rows(soil_sc, layer, row, halo_ref[layers + layer])
            land_sc[pl.ds(row, HALO), :] = land_halo_ref[...]
            dtop_sc[pl.ds(block, side), :] = riv_halo_ref[0]
            rtop_sc[pl.ds(block, side), :] = riv_halo_ref[1]

    def get(ref, row):
        spot = pl.ds(pl.multiple_of(row * layers, layers), layers)
        return jnp.concatenate([ref[part, spot, :] for part in range(per_row)], axis=1)

    def put(ref, row, value):
        spot = pl.ds(pl.multiple_of(row * layers, layers), layers)
        for part in range(per_row):
            ref[part, spot, :] = value[:, part * LANES:(part + 1) * LANES]

    level = lax.broadcasted_iota(jnp.int32, (layers, breadth), 0)
    column = lax.broadcasted_iota(jnp.int32, (layers, breadth), 1)
    top = level == 0
    not_bottom = level < layers - 1
    not_last = column < breadth - 1

    def riv_row(ref, row):
        first = (row - low) * per_row
        parts = [
            jnp.broadcast_to(ref[pl.ds(first + part, 1), :], (layers, LANES)) for part in range(per_row)
        ]
        return jnp.where(top, jnp.concatenate(parts, axis=1), 0.0)

    def prepare(row, _):
        soil = get(soil_sc, row)
        ks = jnp.full(soil.shape, ks_ref[0])
        alpha = jnp.full(soil.shape, alpha_ref[0])
        store = jnp.full(soil.shape, store_ref[0])
        for kind in range(1, ks_ref.shape[0]):
            hit = soil == float(kind)
            ks = jnp.where(hit, ks_ref[kind], ks)
            alpha = jnp.where(hit, alpha_ref[kind], alpha)
            store = jnp.where(hit, store_ref[kind], store)
        put(ks_sc, row, ks)
        put(alpha_sc, row, alpha)
        put(diag_sc, row, store + riv_row(dtop_sc, row))
        put(rhs_sc, row, store * get(first_sc, row) + riv_row(rtop_sc, row))
        return 0

    lax.fori_loop(low, window - low, prepare, 0)

    def east(field):
        return pltpu.roll(field, breadth - 1, 1)

    def west(field):
        return pltpu.roll(field, 1, 1)

    def below(field):
        return pltpu.roll(field, layers - 1, 0)

    def above(field):
        return pltpu.roll(field, 1, 0)

    def make_weights(now_sc, first, last):
        def conduct(row):
            cond = get(ks_sc, row) * jnp.exp(get(alpha_sc, row) * jnp.minimum(get(now_sc, row), 0.0))
            return cond, cond * land_sc[pl.ds(row, 1), :]

        def face(factor, cond, opened, far, far_open):
            return factor * 2.0 * opened * far_open / (cond + far)

        def step(row, carried):
            cond, opened, wx_before = carried
            far, far_open = conduct(row + 1)
            wx = face(LATERAL, cond, opened, far, far_open)
            wy = jnp.where(not_last, face(LATERAL, cond, opened, east(cond), east(opened)), 0.0)
            wz = jnp.where(not_bottom, face(VERTICAL, cond, opened, below(cond), below(opened)), 0.0)
            wz_above = above(wz)
            total = get(diag_sc, row) + wx_before + wx + wy + west(wy) + wz + wz_above
            inverse = 1.0 / total
            put(wx_sc, row, wx)
            put(wy_sc, row, wy)
            put(wz_sc, row, wz)
            put(inv_sc, row, inverse)
            put(base_sc, row, get(rhs_sc, row) + GRAVITY * (wz_above - wz))
            return far, far_open, wx

        cond, opened = conduct(first)
        far, far_open = conduct(first + 1)
        wx = face(LATERAL, cond, opened, far, far_open)
        put(wx_sc, first, wx)
        lax.fori_loop(first + 1, last, step, (far, far_open, wx))

    def sweep(now_sc, later_sc, first, last):
        def step(row, carried):
            before, here, wx_before = carried
            after = get(now_sc, row + 1)
            wx = get(wx_sc, row)
            wy = get(wy_sc, row)
            wz = get(wz_sc, row)
            total = get(base_sc, row) + wx_before * before + wx * after
            total = total + wy * east(here) + west(wy * here)
            total = total + wz * below(here) + above(wz * here)
            put(later_sc, row, total * get(inv_sc, row))
            return here, after, wx

        lax.fori_loop(
            first, last, step, (get(now_sc, first - 1), get(now_sc, first), get(wx_sc, first - 1))
        )

    now_sc, spare = first_sc, [ping_sc, pong_sc]
    first, last = low, window - low
    for picard in range(ITERS):
        make_weights(now_sc, first, last - 1)
        for _ in range(SWEEPS):
            first, last = first + 1, last - 1
            later_sc = spare[0]
            sweep(now_sc, later_sc, first, last)
            spare = [spare[1], later_sc]
            now_sc = later_sc
    for layer in range(layers):
        for part in range(per_row):
            spot = pl.ds(PAD * layers + layer, span, stride=layers)
            head_ref[layer, :, pl.ds(part * LANES, LANES)] = now_sc[part, spot, :]


def inflow_kernel(
    place_ref, top_ref, cells_ref, bed_ref, slot_section_ref, row_ref, out_ref,
    block_sc, lane_sc, head_sc, turned_sc,
):
    span, breadth = top_ref.shape
    per_row = breadth // LANES
    blocks = span * per_row
    cells = cells_ref[...]
    block, lane = split_cells(cells, place_ref[0], breadth)
    block_sc[...] = block
    lane_sc[...] = lane
    for part in range(per_row):
        turned_sc[pl.ds(part, span, stride=per_row), :] = top_ref[:, part * LANES:(part + 1) * LANES]
    pieces = bf16_pieces(turned_sc[...].T, 3)
    table = jnp.concatenate(pieces, axis=1)
    slots = cells.shape[0]
    group = 8
    one = jnp.ones((16, LANES), jnp.bfloat16)
    index = lax.broadcasted_iota(jnp.int32, (LANES, LANES), 0).astype(jnp.float32)

    def step(number, _):
        hots = []
        for place in range(group):
            hot = one_hot(row_copies(block_sc, number * group + place), blocks, one)
            hots.append(jnp.concatenate([hot] * len(pieces), axis=0))
        found = lax.dot_general(
            table, jnp.concatenate(hots, axis=1), (((1,), (0,)), ((), ())),
            preferred_element_type=jnp.float32,
        )
        for place in range(group):
            slot = number * group + place
            lanes = jnp.broadcast_to(lane_sc[pl.ds(slot, 1), :], (LANES, LANES))
            mine = jnp.where(index == lanes, found[:, place * LANES:(place + 1) * LANES], 0.0)
            head_sc[pl.ds(slot, 1), :] = jnp.sum(mine, axis=0, keepdims=True)
        return 0

    lax.fori_loop(0, slots // group, step, 0)
    block = block_sc[...]
    inside = (block >= 0.0) & (block < float(blocks))
    slot_in = jnp.where(inside, bed_ref[...] * (head_sc[...] - slot_section_ref[...]), 0.0)
    rows = out_ref.shape[0]
    index = lax.broadcasted_iota(jnp.int32, (rows, slots), 0)
    put = jnp.where(index == row_ref[...], 1.0, 0.0).astype(jnp.bfloat16)
    total = jnp.zeros(out_ref.shape, jnp.float32)
    for piece in bf16_pieces(slot_in, 3):
        total = total + lax.dot_general(
            put, piece, (((1,), (0,)), ((), ())), preferred_element_type=jnp.float32
        )
    out_ref[...] = total


def call(kernel, out_shape, in_specs, scratch, flops, moved):
    single = not isinstance(out_shape, (tuple, list))
    return pl.pallas_call(
        kernel,
        out_shape=out_shape,
        in_specs=in_specs,
        out_specs=in_vmem if single else tuple(in_vmem for _ in out_shape),
        scratch_shapes=scratch,
        compiler_params=pltpu.CompilerParams(vmem_limit_bytes=VMEM_LIMIT),
        cost_estimate=pl.CostEstimate(flops=flops, bytes_accessed=moved, transcendentals=0),
    )


def on_device(
    head_start,
    soil_class,
    land_mask,
    ks_table,
    alpha_table,
    store_table,
    section,
    cross_owner,
    cross_local,
    node_cell,
    bed_cond,
):
    held, across, breadth = head_start.shape
    reach_rows, node_count = section.shape
    tiles = lax.axis_size("tile")
    groups = lax.axis_size("layer")
    layers = held * groups
    span = across // groups
    window = span + 2 * PAD
    per_row = breadth // LANES
    blocks = (span + 2 * HALO) * per_row
    part = lax.axis_index("layer")
    is_first = part == 0
    is_last = part == groups - 1
    place = jnp.stack([part * span, is_first.astype(jnp.int32), is_last.astype(jnp.int32)]).astype(jnp.int32)
    swap = []
    for tile in range(tiles - 1):
        end, start = tile * groups + groups - 1, (tile + 1) * groups
        swap += [(end, start), (start, end)]

    cells = node_cell[0]
    bed = bed_cond[0]
    slots = cells.shape[0]
    reach = cross_owner * reach_rows + cross_local

    both = jnp.stack([head_start, soil_class.astype(jnp.float32)])
    both = jnp.pad(both, ((0, 0), (0, 0), (PAD, PAD), (0, 0)))
    windows = jnp.stack([both[:, :, p * span:p * span + window] for p in range(groups)])
    block = lax.all_to_all(windows, "layer", 0, 0)

    spread = jnp.broadcast_to(section[None], (tiles, reach_rows, node_count))
    whole_section = lax.all_to_all(spread, "tile", 0, 0).reshape(tiles * reach_rows, node_count)

    node_scratch = [pltpu.VMEM((slots, LANES), jnp.float32) for _ in range(4)]
    riv_shape = jax.ShapeDtypeStruct((blocks, LANES), jnp.float32)
    flops = 2 * blocks * 2 * LANES * slots * LANES
    node_bytes = slots * LANES * 4
    diag = call(
        functools.partial(diag_kernel, breadth, blocks), riv_shape, [in_smem, in_vmem, in_vmem],
        node_scratch, flops, 2 * node_bytes,
    )(place, cells, bed)
    rhs, slot_section = call(
        functools.partial(rhs_kernel, breadth, blocks),
        (riv_shape, jax.ShapeDtypeStruct((slots, node_count), jnp.float32)),
        [in_smem] + [in_vmem] * 4, node_scratch, flops, 4 * node_bytes,
    )(place, cells, bed, whole_section, reach)

    land = jnp.pad(land_mask.astype(jnp.float32), ((PAD, PAD), (0, 0)))
    land = lax.dynamic_slice_in_dim(land, part * span, window, 0)

    send_row = jnp.where(is_first, PAD, PAD + span - HALO)
    edge = lax.dynamic_slice_in_dim(block, send_row, HALO, 3)
    edge = jnp.moveaxis(edge, 1, 0).reshape(2 * layers, HALO, breadth)
    edge = jnp.concatenate([edge, lax.dynamic_slice_in_dim(land, send_row, HALO, 0)[None]])
    halo = lax.ppermute(edge, FLAT, swap)
    side = HALO * per_row
    riv = jnp.stack([diag, rhs])
    riv_edge = jnp.where(is_first, riv[:, side:2 * side], riv[:, blocks - 2 * side:blocks - side])
    riv_halo = lax.ppermute(riv_edge, FLAT, swap)

    field = pltpu.VMEM((per_row, window * layers, LANES), jnp.float32)
    out = call(
        flow_kernel, jax.ShapeDtypeStruct((layers, span, breadth), jnp.float32),
        [in_smem] * 4 + [in_vmem] * 7,
        [field] * 13
        + [pltpu.VMEM((window, breadth), jnp.float32)]
        + [pltpu.VMEM((blocks, LANES), jnp.float32)] * 2,
        100 * layers * window * breadth, 8 * layers * window * breadth,
    )(
        place, ks_table, alpha_table, store_table, block, land, halo[:2 * layers], halo[2 * layers],
        diag, rhs, riv_halo,
    )
    back = lax.all_to_all(out.reshape(groups, held, span, breadth), "layer", 0, 0)
    head = jnp.moveaxis(back, 0, 1).reshape(held, across, breadth)

    partial = call(
        inflow_kernel, jax.ShapeDtypeStruct((tiles * reach_rows, node_count), jnp.float32),
        [in_smem] + [in_vmem] * 5,
        [pltpu.VMEM((slots, LANES), jnp.float32)] * 3 + [pltpu.VMEM((span * per_row, LANES), jnp.float32)],
        flops, 4 * node_bytes,
    )(place, out[0], cells, bed, slot_section, reach)
    quarter = node_count // groups
    terms = partial.reshape(tiles, reach_rows, groups, quarter)
    terms = jnp.moveaxis(terms, 2, 1).reshape(tiles * groups, reach_rows, quarter)
    inflow = jnp.sum(lax.all_to_all(terms, FLAT, 0, 0), axis=0)
    return head, inflow


def solution(mesh):
    placed = (
        P("layer", "tile", None),
        P("layer", "tile", None),
        P("tile", None),
        P(),
        P(),
        P(),
        P("tile", None),
        P("tile", None),
        P("tile", None),
        P("tile", None, None),
        P("tile", None, None),
    )
    return jax.shard_map(
        on_device,
        mesh=mesh,
        in_specs=placed,
        out_specs=(P("layer", "tile", None), P("tile", "layer")),
        check_vma=False,
    )
```

time: 710 us -> 103 us (0.15)
  other arithmetic: 386 us -> 3.82 us
  waiting for transfers between devices: 114 us -> 13.2 us
  starting transfers between devices: 105 us -> 15.6 us
  local copies, waits for them, and re-layouts: 56.9 us -> 4.75 us
  Pallas kernels: 0 us -> 49.8 us
  blocking collectives: 30.7 us -> 14.1 us
  between operations: 15.1 us -> 0.91 us
    scatter-add x3 -> x0, other arithmetic: 344 us -> none  [the longest x1 171 us: on_device(): rhs_top = jnp.zeros((across * breadth,), jnp.float32).at[flat_index.resha...]
    ppermute x32 -> x2, starting transfers between devices: 105 us -> 1.34 us  [the longest x1 0.68 us: on_device(): halo = lax.ppermute(edge, FLAT, swap)]
    reduce_scatter x1 -> x0, waiting for transfers between devices: 61.4 us -> none  [on_device(): inflow = lax.psum_scatter(dense, 'tile', scatter_dimension=0, tiled=True)]
    pallas_call x0 -> x4, Pallas kernels: none -> 49.8 us  [the longest x1 20.3 us: on_device(): call(flow_kernel, jax.ShapeDtypeStruct((layers, span, breadth), jnp.float...]
    gather x17 -> x0, local copies, waits for them, and re-layouts: 47.7 us -> none  [the longest x16 46.9 us: one_group(): picked_rows = jnp.take(top_head, flat_cells // breadth, axis=0)]
    psum x1 -> x0, waiting for transfers between devices: 41.5 us -> none  [from_root(): return lax.psum(kept, axis)]
    all_gather x1 -> x0, blocking collectives: 30.7 us -> none  [on_device(): whole_section = lax.all_gather(section, 'tile', axis=0, tiled=True)]
    another operation x4 -> x5, other arithmetic: 17.8 us -> 2.33 us  [the longest x2 1.2 us: on_device(): jnp.stack([both[:, :, p * span:p * span + window] for p in range(groups)])]
  transfers between devices with their start and end apart: 34 -> 5, of which waited for: 13 -> 3; matrix products, arithmetic and copies ran while one was open for 49% -> 2% of each run, Pallas kernels for 0% -> 20%
where the time goes in v1:
time: 103 us; the launch traced here: 102 us
  Pallas kernels  49.8 us (48%)
  starting transfers between devices  15.6 us (15%)
  blocking collectives  14.1 us (14%)
  waiting for transfers between devices  13.2 us (13%)
  local copies, waits for them, and re-layouts  4.75 us (5%)
  other arithmetic  3.82 us (4%)
    pallas_call x1, Pallas kernels, on_device(): call(flow_kernel, jax.ShapeDtypeStruct((layers, span, breadth), jnp.float...  20.3 us
    all_to_all x1, blocking collectives, on_device(): inflow = jnp.sum(lax.all_to_all(terms, FLAT, 0, 0), axis=0)  14.1 us
    pallas_call x1, Pallas kernels, on_device(): call(functools.partial(rhs_kernel, breadth, blocks), (riv_shape, jax.Shap...  10.6 us
    pallas_call x1, Pallas kernels, on_device(): call(functools.partial(diag_kernel, breadth, blocks), riv_shape, [in_smem...  10.3 us
    pallas_call x1, Pallas kernels, on_device(): call(inflow_kernel, jax.ShapeDtypeStruct((tiles * reach_rows, node_count)...  8.5 us
    all_to_all x1, starting transfers between devices, on_device(): lax.all_to_all(spread, 'tile', 0, 0).reshape(tiles * reach_rows, node_count)  6.5 us
    all_to_all x1, waiting for transfers between devices, on_device(): lax.all_to_all(spread, 'tile', 0, 0).reshape(tiles * reach_rows, node_count)  6.22 us
    all_to_all x1, starting transfers between devices, on_device(): block = lax.all_to_all(windows, 'layer', 0, 0)  4.37 us
  transfers between devices with their start and end apart: 5, of which 3 were waited for; matrix products, arithmetic and copies ran while one was open for 2% of the time, Pallas kernels for 20%

profile of v1, /device:TPU:0, one launch (start us, length us, event | category | flops | bytes accessed | tf_op | source)
XLA Modules:
  0.0 102.1 jit_solution(17998429023073772291)
XLA Ops:
  0.6 1.0 convert_bitcast_fusion
  1.8 1.1 %pad_maximum_fusion = f32[4,2,2,32,512]{4,3,2,1,0:T(8,128)} fusion(f32[1,2,2,32,512]{4,3,2,1,0:T(8,128)S(1)} %get-tuple-element.7, f32[1,2,2,32,512]{4,3,2,1,0:T(8,128)S(1)} %get-tuple-element.10, f32[1,2,2,32,512]{4,3,2,1,0:T(8,128)S(1)} %get-tuple-element.11, f32[1,2,2,32,512]{4,3,2,1,0:T(8,128)S(1)} %get-tuple-element.6), kind=kLoop, calls=%fused_computation | loop fusion | flops 786432 | bytes 2097152 | tf_op jit(solution)/shard_map/stack | solution.py:372
  2.9 4.4 %all-to-all-start = ((f32[4,2,2,32,512]{4,3,2,1,0:T(8,128)}), f32[4,2,2,32,512]{4,3,2,1,0:T(8,128)S(1)}, u32[]{:S(2)}, u32[]{:S(2)}) async-start(f32[4,2,2,32,512]{4,3,2,1,0:T(8,128)} %pad_maximum_fusion), calls=%async_computation | async-start | bytes 2097152 | tf_op jit(solution)/shard_map/all_to_all | solution.py:373
  7.5 0.9 copy-done.4
  8.4 10.3 %shard_map.122.diag_ref = f32[112,128]{1,0:T(8,128)S(1)} custom-call(s32[3]{0:T(128)S(1)} %pad_add_fusion.place_ref, s32[256,128]{1,0:T(8,128)S(1)} %bitcast.37, f32[256,128]{1,0:T(8,128)S(1)} %bitcast.40), custom_call_target="tpu_custom_call" | custom-call | flops 1879048192 | bytes 262144 | tf_op jit(solution)/shard_map/pallas_call | solution.py:382
  18.7 3.0 %all-to-all-done.block_ref = f32[4,2,2,32,512]{4,3,2,1,0:T(8,128)S(1)} async-done(((f32[4,2,2,32,512]{4,3,2,1,0:T(8,128)}), f32[4,2,2,32,512]{4,3,2,1,0:T(8,128)S(1)}, u32[]{:S(2)}, u32[]{:S(2)}) %all-to-all-start) | async-done | bytes 1048608 | tf_op jit(solution)/shard_map/all_to_all | solution.py:373
  21.8 0.6 broadcast_in_dim.10
  22.4 6.5 %all-to-all-start.1 = ((f32[8,16,128]{2,1,0:T(8,128)}), f32[8,16,128]{2,1,0:T(8,128)S(1)}, u32[]{:S(2)}, u32[]{:S(2)}) async-start(f32[8,16,128]{2,1,0:T(8,128)} %broadcast_in_dim.10), calls=%async_computation.1 | async-start | bytes 131072 | tf_op jit(solution)/shard_map/all_to_all | solution.py:376
  29.0 0.7 collective-permute-start
  29.7 6.2 %all-to-all-done.1 = f32[8,16,128]{2,1,0:T(8,128)S(1)} async-done(((f32[8,16,128]{2,1,0:T(8,128)}), f32[8,16,128]{2,1,0:T(8,128)S(1)}, u32[]{:S(2)}, u32[]{:S(2)}) %all-to-all-start.1) | async-done | bytes 65568 | tf_op jit(solution)/shard_map/all_to_all | solution.py:376
  35.9 10.6 %shard_map.123 = (f32[112,128]{1,0:T(8,128)S(1)}, f32[256,128]{1,0:T(8,128)S(1)}) custom-call(s32[3]{0:T(128)S(1)} %pad_add_fusion.place_ref, s32[256,128]{1,0:T(8,128)S(1)} %bitcast.38, f32[256,128]{1,0:T(8,128)S(1)} %bitcast.41, f32[128,128]{1,0:T(8,128)S(1)} %bitcast.36, s32[1,256]{1,0:T(1,128)S(1)} %multiply_add_fusion.row_ref), custom_call_target="tpu_custom_call" | custom-call | flops 1879048192 | bytes 524288 | tf_op jit(solution)/shard_map/pallas_call | solution.py:386
  46.5 0.7 collective-permute-start.1
  47.3 0.6 copy-done
  47.9 20.3 %shard_map.124 = f32[8,16,512]{2,1,0:T(8,128)} custom-call(s32[3]{0:T(128)S(1)} %pad_add_fusion.place_ref, f32[12]{0:T(128)S(1)} %copy-done, f32[12]{0:T(128)S(1)} %copy-done.1, f32[12]{0:T(128)S(1)} %copy-done.2, f32[4,2,2,32,512]{4,3,2,1,0:T(8,128)S(1)} %all-to-all-done.block_ref, f32[32,512]{1,0:T(8,128)S(1)} %pad_dynamic-slice_fusion.1.land_ref, ...), custom_call_target="tpu_custom_call" | custom-call | flops 13107200 | bytes 1048576 | tf_op jit(solution)/shard_map/pallas_call | solution.py:406
  68.3 0.8 slice_bitcast_fusion.top_ref
  69.0 8.5 %shard_map.125 = f32[128,128]{1,0:T(8,128)S(1)} custom-call(s32[3]{0:T(128)S(1)} %pad_add_fusion.place_ref, f32[16,512]{1,0:T(8,128)S(1)} %slice_bitcast_fusion.top_ref, s32[256,128]{1,0:T(8,128)S(1)} %bitcast.39, f32[256,128]{1,0:T(8,128)S(1)} %bitcast.42, f32[256,128]{1,0:T(8,128)S(1)} %get-tuple-element.5.slot_section_ref, ...), custom_call_target="tpu_custom_call" | custom-call | flops 1879048192 | bytes 524288 | tf_op jit(solution)/shard_map/pallas_call | solution.py:420
  77.5 0.2 reshape.27
  77.9 14.1 %all_to_all.20 = f32[32,1,512]{2,1,0:T(1,128)S(1)} all-to-all(f32[32,1,512]{2,1,0:T(1,128)S(1)} %reshape.31), channel_id=1, replica_groups=mesh['tile'=8,'layer'=4] {'tile','layer'}, dimensions={0} | all-to-all | bytes 131072 | tf_op jit(solution)/shard_map/all_to_all | solution.py:429
  92.0 3.4 %all-to-all-start.2 = ((f32[4,2,16,512]{3,2,1,0:T(8,128)}), f32[4,2,16,512]{3,2,1,0:T(8,128)S(1)}, u32[]{:S(2)}, u32[]{:S(2)}) async-start(f32[4,2,16,512]{3,2,1,0:T(8,128)} %bitcast.18), calls=%async_computation.2 | async-start | bytes 524288 | tf_op jit(solution)/shard_map/all_to_all | solution.py:417
  95.4 0.5 broadcast.5
  95.9 0.8 reduce
  96.8 0.6 reduce_sum.9
  97.5 3.9 %all-to-all-done.2 = f32[4,2,16,512]{3,2,1,0:T(8,128)S(1)} async-done(((f32[4,2,16,512]{3,2,1,0:T(8,128)}), f32[4,2,16,512]{3,2,1,0:T(8,128)S(1)}, u32[]{:S(2)}, u32[]{:S(2)}) %all-to-all-start.2) | async-done | bytes 262176 | tf_op jit(solution)/shard_map/all_to_all | solution.py:417
  101.4 0.7 copy.16
  (36 shorter events, 0.8 us)
Async XLA Ops:
  0.6 1.0 %copy-start.5 = (f32[2,64,512]{2,1,0:T(8,128)S(1)}, f32[2,64,512]{2,1,0:T(8,128)}, u32[]{:S(2)}) copy-start(f32[2,64,512]{2,1,0:T(8,128)} %param.11) | copy-start | bytes 786436
  2.9 4.4 %copy-start.6 = (s32[64,512]{1,0:T(8,128)S(1)}, s32[64,512]{1,0:T(8,128)}, u32[]{:S(2)}) copy-start(s32[64,512]{1,0:T(8,128)} %param.13) | copy-start | bytes 393220
  2.9 18.8 %all-to-all-start = ((f32[4,2,2,32,512]{4,3,2,1,0:T(8,128)}), f32[4,2,2,32,512]{4,3,2,1,0:T(8,128)S(1)}, u32[]{:S(2)}, u32[]{:S(2)}) async-start(f32[4,2,2,32,512]{4,3,2,1,0:T(8,128)} %pad_maximum_fusion), calls=%async_computation | async-start | bytes 2097152 | tf_op jit(solution)/shard_map/all_to_all | solution.py:373
  7.4 0.9 copy-start.4
  7.4 1.0 copy-start.3
  8.4 10.3 %copy-start.8 = (s32[1,256]{1,0:T(1,128)S(1)}, s32[1,256]{1,0:T(1,128)}, u32[]{:S(2)}) copy-start(s32[1,256]{1,0:T(1,128)} %param.19) | copy-start | bytes 3076
  8.4 10.3 %copy-start.9 = (s32[1,256]{1,0:T(1,128)S(1)}, s32[1,256]{1,0:T(1,128)}, u32[]{:S(2)}) copy-start(s32[1,256]{1,0:T(1,128)} %param.18) | copy-start | bytes 3076
  8.4 13.4 %copy-start.7 = (f32[16,128]{1,0:T(8,128)S(1)}, f32[16,128]{1,0:T(8,128)}, u32[]{:S(2)}) copy-start(f32[16,128]{1,0:T(8,128)} %param.17) | copy-start | bytes 24580
  22.4 13.5 %all-to-all-start.1 = ((f32[8,16,128]{2,1,0:T(8,128)}), f32[8,16,128]{2,1,0:T(8,128)S(1)}, u32[]{:S(2)}, u32[]{:S(2)}) async-start(f32[8,16,128]{2,1,0:T(8,128)} %broadcast_in_dim.10), calls=%async_computation.1 | async-start | bytes 131072 | tf_op jit(solution)/shard_map/all_to_all | solution.py:376
  29.0 18.2 %collective-permute-start = (f32[17,6,512]{2,1,0:T(8,128)S(1)}, f32[17,6,512]{2,1,0:T(8,128)S(1)}, u32[]{:S(2)}, u32[]{:S(2)}) collective-permute-start(f32[17,6,512]{2,1,0:T(8,128)S(1)} %pad_maximum_fusion.2), channel_id=1, source_target_pairs={{3,4},{4,3},{7,8},{8,7},{11,12},{12,11},{15,16},{16,15},{19,20},{2... | collective-permute-start | bytes 626696 | tf_op jit(solution)/shard_map/ppermute | solution.py:399
  46.5 0.8 collective-permute-start.1
  47.2 0.7 copy-start
  47.3 0.7 copy-start.1
  47.3 0.7 copy-start.2
  92.0 9.4 %all-to-all-start.2 = ((f32[4,2,16,512]{3,2,1,0:T(8,128)}), f32[4,2,16,512]{3,2,1,0:T(8,128)S(1)}, u32[]{:S(2)}, u32[]{:S(2)}) async-start(f32[4,2,16,512]{3,2,1,0:T(8,128)} %bitcast.18), calls=%async_computation.2 | async-start | bytes 524288 | tf_op jit(solution)/shard_map/all_to_all | solution.py:417

commit v2 on v1

v2 whole, which is shorter than its diff:
```python
import functools

import jax
import jax.numpy as jnp
from jax import lax
from jax.experimental import pallas as pl
from jax.experimental.pallas import tpu as pltpu
from jax.sharding import PartitionSpec as P

ITERS = 2
SWEEPS = 3

LATERAL = 1.0
VERTICAL = 2.0
GRAVITY = 1.0

PAD = 8
HALO = ITERS * SWEEPS
LANES = 128
VMEM_LIMIT = 48 * 1024 * 1024
FLAT = ("tile", "layer")

in_vmem = pl.BlockSpec(memory_space=pltpu.VMEM)
in_smem = pl.BlockSpec(memory_space=pltpu.SMEM)


def bf16_pieces(value, count):
    pieces = []
    for _ in range(count):
        piece = value.astype(jnp.bfloat16)
        pieces.append(piece)
        value = value - piece.astype(jnp.float32)
    return pieces


def one_hot(row, size, on):
    index = lax.broadcasted_iota(jnp.int32, (16, LANES), 0)
    zero = jnp.zeros((16, LANES), jnp.bfloat16)
    tiles = []
    for start in range(0, size, 16):
        here = (index + start).astype(jnp.float32).astype(jnp.bfloat16)
        tiles.append(jnp.where(row == here, on, zero))
    return jnp.concatenate(tiles, axis=0)


def row_copies(ref, slot):
    return jnp.broadcast_to(ref[pl.ds(slot, 1), :], (16, LANES)).astype(jnp.bfloat16)


def split_cells(cells, first_row, breadth, width):
    local = cells - first_row * breadth
    shift = width.bit_length() - 1
    block = jnp.where(cells < 0, -1, local >> shift)
    return block.astype(jnp.float32), (local & (width - 1)).astype(jnp.float32)


def river_kernel(
    breadth, place_ref, cells_ref, bed_ref, section_ref, row_ref, diag_ref, rhs_ref, slot_section_ref,
    spot_sc, dhigh_sc, dlow_sc, rhigh_sc, rlow_sc, turned_sc, sum_sc,
):
    rows = section_ref.shape[0]
    slots = row_ref.shape[1]
    index = lax.broadcasted_iota(jnp.int32, (rows, slots), 0)
    pick = jnp.where(index == row_ref[...], 1.0, 0.0).astype(jnp.bfloat16)
    picked = jnp.zeros(slot_section_ref.shape, jnp.float32)
    for piece in bf16_pieces(section_ref[...], 3):
        picked = picked + lax.dot_general(
            pick, piece, (((0,), (0,)), ((), ())), preferred_element_type=jnp.float32
        )
    slot_section_ref[...] = picked

    half = LANES // 2
    block, spot = split_cells(cells_ref[...], place_ref[0] - HALO, breadth, half)
    spot_sc[...] = spot
    bed = bed_ref[...]
    for value, high_sc, low_sc in ((bed, dhigh_sc, dlow_sc), (bed * picked, rhigh_sc, rlow_sc)):
        high, low = bf16_pieces(value, 2)
        high_sc[...] = high.astype(jnp.float32)
        low_sc[...] = low.astype(jnp.float32)
    blocks = 2 * diag_ref.shape[0]
    group = 32
    tiles = slots // LANES
    for part in range(tiles):
        turned_sc[part] = block[part * LANES:(part + 1) * LANES, :].T
    names = lax.broadcasted_iota(jnp.int32, (LANES, LANES), 1)
    names = [(names + start).astype(jnp.float32).astype(jnp.bfloat16) for start in range(0, blocks, LANES)]
    one = jnp.ones((LANES, LANES), jnp.bfloat16)
    zero = jnp.zeros((LANES, LANES), jnp.bfloat16)

    def step(number, total):
        first = number * group
        columns = turned_sc[first // LANES]
        columns = pltpu.roll(columns, lax.rem(LANES - lax.rem(first, LANES), LANES), 1)
        left, right = [], []
        for place in range(group):
            slot = first + place
            spots = row_copies(spot_sc, slot)
            left.append(
                jnp.concatenate(
                    [one_hot(spots, half, row_copies(ref, slot)) for ref in (dhigh_sc, dlow_sc, rhigh_sc, rlow_sc)],
                    axis=0,
                )
            )
            column = jnp.broadcast_to(columns[:, place:place + 1], (LANES, LANES)).astype(jnp.bfloat16)
            right.append(jnp.concatenate([jnp.where(column == name, one, zero) for name in names], axis=1))
        return total + lax.dot_general(
            jnp.concatenate(left, axis=1),
            jnp.concatenate(right, axis=0),
            (((1,), (0,)), ((), ())),
            preferred_element_type=jnp.float32,
        )

    total = lax.fori_loop(0, slots // group, step, jnp.zeros((4 * half, len(names) * LANES), jnp.float32))
    both = jnp.concatenate([total[:half] + total[half:2 * half], total[2 * half:3 * half] + total[3 * half:]], axis=0)
    for part in range(len(names)):
        sum_sc[pl.ds(part * LANES, LANES), :] = both[:, part * LANES:(part + 1) * LANES].T
    low_half = lax.broadcasted_iota(jnp.int32, diag_ref.shape, 1) < half
    even = sum_sc[pl.ds(0, blocks // 2, stride=2), :]
    odd = sum_sc[pl.ds(1, blocks // 2, stride=2), :]
    diag_ref[...] = jnp.where(low_half, even, pltpu.roll(odd, half, 1))
    rhs_ref[...] = jnp.where(low_half, pltpu.roll(even, half, 1), odd)


def prepare_kernel(place_ref, head_ref, soil_ref, section_ref, land_ref, *out_refs):
    window_refs, spread_ref, land_out_ref = out_refs[:-2], out_refs[-2], out_refs[-1]
    groups = len(window_refs)
    _, held, window, _ = window_refs[0].shape
    across = head_ref.shape[1]
    span = across // groups

    def span_of(target):
        return jnp.where(place_ref[3] == 1, groups - 1 - target, target)

    def pieces(number):
        for start in range(0, window, PAD):
            row = jnp.clip(number * span - PAD + start, 0, across - PAD)
            yield pl.ds(start, PAD), pl.ds(pl.multiple_of(row, PAD), PAD)

    for step, out_ref in enumerate(window_refs):
        for to, spot in pieces(span_of(place_ref[4] ^ step)):
            for layer in range(held):
                out_ref[0, layer, to, :] = head_ref[layer, spot, :]
                out_ref[1, layer, to, :] = soil_ref[layer, spot, :].astype(jnp.float32)
    for to, spot in pieces(span_of(place_ref[4])):
        land_out_ref[to, :] = land_ref[spot, :].astype(jnp.float32)
    section = section_ref[...]
    for tile in range(spread_ref.shape[0]):
        spread_ref[tile] = section


def flow_kernel(
    groups, place_ref, ks_ref, alpha_ref, store_ref, land_ref, halo_ref, diag_ref, rhs_ref, *refs,
):
    block_refs, head_refs = refs[:groups], refs[groups:2 * groups]
    (
        soil_sc, first_sc, ks_sc, alpha_sc, diag_sc, rhs_sc, wx_sc, wy_sc, wz_sc, base_sc, inv_sc,
        ping_sc, pong_sc, land_sc, dtop_sc, rtop_sc,
    ) = refs[2 * groups:]
    _, held, window, breadth = block_refs[0].shape
    layers = groups * held
    span = window - 2 * PAD
    low, high = PAD - HALO, PAD + span
    is_first = place_ref[1] == 1
    is_last = place_ref[2] == 1
    per_row = breadth // LANES

    def put_rows(ref, layer, row, value):
        for part in range(per_row):
            spot = pl.ds(row * layers + layer, value.shape[0], stride=layers)
            ref[part, spot, :] = value[:, part * LANES:(part + 1) * LANES]

    for step, block_ref in enumerate(block_refs):
        for held_layer in range(held):
            layer = (place_ref[4] ^ step) * held + held_layer
            put_rows(first_sc, layer, 0, block_ref[0, held_layer])
            put_rows(soil_sc, layer, 0, block_ref[1, held_layer])
    land_sc[...] = land_ref[...]
    dtop_sc[...] = diag_ref[...]
    rtop_sc[...] = rhs_ref[...]
    for chosen, row in ((is_first, low), (is_last, high)):
        @pl.when(chosen)
        def _(row=row):
            for entry in range(layers):
                layer = (place_ref[4] ^ (entry // held)) * held + entry % held
                put_rows(first_sc, layer, row, halo_ref[entry])
                put_rows(soil_sc, layer, row, halo_ref[layers + entry])
            land_sc[pl.ds(row, HALO), :] = halo_ref[2 * layers]
            for part in range(per_row):
                spot = pl.ds((row - low) * per_row + part, HALO, stride=per_row)
                lanes = pl.ds(part * LANES, LANES)
                dtop_sc[spot, :] = halo_ref[2 * layers + 1, :, lanes]
                rtop_sc[spot, :] = halo_ref[2 * layers + 2, :, lanes]

    def get(ref, row):
        spot = pl.ds(row * layers, layers)
        return jnp.concatenate([ref[part, spot, :] for part in range(per_row)], axis=1)

    def put(ref, row, value):
        spot = pl.ds(row * layers, layers)
        for part in range(per_row):
            ref[part, spot, :] = value[:, part * LANES:(part + 1) * LANES]

    level = lax.broadcasted_iota(jnp.int32, (layers, breadth), 0)
    column = lax.broadcasted_iota(jnp.int32, (layers, breadth), 1)
    top = level == 0
    not_bottom = level < layers - 1
    not_last = column < breadth - 1

    def riv_row(ref, row):
        first = (row - low) * per_row
        parts = [
            jnp.broadcast_to(ref[pl.ds(first + part, 1), :], (layers, LANES)) for part in range(per_row)
        ]
        return jnp.where(top, jnp.concatenate(parts, axis=1), 0.0)

    lane = lax.broadcasted_iota(jnp.int32, (layers, LANES), 1)

    def lane_table(ref):
        table = jnp.zeros((layers, LANES), jnp.float32)
        for kind in range(ref.shape[0]):
            table = jnp.where(lane == kind, ref[kind], table)
        return table

    tables = [lane_table(ref) for ref in (ks_ref, alpha_ref, store_ref)]

    def lookup(soil):
        found = []
        for table in tables:
            parts = [
                jnp.take_along_axis(
                    table, soil[:, part * LANES:(part + 1) * LANES], axis=1, mode="promise_in_bounds"
                )
                for part in range(per_row)
            ]
            found.append(jnp.concatenate(parts, axis=1))
        return found

    for row in range(low, window - low):
        ks, alpha, store = lookup(get(soil_sc, row).astype(jnp.int32))
        put(ks_sc, row, ks)
        put(alpha_sc, row, alpha)
        put(diag_sc, row, store + riv_row(dtop_sc, row))
        put(rhs_sc, row, store * get(first_sc, row) + riv_row(rtop_sc, row))

    def east(field):
        return pltpu.roll(field, breadth - 1, 1)

    def west(field):
        return pltpu.roll(field, 1, 1)

    def below(field):
        return pltpu.roll(field, layers - 1, 0)

    def above(field):
        return pltpu.roll(field, 1, 0)

    def make_weights(now_sc, first, last):
        def conduct(row):
            cond = get(ks_sc, row) * jnp.exp(get(alpha_sc, row) * jnp.minimum(get(now_sc, row), 0.0))
            return cond, cond * land_sc[pl.ds(row, 1), :]

        def face(factor, cond, opened, far, far_open):
            return factor * 2.0 * opened * far_open / (cond + far)

        def step(row, carried):
            cond, opened, wx_before = carried
            far, far_open = conduct(row + 1)
            wx = face(LATERAL, cond, opened, far, far_open)
            wy = jnp.where(not_last, face(LATERAL, cond, opened, east(cond), east(opened)), 0.0)
            wz = jnp.where(not_bottom, face(VERTICAL, cond, opened, below(cond), below(opened)), 0.0)
            wz_above = above(wz)
            total = get(diag_sc, row) + wx_before + wx + wy + west(wy) + wz + wz_above
            inverse = 1.0 / total
            put(wx_sc, row, wx)
            put(wy_sc, row, wy)
            put(wz_sc, row, wz)
            put(inv_sc, row, inverse)
            put(base_sc, row, get(rhs_sc, row) + GRAVITY * (wz_above - wz))
            return far, far_open, wx

        cond, opened = conduct(first)
        far, far_open = conduct(first + 1)
        wx = face(LATERAL, cond, opened, far, far_open)
        put(wx_sc, first, wx)
        carried = far, far_open, wx
        for row in range(first + 1, last):
            carried = step(row, carried)

    def sweep(now_sc, later_sc, first, last):
        def step(row, carried):
            before, here, wx_before = carried
            after = get(now_sc, row + 1)
            wx = get(wx_sc, row)
            wy = get(wy_sc, row)
            wz = get(wz_sc, row)
            total = get(base_sc, row) + wx_before * before + wx * after
            total = total + wy * east(here) + west(wy * here)
            total = total + wz * below(here) + above(wz * here)
            put(later_sc, row, total * get(inv_sc, row))
            return here, after, wx

        carried = get(now_sc, first - 1), get(now_sc, first), get(wx_sc, first - 1)
        for row in range(first, last):
            carried = step(row, carried)

    now_sc, spare = first_sc, [ping_sc, pong_sc]
    first, last = low, window - low
    for picard in range(ITERS):
        make_weights(now_sc, first, last - 1)
        for _ in range(SWEEPS):
            first, last = first + 1, last - 1
            later_sc = spare[0]
            sweep(now_sc, later_sc, first, last)
            spare = [spare[1], later_sc]
            now_sc = later_sc
    for part in range(per_row):
        lanes = pl.ds(part * LANES, LANES)
        top_rows = now_sc[part, pl.ds(PAD * layers, span, stride=layers), :]
        for step, head_ref in enumerate(head_refs):
            for held_layer in range(held):
                layer = (place_ref[4] ^ step) * held + held_layer
                head_ref[held_layer, :, lanes] = now_sc[part, pl.ds(PAD * layers + layer, span, stride=layers), :]
            head_ref[held, :, lanes] = top_rows


def inflow_kernel(
    groups, place_ref, cells_ref, bed_ref, slot_section_ref, row_ref, *refs,
):
    back_refs = refs[:groups]
    head_ref, out_ref, block_sc, lane_sc, found_sc, turned_sc = refs[groups:]
    _, span, breadth = back_refs[0].shape
    held, across, _ = head_ref.shape
    per_row = breadth // LANES
    blocks = across * per_row
    slots = cells_ref.shape[0]
    quarter = LANES // groups
    packed = slots // groups
    flip = place_ref[3]
    for step, back_ref in enumerate(back_refs):
        source = place_ref[4] ^ step
        number = jnp.where(flip == 1, groups - 1 - source, source)
        rows = pl.ds(pl.multiple_of(number * span, span), span)
        for layer in range(held):
            head_ref[layer, rows, :] = back_ref[layer]
        for part in range(per_row):
            spot = pl.ds(number * span * per_row + part, span, stride=per_row)
            turned_sc[spot, :] = back_ref[held, :, part * LANES:(part + 1) * LANES]

    own = lax.broadcasted_iota(jnp.int32, (packed, LANES), 1) // quarter

    def pack(ref):
        result = None
        for number in range(groups):
            shift = lax.rem((number + groups - place_ref[4]) * quarter, LANES)
            moved = pltpu.roll(ref[pl.ds(number * packed, packed), :], shift, 1)
            result = moved if result is None else jnp.where(own == number, moved, result)
        return result

    cells = pack(cells_ref)
    block, lane = split_cells(cells, 0, breadth, LANES)
    block_sc[...] = block
    lane_sc[...] = lane
    pieces = bf16_pieces(turned_sc[...].T, 2)
    group = 32
    one = jnp.ones((16, LANES), jnp.bfloat16)
    index = lax.broadcasted_iota(jnp.int32, (LANES, LANES), 0).astype(jnp.float32)

    def step(number, _):
        hots = jnp.concatenate(
            [one_hot(row_copies(block_sc, number * group + place), blocks, one) for place in range(group)], axis=1
        )
        found = jnp.zeros((LANES, group * LANES), jnp.float32)
        for piece in pieces:
            found = found + lax.dot_general(
                piece, hots, (((1,), (0,)), ((), ())), preferred_element_type=jnp.float32
            )
        for place in range(group):
            row = number * group + place
            lanes = jnp.broadcast_to(lane_sc[pl.ds(row, 1), :], (LANES, LANES))
            mine = jnp.where(index == lanes, found[:, place * LANES:(place + 1) * LANES], 0.0)
            found_sc[pl.ds(row, 1), :] = jnp.sum(mine, axis=0, keepdims=True)
        return 0

    lax.fori_loop(0, packed // group, step, 0)
    slot_in = jnp.where(cells >= 0, pack(bed_ref) * (found_sc[...] - pack(slot_section_ref)), 0.0)
    spread = jnp.concatenate(
        [slot_in if number == 0 else pltpu.roll(slot_in, LANES - number * quarter, 1) for number in range(groups)],
        axis=0,
    )
    rows = out_ref.shape[0]
    index = lax.broadcasted_iota(jnp.int32, (rows, slots), 0)
    put = jnp.where(index == row_ref[...], 1.0, 0.0).astype(jnp.bfloat16)
    total = jnp.zeros((rows, LANES), jnp.float32)
    for piece in bf16_pieces(spread, 3):
        total = total + lax.dot_general(
            put, piece, (((1,), (0,)), ((), ())), preferred_element_type=jnp.float32
        )
    out_ref[...] = total


def call(kernel, out_shape, in_specs, scratch, flops, moved):
    single = not isinstance(out_shape, (tuple, list))
    return pl.pallas_call(
        kernel,
        out_shape=out_shape,
        in_specs=in_specs,
        out_specs=in_vmem if single else tuple(in_vmem for _ in out_shape),
        scratch_shapes=scratch,
        compiler_params=pltpu.CompilerParams(vmem_limit_bytes=VMEM_LIMIT),
        cost_estimate=pl.CostEstimate(flops=flops, bytes_accessed=moved, transcendentals=0),
    )


def on_device(
    head_start,
    soil_class,
    land_mask,
    ks_table,
    alpha_table,
    store_table,
    section,
    cross_owner,
    cross_local,
    node_cell,
    bed_cond,
):
    held, across, breadth = head_start.shape
    reach_rows, node_count = section.shape
    tiles = lax.axis_size("tile")
    groups = lax.axis_size("layer")
    layers = held * groups
    span = across // groups
    window = span + 2 * PAD
    per_row = breadth // LANES
    blocks = (span + 2 * HALO) * per_row
    tile = lax.axis_index("tile")
    layer = lax.axis_index("layer")
    flip = lax.rem(tile, 2) == 1
    number = jnp.where(flip, groups - 1 - layer, layer)
    is_first = number == 0
    is_last = number == groups - 1
    place = jnp.stack([number * span, is_first, is_last, flip, layer]).astype(jnp.int32)
    swap = []
    for upper in range(tiles - 1):
        index = groups - 1 if upper % 2 == 0 else 0
        one, two = upper * groups + index, (upper + 1) * groups + index
        swap += [(one, two), (two, one)]

    cells = node_cell[0]
    bed = bed_cond[0]
    slots = cells.shape[0]
    reach = cross_owner * reach_rows + cross_local

    def exchange(parts):
        received = [parts[0]]
        for step in range(1, groups):
            received.append(lax.ppermute(parts[step], "layer", [(i, i ^ step) for i in range(groups)]))
        return received

    field_bytes = held * across * breadth * 4
    window_shape = jax.ShapeDtypeStruct((2, held, window, breadth), jnp.float32)
    *windows, spread, land = call(
        prepare_kernel,
        (window_shape,) * groups
        + (
            jax.ShapeDtypeStruct((tiles, reach_rows, node_count), jnp.float32),
            jax.ShapeDtypeStruct((window, breadth), jnp.float32),
        ),
        [in_smem] + [in_vmem] * 4, [], 0, 8 * field_bytes,
    )(place, head_start, soil_class, section, land_mask)
    whole_section = lax.all_to_all(spread, "tile", 0, 0).reshape(tiles * reach_rows, node_count)
    received = exchange(windows)

    node_scratch = pltpu.VMEM((slots, LANES), jnp.float32)
    riv_shape = jax.ShapeDtypeStruct((blocks, LANES), jnp.float32)
    node_bytes = slots * LANES * 4
    diag, rhs, slot_section = call(
        functools.partial(river_kernel, breadth),
        (riv_shape, riv_shape, jax.ShapeDtypeStruct((slots, node_count), jnp.float32)),
        [in_smem] + [in_vmem] * 4,
        [node_scratch] * 5
        + [pltpu.VMEM((slots // LANES, LANES, LANES), jnp.float32)]
        + [pltpu.VMEM((-(-2 * blocks // LANES) * LANES, LANES), jnp.float32)],
        2 * blocks * 4 * LANES * slots * LANES, 4 * node_bytes,
    )(place, cells, bed, whole_section, reach)

    send_row = jnp.where(is_first, PAD, PAD + span - HALO)
    edges = [lax.dynamic_slice_in_dim(block, send_row, HALO, 2) for block in received]
    edge = jnp.stack(edges, axis=1).reshape(2 * layers, HALO, breadth)
    edge = jnp.concatenate([edge, lax.dynamic_slice_in_dim(land, send_row, HALO, 0)[None]])
    side = HALO * per_row
    riv = jnp.stack([diag, rhs])
    riv_edge = jnp.where(is_first, riv[:, side:2 * side], riv[:, blocks - 2 * side:blocks - side])
    edge = jnp.concatenate([edge, riv_edge.reshape(2, HALO, breadth)])
    halo = lax.ppermute(edge, FLAT, swap)

    field = pltpu.VMEM((per_row, window * layers, LANES), jnp.float32)
    out_shape = jax.ShapeDtypeStruct((held + 1, span, breadth), jnp.float32)
    out = call(
        functools.partial(flow_kernel, groups), (out_shape,) * groups,
        [in_smem] * 4 + [in_vmem] * (4 + groups),
        [field] * 13
        + [pltpu.VMEM((window, breadth), jnp.float32)]
        + [pltpu.VMEM((blocks, LANES), jnp.float32)] * 2,
        100 * layers * window * breadth, 8 * layers * window * breadth,
    )(place, ks_table, alpha_table, store_table, land, halo, diag, rhs, *received)
    back = exchange(out)

    packed = pltpu.VMEM((slots // groups, LANES), jnp.float32)
    head, partial = call(
        functools.partial(inflow_kernel, groups),
        (
            jax.ShapeDtypeStruct(head_start.shape, jnp.float32),
            jax.ShapeDtypeStruct((tiles * reach_rows, node_count), jnp.float32),
        ),
        [in_smem] + [in_vmem] * (4 + groups),
        [packed] * 3 + [pltpu.VMEM((across * per_row, LANES), jnp.float32)],
        4 * across * breadth * slots * node_count // groups, 8 * node_bytes,
    )(place, cells, bed, slot_section, reach, *back)
    terms = lax.all_to_all(partial.reshape(tiles, reach_rows, node_count), "tile", 0, 0)
    return head, jnp.sum(terms, axis=0)[:, :node_count // groups]


def solution(mesh):
    placed = (
        P("layer", "tile", None),
        P("layer", "tile", None),
        P("tile", None),
        P(),
        P(),
        P(),
        P("tile", None),
        P("tile", None),
        P("tile", None),
        P("tile", None, None),
        P("tile", None, None),
    )
    return jax.shard_map(
        on_device,
        mesh=mesh,
        in_specs=placed,
        out_specs=(P("layer", "tile", None), P("tile", "layer")),
        check_vma=False,
    )
```

time: 103 us -> 66.3 us (0.64)
  Pallas kernels: 49.8 us -> 20 us
  other arithmetic: 3.82 us -> 0.68 us
  waiting for transfers between devices: 13.2 us -> 10.1 us
  starting transfers between devices: 15.6 us -> 17.1 us
  local copies, waits for them, and re-layouts: 4.75 us -> 3.61 us
    pallas_call x4, Pallas kernels: 49.8 us -> 20 us  [the longest x1 8.71 us: on_device(): call(functools.partial(river_kernel, breadth), (riv_shape, riv_shape, jax...]
    ppermute x1 -> x6, starting transfers between devices: 0.66 us -> 9.06 us  [exchange(): lax.ppermute(parts[step], 'layer', [(i, i ^ step) for i in range(groups)])]
    all_to_all x2 -> x0, starting transfers between devices: 7.77 us -> none  [the longest x1 4.37 us: on_device(): block = lax.all_to_all(windows, 'layer', 0, 0)]
    all_to_all x2 -> x0, waiting for transfers between devices: 6.97 us -> none  [the longest x1 3.93 us: on_device(): lax.all_to_all(out.reshape(groups, held, span, breadth), 'layer', 0, 0)]
    ppermute x1 -> x6, waiting for transfers between devices: 0.01 us -> 5.15 us  [exchange(): lax.ppermute(parts[step], 'layer', [(i, i ^ step) for i in range(groups)])]
    another operation x5 -> x1, other arithmetic: 2.33 us -> 0.03 us  [on_device(): edge = jnp.stack(edges, axis=1).reshape(2 * layers, HALO, breadth)]
    unnamed x22, local copies, waits for them, and re-layouts: 1.85 us -> 3.44 us
    all_to_all x1, waiting for transfers between devices: 6.22 us -> 4.99 us  [on_device(): lax.all_to_all(spread, 'tile', 0, 0).reshape(tiles * reach_rows, node_count)]
  transfers between devices with their start and end apart: 5 -> 8, of which waited for: 3 -> 3; matrix products, arithmetic and copies ran while one was open for 2% -> 0% of each run, Pallas kernels for 20% -> 13%
where the time goes in v2:
time: 66.3 us; the launch traced here: 66 us
  Pallas kernels  20 us (30%)
  starting transfers between devices  17.1 us (26%)
  blocking collectives  13.6 us (21%)
  waiting for transfers between devices  10.1 us (15%)
  local copies, waits for them, and re-layouts  3.61 us (5%)
  between operations  0.85 us (1%)
  other arithmetic  0.68 us (1%)
    all_to_all x1, blocking collectives, on_device(): lax.all_to_all(partial.reshape(tiles, reach_rows, node_count), 'tile', 0, 0)  13.6 us
    ppermute x6, starting transfers between devices, exchange(): lax.ppermute(parts[step], 'layer', [(i, i ^ step) for i in range(groups)])  9.06 us
    pallas_call x1, Pallas kernels, on_device(): call(functools.partial(river_kernel, breadth), (riv_shape, riv_shape, jax...  8.71 us
    all_to_all x1, starting transfers between devices, on_device(): lax.all_to_all(spread, 'tile', 0, 0).reshape(tiles * reach_rows, node_count)  7.38 us
    pallas_call x1, Pallas kernels, on_device(): call(functools.partial(flow_kernel, groups), (out_shape,) * groups, [in_s...  6.92 us
    ppermute x6, waiting for transfers between devices, exchange(): lax.ppermute(parts[step], 'layer', [(i, i ^ step) for i in range(groups)])  5.15 us
    all_to_all x1, waiting for transfers between devices, on_device(): lax.all_to_all(spread, 'tile', 0, 0).reshape(tiles * reach_rows, node_count)  4.99 us
    unnamed x22, local copies, waits for them, and re-layouts  3.44 us
  transfers between devices with their start and end apart: 8, of which 3 were waited for; matrix products, arithmetic and copies ran while one was open for 0% of the time, Pallas kernels for 13%

profile of v2, /device:TPU:0, one launch (start us, length us, event | category | flops | bytes accessed | tf_op | source)
XLA Modules:
  0.0 66.0 jit_solution(11936445261140423587)
XLA Ops:
  0.7 0.1 stack.59.place_ref
  0.7 0.6 copy-done.3
  1.3 0.9 %copy-done = f32[2,64,512]{2,1,0:T(8,128)S(1)} copy-done((f32[2,64,512]{2,1,0:T(8,128)S(1)}, f32[2,64,512]{2,1,0:T(8,128)}, u32[]{:S(2)}) %copy-start) | copy-done | bytes 262168
  2.3 0.9 %copy-done.1 = s32[2,64,512]{2,1,0:T(8,128)S(1)} copy-done((s32[2,64,512]{2,1,0:T(8,128)S(1)}, s32[2,64,512]{2,1,0:T(8,128)}, u32[]{:S(2)}) %copy-start.1) | copy-done | bytes 262168
  3.2 0.9 %copy-done.2 = s32[64,512]{1,0:T(8,128)S(1)} copy-done((s32[64,512]{1,0:T(8,128)S(1)}, s32[64,512]{1,0:T(8,128)}, u32[]{:S(2)}) %copy-start.2) | copy-done | bytes 131096
  4.2 1.2 %shard_map.122 = (f32[2,2,32,512]{3,2,1,0:T(8,128)S(1)}, f32[2,2,32,512]{3,2,1,0:T(8,128)S(1)}, f32[2,2,32,512]{3,2,1,0:T(8,128)S(1)}, f32[2,2,32,512]{3,2,1,0:T...) custom-call(s32[5]{0:T(128)S(1)} %stack.59.place_ref, f32[2,64,512]{2,1,0:T(8,128)S(1)} %copy-done, ...), custom_call_target="tpu_custom_call" | custom-call | bytes 2097152 | tf_op jit(solution)/shard_map/pallas_call | solution.py:462
  5.4 7.4 %all-to-all-start = ((f32[8,16,128]{2,1,0:T(8,128)}), f32[8,16,128]{2,1,0:T(8,128)S(1)}, u32[]{:S(2)}, u32[]{:S(2)}) async-start(f32[8,16,128]{2,1,0:T(8,128)} %get-tuple-element.17), calls=%async_computation | async-start | bytes 131072 | tf_op jit(solution)/shard_map/all_to_all | solution.py:471
  12.8 1.6 %collective-permute-start.1 = (f32[2,2,32,512]{3,2,1,0:T(8,128)S(1)}, f32[2,2,32,512]{3,2,1,0:T(8,128)S(1)}, u32[]{:S(2)}, u32[]{:S(2)}) collective-permute-start(f32[2,2,32,512]{3,2,1,0:T(8,128)S(1)} %get-tuple-element.22), channel_id=1, source_target_pairs={{0,2},{1,3},{2,0},{3,1},{4,6},{5,7},{6,4},{7,5},{8,10},{9,11},{10,... | collective-permute-start | bytes 786440 | tf_op jit(solution)/shard_map/ppermute | solution.py:457
  14.4 0.3 collective-permute-start.2
  14.7 5.0 %all-to-all-done = f32[8,16,128]{2,1,0:T(8,128)S(1)} async-done(((f32[8,16,128]{2,1,0:T(8,128)}), f32[8,16,128]{2,1,0:T(8,128)S(1)}, u32[]{:S(2)}, u32[]{:S(2)}) %all-to-all-start) | async-done | bytes 65568 | tf_op jit(solution)/shard_map/all_to_all | solution.py:471
  19.7 8.7 %shard_map.123 = (f32[112,128]{1,0:T(8,128)S(1)}, f32[112,128]{1,0:T(8,128)S(1)}, f32[256,128]{1,0:T(8,128)S(1)}) custom-call(s32[5]{0:T(128)S(1)} %stack.59.place_ref, s32[256,128]{1,0:T(8,128)S(1)} %bitcast.27, f32[256,128]{1,0:T(8,128)S(1)} %bitcast.29, f32[128,128]{1,0:T(8,128)S(1)} %bitcast.25, s32[1,256]{1,0:T(1,128)S(1)} %multiply_add_fusion.row_ref), custom_call_target="tpu_custom_call" | custom-call | flops 3758096384 | bytes 524288 | tf_op jit(solution)/shard_map/pallas_call | solution.py:477
  28.5 0.0 collective-permute-done.1.refs_2_
  28.6 0.0 copy-start.4
  28.6 0.0 copy-start.5
  28.6 0.0 copy-start.6
  28.7 0.7 %collective-permute-start.3 = (f32[19,6,512]{2,1,0:T(8,128)S(1)}, f32[19,6,512]{2,1,0:T(8,128)S(1)}, u32[]{:S(2)}, u32[]{:S(2)}) collective-permute-start(f32[19,6,512]{2,1,0:T(8,128)S(1)} %pad_maximum_fusion), channel_id=1, source_target_pairs={{3,7},{7,3},{4,8},{8,4},{11,15},{15,11},{12,16},{16,12},{19,23},{2... | collective-permute-start | bytes 700424 | tf_op jit(solution)/shard_map/ppermute | solution.py:495
  29.4 6.9 %shard_map.124 = (f32[3,16,512]{2,1,0:T(8,128)S(1)}, f32[3,16,512]{2,1,0:T(8,128)S(1)}, f32[3,16,512]{2,1,0:T(8,128)S(1)}, f32[3,16,512]{2,1,0:T(8,128)S(1)}) custom-call(s32[5]{0:T(128)S(1)} %stack.59.place_ref, f32[12]{0:T(128)S(1)} %copy-done.4, f32[12]{0:T(128)S(1)} %copy-done.5, f32[12]{0:T(128)S(1)} %copy-done.6, ...), custom_call_target="tpu_custom_call" | custom-call | flops 13107200 | bytes 1048576 | tf_op jit(solution)/shard_map/pallas_call | solution.py:499
  36.3 0.1 collective-permute-start.4
  36.4 7.1 %collective-permute-start.5 = (f32[3,16,512]{2,1,0:T(8,128)S(1)}, f32[3,16,512]{2,1,0:T(8,128)S(1)}, u32[]{:S(2)}, u32[]{:S(2)}) collective-permute-start(f32[3,16,512]{2,1,0:T(8,128)S(1)} %get-tuple-element.28), channel_id=1, source_target_pairs={{0,2},{1,3},{2,0},{3,1},{4,6},{5,7},{6,4},{7,5},{8,10},{9,11},{10,... | collective-permute-start | bytes 294920 | tf_op jit(solution)/shard_map/ppermute | solution.py:457
  43.5 3.2 %collective-permute-done.5.refs_2_ = f32[3,16,512]{2,1,0:T(8,128)S(1)} collective-permute-done((f32[3,16,512]{2,1,0:T(8,128)S(1)}, f32[3,16,512]{2,1,0:T(8,128)S(1)}, u32[]{:S(2)}, u32[]{:S(2)}) %collective-permute-start.5) | collective-permute-done | bytes 98336 | tf_op jit(solution)/shard_map/ppermute | solution.py:457
  46.7 2.0 %collective-permute-done.6.refs_3_ = f32[3,16,512]{2,1,0:T(8,128)S(1)} collective-permute-done((f32[3,16,512]{2,1,0:T(8,128)S(1)}, f32[3,16,512]{2,1,0:T(8,128)S(1)}, u32[]{:S(2)}, u32[]{:S(2)}) %collective-permute-start.6) | collective-permute-done | bytes 98336 | tf_op jit(solution)/shard_map/ppermute | solution.py:457
  48.7 3.1 %shard_map.125 = (f32[2,64,512]{2,1,0:T(8,128)}, f32[128,128]{1,0:T(8,128)S(1)}) custom-call(s32[5]{0:T(128)S(1)} %stack.59.place_ref, s32[256,128]{1,0:T(8,128)S(1)} %bitcast.28, f32[256,128]{1,0:T(8,128)S(1)} %bitcast.30, f32[256,128]{1,0:T(8,128)S(1)} %get-tuple-element.18.slot_section_ref, s32[1,256]{1,0:T(1,128)S(1)} %multiply_add_fusion.row_ref, ...), custom_call_target="tpu_custom_call" | custom-call | flops 1073741824 | bytes 1048576 | tf_op jit(solution)/shard_map/pallas_call | solution.py:510
  51.8 13.6 %all_to_all.10 = f32[8,16,128]{2,1,0:T(8,128)S(1)} all-to-all(f32[8,16,128]{2,1,0:T(8,128)S(1)} %bitcast.26), channel_id=1, replica_groups=mesh['tile'=8,'layer'=4] {'tile'}, dimensions={0} | all-to-all | bytes 131072 | tf_op jit(solution)/shard_map/all_to_all | solution.py:520
  65.4 0.6 reduce_sum.9
  (31 shorter events, 0.2 us)
Async XLA Ops:
  0.6 0.7 %copy-start.3 = (f32[16,128]{1,0:T(8,128)S(1)}, f32[16,128]{1,0:T(8,128)}, u32[]{:S(2)}) copy-start(f32[16,128]{1,0:T(8,128)} %section_ref.1) | copy-start | bytes 24580
  1.3 0.9 %copy-start = (f32[2,64,512]{2,1,0:T(8,128)S(1)}, f32[2,64,512]{2,1,0:T(8,128)}, u32[]{:S(2)}) copy-start(f32[2,64,512]{2,1,0:T(8,128)} %head_ref.1) | copy-start | bytes 786436
  2.3 0.9 %copy-start.1 = (s32[2,64,512]{2,1,0:T(8,128)S(1)}, s32[2,64,512]{2,1,0:T(8,128)}, u32[]{:S(2)}) copy-start(s32[2,64,512]{2,1,0:T(8,128)} %soil_ref.1) | copy-start | bytes 786436
  3.2 0.9 %copy-start.2 = (s32[64,512]{1,0:T(8,128)S(1)}, s32[64,512]{1,0:T(8,128)}, u32[]{:S(2)}) copy-start(s32[64,512]{1,0:T(8,128)} %land_ref.1) | copy-start | bytes 393220
  4.1 10.5 %copy-start.9 = (s32[1,256]{1,0:T(1,128)S(1)}, s32[1,256]{1,0:T(1,128)}, u32[]{:S(2)}) copy-start(s32[1,256]{1,0:T(1,128)} %param.19) | copy-start | bytes 3076
  4.1 10.5 %copy-start.10 = (s32[1,256]{1,0:T(1,128)S(1)}, s32[1,256]{1,0:T(1,128)}, u32[]{:S(2)}) copy-start(s32[1,256]{1,0:T(1,128)} %param.18) | copy-start | bytes 3076
  5.4 14.3 %copy-start.7 = (s32[1,256,128]{2,1,0:T(8,128)S(1)}, s32[1,256,128]{2,1,0:T(8,128)}, u32[]{:S(2)}) copy-start(s32[1,256,128]{2,1,0:T(8,128)} %param.20) | copy-start | bytes 393220
  5.4 14.3 %copy-start.8 = (f32[1,256,128]{2,1,0:T(8,128)S(1)}, f32[1,256,128]{2,1,0:T(8,128)}, u32[]{:S(2)}) copy-start(f32[1,256,128]{2,1,0:T(8,128)} %param.21) | copy-start | bytes 393220
  5.4 14.3 %all-to-all-start = ((f32[8,16,128]{2,1,0:T(8,128)}), f32[8,16,128]{2,1,0:T(8,128)S(1)}, u32[]{:S(2)}, u32[]{:S(2)}) async-start(f32[8,16,128]{2,1,0:T(8,128)} %get-tuple-element.17), calls=%async_computation | async-start | bytes 131072 | tf_op jit(solution)/shard_map/all_to_all | solution.py:471
  12.8 15.7 %collective-permute-start = (f32[2,2,32,512]{3,2,1,0:T(8,128)S(1)}, f32[2,2,32,512]{3,2,1,0:T(8,128)S(1)}, u32[]{:S(2)}, u32[]{:S(2)}) collective-permute-start(f32[2,2,32,512]{3,2,1,0:T(8,128)S(1)} %get-tuple-element.21), channel_id=1, source_target_pairs={{0,1},{1,0},{2,3},{3,2},{4,5},{5,4},{6,7},{7,6},{8,9},{9,8},{10,11... | collective-permute-start | bytes 786440 | tf_op jit(solution)/shard_map/ppermute | solution.py:457
  12.8 15.7 %collective-permute-start.1 = (f32[2,2,32,512]{3,2,1,0:T(8,128)S(1)}, f32[2,2,32,512]{3,2,1,0:T(8,128)S(1)}, u32[]{:S(2)}, u32[]{:S(2)}) collective-permute-start(f32[2,2,32,512]{3,2,1,0:T(8,128)S(1)} %get-tuple-element.22), channel_id=1, source_target_pairs={{0,2},{1,3},{2,0},{3,1},{4,6},{5,7},{6,4},{7,5},{8,10},{9,11},{10,... | collective-permute-start | bytes 786440 | tf_op jit(solution)/shard_map/ppermute | solution.py:457
  14.4 14.1 %collective-permute-start.2 = (f32[2,2,32,512]{3,2,1,0:T(8,128)S(1)}, f32[2,2,32,512]{3,2,1,0:T(8,128)S(1)}, u32[]{:S(2)}, u32[]{:S(2)}) collective-permute-start(f32[2,2,32,512]{3,2,1,0:T(8,128)S(1)} %get-tuple-element.23), channel_id=1, source_target_pairs={{0,3},{1,2},{2,1},{3,0},{4,7},{5,6},{6,5},{7,4},{8,11},{9,10},{10,... | collective-permute-start | bytes 786440 | tf_op jit(solution)/shard_map/ppermute | solution.py:457
  28.6 0.8 %copy-start.4 = (f32[12]{0:T(128)S(1)}, f32[12]{0:T(128)}, u32[]{:S(2)}) copy-start(f32[12]{0:T(128)} %ks_ref.1) | copy-start | bytes 148
  28.6 0.8 %copy-start.5 = (f32[12]{0:T(128)S(1)}, f32[12]{0:T(128)}, u32[]{:S(2)}) copy-start(f32[12]{0:T(128)} %alpha_ref.1) | copy-start | bytes 148
  28.6 0.8 %copy-start.6 = (f32[12]{0:T(128)S(1)}, f32[12]{0:T(128)}, u32[]{:S(2)}) copy-start(f32[12]{0:T(128)} %store_ref.1) | copy-start | bytes 148
  28.7 0.7 %collective-permute-start.3 = (f32[19,6,512]{2,1,0:T(8,128)S(1)}, f32[19,6,512]{2,1,0:T(8,128)S(1)}, u32[]{:S(2)}, u32[]{:S(2)}) collective-permute-start(f32[19,6,512]{2,1,0:T(8,128)S(1)} %pad_maximum_fusion), channel_id=1, source_target_pairs={{3,7},{7,3},{4,8},{8,4},{11,15},{15,11},{12,16},{16,12},{19,23},{2... | collective-permute-start | bytes 700424 | tf_op jit(solution)/shard_map/ppermute | solution.py:495
  36.3 7.2 %collective-permute-start.4 = (f32[3,16,512]{2,1,0:T(8,128)S(1)}, f32[3,16,512]{2,1,0:T(8,128)S(1)}, u32[]{:S(2)}, u32[]{:S(2)}) collective-permute-start(f32[3,16,512]{2,1,0:T(8,128)S(1)} %get-tuple-element.27), channel_id=1, source_target_pairs={{0,1},{1,0},{2,3},{3,2},{4,5},{5,4},{6,7},{7,6},{8,9},{9,8},{10,11... | collective-permute-start | bytes 294920 | tf_op jit(solution)/shard_map/ppermute | solution.py:457
  36.4 10.3 %collective-permute-start.5 = (f32[3,16,512]{2,1,0:T(8,128)S(1)}, f32[3,16,512]{2,1,0:T(8,128)S(1)}, u32[]{:S(2)}, u32[]{:S(2)}) collective-permute-start(f32[3,16,512]{2,1,0:T(8,128)S(1)} %get-tuple-element.28), channel_id=1, source_target_pairs={{0,2},{1,3},{2,0},{3,1},{4,6},{5,7},{6,4},{7,5},{8,10},{9,11},{10,... | collective-permute-start | bytes 294920 | tf_op jit(solution)/shard_map/ppermute | solution.py:457
  43.5 5.1 %collective-permute-start.6 = (f32[3,16,512]{2,1,0:T(8,128)S(1)}, f32[3,16,512]{2,1,0:T(8,128)S(1)}, u32[]{:S(2)}, u32[]{:S(2)}) collective-permute-start(f32[3,16,512]{2,1,0:T(8,128)S(1)} %get-tuple-element.29), channel_id=1, source_target_pairs={{0,3},{1,2},{2,1},{3,0},{4,7},{5,6},{6,5},{7,4},{8,11},{9,10},{10,... | collective-permute-start | bytes 294920 | tf_op jit(solution)/shard_map/ppermute | solution.py:457

commit v3 on v2

--- a/solution.py
+++ b/solution.py
@@ -14,8 +14,8 @@
 VERTICAL = 2.0
 GRAVITY = 1.0
 
-PAD = 8
 HALO = ITERS * SWEEPS
+BLOCK = 32
 LANES = 128
 VMEM_LIMIT = 48 * 1024 * 1024
 FLAT = ("tile", "layer")
@@ -31,6 +31,11 @@
         pieces.append(piece)
         value = value - piece.astype(jnp.float32)
     return pieces
+
+
+def reciprocal(value):
+    guess = pl.reciprocal(value, approx=True)
+    return guess * (2.0 - value * guess)
 
 
 def one_hot(row, size, on):
@@ -69,15 +74,15 @@
         )
     slot_section_ref[...] = picked
 
-    half = LANES // 2
-    block, spot = split_cells(cells_ref[...], place_ref[0] - HALO, breadth, half)
+    block, spot = split_cells(cells_ref[...], place_ref[0], breadth, BLOCK)
     spot_sc[...] = spot
     bed = bed_ref[...]
     for value, high_sc, low_sc in ((bed, dhigh_sc, dlow_sc), (bed * picked, rhigh_sc, rlow_sc)):
         high, low = bf16_pieces(value, 2)
         high_sc[...] = high.astype(jnp.float32)
         low_sc[...] = low.astype(jnp.float32)
-    blocks = 2 * diag_ref.shape[0]
+    share = LANES // BLOCK
+    blocks = share * diag_ref.shape[0]
     group = 32
     tiles = slots // LANES
     for part in range(tiles):
@@ -97,7 +102,7 @@
             spots = row_copies(spot_sc, slot)
             left.append(
                 jnp.concatenate(
-                    [one_hot(spots, half, row_copies(ref, slot)) for ref in (dhigh_sc, dlow_sc, rhigh_sc, rlow_sc)],
+                    [one_hot(spots, BLOCK, row_copies(ref, slot)) for ref in (dhigh_sc, dlow_sc, rhigh_sc, rlow_sc)],
                     axis=0,
                 )
             )
@@ -110,59 +115,64 @@
             preferred_element_type=jnp.float32,
         )
 
-    total = lax.fori_loop(0, slots // group, step, jnp.zeros((4 * half, len(names) * LANES), jnp.float32))
-    both = jnp.concatenate([total[:half] + total[half:2 * half], total[2 * half:3 * half] + total[3 * half:]], axis=0)
-    for part in range(len(names)):
-        sum_sc[pl.ds(part * LANES, LANES), :] = both[:, part * LANES:(part + 1) * LANES].T
-    low_half = lax.broadcasted_iota(jnp.int32, diag_ref.shape, 1) < half
-    even = sum_sc[pl.ds(0, blocks // 2, stride=2), :]
-    odd = sum_sc[pl.ds(1, blocks // 2, stride=2), :]
-    diag_ref[...] = jnp.where(low_half, even, pltpu.roll(odd, half, 1))
-    rhs_ref[...] = jnp.where(low_half, pltpu.roll(even, half, 1), odd)
-
-
-def prepare_kernel(place_ref, head_ref, soil_ref, section_ref, land_ref, *out_refs):
-    window_refs, spread_ref, land_out_ref = out_refs[:-2], out_refs[-2], out_refs[-1]
-    groups = len(window_refs)
-    _, held, window, _ = window_refs[0].shape
-    across = head_ref.shape[1]
+    total = lax.fori_loop(0, slots // group, step, jnp.zeros((4 * BLOCK, blocks), jnp.float32))
+    lane = lax.broadcasted_iota(jnp.int32, diag_ref.shape, 1) // BLOCK
+    for number, ref in ((0, diag_ref), (2, rhs_ref)):
+        first = number * BLOCK
+        both = total[first:first + BLOCK] + total[first + BLOCK:first + 2 * BLOCK]
+        both = jnp.concatenate([both] * share, axis=0)
+        for part in range(blocks // LANES):
+            sum_sc[pl.ds(part * LANES, LANES), :] = both[:, part * LANES:(part + 1) * LANES].T
+        result = sum_sc[pl.ds(0, blocks // share, stride=share), :]
+        for part in range(1, share):
+            result = jnp.where(lane == part, sum_sc[pl.ds(part, blocks // share, stride=share), :], result)
+        ref[...] = result
+
+
+def prepare_kernel(groups, place_ref, head_hbm, soil_hbm, section_hbm, land_hbm, *refs):
+    block_refs, spread_ref, land_out_ref = refs[:groups], refs[groups], refs[groups + 1]
+    head_ref, soil_ref, section_ref, land_ref, sems = refs[groups + 2:]
+    held, across, _ = head_ref.shape
     span = across // groups
-
-    def span_of(target):
-        return jnp.where(place_ref[3] == 1, groups - 1 - target, target)
-
-    def pieces(number):
-        for start in range(0, window, PAD):
-            row = jnp.clip(number * span - PAD + start, 0, across - PAD)
-            yield pl.ds(start, PAD), pl.ds(pl.multiple_of(row, PAD), PAD)
-
-    for step, out_ref in enumerate(window_refs):
-        for to, spot in pieces(span_of(place_ref[4] ^ step)):
-            for layer in range(held):
-                out_ref[0, layer, to, :] = head_ref[layer, spot, :]
-                out_ref[1, layer, to, :] = soil_ref[layer, spot, :].astype(jnp.float32)
-    for to, spot in pieces(span_of(place_ref[4])):
-        land_out_ref[to, :] = land_ref[spot, :].astype(jnp.float32)
+    pairs = [(section_hbm, section_ref), (land_hbm, land_ref)]
+    for layer in range(held):
+        pairs += [(head_hbm.at[layer], head_ref.at[layer]), (soil_hbm.at[layer], soil_ref.at[layer])]
+    copies = [pltpu.make_async_copy(here, there, sems.at[k]) for k, (here, there) in enumerate(pairs)]
+    for copy in copies:
+        copy.start()
+
+    def rows_of(target):
+        number = jnp.where(place_ref[1] == 1, groups - 1 - target, target)
+        return pl.ds(pl.multiple_of(number * span, span), span)
+
+    copies[0].wait()
     section = section_ref[...]
     for tile in range(spread_ref.shape[0]):
         spread_ref[tile] = section
+    copies[1].wait()
+    land_out_ref[...] = land_ref[rows_of(place_ref[2]), :].astype(jnp.float32)
+    for layer in range(held):
+        copies[2 + 2 * layer].wait()
+        copies[3 + 2 * layer].wait()
+        for step, out_ref in enumerate(block_refs):
+            rows = rows_of(place_ref[2] ^ step)
+            out_ref[0, layer] = head_ref[layer, rows, :]
+            out_ref[1, layer] = soil_ref[layer, rows, :].astype(jnp.float32)
 
 
 def flow_kernel(
-    groups, place_ref, ks_ref, alpha_ref, store_ref, land_ref, halo_ref, diag_ref, rhs_ref, *refs,
+    groups, place_ref, ks_ref, alpha_ref, store_ref, land_ref, near_ref, far_ref, diag_ref, rhs_ref, *refs,
 ):
     block_refs, head_refs = refs[:groups], refs[groups:2 * groups]
     (
         soil_sc, first_sc, ks_sc, alpha_sc, diag_sc, rhs_sc, wx_sc, wy_sc, wz_sc, base_sc, inv_sc,
         ping_sc, pong_sc, land_sc, dtop_sc, rtop_sc,
     ) = refs[2 * groups:]
-    _, held, window, breadth = block_refs[0].shape
+    _, held, span, breadth = block_refs[0].shape
     layers = groups * held
-    span = window - 2 * PAD
-    low, high = PAD - HALO, PAD + span
-    is_first = place_ref[1] == 1
-    is_last = place_ref[2] == 1
+    window = span + 2 * HALO
     per_row = breadth // LANES
+    side = HALO * per_row
 
     def put_rows(ref, layer, row, value):
         for part in range(per_row):
@@ -171,25 +181,33 @@
 
     for step, block_ref in enumerate(block_refs):
         for held_layer in range(held):
-            layer = (place_ref[4] ^ step) * held + held_layer
-            put_rows(first_sc, layer, 0, block_ref[0, held_layer])
-            put_rows(soil_sc, layer, 0, block_ref[1, held_layer])
-    land_sc[...] = land_ref[...]
-    dtop_sc[...] = diag_ref[...]
-    rtop_sc[...] = rhs_ref[...]
-    for chosen, row in ((is_first, low), (is_last, high)):
-        @pl.when(chosen)
-        def _(row=row):
-            for entry in range(layers):
-                layer = (place_ref[4] ^ (entry // held)) * held + entry % held
-                put_rows(first_sc, layer, row, halo_ref[entry])
-                put_rows(soil_sc, layer, row, halo_ref[layers + entry])
-            land_sc[pl.ds(row, HALO), :] = halo_ref[2 * layers]
+            layer = (place_ref[2] ^ step) * held + held_layer
+            put_rows(first_sc, layer, HALO, block_ref[0, held_layer])
+            put_rows(soil_sc, layer, HALO, block_ref[1, held_layer])
+    land_sc[pl.ds(HALO, span), :] = land_ref[...]
+    dtop_sc[pl.ds(side, span * per_row), :] = diag_ref[...]
+    rtop_sc[pl.ds(side, span * per_row), :] = rhs_ref[...]
+
+    def put_halo(ref, partner, row):
+        def entry(number):
+            return ref[pl.ds(number * HALO, HALO), :]
+
+        for number in range(layers):
+            layer = (partner ^ (number // held)) * held + number % held
+            put_rows(first_sc, layer, row, entry(number))
+            put_rows(soil_sc, layer, row, entry(layers + number))
+        land_sc[pl.ds(row, HALO), :] = entry(2 * layers)
+        for number, top_sc in ((2 * layers + 1, dtop_sc), (2 * layers + 2, rtop_sc)):
+            value = entry(number)
             for part in range(per_row):
-                spot = pl.ds((row - low) * per_row + part, HALO, stride=per_row)
-                lanes = pl.ds(part * LANES, LANES)
-                dtop_sc[spot, :] = halo_ref[2 * layers + 1, :, lanes]
-                rtop_sc[spot, :] = halo_ref[2 * layers + 2, :, lanes]
+                spot = pl.ds(row * per_row + part, HALO, stride=per_row)
+                top_sc[spot, :] = value[:, part * LANES:(part + 1) * LANES]
+
+    for odd, above_ref, below_ref in ((0, far_ref, near_ref), (1, near_ref, far_ref)):
+        @pl.when(place_ref[3] == odd)
+        def _(above_ref=above_ref, below_ref=below_ref):
+            for ref, row in ((above_ref, 0), (below_ref, HALO + span)):
+                put_halo(ref, place_ref[4] if ref is near_ref else place_ref[5], row)
 
     def get(ref, row):
         spot = pl.ds(row * layers, layers)
@@ -207,7 +225,7 @@
     not_last = column < breadth - 1
 
     def riv_row(ref, row):
-        first = (row - low) * per_row
+        first = row * per_row
         parts = [
             jnp.broadcast_to(ref[pl.ds(first + part, 1), :], (layers, LANES)) for part in range(per_row)
         ]
@@ -235,7 +253,7 @@
             found.append(jnp.concatenate(parts, axis=1))
         return found
 
-    for row in range(low, window - low):
+    for row in range(window):
         ks, alpha, store = lookup(get(soil_sc, row).astype(jnp.int32))
         put(ks_sc, row, ks)
         put(alpha_sc, row, alpha)
@@ -260,7 +278,7 @@
             return cond, cond * land_sc[pl.ds(row, 1), :]
 
         def face(factor, cond, opened, far, far_open):
-            return factor * 2.0 * opened * far_open / (cond + far)
+            return factor * 2.0 * opened * far_open * reciprocal(cond + far)
 
         def step(row, carried):
             cond, opened, wx_before = carried
@@ -270,7 +288,7 @@
             wz = jnp.where(not_bottom, face(VERTICAL, cond, opened, below(cond), below(opened)), 0.0)
             wz_above = above(wz)
             total = get(diag_sc, row) + wx_before + wx + wy + west(wy) + wz + wz_above
-            inverse = 1.0 / total
+            inverse = reciprocal(total)
             put(wx_sc, row, wx)
             put(wy_sc, row, wy)
             put(wz_sc, row, wz)
@@ -304,7 +322,7 @@
             carried = step(row, carried)
 
     now_sc, spare = first_sc, [ping_sc, pong_sc]
-    first, last = low, window - low
+    first, last = 0, window
     for picard in range(ITERS):
         make_weights(now_sc, first, last - 1)
         for _ in range(SWEEPS):
@@ -315,11 +333,11 @@
             now_sc = later_sc
     for part in range(per_row):
         lanes = pl.ds(part * LANES, LANES)
-        top_rows = now_sc[part, pl.ds(PAD * layers, span, stride=layers), :]
+        top_rows = now_sc[part, pl.ds(HALO * layers, span, stride=layers), :]
         for step, head_ref in enumerate(head_refs):
             for held_layer in range(held):
-                layer = (place_ref[4] ^ step) * held + held_layer
-                head_ref[held_layer, :, lanes] = now_sc[part, pl.ds(PAD * layers + layer, span, stride=layers), :]
+                layer = (place_ref[2] ^ step) * held + held_layer
+                head_ref[held_layer, :, lanes] = now_sc[part, pl.ds(HALO * layers + layer, span, stride=layers), :]
             head_ref[held, :, lanes] = top_rows
 
 
@@ -335,9 +353,9 @@
     slots = cells_ref.shape[0]
     quarter = LANES // groups
     packed = slots // groups
-    flip = place_ref[3]
+    flip = place_ref[1]
     for step, back_ref in enumerate(back_refs):
-        source = place_ref[4] ^ step
+        source = place_ref[2] ^ step
         number = jnp.where(flip == 1, groups - 1 - source, source)
         rows = pl.ds(pl.multiple_of(number * span, span), span)
         for layer in range(held):
@@ -351,7 +369,7 @@
     def pack(ref):
         result = None
         for number in range(groups):
-            shift = lax.rem((number + groups - place_ref[4]) * quarter, LANES)
+            shift = lax.rem((number + groups - place_ref[2]) * quarter, LANES)
             moved = pltpu.roll(ref[pl.ds(number * packed, packed), :], shift, 1)
             result = moved if result is None else jnp.where(own == number, moved, result)
         return result
@@ -430,21 +448,24 @@
     groups = lax.axis_size("layer")
     layers = held * groups
     span = across // groups
-    window = span + 2 * PAD
     per_row = breadth // LANES
-    blocks = (span + 2 * HALO) * per_row
+    blocks = span * per_row
     tile = lax.axis_index("tile")
     layer = lax.axis_index("layer")
-    flip = lax.rem(tile, 2) == 1
-    number = jnp.where(flip, groups - 1 - layer, layer)
-    is_first = number == 0
-    is_last = number == groups - 1
-    place = jnp.stack([number * span, is_first, is_last, flip, layer]).astype(jnp.int32)
-    swap = []
-    for upper in range(tiles - 1):
-        index = groups - 1 if upper % 2 == 0 else 0
-        one, two = upper * groups + index, (upper + 1) * groups + index
-        swap += [(one, two), (two, one)]
+    flip = lax.rem(tile, 2)
+    number = jnp.where(flip == 1, groups - 1 - layer, layer)
+    odd = lax.rem(number, 2)
+    end = (number == 0) | (number == groups - 1)
+    far_partner = jnp.where(end, layer, layer ^ (groups - 1))
+    place = jnp.stack([number * span, flip, layer, odd, layer ^ 1, far_partner]).astype(jnp.int32)
+    near = [(i, i ^ 1) for i in range(groups)]
+    far = []
+    for upper in range(tiles):
+        far += [(upper * groups + i, upper * groups + (i ^ (groups - 1))) for i in range(1, groups - 1)]
+        if upper + 1 < tiles:
+            index = groups - 1 if upper % 2 == 0 else 0
+            one, two = upper * groups + index, (upper + 1) * groups + index
+            far += [(one, two), (two, one)]
 
     cells = node_cell[0]
     bed = bed_cond[0]
@@ -458,18 +479,25 @@
         return received
 
     field_bytes = held * across * breadth * 4
-    window_shape = jax.ShapeDtypeStruct((2, held, window, breadth), jnp.float32)
-    *windows, spread, land = call(
-        prepare_kernel,
-        (window_shape,) * groups
+    *own_blocks, spread, land = call(
+        functools.partial(prepare_kernel, groups),
+        (jax.ShapeDtypeStruct((2, held, span, breadth), jnp.float32),) * groups
         + (
             jax.ShapeDtypeStruct((tiles, reach_rows, node_count), jnp.float32),
-            jax.ShapeDtypeStruct((window, breadth), jnp.float32),
+            jax.ShapeDtypeStruct((span, breadth), jnp.float32),
         ),
-        [in_smem] + [in_vmem] * 4, [], 0, 8 * field_bytes,
+        [in_smem] + [pl.BlockSpec(memory_space=pl.ANY)] * 4,
+        [
+            pltpu.VMEM(head_start.shape, jnp.float32),
+            pltpu.VMEM(soil_class.shape, jnp.int32),
+            pltpu.VMEM(section.shape, jnp.float32),
+            pltpu.VMEM(land_mask.shape, jnp.int32),
+            pltpu.SemaphoreType.DMA((2 + 2 * held,)),
+        ],
+        0, 4 * field_bytes,
     )(place, head_start, soil_class, section, land_mask)
     whole_section = lax.all_to_all(spread, "tile", 0, 0).reshape(tiles * reach_rows, node_count)
-    received = exchange(windows)
+    received = exchange(own_blocks)
 
     node_scratch = pltpu.VMEM((slots, LANES), jnp.float32)
     riv_shape = jax.ShapeDtypeStruct((blocks, LANES), jnp.float32)
@@ -480,30 +508,37 @@
         [in_smem] + [in_vmem] * 4,
         [node_scratch] * 5
         + [pltpu.VMEM((slots // LANES, LANES, LANES), jnp.float32)]
-        + [pltpu.VMEM((-(-2 * blocks // LANES) * LANES, LANES), jnp.float32)],
-        2 * blocks * 4 * LANES * slots * LANES, 4 * node_bytes,
+        + [pltpu.VMEM((span * breadth // BLOCK, LANES), jnp.float32)],
+        8 * span * breadth * slots * LANES, 4 * node_bytes,
     )(place, cells, bed, whole_section, reach)
 
-    send_row = jnp.where(is_first, PAD, PAD + span - HALO)
-    edges = [lax.dynamic_slice_in_dim(block, send_row, HALO, 2) for block in received]
-    edge = jnp.stack(edges, axis=1).reshape(2 * layers, HALO, breadth)
-    edge = jnp.concatenate([edge, lax.dynamic_slice_in_dim(land, send_row, HALO, 0)[None]])
+    def edge(bottom):
+        row = jnp.where(bottom, span - HALO, 0)
+        grid = [lax.dynamic_slice_in_dim(block, row, HALO, 2) for block in received]
+        river = [jnp.where(bottom, term[blocks - side:], term[:side]) for term in (diag, rhs)]
+        return jnp.concatenate(
+            [
+                jnp.stack(grid, axis=1).reshape(2 * layers * HALO, breadth),
+                lax.dynamic_slice_in_dim(land, row, HALO, 0),
+                jnp.concatenate(river).reshape(2 * HALO, breadth),
+            ]
+        )
+
     side = HALO * per_row
-    riv = jnp.stack([diag, rhs])
-    riv_edge = jnp.where(is_first, riv[:, side:2 * side], riv[:, blocks - 2 * side:blocks - side])
-    edge = jnp.concatenate([edge, riv_edge.reshape(2, HALO, breadth)])
-    halo = lax.ppermute(edge, FLAT, swap)
-
+    near_halo = lax.ppermute(edge(odd == 0), "layer", near)
+    far_halo = lax.ppermute(edge(odd == 1), FLAT, far)
+
+    window = span + 2 * HALO
     field = pltpu.VMEM((per_row, window * layers, LANES), jnp.float32)
     out_shape = jax.ShapeDtypeStruct((held + 1, span, breadth), jnp.float32)
     out = call(
         functools.partial(flow_kernel, groups), (out_shape,) * groups,
-        [in_smem] * 4 + [in_vmem] * (4 + groups),
+        [in_smem] * 4 + [in_vmem] * (5 + groups),
         [field] * 13
         + [pltpu.VMEM((window, breadth), jnp.float32)]
-        + [pltpu.VMEM((blocks, LANES), jnp.float32)] * 2,
+        + [pltpu.VMEM((window * per_row, LANES), jnp.float32)] * 2,
         100 * layers * window * breadth, 8 * layers * window * breadth,
-    )(place, ks_table, alpha_table, store_table, land, halo, diag, rhs, *received)
+    )(place, ks_table, alpha_table, store_table, land, near_halo, far_halo, diag, rhs, *received)
     back = exchange(out)
 
     packed = pltpu.VMEM((slots // groups, LANES), jnp.float32)

time: 66.3 us -> 65.2 us (0.983)
  blocking collectives: 13.6 us -> 10.3 us
  waiting for transfers between devices: 10.1 us -> 12.3 us
  Pallas kernels: 20 us -> 19.1 us
  local copies, waits for them, and re-layouts: 3.61 us -> 4.37 us
    all_to_all x1, blocking collectives: 13.6 us -> 10.3 us  [on_device(): lax.all_to_all(partial.reshape(tiles, reach_rows, node_count), 'tile', 0, 0)]
    ppermute x1 -> x2, starting transfers between devices: 0.68 us -> 3.61 us  [the longest x1 2.93 us: on_device(): near_halo = lax.ppermute(edge(odd == 0), 'layer', near)]
    pallas_call x1, Pallas kernels: 8.71 us -> 6.83 us  [on_device(): call(functools.partial(river_kernel, breadth), (riv_shape, riv_shape, jax...]
    ppermute x6, starting transfers between devices: 9.06 us -> 7.59 us  [exchange(): lax.ppermute(parts[step], 'layer', [(i, i ^ step) for i in range(groups)])]
    all_to_all x1, starting transfers between devices: 7.38 us -> 6.01 us  [on_device(): lax.all_to_all(spread, 'tile', 0, 0).reshape(tiles * reach_rows, node_count)]
    all_to_all x1, waiting for transfers between devices: 4.99 us -> 6.14 us  [on_device(): lax.all_to_all(spread, 'tile', 0, 0).reshape(tiles * reach_rows, node_count)]
    ppermute x1 -> x2, waiting for transfers between devices: 0.01 us -> 1.14 us  [the longest x1 1.14 us: on_device(): near_halo = lax.ppermute(edge(odd == 0), 'layer', near)]
    pallas_call x1, Pallas kernels: 1.25 us -> 2.12 us  [on_device(): call(functools.partial(prepare_kernel, groups), (jax.ShapeDtypeStruct((2,...]
  transfers between devices with their start and end apart: 8 -> 9, of which waited for: 3 -> 4; matrix products, arithmetic and copies ran while one was open for 0% -> 0% of each run, Pallas kernels for 13% -> 11%
where the time goes in v3:
time: 65.2 us; the launch traced here: 64.9 us
  Pallas kernels  19.1 us (29%)
  starting transfers between devices  17.2 us (26%)
  waiting for transfers between devices  12.3 us (19%)
  blocking collectives  10.3 us (16%)
  local copies, waits for them, and re-layouts  4.37 us (7%)
  between operations  0.89 us (1%)
  other arithmetic  0.73 us (1%)
    all_to_all x1, blocking collectives, on_device(): lax.all_to_all(partial.reshape(tiles, reach_rows, node_count), 'tile', 0, 0)  10.3 us
    ppermute x6, starting transfers between devices, exchange(): lax.ppermute(parts[step], 'layer', [(i, i ^ step) for i in range(groups)])  7.59 us
    pallas_call x1, Pallas kernels, on_device(): call(functools.partial(flow_kernel, groups), (out_shape,) * groups, [in_s...  7 us
    pallas_call x1, Pallas kernels, on_device(): call(functools.partial(river_kernel, breadth), (riv_shape, riv_shape, jax...  6.83 us
    all_to_all x1, waiting for transfers between devices, on_device(): lax.all_to_all(spread, 'tile', 0, 0).reshape(tiles * reach_rows, node_count)  6.14 us
    all_to_all x1, starting transfers between devices, on_device(): lax.all_to_all(spread, 'tile', 0, 0).reshape(tiles * reach_rows, node_count)  6.01 us
    ppermute x6, waiting for transfers between devices, exchange(): lax.ppermute(parts[step], 'layer', [(i, i ^ step) for i in range(groups)])  5.05 us
    unnamed x22, local copies, waits for them, and re-layouts  4.12 us
  transfers between devices with their start and end apart: 9, of which 4 were waited for; matrix products, arithmetic and copies ran while one was open for 0% of the time, Pallas kernels for 11%

profile of v3, /device:TPU:0, one launch (start us, length us, event | category | flops | bytes accessed | tf_op | source)
XLA Modules:
  0.0 64.9 jit_solution(7019681576224568770)
XLA Ops:
  0.7 0.1 stack.57.place_ref
  0.7 0.6 copy-done.3
  1.3 0.9 %copy-done = f32[2,64,512]{2,1,0:T(8,128)S(1)} copy-done((f32[2,64,512]{2,1,0:T(8,128)S(1)}, f32[2,64,512]{2,1,0:T(8,128)}, u32[]{:S(2)}) %copy-start) | copy-done | bytes 262168
  2.3 0.9 %copy-done.1 = s32[2,64,512]{2,1,0:T(8,128)S(1)} copy-done((s32[2,64,512]{2,1,0:T(8,128)S(1)}, s32[2,64,512]{2,1,0:T(8,128)}, u32[]{:S(2)}) %copy-start.1) | copy-done | bytes 262168
  3.2 0.9 %copy-done.2 = s32[64,512]{1,0:T(8,128)S(1)} copy-done((s32[64,512]{1,0:T(8,128)S(1)}, s32[64,512]{1,0:T(8,128)}, u32[]{:S(2)}) %copy-start.2) | copy-done | bytes 131096
  4.1 2.1 %shard_map.122 = (f32[2,2,16,512]{3,2,1,0:T(8,128)S(1)}, f32[2,2,16,512]{3,2,1,0:T(8,128)S(1)}, f32[2,2,16,512]{3,2,1,0:T(8,128)S(1)}, f32[2,2,16,512]{3,2,1,0:T...) custom-call(s32[6]{0:T(128)S(1)} %stack.57.place_ref, f32[2,64,512]{2,1,0:T(8,128)S(1)} %copy-done, ...), custom_call_target="tpu_custom_call" | custom-call | bytes 1048576 | tf_op jit(solution)/shard_map/pallas_call | solution.py:482
  6.3 0.5 collective-permute-start
  6.8 2.6 %collective-permute-start.1 = (f32[2,2,16,512]{3,2,1,0:T(8,128)S(1)}, f32[2,2,16,512]{3,2,1,0:T(8,128)S(1)}, u32[]{:S(2)}, u32[]{:S(2)}) collective-permute-start(f32[2,2,16,512]{3,2,1,0:T(8,128)S(1)} %get-tuple-element.22), channel_id=1, source_target_pairs={{0,2},{1,3},{2,0},{3,1},{4,6},{5,7},{6,4},{7,5},{8,10},{9,11},{10,... | collective-permute-start | bytes 393224 | tf_op jit(solution)/shard_map/ppermute | solution.py:478
  9.4 0.1 collective-permute-start.2
  9.5 6.0 %all-to-all-start = ((f32[8,16,128]{2,1,0:T(8,128)}), f32[8,16,128]{2,1,0:T(8,128)S(1)}, u32[]{:S(2)}, u32[]{:S(2)}) async-start(f32[8,16,128]{2,1,0:T(8,128)} %get-tuple-element.17), calls=%async_computation | async-start | bytes 131072 | tf_op jit(solution)/shard_map/all_to_all | solution.py:499
  15.5 0.7 %copy-done.9 = s32[1,256]{1,0:T(1,128)S(1)} copy-done((s32[1,256]{1,0:T(1,128)S(1)}, s32[1,256]{1,0:T(1,128)}, u32[]{:S(2)}) %copy-start.9) | copy-done | bytes 1048
  16.2 6.1 %all-to-all-done = f32[8,16,128]{2,1,0:T(8,128)S(1)} async-done(((f32[8,16,128]{2,1,0:T(8,128)}), f32[8,16,128]{2,1,0:T(8,128)S(1)}, u32[]{:S(2)}, u32[]{:S(2)}) %all-to-all-start) | async-done | bytes 65568 | tf_op jit(solution)/shard_map/all_to_all | solution.py:499
  22.4 6.8 %shard_map.123 = (f32[64,128]{1,0:T(8,128)S(1)}, f32[64,128]{1,0:T(8,128)S(1)}, f32[256,128]{1,0:T(8,128)S(1)}) custom-call(s32[6]{0:T(128)S(1)} %stack.57.place_ref, s32[256,128]{1,0:T(8,128)S(1)} %bitcast.29, f32[256,128]{1,0:T(8,128)S(1)} %bitcast.31, f32[128,128]{1,0:T(8,128)S(1)} %bitcast.27, s32[1,256]{1,0:T(1,128)S(1)} %multiply_add_fusion.row_ref), custom_call_target="tpu_custom_call" | custom-call | flops 2147483648 | bytes 524288 | tf_op jit(solution)/shard_map/pallas_call | solution.py:505
  29.5 0.7 %collective-permute-start.4 = (f32[114,512]{1,0:T(8,128)S(1)}, f32[114,512]{1,0:T(8,128)S(1)}, u32[]{:S(2)}, u32[]{:S(2)}) collective-permute-start(f32[114,512]{1,0:T(8,128)S(1)} %pad_maximum_fusion.3), channel_id=1, source_target_pairs={{1,2},{2,1},{3,7},{7,3},{5,6},{6,5},{4,8},{8,4},{9,10},{10,9},{11,... | collective-permute-start | bytes 700424 | tf_op jit(solution)/shard_map/ppermute | solution.py:529
  30.3 2.9 %collective-permute-start.3 = (f32[114,512]{1,0:T(8,128)S(1)}, f32[114,512]{1,0:T(8,128)S(1)}, u32[]{:S(2)}, u32[]{:S(2)}) collective-permute-start(f32[114,512]{1,0:T(8,128)S(1)} %pad_maximum_fusion.2), channel_id=1, source_target_pairs={{0,1},{1,0},{2,3},{3,2},{4,5},{5,4},{6,7},{7,6},{8,9},{9,8},{10,11... | collective-permute-start | bytes 700424 | tf_op jit(solution)/shard_map/ppermute | solution.py:528
  33.3 1.1 %collective-permute-done.3.near_ref = f32[114,512]{1,0:T(8,128)S(1)} collective-permute-done((f32[114,512]{1,0:T(8,128)S(1)}, f32[114,512]{1,0:T(8,128)S(1)}, u32[]{:S(2)}, u32[]{:S(2)}) %collective-permute-start.3) | collective-permute-done | bytes 233504 | tf_op jit(solution)/shard_map/ppermute | solution.py:528
  34.4 7.0 %shard_map.124 = (f32[3,16,512]{2,1,0:T(8,128)S(1)}, f32[3,16,512]{2,1,0:T(8,128)S(1)}, f32[3,16,512]{2,1,0:T(8,128)S(1)}, f32[3,16,512]{2,1,0:T(8,128)S(1)}) custom-call(s32[6]{0:T(128)S(1)} %stack.57.place_ref, f32[12]{0:T(128)S(1)} %copy-done.4, f32[12]{0:T(128)S(1)} %copy-done.5, f32[12]{0:T(128)S(1)} %copy-done.6, ...), custom_call_target="tpu_custom_call" | custom-call | flops 11468800 | bytes 917504 | tf_op jit(solution)/shard_map/pallas_call | solution.py:534
  41.4 2.6 %collective-permute-start.5 = (f32[3,16,512]{2,1,0:T(8,128)S(1)}, f32[3,16,512]{2,1,0:T(8,128)S(1)}, u32[]{:S(2)}, u32[]{:S(2)}) collective-permute-start(f32[3,16,512]{2,1,0:T(8,128)S(1)} %get-tuple-element.27), channel_id=1, source_target_pairs={{0,1},{1,0},{2,3},{3,2},{4,5},{5,4},{6,7},{7,6},{8,9},{9,8},{10,11... | collective-permute-start | bytes 294920 | tf_op jit(solution)/shard_map/ppermute | solution.py:478
  44.1 1.7 %collective-permute-start.6 = (f32[3,16,512]{2,1,0:T(8,128)S(1)}, f32[3,16,512]{2,1,0:T(8,128)S(1)}, u32[]{:S(2)}, u32[]{:S(2)}) collective-permute-start(f32[3,16,512]{2,1,0:T(8,128)S(1)} %get-tuple-element.28), channel_id=1, source_target_pairs={{0,2},{1,3},{2,0},{3,1},{4,6},{5,7},{6,4},{7,5},{8,10},{9,11},{10,... | collective-permute-start | bytes 294920 | tf_op jit(solution)/shard_map/ppermute | solution.py:478
  45.8 3.7 %collective-permute-done.6.refs_2_ = f32[3,16,512]{2,1,0:T(8,128)S(1)} collective-permute-done((f32[3,16,512]{2,1,0:T(8,128)S(1)}, f32[3,16,512]{2,1,0:T(8,128)S(1)}, u32[]{:S(2)}, u32[]{:S(2)}) %collective-permute-start.6) | collective-permute-done | bytes 98336 | tf_op jit(solution)/shard_map/ppermute | solution.py:478
  49.5 1.3 %collective-permute-done.7.refs_3_ = f32[3,16,512]{2,1,0:T(8,128)S(1)} collective-permute-done((f32[3,16,512]{2,1,0:T(8,128)S(1)}, f32[3,16,512]{2,1,0:T(8,128)S(1)}, u32[]{:S(2)}, u32[]{:S(2)}) %collective-permute-start.7) | collective-permute-done | bytes 98336 | tf_op jit(solution)/shard_map/ppermute | solution.py:478
  50.9 3.1 %shard_map.125 = (f32[2,64,512]{2,1,0:T(8,128)}, f32[128,128]{1,0:T(8,128)S(1)}) custom-call(s32[6]{0:T(128)S(1)} %stack.57.place_ref, s32[256,128]{1,0:T(8,128)S(1)} %bitcast.30, f32[256,128]{1,0:T(8,128)S(1)} %bitcast.32, f32[256,128]{1,0:T(8,128)S(1)} %get-tuple-element.18.slot_section_ref, s32[1,256]{1,0:T(1,128)S(1)} %multiply_add_fusion.row_ref, ...), custom_call_target="tpu_custom_call" | custom-call | flops 1073741824 | bytes 1048576 | tf_op jit(solution)/shard_map/pallas_call | solution.py:545
  54.0 10.3 %all_to_all.10 = f32[8,16,128]{2,1,0:T(8,128)S(1)} all-to-all(f32[8,16,128]{2,1,0:T(8,128)S(1)} %bitcast.28), channel_id=1, replica_groups=mesh['tile'=8,'layer'=4] {'tile'}, dimensions={0} | all-to-all | bytes 131072 | tf_op jit(solution)/shard_map/all_to_all | solution.py:555
  64.3 0.6 reduce_sum.9
  (39 shorter events, 0.4 us)
Async XLA Ops:
  0.6 0.7 %copy-start.3 = (f32[16,128]{1,0:T(8,128)S(1)}, f32[16,128]{1,0:T(8,128)}, u32[]{:S(2)}) copy-start(f32[16,128]{1,0:T(8,128)} %section_hbm.1) | copy-start | bytes 24580
  1.3 0.9 %copy-start = (f32[2,64,512]{2,1,0:T(8,128)S(1)}, f32[2,64,512]{2,1,0:T(8,128)}, u32[]{:S(2)}) copy-start(f32[2,64,512]{2,1,0:T(8,128)} %head_hbm.1) | copy-start | bytes 786436
  2.3 0.9 %copy-start.1 = (s32[2,64,512]{2,1,0:T(8,128)S(1)}, s32[2,64,512]{2,1,0:T(8,128)}, u32[]{:S(2)}) copy-start(s32[2,64,512]{2,1,0:T(8,128)} %soil_hbm.1) | copy-start | bytes 786436
  3.2 0.9 %copy-start.2 = (s32[64,512]{1,0:T(8,128)S(1)}, s32[64,512]{1,0:T(8,128)}, u32[]{:S(2)}) copy-start(s32[64,512]{1,0:T(8,128)} %land_hbm.1) | copy-start | bytes 393220
  6.3 23.0 %collective-permute-start = (f32[2,2,16,512]{3,2,1,0:T(8,128)S(1)}, f32[2,2,16,512]{3,2,1,0:T(8,128)S(1)}, u32[]{:S(2)}, u32[]{:S(2)}) collective-permute-start(f32[2,2,16,512]{3,2,1,0:T(8,128)S(1)} %get-tuple-element.21), channel_id=1, source_target_pairs={{0,1},{1,0},{2,3},{3,2},{4,5},{5,4},{6,7},{7,6},{8,9},{9,8},{10,11... | collective-permute-start | bytes 393224 | tf_op jit(solution)/shard_map/ppermute | solution.py:478
  6.8 22.5 %collective-permute-start.1 = (f32[2,2,16,512]{3,2,1,0:T(8,128)S(1)}, f32[2,2,16,512]{3,2,1,0:T(8,128)S(1)}, u32[]{:S(2)}, u32[]{:S(2)}) collective-permute-start(f32[2,2,16,512]{3,2,1,0:T(8,128)S(1)} %get-tuple-element.22), channel_id=1, source_target_pairs={{0,2},{1,3},{2,0},{3,1},{4,6},{5,7},{6,4},{7,5},{8,10},{9,11},{10,... | collective-permute-start | bytes 393224 | tf_op jit(solution)/shard_map/ppermute | solution.py:478
  9.4 20.0 %collective-permute-start.2 = (f32[2,2,16,512]{3,2,1,0:T(8,128)S(1)}, f32[2,2,16,512]{3,2,1,0:T(8,128)S(1)}, u32[]{:S(2)}, u32[]{:S(2)}) collective-permute-start(f32[2,2,16,512]{3,2,1,0:T(8,128)S(1)} %get-tuple-element.23), channel_id=1, source_target_pairs={{0,3},{1,2},{2,1},{3,0},{4,7},{5,6},{6,5},{7,4},{8,11},{9,10},{10,... | collective-permute-start | bytes 393224 | tf_op jit(solution)/shard_map/ppermute | solution.py:478
  9.5 12.9 %all-to-all-start = ((f32[8,16,128]{2,1,0:T(8,128)}), f32[8,16,128]{2,1,0:T(8,128)S(1)}, u32[]{:S(2)}, u32[]{:S(2)}) async-start(f32[8,16,128]{2,1,0:T(8,128)} %get-tuple-element.17), calls=%async_computation | async-start | bytes 131072 | tf_op jit(solution)/shard_map/all_to_all | solution.py:499
  15.5 0.7 %copy-start.9 = (s32[1,256]{1,0:T(1,128)S(1)}, s32[1,256]{1,0:T(1,128)}, u32[]{:S(2)}) copy-start(s32[1,256]{1,0:T(1,128)} %param.19) | copy-start | bytes 3076
  15.5 0.7 %copy-start.10 = (s32[1,256]{1,0:T(1,128)S(1)}, s32[1,256]{1,0:T(1,128)}, u32[]{:S(2)}) copy-start(s32[1,256]{1,0:T(1,128)} %param.18) | copy-start | bytes 3076
  16.2 6.2 %copy-start.7 = (s32[1,256,128]{2,1,0:T(8,128)S(1)}, s32[1,256,128]{2,1,0:T(8,128)}, u32[]{:S(2)}) copy-start(s32[1,256,128]{2,1,0:T(8,128)} %param.20) | copy-start | bytes 393220
  16.2 6.2 %copy-start.8 = (f32[1,256,128]{2,1,0:T(8,128)S(1)}, f32[1,256,128]{2,1,0:T(8,128)}, u32[]{:S(2)}) copy-start(f32[1,256,128]{2,1,0:T(8,128)} %param.21) | copy-start | bytes 393220
  29.5 3.7 %collective-permute-start.4 = (f32[114,512]{1,0:T(8,128)S(1)}, f32[114,512]{1,0:T(8,128)S(1)}, u32[]{:S(2)}, u32[]{:S(2)}) collective-permute-start(f32[114,512]{1,0:T(8,128)S(1)} %pad_maximum_fusion.3), channel_id=1, source_target_pairs={{1,2},{2,1},{3,7},{7,3},{5,6},{6,5},{4,8},{8,4},{9,10},{10,9},{11,... | collective-permute-start | bytes 700424 | tf_op jit(solution)/shard_map/ppermute | solution.py:529
  30.3 4.1 %copy-start.4 = (f32[12]{0:T(128)S(1)}, f32[12]{0:T(128)}, u32[]{:S(2)}) copy-start(f32[12]{0:T(128)} %ks_ref.1) | copy-start | bytes 148
  30.3 4.1 %copy-start.5 = (f32[12]{0:T(128)S(1)}, f32[12]{0:T(128)}, u32[]{:S(2)}) copy-start(f32[12]{0:T(128)} %alpha_ref.1) | copy-start | bytes 148
  30.3 4.1 %copy-start.6 = (f32[12]{0:T(128)S(1)}, f32[12]{0:T(128)}, u32[]{:S(2)}) copy-start(f32[12]{0:T(128)} %store_ref.1) | copy-start | bytes 148
  30.3 4.1 %collective-permute-start.3 = (f32[114,512]{1,0:T(8,128)S(1)}, f32[114,512]{1,0:T(8,128)S(1)}, u32[]{:S(2)}, u32[]{:S(2)}) collective-permute-start(f32[114,512]{1,0:T(8,128)S(1)} %pad_maximum_fusion.2), channel_id=1, source_target_pairs={{0,1},{1,0},{2,3},{3,2},{4,5},{5,4},{6,7},{7,6},{8,9},{9,8},{10,11... | collective-permute-start | bytes 700424 | tf_op jit(solution)/shard_map/ppermute | solution.py:528
  41.4 4.4 %collective-permute-start.5 = (f32[3,16,512]{2,1,0:T(8,128)S(1)}, f32[3,16,512]{2,1,0:T(8,128)S(1)}, u32[]{:S(2)}, u32[]{:S(2)}) collective-permute-start(f32[3,16,512]{2,1,0:T(8,128)S(1)} %get-tuple-element.27), channel_id=1, source_target_pairs={{0,1},{1,0},{2,3},{3,2},{4,5},{5,4},{6,7},{7,6},{8,9},{9,8},{10,11... | collective-permute-start | bytes 294920 | tf_op jit(solution)/shard_map/ppermute | solution.py:478
  44.1 5.5 %collective-permute-start.6 = (f32[3,16,512]{2,1,0:T(8,128)S(1)}, f32[3,16,512]{2,1,0:T(8,128)S(1)}, u32[]{:S(2)}, u32[]{:S(2)}) collective-permute-start(f32[3,16,512]{2,1,0:T(8,128)S(1)} %get-tuple-element.28), channel_id=1, source_target_pairs={{0,2},{1,3},{2,0},{3,1},{4,6},{5,7},{6,4},{7,5},{8,10},{9,11},{10,... | collective-permute-start | bytes 294920 | tf_op jit(solution)/shard_map/ppermute | solution.py:478
  45.8 5.1 %collective-permute-start.7 = (f32[3,16,512]{2,1,0:T(8,128)S(1)}, f32[3,16,512]{2,1,0:T(8,128)S(1)}, u32[]{:S(2)}, u32[]{:S(2)}) collective-permute-start(f32[3,16,512]{2,1,0:T(8,128)S(1)} %get-tuple-element.29), channel_id=1, source_target_pairs={{0,3},{1,2},{2,1},{3,0},{4,7},{5,6},{6,5},{7,4},{8,11},{9,10},{10,... | collective-permute-start | bytes 294920 | tf_op jit(solution)/shard_map/ppermute | solution.py:478

commit v4 on v3

--- a/solution.py
+++ b/solution.py
@@ -21,6 +21,7 @@
 FLAT = ("tile", "layer")
 
 in_vmem = pl.BlockSpec(memory_space=pltpu.VMEM)
+in_hbm = pl.BlockSpec(memory_space=pltpu.HBM)
 in_smem = pl.BlockSpec(memory_space=pltpu.SMEM)
 
 
@@ -61,7 +62,7 @@
 
 def river_kernel(
     breadth, place_ref, cells_ref, bed_ref, section_ref, row_ref, diag_ref, rhs_ref, slot_section_ref,
-    spot_sc, dhigh_sc, dlow_sc, rhigh_sc, rlow_sc, turned_sc, sum_sc,
+    block_sc, spot_sc, dhigh_sc, dlow_sc, rhigh_sc, rlow_sc, sum_sc,
 ):
     rows = section_ref.shape[0]
     slots = row_ref.shape[1]
@@ -75,6 +76,7 @@
     slot_section_ref[...] = picked
 
     block, spot = split_cells(cells_ref[...], place_ref[0], breadth, BLOCK)
+    block_sc[...] = block
     spot_sc[...] = spot
     bed = bed_ref[...]
     for value, high_sc, low_sc in ((bed, dhigh_sc, dlow_sc), (bed * picked, rhigh_sc, rlow_sc)):
@@ -84,48 +86,37 @@
     share = LANES // BLOCK
     blocks = share * diag_ref.shape[0]
     group = 32
-    tiles = slots // LANES
-    for part in range(tiles):
-        turned_sc[part] = block[part * LANES:(part + 1) * LANES, :].T
-    names = lax.broadcasted_iota(jnp.int32, (LANES, LANES), 1)
-    names = [(names + start).astype(jnp.float32).astype(jnp.bfloat16) for start in range(0, blocks, LANES)]
-    one = jnp.ones((LANES, LANES), jnp.bfloat16)
-    zero = jnp.zeros((LANES, LANES), jnp.bfloat16)
+    one = jnp.ones((16, LANES), jnp.bfloat16)
 
     def step(number, total):
-        first = number * group
-        columns = turned_sc[first // LANES]
-        columns = pltpu.roll(columns, lax.rem(LANES - lax.rem(first, LANES), LANES), 1)
         left, right = [], []
         for place in range(group):
-            slot = first + place
+            slot = number * group + place
             spots = row_copies(spot_sc, slot)
-            left.append(
+            left.append(one_hot(row_copies(block_sc, slot), blocks, one))
+            right.append(
                 jnp.concatenate(
                     [one_hot(spots, BLOCK, row_copies(ref, slot)) for ref in (dhigh_sc, dlow_sc, rhigh_sc, rlow_sc)],
                     axis=0,
                 )
             )
-            column = jnp.broadcast_to(columns[:, place:place + 1], (LANES, LANES)).astype(jnp.bfloat16)
-            right.append(jnp.concatenate([jnp.where(column == name, one, zero) for name in names], axis=1))
         return total + lax.dot_general(
             jnp.concatenate(left, axis=1),
-            jnp.concatenate(right, axis=0),
-            (((1,), (0,)), ((), ())),
+            jnp.concatenate(right, axis=1),
+            (((1,), (1,)), ((), ())),
             preferred_element_type=jnp.float32,
         )
 
-    total = lax.fori_loop(0, slots // group, step, jnp.zeros((4 * BLOCK, blocks), jnp.float32))
+    total = lax.fori_loop(0, slots // group, step, jnp.zeros((blocks, 4 * BLOCK), jnp.float32))
+    sum_sc[...] = total + pltpu.roll(total, LANES - BLOCK, 1)
     lane = lax.broadcasted_iota(jnp.int32, diag_ref.shape, 1) // BLOCK
-    for number, ref in ((0, diag_ref), (2, rhs_ref)):
-        first = number * BLOCK
-        both = total[first:first + BLOCK] + total[first + BLOCK:first + 2 * BLOCK]
-        both = jnp.concatenate([both] * share, axis=0)
-        for part in range(blocks // LANES):
-            sum_sc[pl.ds(part * LANES, LANES), :] = both[:, part * LANES:(part + 1) * LANES].T
-        result = sum_sc[pl.ds(0, blocks // share, stride=share), :]
-        for part in range(1, share):
-            result = jnp.where(lane == part, sum_sc[pl.ds(part, blocks // share, stride=share), :], result)
+    parts = [sum_sc[pl.ds(part, blocks // share, stride=share), :] for part in range(share)]
+    for ref, first in ((diag_ref, 0), (rhs_ref, 2)):
+        result = None
+        for part in range(share):
+            shift = (part - first) * BLOCK % LANES
+            moved = pltpu.roll(parts[part], shift, 1) if shift else parts[part]
+            result = moved if result is None else jnp.where(lane == part, moved, result)
         ref[...] = result
 
 
@@ -160,33 +151,87 @@
             out_ref[1, layer] = soil_ref[layer, rows, :].astype(jnp.float32)
 
 
-def flow_kernel(
-    groups, place_ref, ks_ref, alpha_ref, store_ref, land_ref, near_ref, far_ref, diag_ref, rhs_ref, *refs,
-):
-    block_refs, head_refs = refs[:groups], refs[groups:2 * groups]
+class Rows:
+    def __init__(self, layers, breadth):
+        self.layers, self.breadth, self.per_row = layers, breadth, breadth // LANES
+
+    def get(self, ref, row):
+        spot = pl.ds(row * self.layers, self.layers)
+        return jnp.concatenate([ref[part, spot, :] for part in range(self.per_row)], axis=1)
+
+    def put(self, ref, row, value):
+        spot = pl.ds(row * self.layers, self.layers)
+        for part in range(self.per_row):
+            ref[part, spot, :] = value[:, part * LANES:(part + 1) * LANES]
+
+    def put_layer(self, ref, layer, row, value):
+        for part in range(self.per_row):
+            spot = pl.ds(row * self.layers + layer, value.shape[0], stride=self.layers)
+            ref[part, spot, :] = value[:, part * LANES:(part + 1) * LANES]
+
+    def east(self, field):
+        return pltpu.roll(field, self.breadth - 1, 1)
+
+    def west(self, field):
+        return pltpu.roll(field, 1, 1)
+
+    def below(self, field):
+        return pltpu.roll(field, self.layers - 1, 0)
+
+    def above(self, field):
+        return pltpu.roll(field, 1, 0)
+
+
+def face_weights(rows, refs, first, last, diag_of, base_of, finish):
+    now_ref, ks_ref, alpha_ref, land_ref, wx_ref, wy_ref, wz_ref = refs
+    level = lax.broadcasted_iota(jnp.int32, (rows.layers, rows.breadth), 0)
+    column = lax.broadcasted_iota(jnp.int32, (rows.layers, rows.breadth), 1)
+    not_bottom = level < rows.layers - 1
+    not_last = column < rows.breadth - 1
+
+    def conduct(row):
+        cond = rows.get(ks_ref, row) * jnp.exp(rows.get(alpha_ref, row) * jnp.minimum(rows.get(now_ref, row), 0.0))
+        return cond, cond * land_ref[pl.ds(row, 1), :]
+
+    def face(factor, cond, opened, far, far_open):
+        return factor * 2.0 * opened * far_open * reciprocal(cond + far)
+
+    cond, opened = conduct(first)
+    far, far_open = conduct(first + 1)
+    wx = face(LATERAL, cond, opened, far, far_open)
+    rows.put(wx_ref, first, wx)
+    for row in range(first + 1, last):
+        cond, opened, wx_before = far, far_open, wx
+        far, far_open = conduct(row + 1)
+        wx = face(LATERAL, cond, opened, far, far_open)
+        wy = face(LATERAL, cond, opened, rows.east(cond), rows.east(opened))
+        wz = face(VERTICAL, cond, opened, rows.below(cond), rows.below(opened))
+        wy = jnp.where(not_last, wy, 0.0)
+        wz = jnp.where(not_bottom, wz, 0.0)
+        wz_above = rows.above(wz)
+        rows.put(wx_ref, row, wx)
+        rows.put(wy_ref, row, wy)
+        rows.put(wz_ref, row, wz)
+        diagonal = diag_of(row) + wx_before + wx + wy + rows.west(wy) + wz + wz_above
+        finish(row, diagonal, base_of(row) + GRAVITY * (wz_above - wz))
+
+
+def stage_kernel(groups, place_ref, ks_ref, alpha_ref, store_ref, land_ref, near_ref, far_ref, after_ref, *refs):
+    block_refs = refs[:groups]
     (
-        soil_sc, first_sc, ks_sc, alpha_sc, diag_sc, rhs_sc, wx_sc, wy_sc, wz_sc, base_sc, inv_sc,
-        ping_sc, pong_sc, land_sc, dtop_sc, rtop_sc,
-    ) = refs[2 * groups:]
+        first_out, ks_out, alpha_out, store_out, land_out, wx_out, wy_out, wz_out, diag_out, base_out, soil_sc,
+    ) = refs[groups:]
     _, held, span, breadth = block_refs[0].shape
     layers = groups * held
     window = span + 2 * HALO
-    per_row = breadth // LANES
-    side = HALO * per_row
-
-    def put_rows(ref, layer, row, value):
-        for part in range(per_row):
-            spot = pl.ds(row * layers + layer, value.shape[0], stride=layers)
-            ref[part, spot, :] = value[:, part * LANES:(part + 1) * LANES]
+    rows = Rows(layers, breadth)
 
     for step, block_ref in enumerate(block_refs):
         for held_layer in range(held):
             layer = (place_ref[2] ^ step) * held + held_layer
-            put_rows(first_sc, layer, HALO, block_ref[0, held_layer])
-            put_rows(soil_sc, layer, HALO, block_ref[1, held_layer])
-    land_sc[pl.ds(HALO, span), :] = land_ref[...]
-    dtop_sc[pl.ds(side, span * per_row), :] = diag_ref[...]
-    rtop_sc[pl.ds(side, span * per_row), :] = rhs_ref[...]
+            rows.put_layer(first_out, layer, HALO, block_ref[0, held_layer])
+            rows.put_layer(soil_sc, layer, HALO, block_ref[1, held_layer])
+    land_out[pl.ds(HALO, span), :] = land_ref[...]
 
     def put_halo(ref, partner, row):
         def entry(number):
@@ -194,14 +239,9 @@
 
         for number in range(layers):
             layer = (partner ^ (number // held)) * held + number % held
-            put_rows(first_sc, layer, row, entry(number))
-            put_rows(soil_sc, layer, row, entry(layers + number))
-        land_sc[pl.ds(row, HALO), :] = entry(2 * layers)
-        for number, top_sc in ((2 * layers + 1, dtop_sc), (2 * layers + 2, rtop_sc)):
-            value = entry(number)
-            for part in range(per_row):
-                spot = pl.ds(row * per_row + part, HALO, stride=per_row)
-                top_sc[spot, :] = value[:, part * LANES:(part + 1) * LANES]
+            rows.put_layer(first_out, layer, row, entry(number))
+            rows.put_layer(soil_sc, layer, row, entry(layers + number))
+        land_out[pl.ds(row, HALO), :] = entry(2 * layers)
 
     for odd, above_ref, below_ref in ((0, far_ref, near_ref), (1, near_ref, far_ref)):
         @pl.when(place_ref[3] == odd)
@@ -209,28 +249,6 @@
             for ref, row in ((above_ref, 0), (below_ref, HALO + span)):
                 put_halo(ref, place_ref[4] if ref is near_ref else place_ref[5], row)
 
-    def get(ref, row):
-        spot = pl.ds(row * layers, layers)
-        return jnp.concatenate([ref[part, spot, :] for part in range(per_row)], axis=1)
-
-    def put(ref, row, value):
-        spot = pl.ds(row * layers, layers)
-        for part in range(per_row):
-            ref[part, spot, :] = value[:, part * LANES:(part + 1) * LANES]
-
-    level = lax.broadcasted_iota(jnp.int32, (layers, breadth), 0)
-    column = lax.broadcasted_iota(jnp.int32, (layers, breadth), 1)
-    top = level == 0
-    not_bottom = level < layers - 1
-    not_last = column < breadth - 1
-
-    def riv_row(ref, row):
-        first = row * per_row
-        parts = [
-            jnp.broadcast_to(ref[pl.ds(first + part, 1), :], (layers, LANES)) for part in range(per_row)
-        ]
-        return jnp.where(top, jnp.concatenate(parts, axis=1), 0.0)
-
     lane = lax.broadcasted_iota(jnp.int32, (layers, LANES), 1)
 
     def lane_table(ref):
@@ -240,104 +258,102 @@
         return table
 
     tables = [lane_table(ref) for ref in (ks_ref, alpha_ref, store_ref)]
-
-    def lookup(soil):
-        found = []
-        for table in tables:
+    for row in range(window):
+        soil = rows.get(soil_sc, row).astype(jnp.int32)
+        for table, out in zip(tables, (ks_out, alpha_out, store_out)):
             parts = [
                 jnp.take_along_axis(
                     table, soil[:, part * LANES:(part + 1) * LANES], axis=1, mode="promise_in_bounds"
                 )
-                for part in range(per_row)
+                for part in range(rows.per_row)
             ]
-            found.append(jnp.concatenate(parts, axis=1))
-        return found
-
-    for row in range(window):
-        ks, alpha, store = lookup(get(soil_sc, row).astype(jnp.int32))
-        put(ks_sc, row, ks)
-        put(alpha_sc, row, alpha)
-        put(diag_sc, row, store + riv_row(dtop_sc, row))
-        put(rhs_sc, row, store * get(first_sc, row) + riv_row(rtop_sc, row))
-
-    def east(field):
-        return pltpu.roll(field, breadth - 1, 1)
-
-    def west(field):
-        return pltpu.roll(field, 1, 1)
-
-    def below(field):
-        return pltpu.roll(field, layers - 1, 0)
-
-    def above(field):
-        return pltpu.roll(field, 1, 0)
-
-    def make_weights(now_sc, first, last):
-        def conduct(row):
-            cond = get(ks_sc, row) * jnp.exp(get(alpha_sc, row) * jnp.minimum(get(now_sc, row), 0.0))
-            return cond, cond * land_sc[pl.ds(row, 1), :]
-
-        def face(factor, cond, opened, far, far_open):
-            return factor * 2.0 * opened * far_open * reciprocal(cond + far)
-
-        def step(row, carried):
-            cond, opened, wx_before = carried
-            far, far_open = conduct(row + 1)
-            wx = face(LATERAL, cond, opened, far, far_open)
-            wy = jnp.where(not_last, face(LATERAL, cond, opened, east(cond), east(opened)), 0.0)
-            wz = jnp.where(not_bottom, face(VERTICAL, cond, opened, below(cond), below(opened)), 0.0)
-            wz_above = above(wz)
-            total = get(diag_sc, row) + wx_before + wx + wy + west(wy) + wz + wz_above
-            inverse = reciprocal(total)
-            put(wx_sc, row, wx)
-            put(wy_sc, row, wy)
-            put(wz_sc, row, wz)
-            put(inv_sc, row, inverse)
-            put(base_sc, row, get(rhs_sc, row) + GRAVITY * (wz_above - wz))
-            return far, far_open, wx
-
-        cond, opened = conduct(first)
-        far, far_open = conduct(first + 1)
-        wx = face(LATERAL, cond, opened, far, far_open)
-        put(wx_sc, first, wx)
-        carried = far, far_open, wx
-        for row in range(first + 1, last):
-            carried = step(row, carried)
-
-    def sweep(now_sc, later_sc, first, last):
-        def step(row, carried):
-            before, here, wx_before = carried
-            after = get(now_sc, row + 1)
-            wx = get(wx_sc, row)
-            wy = get(wy_sc, row)
-            wz = get(wz_sc, row)
-            total = get(base_sc, row) + wx_before * before + wx * after
-            total = total + wy * east(here) + west(wy * here)
-            total = total + wz * below(here) + above(wz * here)
-            put(later_sc, row, total * get(inv_sc, row))
-            return here, after, wx
-
-        carried = get(now_sc, first - 1), get(now_sc, first), get(wx_sc, first - 1)
+            rows.put(out, row, jnp.concatenate(parts, axis=1))
+
+    def finish(row, diagonal, base):
+        rows.put(diag_out, row, diagonal)
+        rows.put(base_out, row, base)
+
+    face_weights(
+        rows, (first_out, ks_out, alpha_out, land_out, wx_out, wy_out, wz_out), 0, window - 1,
+        lambda row: rows.get(store_out, row),
+        lambda row: rows.get(store_out, row) * rows.get(first_out, row),
+        finish,
+    )
+
+
+def flow_kernel(groups, place_ref, near_ref, far_ref, diag_ref, rhs_ref, *refs):
+    first_ref, ks_ref, alpha_ref, store_ref, land_ref, wx_ref, wy_ref, wz_ref, partial_ref, gravity_ref = refs[:10]
+    head_refs = refs[10:10 + groups]
+    wx_sc, wy_sc, wz_sc, base_sc, inv_sc, ping_sc, pong_sc, dtop_sc, rtop_sc = refs[10 + groups:]
+    held, span, breadth = head_refs[0].shape
+    held -= 1
+    layers = groups * held
+    window = span + 2 * HALO
+    rows = Rows(layers, breadth)
+    side = HALO * rows.per_row
+    inner = span * rows.per_row
+
+    is_odd = place_ref[3] == 1
+    for number, (own_ref, top_sc) in enumerate(((diag_ref, dtop_sc), (rhs_ref, rtop_sc))):
+        spot = pl.ds(number * side, side)
+        near, far = near_ref[spot, :], far_ref[spot, :]
+        top_sc[pl.ds(0, side), :] = jnp.where(is_odd, near, far)
+        top_sc[pl.ds(side, inner), :] = own_ref[...]
+        top_sc[pl.ds(side + inner, side), :] = jnp.where(is_odd, far, near)
+
+    top = lax.broadcasted_iota(jnp.int32, (layers, breadth), 0) == 0
+
+    def riv_row(ref, row):
+        parts = [
+            jnp.broadcast_to(ref[pl.ds(row * rows.per_row + part, 1), :], (layers, LANES))
+            for part in range(rows.per_row)
+        ]
+        return jnp.where(top, jnp.concatenate(parts, axis=1), 0.0)
+
+    def finish(row, diagonal, base):
+        rows.put(inv_sc, row, reciprocal(diagonal + riv_row(dtop_sc, row)))
+        rows.put(base_sc, row, base + riv_row(rtop_sc, row))
+
+    def sweep(now_ref, later_ref, weights, first, last):
+        before, here = rows.get(now_ref, first - 1), rows.get(now_ref, first)
+        wx_before = rows.get(weights[0], first - 1)
         for row in range(first, last):
-            carried = step(row, carried)
-
-    now_sc, spare = first_sc, [ping_sc, pong_sc]
+            after = rows.get(now_ref, row + 1)
+            wx, wy, wz = [rows.get(ref, row) for ref in weights]
+            total = rows.get(base_sc, row) + wx_before * before + wx * after
+            total = total + wy * rows.east(here) + rows.west(wy * here)
+            total = total + wz * rows.below(here) + rows.above(wz * here)
+            rows.put(later_ref, row, total * rows.get(inv_sc, row))
+            before, here, wx_before = here, after, wx
+
+    now_ref, spare = first_ref, [ping_sc, pong_sc]
     first, last = 0, window
     for picard in range(ITERS):
-        make_weights(now_sc, first, last - 1)
+        if picard == 0:
+            weights = wx_ref, wy_ref, wz_ref
+            for row in range(first + 1, last - 1):
+                finish(row, rows.get(partial_ref, row), rows.get(gravity_ref, row))
+        else:
+            weights = wx_sc, wy_sc, wz_sc
+            face_weights(
+                rows, (now_ref, ks_ref, alpha_ref, land_ref, *weights), first, last - 1,
+                lambda row: rows.get(store_ref, row),
+                lambda row: rows.get(store_ref, row) * rows.get(first_ref, row),
+                finish,
+            )
         for _ in range(SWEEPS):
             first, last = first + 1, last - 1
-            later_sc = spare[0]
-            sweep(now_sc, later_sc, first, last)
-            spare = [spare[1], later_sc]
-            now_sc = later_sc
-    for part in range(per_row):
+            later_ref = spare[0]
+            sweep(now_ref, later_ref, weights, first, last)
+            spare = [spare[1], later_ref]
+            now_ref = later_ref
+    for part in range(rows.per_row):
         lanes = pl.ds(part * LANES, LANES)
-        top_rows = now_sc[part, pl.ds(HALO * layers, span, stride=layers), :]
+        top_rows = now_ref[part, pl.ds(HALO * layers, span, stride=layers), :]
         for step, head_ref in enumerate(head_refs):
             for held_layer in range(held):
                 layer = (place_ref[2] ^ step) * held + held_layer
-                head_ref[held_layer, :, lanes] = now_sc[part, pl.ds(HALO * layers + layer, span, stride=layers), :]
+                head_ref[held_layer, :, lanes] = now_ref[part, pl.ds(HALO * layers + layer, span, stride=layers), :]
             head_ref[held, :, lanes] = top_rows
 
 
@@ -486,7 +502,7 @@
             jax.ShapeDtypeStruct((tiles, reach_rows, node_count), jnp.float32),
             jax.ShapeDtypeStruct((span, breadth), jnp.float32),
         ),
-        [in_smem] + [pl.BlockSpec(memory_space=pl.ANY)] * 4,
+        [in_smem] + [in_hbm] * 4,
         [
             pltpu.VMEM(head_start.shape, jnp.float32),
             pltpu.VMEM(soil_class.shape, jnp.int32),
@@ -506,39 +522,43 @@
         functools.partial(river_kernel, breadth),
         (riv_shape, riv_shape, jax.ShapeDtypeStruct((slots, node_count), jnp.float32)),
         [in_smem] + [in_vmem] * 4,
-        [node_scratch] * 5
-        + [pltpu.VMEM((slots // LANES, LANES, LANES), jnp.float32)]
+        [node_scratch] * 6
         + [pltpu.VMEM((span * breadth // BLOCK, LANES), jnp.float32)],
         8 * span * breadth * slots * LANES, 4 * node_bytes,
     )(place, cells, bed, whole_section, reach)
 
-    def edge(bottom):
+    side = HALO * per_row
+
+    def grid_edge(bottom):
         row = jnp.where(bottom, span - HALO, 0)
         grid = [lax.dynamic_slice_in_dim(block, row, HALO, 2) for block in received]
-        river = [jnp.where(bottom, term[blocks - side:], term[:side]) for term in (diag, rhs)]
-        return jnp.concatenate(
-            [
-                jnp.stack(grid, axis=1).reshape(2 * layers * HALO, breadth),
-                lax.dynamic_slice_in_dim(land, row, HALO, 0),
-                jnp.concatenate(river).reshape(2 * HALO, breadth),
-            ]
-        )
-
-    side = HALO * per_row
-    near_halo = lax.ppermute(edge(odd == 0), "layer", near)
-    far_halo = lax.ppermute(edge(odd == 1), FLAT, far)
+        grid = jnp.stack(grid, axis=1).reshape(2 * layers * HALO, breadth)
+        return jnp.concatenate([grid, lax.dynamic_slice_in_dim(land, row, HALO, 0)])
+
+    def river_edge(bottom):
+        return jnp.concatenate([jnp.where(bottom, term[blocks - side:], term[:side]) for term in (diag, rhs)])
+
+    near_grid = lax.ppermute(grid_edge(odd == 0), "layer", near)
+    far_grid = lax.ppermute(grid_edge(odd == 1), FLAT, far)
+    near_river = lax.ppermute(river_edge(odd == 0), "layer", near)
+    far_river = lax.ppermute(river_edge(odd == 1), FLAT, far)
 
     window = span + 2 * HALO
-    field = pltpu.VMEM((per_row, window * layers, LANES), jnp.float32)
+    cells_held = layers * window * breadth
+    field_shape = jax.ShapeDtypeStruct((per_row, window * layers, LANES), jnp.float32)
+    field = pltpu.VMEM(field_shape.shape, jnp.float32)
+    staged = call(
+        functools.partial(stage_kernel, groups),
+        (field_shape,) * 4 + (jax.ShapeDtypeStruct((window, breadth), jnp.float32),) + (field_shape,) * 5,
+        [in_smem] * 4 + [in_vmem] * (4 + groups), [field], 60 * cells_held, 40 * cells_held,
+    )(place, ks_table, alpha_table, store_table, land, near_grid, far_grid, diag, *received)
     out_shape = jax.ShapeDtypeStruct((held + 1, span, breadth), jnp.float32)
     out = call(
         functools.partial(flow_kernel, groups), (out_shape,) * groups,
-        [in_smem] * 4 + [in_vmem] * (5 + groups),
-        [field] * 13
-        + [pltpu.VMEM((window, breadth), jnp.float32)]
-        + [pltpu.VMEM((window * per_row, LANES), jnp.float32)] * 2,
-        100 * layers * window * breadth, 8 * layers * window * breadth,
-    )(place, ks_table, alpha_table, store_table, land, near_halo, far_halo, diag, rhs, *received)
+        [in_smem] + [in_vmem] * (4 + len(staged)),
+        [field] * 7 + [pltpu.VMEM((window * per_row, LANES), jnp.float32)] * 2,
+        100 * cells_held, 40 * cells_held,
+    )(place, near_river, far_river, diag, rhs, *staged)
     back = exchange(out)
 
     packed = pltpu.VMEM((slots // groups, LANES), jnp.float32)

time: 65.2 us -> 65.4 us (level)
  waiting for transfers between devices: 12.3 us -> 11.2 us
  starting transfers between devices: 17.2 us -> 17.9 us
    pallas_call x0 -> x1, Pallas kernels: none -> 3.75 us  [on_device(): call(functools.partial(stage_kernel, groups), (field_shape,) * 4 + (jax.S...]
    pallas_call x1, Pallas kernels: 7 us -> 3.77 us  [on_device(): call(functools.partial(flow_kernel, groups), (out_shape,) * groups, [in_s...]
    ppermute x2 -> x4, starting transfers between devices: 3.61 us -> 5.61 us  [the longest x1 2.93 us: on_device(): near_grid = lax.ppermute(grid_edge(odd == 0), 'layer', near)]
    ppermute x6, starting transfers between devices: 7.59 us -> 6.32 us  [exchange(): lax.ppermute(parts[step], 'layer', [(i, i ^ step) for i in range(groups)])]
    ppermute x2 -> x4, waiting for transfers between devices: 1.14 us -> 0.01 us  [the longest x1 0.01 us: on_device(): near_grid = lax.ppermute(grid_edge(odd == 0), 'layer', near)]
  transfers between devices with their start and end apart: 9 -> 11, of which waited for: 4 -> 3; matrix products, arithmetic and copies ran while one was open for 0% -> 0% of each run, Pallas kernels for 11% -> 16%
where the time goes in v4:
time: 65.4 us; the launch traced here: 65 us
  Pallas kernels  19.6 us (30%)
  starting transfers between devices  17.9 us (27%)
  waiting for transfers between devices  11.2 us (17%)
  blocking collectives  10.3 us (16%)
  local copies, waits for them, and re-layouts  4.36 us (7%)
  between operations  0.92 us (1%)
  other arithmetic  0.72 us (1%)
    all_to_all x1, blocking collectives, on_device(): lax.all_to_all(partial.reshape(tiles, reach_rows, node_count), 'tile', 0, 0)  10.3 us
    pallas_call x1, Pallas kernels, on_device(): call(functools.partial(river_kernel, breadth), (riv_shape, riv_shape, jax...  6.8 us
    ppermute x6, starting transfers between devices, exchange(): lax.ppermute(parts[step], 'layer', [(i, i ^ step) for i in range(groups)])  6.32 us
    all_to_all x1, waiting for transfers between devices, on_device(): lax.all_to_all(spread, 'tile', 0, 0).reshape(tiles * reach_rows, node_count)  6.14 us
    all_to_all x1, starting transfers between devices, on_device(): lax.all_to_all(spread, 'tile', 0, 0).reshape(tiles * reach_rows, node_count)  6.01 us
    ppermute x6, waiting for transfers between devices, exchange(): lax.ppermute(parts[step], 'layer', [(i, i ^ step) for i in range(groups)])  5.05 us
    unnamed x22, local copies, waits for them, and re-layouts  4.12 us
    pallas_call x1, Pallas kernels, on_device(): call(functools.partial(flow_kernel, groups), (out_shape,) * groups, [in_s...  3.77 us
  transfers between devices with their start and end apart: 11, of which 3 were waited for; matrix products, arithmetic and copies ran while one was open for 0% of the time, Pallas kernels for 16%

profile of v4, /device:TPU:0, one launch (start us, length us, event | category | flops | bytes accessed | tf_op | source)
XLA Modules:
  0.0 65.0 jit_solution(5275014397474834008)
XLA Ops:
  0.7 0.6 copy-done.3
  1.3 0.9 %copy-done = f32[2,64,512]{2,1,0:T(8,128)S(1)} copy-done((f32[2,64,512]{2,1,0:T(8,128)S(1)}, f32[2,64,512]{2,1,0:T(8,128)}, u32[]{:S(2)}) %copy-start) | copy-done | bytes 262168
  2.3 0.9 %copy-done.1 = s32[2,64,512]{2,1,0:T(8,128)S(1)} copy-done((s32[2,64,512]{2,1,0:T(8,128)S(1)}, s32[2,64,512]{2,1,0:T(8,128)}, u32[]{:S(2)}) %copy-start.1) | copy-done | bytes 262168
  3.2 0.9 %copy-done.2 = s32[64,512]{1,0:T(8,128)S(1)} copy-done((s32[64,512]{1,0:T(8,128)S(1)}, s32[64,512]{1,0:T(8,128)}, u32[]{:S(2)}) %copy-start.2) | copy-done | bytes 131096
  4.1 2.1 %shard_map.122 = (f32[2,2,16,512]{3,2,1,0:T(8,128)S(1)}, f32[2,2,16,512]{3,2,1,0:T(8,128)S(1)}, f32[2,2,16,512]{3,2,1,0:T(8,128)S(1)}, f32[2,2,16,512]{3,2,1,0:T...) custom-call(s32[6]{0:T(128)S(1)} %stack.57.place_ref, f32[2,64,512]{2,1,0:T(8,128)S(1)} %copy-done, ...), custom_call_target="tpu_custom_call" | custom-call | bytes 1048576 | tf_op jit(solution)/shard_map/pallas_call | solution.py:498
  6.3 0.5 collective-permute-start.2
  6.8 2.6 %collective-permute-start.3 = (f32[2,2,16,512]{3,2,1,0:T(8,128)S(1)}, f32[2,2,16,512]{3,2,1,0:T(8,128)S(1)}, u32[]{:S(2)}, u32[]{:S(2)}) collective-permute-start(f32[2,2,16,512]{3,2,1,0:T(8,128)S(1)} %get-tuple-element.34), channel_id=1, source_target_pairs={{0,2},{1,3},{2,0},{3,1},{4,6},{5,7},{6,4},{7,5},{8,10},{9,11},{10,... | collective-permute-start | bytes 393224 | tf_op jit(solution)/shard_map/ppermute | solution.py:494
  9.5 6.0 %all-to-all-start = ((f32[8,16,128]{2,1,0:T(8,128)}), f32[8,16,128]{2,1,0:T(8,128)S(1)}, u32[]{:S(2)}, u32[]{:S(2)}) async-start(f32[8,16,128]{2,1,0:T(8,128)} %get-tuple-element.27), calls=%async_computation | async-start | bytes 131072 | tf_op jit(solution)/shard_map/all_to_all | solution.py:515
  15.5 0.7 %copy-done.9 = s32[1,256]{1,0:T(1,128)S(1)} copy-done((s32[1,256]{1,0:T(1,128)S(1)}, s32[1,256]{1,0:T(1,128)}, u32[]{:S(2)}) %copy-start.9) | copy-done | bytes 1048
  16.2 6.1 %all-to-all-done = f32[8,16,128]{2,1,0:T(8,128)S(1)} async-done(((f32[8,16,128]{2,1,0:T(8,128)}), f32[8,16,128]{2,1,0:T(8,128)S(1)}, u32[]{:S(2)}, u32[]{:S(2)}) %all-to-all-start) | async-done | bytes 65568 | tf_op jit(solution)/shard_map/all_to_all | solution.py:515
  22.4 6.8 %shard_map.123 = (f32[64,128]{1,0:T(8,128)S(1)}, f32[64,128]{1,0:T(8,128)S(1)}, f32[256,128]{1,0:T(8,128)S(1)}) custom-call(s32[6]{0:T(128)S(1)} %stack.57.place_ref, s32[256,128]{1,0:T(8,128)S(1)} %bitcast.29, f32[256,128]{1,0:T(8,128)S(1)} %bitcast.31, f32[128,128]{1,0:T(8,128)S(1)} %bitcast.27, s32[1,256]{1,0:T(1,128)S(1)} %multiply_add_fusion.row_ref), custom_call_target="tpu_custom_call" | custom-call | flops 2147483648 | bytes 524288 | tf_op jit(solution)/shard_map/pallas_call | solution.py:521
  29.5 0.7 %collective-permute-start.6 = (f32[102,512]{1,0:T(8,128)S(1)}, f32[102,512]{1,0:T(8,128)S(1)}, u32[]{:S(2)}, u32[]{:S(2)}) collective-permute-start(f32[102,512]{1,0:T(8,128)S(1)} %pad_maximum_fusion.3), channel_id=1, source_target_pairs={{1,2},{2,1},{3,7},{7,3},{5,6},{6,5},{4,8},{8,4},{9,10},{10,9},{11,... | collective-permute-start | bytes 626696 | tf_op jit(solution)/shard_map/ppermute | solution.py:542
  30.2 2.9 %collective-permute-start.5 = (f32[102,512]{1,0:T(8,128)S(1)}, f32[102,512]{1,0:T(8,128)S(1)}, u32[]{:S(2)}, u32[]{:S(2)}) collective-permute-start(f32[102,512]{1,0:T(8,128)S(1)} %pad_maximum_fusion.2), channel_id=1, source_target_pairs={{0,1},{1,0},{2,3},{3,2},{4,5},{5,4},{6,7},{7,6},{8,9},{9,8},{10,11... | collective-permute-start | bytes 626696 | tf_op jit(solution)/shard_map/ppermute | solution.py:541
  33.1 0.7 %collective-permute-start.1 = (f32[48,128]{1,0:T(8,128)S(1)}, f32[48,128]{1,0:T(8,128)S(1)}, u32[]{:S(2)}, u32[]{:S(2)}) collective-permute-start(f32[48,128]{1,0:T(8,128)S(1)} %pad_maximum_fusion.5), channel_id=1, source_target_pairs={{1,2},{2,1},{3,7},{7,3},{5,6},{6,5},{4,8},{8,4},{9,10},{10,9},{11,... | collective-permute-start | bytes 73736 | tf_op jit(solution)/shard_map/ppermute | solution.py:544
  33.8 1.4 %collective-permute-start = (f32[48,128]{1,0:T(8,128)S(1)}, f32[48,128]{1,0:T(8,128)S(1)}, u32[]{:S(2)}, u32[]{:S(2)}) collective-permute-start(f32[48,128]{1,0:T(8,128)S(1)} %pad_maximum_fusion.4), channel_id=1, source_target_pairs={{0,1},{1,0},{2,3},{3,2},{4,5},{5,4},{6,7},{7,6},{8,9},{9,8},{10,11... | collective-permute-start | bytes 73736 | tf_op jit(solution)/shard_map/ppermute | solution.py:543
  35.2 3.8 %shard_map.124 = (f32[4,224,128]{2,1,0:T(8,128)S(1)}, f32[4,224,128]{2,1,0:T(8,128)S(1)}, f32[4,224,128]{2,1,0:T(8,128)S(1)}, f32[4,224,128]{2,1,0:T(8,128)S(1)}...) custom-call(s32[6]{0:T(128)S(1)} %stack.57.place_ref, ...), custom_call_target="tpu_custom_call" | custom-call | flops 6881280 | bytes 4587520 | tf_op jit(solution)/shard_map/pallas_call | solution.py:550
  39.0 3.8 %shard_map.125 = (f32[3,16,512]{2,1,0:T(8,128)S(1)}, f32[3,16,512]{2,1,0:T(8,128)S(1)}, f32[3,16,512]{2,1,0:T(8,128)S(1)}, f32[3,16,512]{2,1,0:T(8,128)S(1)}) custom-call(s32[6]{0:T(128)S(1)} %stack.57.place_ref, f32[48,128]{1,0:T(8,128)S(1)} %collective-permute-done.near_ref, f32[48,128]{1,0:T(8,128)S(1)} %collective-permute-done.1.far_ref, ...), custom_call_target="tpu_custom_call" | custom-call | flops 11468800 | bytes 4587520 | tf_op jit(solution)/shard_map/pallas_call | solution.py:556
  42.8 1.4 %collective-permute-start.7 = (f32[3,16,512]{2,1,0:T(8,128)S(1)}, f32[3,16,512]{2,1,0:T(8,128)S(1)}, u32[]{:S(2)}, u32[]{:S(2)}) collective-permute-start(f32[3,16,512]{2,1,0:T(8,128)S(1)} %get-tuple-element.47), channel_id=1, source_target_pairs={{0,1},{1,0},{2,3},{3,2},{4,5},{5,4},{6,7},{7,6},{8,9},{9,8},{10,11... | collective-permute-start | bytes 294920 | tf_op jit(solution)/shard_map/ppermute | solution.py:494
  44.2 1.7 %collective-permute-start.8 = (f32[3,16,512]{2,1,0:T(8,128)S(1)}, f32[3,16,512]{2,1,0:T(8,128)S(1)}, u32[]{:S(2)}, u32[]{:S(2)}) collective-permute-start(f32[3,16,512]{2,1,0:T(8,128)S(1)} %get-tuple-element.48), channel_id=1, source_target_pairs={{0,2},{1,3},{2,0},{3,1},{4,6},{5,7},{6,4},{7,5},{8,10},{9,11},{10,... | collective-permute-start | bytes 294920 | tf_op jit(solution)/shard_map/ppermute | solution.py:494
  45.9 3.7 %collective-permute-done.8.refs_2_ = f32[3,16,512]{2,1,0:T(8,128)S(1)} collective-permute-done((f32[3,16,512]{2,1,0:T(8,128)S(1)}, f32[3,16,512]{2,1,0:T(8,128)S(1)}, u32[]{:S(2)}, u32[]{:S(2)}) %collective-permute-start.8) | collective-permute-done | bytes 98336 | tf_op jit(solution)/shard_map/ppermute | solution.py:494
  49.6 1.3 %collective-permute-done.9.refs_3_ = f32[3,16,512]{2,1,0:T(8,128)S(1)} collective-permute-done((f32[3,16,512]{2,1,0:T(8,128)S(1)}, f32[3,16,512]{2,1,0:T(8,128)S(1)}, u32[]{:S(2)}, u32[]{:S(2)}) %collective-permute-start.9) | collective-permute-done | bytes 98336 | tf_op jit(solution)/shard_map/ppermute | solution.py:494
  51.0 3.1 %shard_map.126 = (f32[2,64,512]{2,1,0:T(8,128)}, f32[128,128]{1,0:T(8,128)S(1)}) custom-call(s32[6]{0:T(128)S(1)} %stack.57.place_ref, s32[256,128]{1,0:T(8,128)S(1)} %bitcast.30, f32[256,128]{1,0:T(8,128)S(1)} %bitcast.32, f32[256,128]{1,0:T(8,128)S(1)} %get-tuple-element.28.slot_section_ref, s32[1,256]{1,0:T(1,128)S(1)} %multiply_add_fusion.row_ref, ...), custom_call_target="tpu_custom_call" | custom-call | flops 1073741824 | bytes 1048576 | tf_op jit(solution)/shard_map/pallas_call | solution.py:565
  54.1 10.3 %all_to_all.10 = f32[8,16,128]{2,1,0:T(8,128)S(1)} all-to-all(f32[8,16,128]{2,1,0:T(8,128)S(1)} %bitcast.28), channel_id=1, replica_groups=mesh['tile'=8,'layer'=4] {'tile'}, dimensions={0} | all-to-all | bytes 131072 | tf_op jit(solution)/shard_map/all_to_all | solution.py:575
  64.4 0.6 reduce_sum.9
  (42 shorter events, 0.6 us)
Async XLA Ops:
  0.6 0.7 %copy-start.3 = (f32[16,128]{1,0:T(8,128)S(1)}, f32[16,128]{1,0:T(8,128)}, u32[]{:S(2)}) copy-start(f32[16,128]{1,0:T(8,128)} %section_hbm.1) | copy-start | bytes 24580
  1.3 0.9 %copy-start = (f32[2,64,512]{2,1,0:T(8,128)S(1)}, f32[2,64,512]{2,1,0:T(8,128)}, u32[]{:S(2)}) copy-start(f32[2,64,512]{2,1,0:T(8,128)} %head_hbm.1) | copy-start | bytes 786436
  2.3 0.9 %copy-start.1 = (s32[2,64,512]{2,1,0:T(8,128)S(1)}, s32[2,64,512]{2,1,0:T(8,128)}, u32[]{:S(2)}) copy-start(s32[2,64,512]{2,1,0:T(8,128)} %soil_hbm.1) | copy-start | bytes 786436
  3.2 0.9 %copy-start.2 = (s32[64,512]{1,0:T(8,128)S(1)}, s32[64,512]{1,0:T(8,128)}, u32[]{:S(2)}) copy-start(s32[64,512]{1,0:T(8,128)} %land_hbm.1) | copy-start | bytes 393220
  6.3 22.9 %collective-permute-start.2 = (f32[2,2,16,512]{3,2,1,0:T(8,128)S(1)}, f32[2,2,16,512]{3,2,1,0:T(8,128)S(1)}, u32[]{:S(2)}, u32[]{:S(2)}) collective-permute-start(f32[2,2,16,512]{3,2,1,0:T(8,128)S(1)} %get-tuple-element.33), channel_id=1, source_target_pairs={{0,1},{1,0},{2,3},{3,2},{4,5},{5,4},{6,7},{7,6},{8,9},{9,8},{10,11... | collective-permute-start | bytes 393224 | tf_op jit(solution)/shard_map/ppermute | solution.py:494
  6.8 22.5 %collective-permute-start.3 = (f32[2,2,16,512]{3,2,1,0:T(8,128)S(1)}, f32[2,2,16,512]{3,2,1,0:T(8,128)S(1)}, u32[]{:S(2)}, u32[]{:S(2)}) collective-permute-start(f32[2,2,16,512]{3,2,1,0:T(8,128)S(1)} %get-tuple-element.34), channel_id=1, source_target_pairs={{0,2},{1,3},{2,0},{3,1},{4,6},{5,7},{6,4},{7,5},{8,10},{9,11},{10,... | collective-permute-start | bytes 393224 | tf_op jit(solution)/shard_map/ppermute | solution.py:494
  9.4 19.9 %collective-permute-start.4 = (f32[2,2,16,512]{3,2,1,0:T(8,128)S(1)}, f32[2,2,16,512]{3,2,1,0:T(8,128)S(1)}, u32[]{:S(2)}, u32[]{:S(2)}) collective-permute-start(f32[2,2,16,512]{3,2,1,0:T(8,128)S(1)} %get-tuple-element.35), channel_id=1, source_target_pairs={{0,3},{1,2},{2,1},{3,0},{4,7},{5,6},{6,5},{7,4},{8,11},{9,10},{10,... | collective-permute-start | bytes 393224 | tf_op jit(solution)/shard_map/ppermute | solution.py:494
  9.5 12.9 %all-to-all-start = ((f32[8,16,128]{2,1,0:T(8,128)}), f32[8,16,128]{2,1,0:T(8,128)S(1)}, u32[]{:S(2)}, u32[]{:S(2)}) async-start(f32[8,16,128]{2,1,0:T(8,128)} %get-tuple-element.27), calls=%async_computation | async-start | bytes 131072 | tf_op jit(solution)/shard_map/all_to_all | solution.py:515
  15.5 0.7 %copy-start.9 = (s32[1,256]{1,0:T(1,128)S(1)}, s32[1,256]{1,0:T(1,128)}, u32[]{:S(2)}) copy-start(s32[1,256]{1,0:T(1,128)} %param.19) | copy-start | bytes 3076
  15.5 0.7 %copy-start.10 = (s32[1,256]{1,0:T(1,128)S(1)}, s32[1,256]{1,0:T(1,128)}, u32[]{:S(2)}) copy-start(s32[1,256]{1,0:T(1,128)} %param.18) | copy-start | bytes 3076
  16.2 6.2 %copy-start.7 = (s32[1,256,128]{2,1,0:T(8,128)S(1)}, s32[1,256,128]{2,1,0:T(8,128)}, u32[]{:S(2)}) copy-start(s32[1,256,128]{2,1,0:T(8,128)} %param.20) | copy-start | bytes 393220
  16.2 6.2 %copy-start.8 = (f32[1,256,128]{2,1,0:T(8,128)S(1)}, f32[1,256,128]{2,1,0:T(8,128)}, u32[]{:S(2)}) copy-start(f32[1,256,128]{2,1,0:T(8,128)} %param.21) | copy-start | bytes 393220
  29.5 5.7 %collective-permute-start.6 = (f32[102,512]{1,0:T(8,128)S(1)}, f32[102,512]{1,0:T(8,128)S(1)}, u32[]{:S(2)}, u32[]{:S(2)}) collective-permute-start(f32[102,512]{1,0:T(8,128)S(1)} %pad_maximum_fusion.3), channel_id=1, source_target_pairs={{1,2},{2,1},{3,7},{7,3},{5,6},{6,5},{4,8},{8,4},{9,10},{10,9},{11,... | collective-permute-start | bytes 626696 | tf_op jit(solution)/shard_map/ppermute | solution.py:542
  30.2 5.0 %collective-permute-start.5 = (f32[102,512]{1,0:T(8,128)S(1)}, f32[102,512]{1,0:T(8,128)S(1)}, u32[]{:S(2)}, u32[]{:S(2)}) collective-permute-start(f32[102,512]{1,0:T(8,128)S(1)} %pad_maximum_fusion.2), channel_id=1, source_target_pairs={{0,1},{1,0},{2,3},{3,2},{4,5},{5,4},{6,7},{7,6},{8,9},{9,8},{10,11... | collective-permute-start | bytes 626696 | tf_op jit(solution)/shard_map/ppermute | solution.py:541
  33.1 5.9 %collective-permute-start.1 = (f32[48,128]{1,0:T(8,128)S(1)}, f32[48,128]{1,0:T(8,128)S(1)}, u32[]{:S(2)}, u32[]{:S(2)}) collective-permute-start(f32[48,128]{1,0:T(8,128)S(1)} %pad_maximum_fusion.5), channel_id=1, source_target_pairs={{1,2},{2,1},{3,7},{7,3},{5,6},{6,5},{4,8},{8,4},{9,10},{10,9},{11,... | collective-permute-start | bytes 73736 | tf_op jit(solution)/shard_map/ppermute | solution.py:544
  33.8 1.4 %copy-start.4 = (f32[12]{0:T(128)S(1)}, f32[12]{0:T(128)}, u32[]{:S(2)}) copy-start(f32[12]{0:T(128)} %ks_ref.1) | copy-start | bytes 148
  33.8 1.4 %copy-start.5 = (f32[12]{0:T(128)S(1)}, f32[12]{0:T(128)}, u32[]{:S(2)}) copy-start(f32[12]{0:T(128)} %alpha_ref.1) | copy-start | bytes 148
  33.8 1.4 %copy-start.6 = (f32[12]{0:T(128)S(1)}, f32[12]{0:T(128)}, u32[]{:S(2)}) copy-start(f32[12]{0:T(128)} %store_ref.1) | copy-start | bytes 148
  33.8 5.2 %collective-permute-start = (f32[48,128]{1,0:T(8,128)S(1)}, f32[48,128]{1,0:T(8,128)S(1)}, u32[]{:S(2)}, u32[]{:S(2)}) collective-permute-start(f32[48,128]{1,0:T(8,128)S(1)} %pad_maximum_fusion.4), channel_id=1, source_target_pairs={{0,1},{1,0},{2,3},{3,2},{4,5},{5,4},{6,7},{7,6},{8,9},{9,8},{10,11... | collective-permute-start | bytes 73736 | tf_op jit(solution)/shard_map/ppermute | solution.py:543
  42.8 3.1 %collective-permute-start.7 = (f32[3,16,512]{2,1,0:T(8,128)S(1)}, f32[3,16,512]{2,1,0:T(8,128)S(1)}, u32[]{:S(2)}, u32[]{:S(2)}) collective-permute-start(f32[3,16,512]{2,1,0:T(8,128)S(1)} %get-tuple-element.47), channel_id=1, source_target_pairs={{0,1},{1,0},{2,3},{3,2},{4,5},{5,4},{6,7},{7,6},{8,9},{9,8},{10,11... | collective-permute-start | bytes 294920 | tf_op jit(solution)/shard_map/ppermute | solution.py:494
  44.2 5.5 %collective-permute-start.8 = (f32[3,16,512]{2,1,0:T(8,128)S(1)}, f32[3,16,512]{2,1,0:T(8,128)S(1)}, u32[]{:S(2)}, u32[]{:S(2)}) collective-permute-start(f32[3,16,512]{2,1,0:T(8,128)S(1)} %get-tuple-element.48), channel_id=1, source_target_pairs={{0,2},{1,3},{2,0},{3,1},{4,6},{5,7},{6,4},{7,5},{8,10},{9,11},{10,... | collective-permute-start | bytes 294920 | tf_op jit(solution)/shard_map/ppermute | solution.py:494
  45.9 5.1 %collective-permute-start.9 = (f32[3,16,512]{2,1,0:T(8,128)S(1)}, f32[3,16,512]{2,1,0:T(8,128)S(1)}, u32[]{:S(2)}, u32[]{:S(2)}) collective-permute-start(f32[3,16,512]{2,1,0:T(8,128)S(1)} %get-tuple-element.49), channel_id=1, source_target_pairs={{0,3},{1,2},{2,1},{3,0},{4,7},{5,6},{6,5},{7,4},{8,11},{9,10},{10,... | collective-permute-start | bytes 294920 | tf_op jit(solution)/shard_map/ppermute | solution.py:494

commit v5 on v4

v5 whole, which is shorter than its diff:
```python
import functools

import jax
import jax.numpy as jnp
from jax import lax
from jax.experimental import pallas as pl
from jax.experimental.pallas import tpu as pltpu
from jax.sharding import PartitionSpec as P

ITERS = 2
SWEEPS = 3

LATERAL = 1.0
VERTICAL = 2.0
GRAVITY = 1.0

HALO = ITERS * SWEEPS
BLOCK = 64
LANES = 128
VMEM_LIMIT = 32 * 1024 * 1024
VMEM_MOST = 60 * 1024 * 1024
FLAT = ("tile", "layer")

in_vmem = pl.BlockSpec(memory_space=pltpu.VMEM)
in_hbm = pl.BlockSpec(memory_space=pltpu.HBM)
in_smem = pl.BlockSpec(memory_space=pltpu.SMEM)


def bf16_pieces(value, count):
    pieces = []
    for _ in range(count):
        piece = value.astype(jnp.bfloat16)
        pieces.append(piece)
        value = value - piece.astype(jnp.float32)
    return pieces


def reciprocal(value):
    guess = pl.reciprocal(value, approx=True)
    return guess * (2.0 - value * guess)


def one_hot(row, size, on):
    index = lax.broadcasted_iota(jnp.int32, (16, LANES), 0)
    zero = jnp.zeros((16, LANES), jnp.bfloat16)
    tiles = []
    for start in range(0, size, 16):
        here = (index + start).astype(jnp.float32).astype(jnp.bfloat16)
        tiles.append(jnp.where(row == here, on, zero))
    return jnp.concatenate(tiles, axis=0)


def row_copies(ref, slot):
    return jnp.broadcast_to(ref[pl.ds(slot, 1), :], (16, LANES)).astype(jnp.bfloat16)


def split_cells(cells, first_row, breadth, width):
    local = cells - first_row * breadth
    shift = width.bit_length() - 1
    block = jnp.where(cells < 0, -1, local >> shift)
    return block.astype(jnp.float32), (local & (width - 1)).astype(jnp.float32)


def river_kernel(
    breadth, place_ref, cells_ref, bed_ref, section_ref, row_ref, diag_ref, rhs_ref, slot_section_ref,
    block_sc, spot_sc, dhigh_sc, dlow_sc, rhigh_sc, rlow_sc, sum_sc,
):
    rows = section_ref.shape[0]
    slots = row_ref.shape[1]
    index = lax.broadcasted_iota(jnp.int32, (rows, slots), 0)
    pick = jnp.where(index == row_ref[...], 1.0, 0.0).astype(jnp.bfloat16)
    picked = jnp.zeros(slot_section_ref.shape, jnp.float32)
    for piece in bf16_pieces(section_ref[...], 3):
        picked = picked + lax.dot_general(
            pick, piece, (((0,), (0,)), ((), ())), preferred_element_type=jnp.float32
        )
    slot_section_ref[...] = picked

    block, spot = split_cells(cells_ref[...], place_ref[0], breadth, BLOCK)
    block_sc[...] = block
    spot_sc[...] = spot
    bed = bed_ref[...]
    for value, high_sc, low_sc in ((bed, dhigh_sc, dlow_sc), (bed * picked, rhigh_sc, rlow_sc)):
        high, low = bf16_pieces(value, 2)
        high_sc[...] = high.astype(jnp.float32)
        low_sc[...] = low.astype(jnp.float32)
    share = LANES // BLOCK
    blocks = share * diag_ref.shape[0]
    group = 32
    one = jnp.ones((16, LANES), jnp.bfloat16)

    def step(number, total):
        for pair in range(0, group, 2):
            left, right = [], []
            for slot in (number * group + pair, number * group + pair + 1):
                spots = row_copies(spot_sc, slot)
                left.append(one_hot(row_copies(block_sc, slot), blocks, one))
                right.append(
                    jnp.concatenate(
                        [one_hot(spots, BLOCK, row_copies(ref, slot)) for ref in (dhigh_sc, dlow_sc, rhigh_sc, rlow_sc)],
                        axis=0,
                    )
                )
            total = total + lax.dot_general(
                jnp.concatenate(left, axis=1),
                jnp.concatenate(right, axis=1),
                (((1,), (1,)), ((), ())),
                preferred_element_type=jnp.float32,
            )
        return total

    total = lax.fori_loop(0, slots // group, step, jnp.zeros((blocks, 4 * BLOCK), jnp.float32))
    low_half = lax.broadcasted_iota(jnp.int32, diag_ref.shape, 1) < BLOCK
    for number, ref in ((0, diag_ref), (1, rhs_ref)):
        part = total[:, number * LANES:(number + 1) * LANES]
        sum_sc[...] = part + pltpu.roll(part, BLOCK, 1)
        ref[...] = jnp.where(
            low_half, sum_sc[pl.ds(0, blocks // share, stride=share), :], sum_sc[pl.ds(1, blocks // share, stride=share), :]
        )


def prepare_kernel(groups, place_ref, head_hbm, soil_hbm, section_hbm, land_hbm, *refs):
    block_refs, spread_ref, land_out_ref = refs[:groups], refs[groups], refs[groups + 1]
    head_ref, soil_ref, section_ref, land_ref, sems = refs[groups + 2:]
    held, across, _ = head_ref.shape
    span = across // groups
    pairs = [(section_hbm, section_ref), (land_hbm, land_ref)]
    for layer in range(held):
        pairs += [(head_hbm.at[layer], head_ref.at[layer]), (soil_hbm.at[layer], soil_ref.at[layer])]
    copies = [pltpu.make_async_copy(here, there, sems.at[k]) for k, (here, there) in enumerate(pairs)]
    for copy in copies:
        copy.start()

    def rows_of(target):
        number = jnp.where(place_ref[1] == 1, groups - 1 - target, target)
        return pl.ds(pl.multiple_of(number * span, span), span)

    copies[0].wait()
    section = section_ref[...]
    for tile in range(spread_ref.shape[0]):
        spread_ref[tile] = section
    copies[1].wait()
    land_out_ref[...] = land_ref[rows_of(place_ref[2]), :].astype(jnp.float32)
    for layer in range(held):
        copies[2 + 2 * layer].wait()
        copies[3 + 2 * layer].wait()
        for step, out_ref in enumerate(block_refs):
            rows = rows_of(place_ref[2] ^ step)
            out_ref[0, layer] = head_ref[layer, rows, :]
            out_ref[1, layer] = soil_ref[layer, rows, :].astype(jnp.float32)


class Rows:
    def __init__(self, layers, breadth):
        self.layers, self.breadth, self.per_row = layers, breadth, breadth // LANES

    def get(self, ref, row):
        spot = pl.ds(row * self.layers, self.layers)
        return jnp.concatenate([ref[part, spot, :] for part in range(self.per_row)], axis=1)

    def put(self, ref, row, value):
        spot = pl.ds(row * self.layers, self.layers)
        for part in range(self.per_row):
            ref[part, spot, :] = value[:, part * LANES:(part + 1) * LANES]

    def put_layer(self, ref, layer, row, value):
        for part in range(self.per_row):
            spot = pl.ds(row * self.layers + layer, value.shape[0], stride=self.layers)
            ref[part, spot, :] = value[:, part * LANES:(part + 1) * LANES]

    def east(self, field):
        return pltpu.roll(field, self.breadth - 1, 1)

    def west(self, field):
        return pltpu.roll(field, 1, 1)

    def below(self, field):
        return pltpu.roll(field, self.layers - 1, 0)

    def above(self, field):
        return pltpu.roll(field, 1, 0)


class Joined:
    def __init__(self, rows, own, full, first, last):
        self.rows, self.own, self.full, self.first, self.last = rows, own, full, first, last

    def get(self, row):
        if self.first <= row < self.last:
            return self.rows.get(self.own, row - self.first)
        return self.rows.get(self.full, row)

    def put(self, row, value):
        self.rows.put(self.full, row, value)


class Faces:
    def __init__(self, rows):
        self.rows = rows
        level = lax.broadcasted_iota(jnp.int32, (rows.layers, rows.breadth), 0)
        column = lax.broadcasted_iota(jnp.int32, (rows.layers, rows.breadth), 1)
        self.not_bottom = level < rows.layers - 1
        self.not_last = column < rows.breadth - 1

    def conduct(self, ks, alpha, head, land):
        cond = ks * jnp.exp(alpha * jnp.minimum(head, 0.0))
        return cond, cond * land

    def face(self, factor, here, there):
        return factor * 2.0 * here[1] * there[1] * reciprocal(here[0] + there[0])

    def between_rows(self, here, there):
        return self.face(LATERAL, here, there)

    def in_row(self, here):
        rows = self.rows
        cond, opened = here
        wy = self.face(LATERAL, here, (rows.east(cond), rows.east(opened)))
        wz = self.face(VERTICAL, here, (rows.below(cond), rows.below(opened)))
        wy = jnp.where(self.not_last, wy, 0.0)
        wz = jnp.where(self.not_bottom, wz, 0.0)
        wz_above = rows.above(wz)
        return wy, wz, wy + rows.west(wy) + wz + wz_above, GRAVITY * (wz_above - wz)


def lane_tables(refs, layers):
    lane = lax.broadcasted_iota(jnp.int32, (layers, LANES), 1)
    tables = []
    for ref in refs:
        table = jnp.zeros((layers, LANES), jnp.float32)
        for kind in range(ref.shape[0]):
            table = jnp.where(lane == kind, ref[kind], table)
        tables.append(table)
    return tables


def look_up(rows, table, soil):
    parts = [
        jnp.take_along_axis(table, soil[:, part * LANES:(part + 1) * LANES], axis=1, mode="promise_in_bounds")
        for part in range(rows.per_row)
    ]
    return jnp.concatenate(parts, axis=1)


def stage_kernel(groups, place_ref, ks_ref, alpha_ref, store_ref, land_ref, *refs):
    block_refs = refs[:groups]
    first_out, ks_out, alpha_out, store_out, wx_out, wy_out, wz_out, diag_out, base_out, soil_sc = refs[groups:]
    _, held, span, breadth = block_refs[0].shape
    layers = groups * held
    rows = Rows(layers, breadth)
    faces = Faces(rows)

    for step, block_ref in enumerate(block_refs):
        for held_layer in range(held):
            layer = (place_ref[2] ^ step) * held + held_layer
            rows.put_layer(first_out, layer, 0, block_ref[0, held_layer])
            rows.put_layer(soil_sc, layer, 0, block_ref[1, held_layer])
    tables = lane_tables((ks_ref, alpha_ref, store_ref), layers)
    before = None
    for row in range(span):
        soil = rows.get(soil_sc, row).astype(jnp.int32)
        ks, alpha, store = [look_up(rows, table, soil) for table in tables]
        first = rows.get(first_out, row)
        here = faces.conduct(ks, alpha, first, land_ref[pl.ds(row, 1), :])
        wy, wz, diagonal, gravity = faces.in_row(here)
        for ref, value in (
            (ks_out, ks), (alpha_out, alpha), (store_out, store), (wy_out, wy), (wz_out, wz),
            (diag_out, store + diagonal), (base_out, store * first + gravity),
        ):
            rows.put(ref, row, value)
        if row > 0:
            rows.put(wx_out, row - 1, faces.between_rows(before, here))
        before = here


def flow_kernel(
    groups, place_ref, kst_ref, alphat_ref, storet_ref, land_ref, near_ref, far_ref, diag_ref, rhs_ref, *refs,
):
    first_ref, ks_ref, alpha_ref, store_ref, wx_ref, wy_ref, wz_ref, partial_ref, gravity_ref = refs[:9]
    head_refs, top_ref = refs[9:9 + groups], refs[9 + groups]
    (
        first_sc, soil_sc, ks_sc, alpha_sc, store_sc, wx_sc, wy_sc, wz_sc, base_sc, inv_sc, ping_sc, pong_sc,
        land_sc, dtop_sc, rtop_sc,
    ) = refs[10 + groups:]
    held, span, breadth = head_refs[0].shape
    layers = groups * held
    window = span + 2 * HALO
    last_own = HALO + span
    rows = Rows(layers, breadth)
    faces = Faces(rows)
    side = HALO * rows.per_row

    land_sc[pl.ds(HALO, span), :] = land_ref[...]
    dtop_sc[pl.ds(side, span * rows.per_row), :] = diag_ref[...]
    rtop_sc[pl.ds(side, span * rows.per_row), :] = rhs_ref[...]

    def put_halo(ref, partner, row):
        def entry(number):
            return ref[pl.ds(number * HALO, HALO), :]

        for number in range(layers):
            layer = (partner ^ (number // held)) * held + number % held
            rows.put_layer(first_sc, layer, row, entry(number))
            rows.put_layer(soil_sc, layer, row, entry(layers + number))
        land_sc[pl.ds(row, HALO), :] = entry(2 * layers)
        for number, top_sc in ((2 * layers + 1, dtop_sc), (2 * layers + 2, rtop_sc)):
            value = entry(number)
            for part in range(rows.per_row):
                spot = pl.ds(row * rows.per_row + part, HALO, stride=rows.per_row)
                top_sc[spot, :] = value[:, part * LANES:(part + 1) * LANES]

    for odd, above_ref, below_ref in ((0, far_ref, near_ref), (1, near_ref, far_ref)):
        @pl.when(place_ref[3] == odd)
        def _(above_ref=above_ref, below_ref=below_ref):
            for ref, row in ((above_ref, 0), (below_ref, last_own)):
                put_halo(ref, place_ref[4] if ref is near_ref else place_ref[5], row)

    tables = lane_tables((kst_ref, alphat_ref, storet_ref), layers)
    for row in [*range(HALO), *range(last_own, window)]:
        soil = rows.get(soil_sc, row).astype(jnp.int32)
        for table, ref in zip(tables, (ks_sc, alpha_sc, store_sc)):
            rows.put(ref, row, look_up(rows, table, soil))

    def joined(own, full, last=last_own):
        return Joined(rows, own, full, HALO, last)

    first, ks, alpha, store = [
        joined(own, full)
        for own, full in ((first_ref, first_sc), (ks_ref, ks_sc), (alpha_ref, alpha_sc), (store_ref, store_sc))
    ]
    top = lax.broadcasted_iota(jnp.int32, (layers, breadth), 0) == 0

    def riv_row(ref, row):
        parts = [
            jnp.broadcast_to(ref[pl.ds(row * rows.per_row + part, 1), :], (layers, LANES))
            for part in range(rows.per_row)
        ]
        return jnp.where(top, jnp.concatenate(parts, axis=1), 0.0)

    def finish(row, diagonal, base):
        rows.put(inv_sc, row, reciprocal(diagonal + riv_row(dtop_sc, row)))
        rows.put(base_sc, row, base + riv_row(rtop_sc, row))

    def conduct(now, row):
        return faces.conduct(ks.get(row), alpha.get(row), now.get(row), land_sc[pl.ds(row, 1), :])

    def sweep(now, later_ref, weights, begin, stop):
        wx_of, wy_of, wz_of = weights
        before, here, wx_before = now.get(begin - 1), now.get(begin), wx_of.get(begin - 1)
        for row in range(begin, stop):
            after = now.get(row + 1)
            wx, wy, wz = wx_of.get(row), wy_of.get(row), wz_of.get(row)
            total = rows.get(base_sc, row) + wx_before * before + wx * after
            total = total + wy * rows.east(here) + rows.west(wy * here)
            total = total + wz * rows.below(here) + rows.above(wz * here)
            rows.put(later_ref, row, total * rows.get(inv_sc, row))
            before, here, wx_before = here, after, wx

    now, spare = first, [ping_sc, pong_sc]
    begin, stop = 0, window
    for picard in range(ITERS):
        early = picard == 0
        wx_of = joined(wx_ref, wx_sc, last_own - 1 if early else HALO)
        wy_of, wz_of = [joined(own, full, last_own if early else HALO) for own, full in ((wy_ref, wy_sc), (wz_ref, wz_sc))]
        before, wx_before = None, None
        for row in range(begin, stop):
            staged = early and HALO <= row < last_own
            here = conduct(now, row) if not staged or row in (HALO, last_own - 1) else None
            if row > begin:
                if early and HALO <= row - 1 < last_own - 1:
                    wx = wx_of.get(row - 1)
                else:
                    wx = faces.between_rows(before, here)
                    wx_of.put(row - 1, wx)
                if row - 1 > begin:
                    diagonal, base = pending
                    finish(row - 1, diagonal + wx_before + wx, base)
                wx_before = wx
            if staged:
                pending = rows.get(partial_ref, row - HALO), rows.get(gravity_ref, row - HALO)
            elif begin < row < stop - 1:
                wy, wz, diagonal, gravity = faces.in_row(here)
                wy_of.put(row, wy)
                wz_of.put(row, wz)
                pending = store.get(row) + diagonal, store.get(row) * first.get(row) + gravity
            before = here
        for _ in range(SWEEPS):
            begin, stop = begin + 1, stop - 1
            later_ref = spare[0]
            sweep(now, later_ref, (wx_of, wy_of, wz_of), begin, stop)
            spare = [spare[1], later_ref]
            now = joined(None, later_ref, HALO)
    for part in range(rows.per_row):
        lanes = pl.ds(part * LANES, LANES)
        top_ref[:, lanes] = later_ref[part, pl.ds(HALO * layers, span, stride=layers), :]
        for step, head_ref in enumerate(head_refs):
            for held_layer in range(held):
                layer = (place_ref[2] ^ step) * held + held_layer
                head_ref[held_layer, :, lanes] = later_ref[part, pl.ds(HALO * layers + layer, span, stride=layers), :]


def inflow_kernel(groups, place_ref, cells_ref, bed_ref, slot_section_ref, row_ref, *refs):
    top_refs = refs[:groups]
    out_ref, block_sc, lane_sc, found_sc, turned_sc = refs[groups:]
    span, breadth = top_refs[0].shape
    per_row = breadth // LANES
    blocks = groups * span * per_row
    slots = cells_ref.shape[0]
    quarter = LANES // groups
    packed = slots // groups
    for step, top_ref in enumerate(top_refs):
        source = place_ref[2] ^ step
        number = jnp.where(place_ref[1] == 1, groups - 1 - source, source)
        for part in range(per_row):
            spot = pl.ds(number * span * per_row + part, span, stride=per_row)
            turned_sc[spot, :] = top_ref[:, part * LANES:(part + 1) * LANES]

    own = lax.broadcasted_iota(jnp.int32, (packed, LANES), 1) // quarter

    def pack(ref):
        result = None
        for number in range(groups):
            shift = lax.rem((number + groups - place_ref[2]) * quarter, LANES)
            moved = pltpu.roll(ref[pl.ds(number * packed, packed), :], shift, 1)
            result = moved if result is None else jnp.where(own == number, moved, result)
        return result

    cells = pack(cells_ref)
    block, lane = split_cells(cells, 0, breadth, LANES)
    block_sc[...] = block
    lane_sc[...] = lane
    table = jnp.concatenate(bf16_pieces(turned_sc[...].T, 2), axis=1)
    group = 32
    one = jnp.ones((16, LANES), jnp.bfloat16)
    index = lax.broadcasted_iota(jnp.int32, (LANES, LANES), 0).astype(jnp.float32)

    def step(number, _):
        for pair in range(0, group, 2):
            places = (number * group + pair, number * group + pair + 1)
            hots = jnp.concatenate([one_hot(row_copies(block_sc, row), blocks, one) for row in places], axis=1)
            found = lax.dot_general(
                table, jnp.concatenate([hots, hots], axis=0), (((1,), (0,)), ((), ())),
                preferred_element_type=jnp.float32,
            )
            for place, row in enumerate(places):
                lanes = jnp.broadcast_to(lane_sc[pl.ds(row, 1), :], (LANES, LANES))
                mine = jnp.where(index == lanes, found[:, place * LANES:(place + 1) * LANES], 0.0)
                found_sc[pl.ds(row, 1), :] = jnp.sum(mine, axis=0, keepdims=True)
        return 0

    lax.fori_loop(0, packed // group, step, 0)
    slot_in = jnp.where(cells >= 0, pack(bed_ref) * (found_sc[...] - pack(slot_section_ref)), 0.0)
    spread = jnp.concatenate(
        [slot_in if number == 0 else pltpu.roll(slot_in, LANES - number * quarter, 1) for number in range(groups)],
        axis=0,
    )
    rows = out_ref.shape[0]
    index = lax.broadcasted_iota(jnp.int32, (rows, slots), 0)
    put = jnp.where(index == row_ref[...], 1.0, 0.0).astype(jnp.bfloat16)
    total = jnp.zeros((rows, LANES), jnp.float32)
    for piece in bf16_pieces(spread, 3):
        total = total + lax.dot_general(
            put, piece, (((1,), (0,)), ((), ())), preferred_element_type=jnp.float32
        )
    out_ref[...] = total


def result_kernel(groups, place_ref, terms_ref, *refs):
    back_refs = refs[:groups]
    head_ref, inflow_ref = refs[groups:]
    held, span, _ = back_refs[0].shape
    for step, back_ref in enumerate(back_refs):
        source = place_ref[2] ^ step
        number = jnp.where(place_ref[1] == 1, groups - 1 - source, source)
        for layer in range(held):
            head_ref[layer, pl.ds(pl.multiple_of(number * span, span), span), :] = back_ref[layer]
    total = terms_ref[0]
    for tile in range(1, terms_ref.shape[0]):
        total = total + terms_ref[tile]
    inflow_ref[...] = total[:, :inflow_ref.shape[1]]


def call(kernel, out_shape, in_specs, scratch, flops, moved, vmem=VMEM_LIMIT):
    single = not isinstance(out_shape, (tuple, list))
    return pl.pallas_call(
        kernel,
        out_shape=out_shape,
        in_specs=in_specs,
        out_specs=in_vmem if single else tuple(in_vmem for _ in out_shape),
        scratch_shapes=scratch,
        compiler_params=pltpu.CompilerParams(vmem_limit_bytes=vmem),
        cost_estimate=pl.CostEstimate(flops=flops, bytes_accessed=moved, transcendentals=0),
    )


def on_device(
    head_start,
    soil_class,
    land_mask,
    ks_table,
    alpha_table,
    store_table,
    section,
    cross_owner,
    cross_local,
    node_cell,
    bed_cond,
):
    held, across, breadth = head_start.shape
    reach_rows, node_count = section.shape
    tiles = lax.axis_size("tile")
    groups = lax.axis_size("layer")
    layers = held * groups
    span = across // groups
    per_row = breadth // LANES
    blocks = span * per_row
    tile = lax.axis_index("tile")
    layer = lax.axis_index("layer")
    flip = lax.rem(tile, 2)
    number = jnp.where(flip == 1, groups - 1 - layer, layer)
    odd = lax.rem(number, 2)
    end = (number == 0) | (number == groups - 1)
    far_partner = jnp.where(end, layer, layer ^ (groups - 1))
    place = jnp.stack([number * span, flip, layer, odd, layer ^ 1, far_partner]).astype(jnp.int32)
    near = [(i, i ^ 1) for i in range(groups)]
    far = []
    for upper in range(tiles):
        far += [(upper * groups + i, upper * groups + (i ^ (groups - 1))) for i in range(1, groups - 1)]
        if upper + 1 < tiles:
            index = groups - 1 if upper % 2 == 0 else 0
            one, two = upper * groups + index, (upper + 1) * groups + index
            far += [(one, two), (two, one)]

    cells = node_cell[0]
    bed = bed_cond[0]
    slots = cells.shape[0]
    reach = cross_owner * reach_rows + cross_local

    def exchange(parts):
        received = [parts[0]]
        for step in range(1, groups):
            received.append(lax.ppermute(parts[step], "layer", [(i, i ^ step) for i in range(groups)]))
        return received

    field_bytes = held * across * breadth * 4
    *own_blocks, spread, land = call(
        functools.partial(prepare_kernel, groups),
        (jax.ShapeDtypeStruct((2, held, span, breadth), jnp.float32),) * groups
        + (
            jax.ShapeDtypeStruct((tiles, reach_rows, node_count), jnp.float32),
            jax.ShapeDtypeStruct((span, breadth), jnp.float32),
        ),
        [in_smem] + [in_hbm] * 4,
        [
            pltpu.VMEM(head_start.shape, jnp.float32),
            pltpu.VMEM(soil_class.shape, jnp.int32),
            pltpu.VMEM(section.shape, jnp.float32),
            pltpu.VMEM(land_mask.shape, jnp.int32),
            pltpu.SemaphoreType.DMA((2 + 2 * held,)),
        ],
        0, 4 * field_bytes, VMEM_MOST,
    )(place, head_start, soil_class, section, land_mask)
    whole_section = lax.all_to_all(spread, "tile", 0, 0).reshape(tiles * reach_rows, node_count)
    received = exchange(own_blocks)

    node_scratch = pltpu.VMEM((slots, LANES), jnp.float32)
    riv_shape = jax.ShapeDtypeStruct((blocks, LANES), jnp.float32)
    node_bytes = slots * LANES * 4
    diag, rhs, slot_section = call(
        functools.partial(river_kernel, breadth),
        (riv_shape, riv_shape, jax.ShapeDtypeStruct((slots, node_count), jnp.float32)),
        [in_smem] + [in_vmem] * 4,
        [node_scratch] * 6
        + [pltpu.VMEM((span * breadth // BLOCK, LANES), jnp.float32)],
        8 * span * breadth * slots * LANES, 4 * node_bytes,
    )(place, cells, bed, whole_section, reach)

    side = HALO * per_row

    def edge(bottom):
        row = jnp.where(bottom, span - HALO, 0)
        grid = [lax.dynamic_slice_in_dim(block, row, HALO, 2) for block in received]
        river = [jnp.where(bottom, term[blocks - side:], term[:side]) for term in (diag, rhs)]
        return jnp.concatenate(
            [
                jnp.stack(grid, axis=1).reshape(2 * layers * HALO, breadth),
                lax.dynamic_slice_in_dim(land, row, HALO, 0),
                jnp.concatenate(river).reshape(2 * HALO, breadth),
            ]
        )

    near_halo = lax.ppermute(edge(odd == 0), "layer", near)
    far_halo = lax.ppermute(edge(odd == 1), FLAT, far)

    window = span + 2 * HALO
    cells_held = layers * span * breadth
    own_field = jax.ShapeDtypeStruct((per_row, span * layers, LANES), jnp.float32)
    field = pltpu.VMEM((per_row, window * layers, LANES), jnp.float32)
    staged = call(
        functools.partial(stage_kernel, groups), (own_field,) * 9,
        [in_smem] * 4 + [in_vmem] * (1 + groups), [pltpu.VMEM(own_field.shape, jnp.float32)],
        60 * cells_held, 40 * cells_held,
    )(place, ks_table, alpha_table, store_table, land, *received)
    head_shape = jax.ShapeDtypeStruct((held, span, breadth), jnp.float32)
    *heads, top = call(
        functools.partial(flow_kernel, groups),
        (head_shape,) * groups + (jax.ShapeDtypeStruct((span, breadth), jnp.float32),),
        [in_smem] * 4 + [in_vmem] * (5 + len(staged)),
        [field] * 12
        + [pltpu.VMEM((window, breadth), jnp.float32)]
        + [pltpu.VMEM((window * per_row, LANES), jnp.float32)] * 2,
        200 * cells_held, 60 * cells_held,
    )(place, ks_table, alpha_table, store_table, land, near_halo, far_halo, diag, rhs, *staged)
    tops = exchange([top] * groups)
    backs = exchange(heads)

    packed = pltpu.VMEM((slots // groups, LANES), jnp.float32)
    partial = call(
        functools.partial(inflow_kernel, groups),
        jax.ShapeDtypeStruct((tiles * reach_rows, node_count), jnp.float32),
        [in_smem] + [in_vmem] * (4 + groups),
        [packed] * 3 + [pltpu.VMEM((across * per_row, LANES), jnp.float32)],
        4 * across * breadth * slots * node_count // groups, 8 * node_bytes,
    )(place, cells, bed, slot_section, reach, *tops)
    terms = lax.all_to_all(partial.reshape(tiles, reach_rows, node_count), "tile", 0, 0)
    return call(
        functools.partial(result_kernel, groups),
        (
            jax.ShapeDtypeStruct(head_start.shape, jnp.float32),
            jax.ShapeDtypeStruct((reach_rows, node_count // groups), jnp.float32),
        ),
        [in_smem] + [in_vmem] * (1 + groups), [], 0, 2 * field_bytes,
    )(place, terms, *backs)


def solution(mesh):
    placed = (
        P("layer", "tile", None),
        P("layer", "tile", None),
        P("tile", None),
        P(),
        P(),
        P(),
        P("tile", None),
        P("tile", None),
        P("tile", None),
        P("tile", None, None),
        P("tile", None, None),
    )
    return jax.shard_map(
        on_device,
        mesh=mesh,
        in_specs=placed,
        out_specs=(P("layer", "tile", None), P("tile", "layer")),
        check_vma=False,
    )
```

time: 65.4 us -> 61.5 us (0.940)
  blocking collectives: 10.3 us -> 0 us
  starting transfers between devices: 17.9 us -> 21.3 us
  Pallas kernels: 19.6 us -> 22.3 us
  waiting for transfers between devices: 11.2 us -> 13.3 us
  local copies, waits for them, and re-layouts: 4.36 us -> 2.94 us
    all_to_all x1 -> x0, blocking collectives: 10.3 us -> none  [on_device(): lax.all_to_all(partial.reshape(tiles, reach_rows, node_count), 'tile', 0, 0)]
    all_to_all x0 -> x1, starting transfers between devices: none -> 3.35 us  [on_device(): lax.all_to_all(partial.reshape(tiles, reach_rows, node_count), 'tile', 0, 0)]
    unnamed x22 -> x20, local copies, waits for them, and re-layouts: 4.12 us -> 1.38 us
    ppermute x4 -> x2, starting transfers between devices: 5.61 us -> 3.61 us  [the longest x1 2.93 us: on_device(): near_halo = lax.ppermute(edge(odd == 0), 'layer', near)]
    ppermute x6 -> x9, starting transfers between devices: 6.32 us -> 8.29 us  [exchange(): lax.ppermute(parts[step], 'layer', [(i, i ^ step) for i in range(groups)])]
    ppermute x6 -> x9, waiting for transfers between devices: 5.05 us -> 6.94 us  [exchange(): lax.ppermute(parts[step], 'layer', [(i, i ^ step) for i in range(groups)])]
    pallas_call x3 -> x4, Pallas kernels: 10.7 us -> 12.1 us  [the longest x1 5.03 us: on_device(): call(functools.partial(flow_kernel, groups), (head_shape,) * groups + (ja...]
    all_to_all x0 -> x1, waiting for transfers between devices: none -> 0.98 us  [on_device(): lax.all_to_all(partial.reshape(tiles, reach_rows, node_count), 'tile', 0, 0)]
  transfers between devices with their start and end apart: 11 -> 13, of which waited for: 3 -> 6; matrix products, arithmetic and copies ran while one was open for 0% -> 1% of each run, Pallas kernels for 16% -> 17%
where the time goes in v5:
time: 61.5 us; the launch traced here: 60.9 us
  Pallas kernels  22.3 us (36%)
  starting transfers between devices  21.3 us (35%)
  waiting for transfers between devices  13.3 us (22%)
  local copies, waits for them, and re-layouts  2.94 us (5%)
  between operations  0.93 us (2%)
    ppermute x9, starting transfers between devices, exchange(): lax.ppermute(parts[step], 'layer', [(i, i ^ step) for i in range(groups)])  8.29 us
    pallas_call x1, Pallas kernels, on_device(): call(functools.partial(river_kernel, breadth), (riv_shape, riv_shape, jax...  7.49 us
    ppermute x9, waiting for transfers between devices, exchange(): lax.ppermute(parts[step], 'layer', [(i, i ^ step) for i in range(groups)])  6.94 us
    all_to_all x1, starting transfers between devices, on_device(): lax.all_to_all(spread, 'tile', 0, 0).reshape(tiles * reach_rows, node_count)  6.01 us
    all_to_all x1, waiting for transfers between devices, on_device(): lax.all_to_all(spread, 'tile', 0, 0).reshape(tiles * reach_rows, node_count)  5.4 us
    pallas_call x1, Pallas kernels, on_device(): call(functools.partial(flow_kernel, groups), (head_shape,) * groups + (ja...  5.03 us
    all_to_all x1, starting transfers between devices, on_device(): lax.all_to_all(partial.reshape(tiles, reach_rows, node_count), 'tile', 0, 0)  3.35 us
    pallas_call x1, Pallas kernels, on_device(): call(functools.partial(inflow_kernel, groups), jax.ShapeDtypeStruct((tile...  3.23 us
  transfers between devices with their start and end apart: 13, of which 6 were waited for; matrix products, arithmetic and copies ran while one was open for 1% of the time, Pallas kernels for 17%

profile of v5, /device:TPU:0, one launch (start us, length us, event | category | flops | bytes accessed | tf_op | source)
XLA Modules:
  0.0 60.9 jit_solution(12821208843191636129)
XLA Ops:
  0.6 0.7 %stack.57.place_ref = s32[6]{0:T(128)} concatenate(s32[1]{0:T(128)} %bitcast, s32[1]{0:T(128)} %bitcast.1, s32[1]{0:T(128)} %bitcast.2, s32[1]{0:T(128)} %bitcast.3, s32[1]{0:T(128)} %bitcast.4, s32[1]{0:T(128)} %bitcast.5), dimensions={0} | concatenate | bytes 48 | tf_op jit(solution)/shard_map/stack | solution.py:524
  1.3 2.7 %shard_map.122 = (f32[2,2,16,512]{3,2,1,0:T(8,128)}, f32[2,2,16,512]{3,2,1,0:T(8,128)}, f32[2,2,16,512]{3,2,1,0:T(8,128)}, f32[2,2,16,512]{3,2,1,0:T(8,128)}, f32[8,16,128]{2,1,0:T(8,128)}, /*index=5*/f32[16,512]{1,0:T(8,128)}) custom-call(s32[6]{0:T(128)} %stack.57.place_ref, f32[2,64,512]{2,1,0:T(8,128)} %head_hbm.1, s32[2,64,512]{2,1,0:T(8,128)} %soil_hbm.1, ...), custom_call_target="tpu_custom_call" | custom-call | bytes 1048576 | tf_op jit(solution)/shard_map/pallas_call | solution.py:546
  4.6 2.6 %collective-permute-start.1 = (f32[2,2,16,512]{3,2,1,0:T(8,128)}, f32[2,2,16,512]{3,2,1,0:T(8,128)S(1)}, u32[]{:S(2)}, u32[]{:S(2)}) collective-permute-start(f32[2,2,16,512]{3,2,1,0:T(8,128)} %get-tuple-element.30), channel_id=1, source_target_pairs={{0,2},{1,3},{2,0},{3,1},{4,6},{5,7},{6,4},{7,5},{8,10},{9,11},{10,... | collective-permute-start | bytes 393224 | tf_op jit(solution)/shard_map/ppermute | solution.py:542
  7.2 6.0 %all-to-all-start = ((f32[8,16,128]{2,1,0:T(8,128)}), f32[8,16,128]{2,1,0:T(8,128)S(1)}, u32[]{:S(2)}, u32[]{:S(2)}) async-start(f32[8,16,128]{2,1,0:T(8,128)} %get-tuple-element.25), calls=%async_computation | async-start | bytes 131072 | tf_op jit(solution)/shard_map/all_to_all | solution.py:563
  13.3 0.7 %copy-done.8 = s32[1,256]{1,0:T(1,128)S(1)} copy-done((s32[1,256]{1,0:T(1,128)S(1)}, s32[1,256]{1,0:T(1,128)}, u32[]{:S(2)}) %copy-start.8) | copy-done | bytes 1048
  13.9 0.7 %constant_dynamic-slice_fusion = (f32[6,512]{1,0:T(8,128)S(1)}, f32[6,512]{1,0:T(8,128)S(1)}) fusion(f32[16,512]{1,0:T(8,128)} %get-tuple-element.27.land_ref, s32[]{:T(128)S(6)} %select_n.52, s32[]{:T(128)S(6)} %select_n.48), kind=kLoop, calls=%fused_computation.18 | loop fusion | bytes 49160 | tf_op jit(solution)/shard_map/dynamic_slice | solution.py:587
  14.7 5.4 %all-to-all-done = f32[8,16,128]{2,1,0:T(8,128)S(1)} async-done(((f32[8,16,128]{2,1,0:T(8,128)}), f32[8,16,128]{2,1,0:T(8,128)S(1)}, u32[]{:S(2)}, u32[]{:S(2)}) %all-to-all-start) | async-done | bytes 65568 | tf_op jit(solution)/shard_map/all_to_all | solution.py:563
  20.2 0.7 %copy-done.2 = s32[6]{0:T(128)S(1)} copy-done((s32[6]{0:T(128)S(1)}, s32[6]{0:T(128)}, u32[]{:S(2)}) %copy-start.2) | copy-done | bytes 48
  20.8 7.5 %shard_map.123 = (f32[64,128]{1,0:T(8,128)S(1)}, f32[64,128]{1,0:T(8,128)S(1)}, f32[256,128]{1,0:T(8,128)S(1)}) custom-call(s32[6]{0:T(128)S(1)} %copy-done.2, s32[256,128]{1,0:T(8,128)S(1)} %bitcast.27, f32[256,128]{1,0:T(8,128)S(1)} %bitcast.29, f32[128,128]{1,0:T(8,128)S(1)} %bitcast.26, s32[1,256]{1,0:T(1,128)S(1)} %multiply_add_fusion.row_ref), custom_call_target="tpu_custom_call" | custom-call | flops 2147483648 | bytes 524288 | tf_op jit(solution)/shard_map/pallas_call | solution.py:569
  28.6 0.7 %collective-permute-start.4 = (f32[114,512]{1,0:T(8,128)S(1)}, f32[114,512]{1,0:T(8,128)S(1)}, u32[]{:S(2)}, u32[]{:S(2)}) collective-permute-start(f32[114,512]{1,0:T(8,128)S(1)} %pad_maximum_fusion.3), channel_id=1, source_target_pairs={{1,2},{2,1},{3,7},{7,3},{5,6},{6,5},{4,8},{8,4},{9,10},{10,9},{11,... | collective-permute-start | bytes 700424 | tf_op jit(solution)/shard_map/ppermute | solution.py:593
  29.4 2.9 %collective-permute-start.3 = (f32[114,512]{1,0:T(8,128)S(1)}, f32[114,512]{1,0:T(8,128)S(1)}, u32[]{:S(2)}, u32[]{:S(2)}) collective-permute-start(f32[114,512]{1,0:T(8,128)S(1)} %pad_maximum_fusion.2), channel_id=1, source_target_pairs={{0,1},{1,0},{2,3},{3,2},{4,5},{5,4},{6,7},{7,6},{8,9},{9,8},{10,11... | collective-permute-start | bytes 700424 | tf_op jit(solution)/shard_map/ppermute | solution.py:592
  32.4 2.6 %shard_map.124 = (f32[4,128,128]{2,1,0:T(8,128)S(1)}, f32[4,128,128]{2,1,0:T(8,128)S(1)}, f32[4,128,128]{2,1,0:T(8,128)S(1)}, f32[4,128,128]{2,1,0:T(8,128)S(1)}...) custom-call(s32[6]{0:T(128)S(1)} %copy-done.2, ...), custom_call_target="tpu_custom_call" | custom-call | flops 3932160 | bytes 2621440 | tf_op jit(solution)/shard_map/pallas_call | solution.py:599
  35.0 5.0 %shard_map.125 = (f32[2,16,512]{2,1,0:T(8,128)S(1)}, f32[2,16,512]{2,1,0:T(8,128)S(1)}, f32[2,16,512]{2,1,0:T(8,128)S(1)}, f32[2,16,512]{2,1,0:T(8,128)S(1)}, f32[16,512]{1,0:T(8,128)S(1)}) custom-call(s32[6]{0:T(128)S(1)} %copy-done.2, f32[12]{0:T(128)S(1)} %copy-done.3, f32[12]{0:T(128)S(1)} %copy-done.4, f32[12]{0:T(128)S(1)} %copy-done.5, ...), custom_call_target="tpu_custom_call" | custom-call | flops 13107200 | bytes 3932160 | tf_op jit(solution)/shard_map/pallas_call | solution.py:605
  40.0 1.1 %collective-permute-start.5 = (f32[16,512]{1,0:T(8,128)S(1)}, f32[16,512]{1,0:T(8,128)S(1)}, u32[]{:S(2)}, u32[]{:S(2)}) collective-permute-start(f32[16,512]{1,0:T(8,128)S(1)} %get-tuple-element.43.refs_0_), channel_id=1, source_target_pairs={{0,1},{1,0},{2,3},{3,2},{4,5},{5,4},{6,7},{7,6},{8,9},{9,8},{10,11... | collective-permute-start | bytes 98312 | tf_op jit(solution)/shard_map/ppermute | solution.py:542
  41.1 1.7 %collective-permute-start.6 = (f32[16,512]{1,0:T(8,128)S(1)}, f32[16,512]{1,0:T(8,128)S(1)}, u32[]{:S(2)}, u32[]{:S(2)}) collective-permute-start(f32[16,512]{1,0:T(8,128)S(1)} %get-tuple-element.43.refs_0_), channel_id=1, source_target_pairs={{0,2},{1,3},{2,0},{3,1},{4,6},{5,7},{6,4},{7,5},{8,10},{9,11},{10,... | collective-permute-start | bytes 98312 | tf_op jit(solution)/shard_map/ppermute | solution.py:542
  42.9 2.1 %collective-permute-done.6.refs_2_ = f32[16,512]{1,0:T(8,128)S(1)} collective-permute-done((f32[16,512]{1,0:T(8,128)S(1)}, f32[16,512]{1,0:T(8,128)S(1)}, u32[]{:S(2)}, u32[]{:S(2)}) %collective-permute-start.6) | collective-permute-done | bytes 32800 | tf_op jit(solution)/shard_map/ppermute | solution.py:542
  45.1 1.1 %collective-permute-done.7.refs_3_ = f32[16,512]{1,0:T(8,128)S(1)} collective-permute-done((f32[16,512]{1,0:T(8,128)S(1)}, f32[16,512]{1,0:T(8,128)S(1)}, u32[]{:S(2)}, u32[]{:S(2)}) %collective-permute-start.7) | collective-permute-done | bytes 32800 | tf_op jit(solution)/shard_map/ppermute | solution.py:542
  46.2 3.2 %shard_map.126 = f32[128,128]{1,0:T(8,128)} custom-call(s32[6]{0:T(128)S(1)} %copy-done.2, s32[256,128]{1,0:T(8,128)S(1)} %bitcast.28, f32[256,128]{1,0:T(8,128)S(1)} %bitcast.30, f32[256,128]{1,0:T(8,128)S(1)} %get-tuple-element.26.slot_section_ref, s32[1,256]{1,0:T(1,128)S(1)} %multiply_add_fusion.row_ref, f32[16,512]{1,0:T(8,128)S(1)} %get-tuple-element.43.refs_0_, ...), custom_call_target="tpu_custom_call" | custom-call | flops 1073741824 | bytes 1048576 | tf_op jit(solution)/shard_map/pallas_call | solution.py:618
  49.4 3.4 %all-to-all-start.1 = ((f32[8,16,128]{2,1,0:T(8,128)}), f32[8,16,128]{2,1,0:T(8,128)S(1)}, u32[]{:S(2)}, u32[]{:S(2)}) async-start(f32[8,16,128]{2,1,0:T(8,128)} %bitcast.17), calls=%async_computation.1 | async-start | bytes 131072 | tf_op jit(solution)/shard_map/all_to_all | solution.py:625
  53.7 1.3 %collective-permute-start.9 = (f32[2,16,512]{2,1,0:T(8,128)S(1)}, f32[2,16,512]{2,1,0:T(8,128)S(1)}, u32[]{:S(2)}, u32[]{:S(2)}) collective-permute-start(f32[2,16,512]{2,1,0:T(8,128)S(1)} %get-tuple-element.46), channel_id=1, source_target_pairs={{0,2},{1,3},{2,0},{3,1},{4,6},{5,7},{6,4},{7,5},{8,10},{9,11},{10,... | collective-permute-start | bytes 196616 | tf_op jit(solution)/shard_map/ppermute | solution.py:542
  55.0 1.9 %collective-permute-done.10.refs_3_ = f32[2,16,512]{2,1,0:T(8,128)S(1)} collective-permute-done((f32[2,16,512]{2,1,0:T(8,128)S(1)}, f32[2,16,512]{2,1,0:T(8,128)S(1)}, u32[]{:S(2)}, u32[]{:S(2)}) %collective-permute-start.10) | collective-permute-done | bytes 65568 | tf_op jit(solution)/shard_map/ppermute | solution.py:542
  56.9 1.7 %collective-permute-done.9.refs_2_ = f32[2,16,512]{2,1,0:T(8,128)S(1)} collective-permute-done((f32[2,16,512]{2,1,0:T(8,128)S(1)}, f32[2,16,512]{2,1,0:T(8,128)S(1)}, u32[]{:S(2)}, u32[]{:S(2)}) %collective-permute-start.9) | collective-permute-done | bytes 65568 | tf_op jit(solution)/shard_map/ppermute | solution.py:542
  58.6 1.0 %all-to-all-done.1.terms_ref = f32[8,16,128]{2,1,0:T(8,128)S(1)} async-done(((f32[8,16,128]{2,1,0:T(8,128)}), f32[8,16,128]{2,1,0:T(8,128)S(1)}, u32[]{:S(2)}, u32[]{:S(2)}) %all-to-all-start.1) | async-done | bytes 65568 | tf_op jit(solution)/shard_map/all_to_all | solution.py:625
  59.6 1.3 %shard_map.127 = (f32[2,64,512]{2,1,0:T(8,128)}, f32[16,32]{1,0:T(8,128)}) custom-call(s32[6]{0:T(128)S(1)} %copy-done.2, f32[8,16,128]{2,1,0:T(8,128)S(1)} %all-to-all-done.1.terms_ref, f32[2,16,512]{2,1,0:T(8,128)S(1)} %get-tuple-element.44.refs_0_, f32[2,16,512]{2,1,0:T(8,128)S(1)} %collective-permute-done.8.refs_1_, ...), custom_call_target="tpu_custom_call" | custom-call | bytes 524288 | tf_op jit(solution)/shard_map/pallas_call | solution.py:626
  (45 shorter events, 2.0 us)
Async XLA Ops:
  4.0 10.7 %copy-start = (f32[2,2,16,512]{3,2,1,0:T(8,128)S(1)}, f32[2,2,16,512]{3,2,1,0:T(8,128)}, u32[]{:S(2)}) copy-start(f32[2,2,16,512]{3,2,1,0:T(8,128)} %get-tuple-element.28.refs_0_) | copy-start | bytes 393220
  4.0 24.3 %collective-permute-start = (f32[2,2,16,512]{3,2,1,0:T(8,128)}, f32[2,2,16,512]{3,2,1,0:T(8,128)S(1)}, u32[]{:S(2)}, u32[]{:S(2)}) collective-permute-start(f32[2,2,16,512]{3,2,1,0:T(8,128)} %get-tuple-element.29), channel_id=1, source_target_pairs={{0,1},{1,0},{2,3},{3,2},{4,5},{5,4},{6,7},{7,6},{8,9},{9,8},{10,11... | collective-permute-start | bytes 393224 | tf_op jit(solution)/shard_map/ppermute | solution.py:542
  4.6 23.9 %collective-permute-start.1 = (f32[2,2,16,512]{3,2,1,0:T(8,128)}, f32[2,2,16,512]{3,2,1,0:T(8,128)S(1)}, u32[]{:S(2)}, u32[]{:S(2)}) collective-permute-start(f32[2,2,16,512]{3,2,1,0:T(8,128)} %get-tuple-element.30), channel_id=1, source_target_pairs={{0,2},{1,3},{2,0},{3,1},{4,6},{5,7},{6,4},{7,5},{8,10},{9,11},{10,... | collective-permute-start | bytes 393224 | tf_op jit(solution)/shard_map/ppermute | solution.py:542
  7.2 21.3 %collective-permute-start.2 = (f32[2,2,16,512]{3,2,1,0:T(8,128)}, f32[2,2,16,512]{3,2,1,0:T(8,128)S(1)}, u32[]{:S(2)}, u32[]{:S(2)}) collective-permute-start(f32[2,2,16,512]{3,2,1,0:T(8,128)} %get-tuple-element.31), channel_id=1, source_target_pairs={{0,3},{1,2},{2,1},{3,0},{4,7},{5,6},{6,5},{7,4},{8,11},{9,10},{10,... | collective-permute-start | bytes 393224 | tf_op jit(solution)/shard_map/ppermute | solution.py:542
  7.2 12.9 %all-to-all-start = ((f32[8,16,128]{2,1,0:T(8,128)}), f32[8,16,128]{2,1,0:T(8,128)S(1)}, u32[]{:S(2)}, u32[]{:S(2)}) async-start(f32[8,16,128]{2,1,0:T(8,128)} %get-tuple-element.25), calls=%async_computation | async-start | bytes 131072 | tf_op jit(solution)/shard_map/all_to_all | solution.py:563
  13.2 0.7 %copy-start.8 = (s32[1,256]{1,0:T(1,128)S(1)}, s32[1,256]{1,0:T(1,128)}, u32[]{:S(2)}) copy-start(s32[1,256]{1,0:T(1,128)} %param.19) | copy-start | bytes 3076
  13.2 0.7 %copy-start.9 = (s32[1,256]{1,0:T(1,128)S(1)}, s32[1,256]{1,0:T(1,128)}, u32[]{:S(2)}) copy-start(s32[1,256]{1,0:T(1,128)} %param.18) | copy-start | bytes 3076
  14.7 5.5 %copy-start.6 = (s32[1,256,128]{2,1,0:T(8,128)S(1)}, s32[1,256,128]{2,1,0:T(8,128)}, u32[]{:S(2)}) copy-start(s32[1,256,128]{2,1,0:T(8,128)} %param.20) | copy-start | bytes 393220
  14.7 5.5 %copy-start.7 = (f32[1,256,128]{2,1,0:T(8,128)S(1)}, f32[1,256,128]{2,1,0:T(8,128)}, u32[]{:S(2)}) copy-start(f32[1,256,128]{2,1,0:T(8,128)} %param.21) | copy-start | bytes 393220
  20.1 0.7 %copy-start.2 = (s32[6]{0:T(128)S(1)}, s32[6]{0:T(128)}, u32[]{:S(2)}) copy-start(s32[6]{0:T(128)} %stack.57.place_ref) | copy-start | bytes 76
  28.6 6.3 %collective-permute-start.4 = (f32[114,512]{1,0:T(8,128)S(1)}, f32[114,512]{1,0:T(8,128)S(1)}, u32[]{:S(2)}, u32[]{:S(2)}) collective-permute-start(f32[114,512]{1,0:T(8,128)S(1)} %pad_maximum_fusion.3), channel_id=1, source_target_pairs={{1,2},{2,1},{3,7},{7,3},{5,6},{6,5},{4,8},{8,4},{9,10},{10,9},{11,... | collective-permute-start | bytes 700424 | tf_op jit(solution)/shard_map/ppermute | solution.py:593
  29.4 3.0 %copy-start.1 = (f32[16,512]{1,0:T(8,128)S(1)}, f32[16,512]{1,0:T(8,128)}, u32[]{:S(2)}) copy-start(f32[16,512]{1,0:T(8,128)} %get-tuple-element.27.land_ref) | copy-start | bytes 98308
  29.4 3.0 %copy-start.3 = (f32[12]{0:T(128)S(1)}, f32[12]{0:T(128)}, u32[]{:S(2)}) copy-start(f32[12]{0:T(128)} %kst_ref.1) | copy-start | bytes 148
  29.4 3.0 %copy-start.4 = (f32[12]{0:T(128)S(1)}, f32[12]{0:T(128)}, u32[]{:S(2)}) copy-start(f32[12]{0:T(128)} %alphat_ref.1) | copy-start | bytes 148
  29.4 3.0 %copy-start.5 = (f32[12]{0:T(128)S(1)}, f32[12]{0:T(128)}, u32[]{:S(2)}) copy-start(f32[12]{0:T(128)} %storet_ref.1) | copy-start | bytes 148
  29.4 5.5 %collective-permute-start.3 = (f32[114,512]{1,0:T(8,128)S(1)}, f32[114,512]{1,0:T(8,128)S(1)}, u32[]{:S(2)}, u32[]{:S(2)}) collective-permute-start(f32[114,512]{1,0:T(8,128)S(1)} %pad_maximum_fusion.2), channel_id=1, source_target_pairs={{0,1},{1,0},{2,3},{3,2},{4,5},{5,4},{6,7},{7,6},{8,9},{9,8},{10,11... | collective-permute-start | bytes 700424 | tf_op jit(solution)/shard_map/ppermute | solution.py:592
  40.0 2.9 %collective-permute-start.5 = (f32[16,512]{1,0:T(8,128)S(1)}, f32[16,512]{1,0:T(8,128)S(1)}, u32[]{:S(2)}, u32[]{:S(2)}) collective-permute-start(f32[16,512]{1,0:T(8,128)S(1)} %get-tuple-element.43.refs_0_), channel_id=1, source_target_pairs={{0,1},{1,0},{2,3},{3,2},{4,5},{5,4},{6,7},{7,6},{8,9},{9,8},{10,11... | collective-permute-start | bytes 98312 | tf_op jit(solution)/shard_map/ppermute | solution.py:542
  41.1 3.9 %collective-permute-start.6 = (f32[16,512]{1,0:T(8,128)S(1)}, f32[16,512]{1,0:T(8,128)S(1)}, u32[]{:S(2)}, u32[]{:S(2)}) collective-permute-start(f32[16,512]{1,0:T(8,128)S(1)} %get-tuple-element.43.refs_0_), channel_id=1, source_target_pairs={{0,2},{1,3},{2,0},{3,1},{4,6},{5,7},{6,4},{7,5},{8,10},{9,11},{10,... | collective-permute-start | bytes 98312 | tf_op jit(solution)/shard_map/ppermute | solution.py:542
  42.8 3.3 %collective-permute-start.7 = (f32[16,512]{1,0:T(8,128)S(1)}, f32[16,512]{1,0:T(8,128)S(1)}, u32[]{:S(2)}, u32[]{:S(2)}) collective-permute-start(f32[16,512]{1,0:T(8,128)S(1)} %get-tuple-element.43.refs_0_), channel_id=1, source_target_pairs={{0,3},{1,2},{2,1},{3,0},{4,7},{5,6},{6,5},{7,4},{8,11},{9,10},{10,... | collective-permute-start | bytes 98312 | tf_op jit(solution)/shard_map/ppermute | solution.py:542
  49.4 10.2 %all-to-all-start.1 = ((f32[8,16,128]{2,1,0:T(8,128)}), f32[8,16,128]{2,1,0:T(8,128)S(1)}, u32[]{:S(2)}, u32[]{:S(2)}) async-start(f32[8,16,128]{2,1,0:T(8,128)} %bitcast.17), calls=%async_computation.1 | async-start | bytes 131072 | tf_op jit(solution)/shard_map/all_to_all | solution.py:625
  52.8 4.1 %collective-permute-start.10 = (f32[2,16,512]{2,1,0:T(8,128)S(1)}, f32[2,16,512]{2,1,0:T(8,128)S(1)}, u32[]{:S(2)}, u32[]{:S(2)}) collective-permute-start(f32[2,16,512]{2,1,0:T(8,128)S(1)} %get-tuple-element.47), channel_id=1, source_target_pairs={{0,3},{1,2},{2,1},{3,0},{4,7},{5,6},{6,5},{7,4},{8,11},{9,10},{10,... | collective-permute-start | bytes 196616 | tf_op jit(solution)/shard_map/ppermute | solution.py:542
  53.4 3.5 %collective-permute-start.8 = (f32[2,16,512]{2,1,0:T(8,128)S(1)}, f32[2,16,512]{2,1,0:T(8,128)S(1)}, u32[]{:S(2)}, u32[]{:S(2)}) collective-permute-start(f32[2,16,512]{2,1,0:T(8,128)S(1)} %get-tuple-element.45), channel_id=1, source_target_pairs={{0,1},{1,0},{2,3},{3,2},{4,5},{5,4},{6,7},{7,6},{8,9},{9,8},{10,11... | collective-permute-start | bytes 196616 | tf_op jit(solution)/shard_map/ppermute | solution.py:542
  53.7 4.9 %collective-permute-start.9 = (f32[2,16,512]{2,1,0:T(8,128)S(1)}, f32[2,16,512]{2,1,0:T(8,128)S(1)}, u32[]{:S(2)}, u32[]{:S(2)}) collective-permute-start(f32[2,16,512]{2,1,0:T(8,128)S(1)} %get-tuple-element.46), channel_id=1, source_target_pairs={{0,2},{1,3},{2,0},{3,1},{4,6},{5,7},{6,4},{7,5},{8,10},{9,11},{10,... | collective-permute-start | bytes 196616 | tf_op jit(solution)/shard_map/ppermute | solution.py:542

commit v6 on v5

--- a/solution.py
+++ b/solution.py
@@ -40,18 +40,31 @@
     return guess * (2.0 - value * guess)
 
 
-def one_hot(row, size, on):
+def names_of(size):
     index = lax.broadcasted_iota(jnp.int32, (16, LANES), 0)
+    return [(index + start).astype(jnp.float32).astype(jnp.bfloat16) for start in range(0, size, 16)]
+
+
+def one_hot(row, names):
+    one = jnp.ones((16, LANES), jnp.bfloat16)
     zero = jnp.zeros((16, LANES), jnp.bfloat16)
-    tiles = []
-    for start in range(0, size, 16):
-        here = (index + start).astype(jnp.float32).astype(jnp.bfloat16)
-        tiles.append(jnp.where(row == here, on, zero))
-    return jnp.concatenate(tiles, axis=0)
-
-
-def row_copies(ref, slot):
-    return jnp.broadcast_to(ref[pl.ds(slot, 1), :], (16, LANES)).astype(jnp.bfloat16)
+    return [jnp.maximum(one - jnp.abs(row - name), zero) for name in names]
+
+
+def row_copies(ref, first, place):
+    rows = ref[pl.ds(pl.multiple_of(first + place // 8 * 8, 8), 8), :]
+    return jnp.broadcast_to(rows[place % 8:place % 8 + 1, :], (16, LANES)).astype(jnp.bfloat16)
+
+
+def position():
+    tile, layer = lax.axis_index("tile"), lax.axis_index("layer")
+    groups = lax.axis_size("layer")
+    flip = lax.rem(tile, 2)
+    return layer, flip, jnp.where(flip == 1, groups - 1 - layer, layer)
+
+
+def span_at(flip, groups, layer):
+    return jnp.where(flip == 1, groups - 1 - layer, layer)
 
 
 def split_cells(cells, first_row, breadth, width):
@@ -62,13 +75,21 @@
 
 
 def river_kernel(
-    breadth, place_ref, cells_ref, bed_ref, section_ref, row_ref, diag_ref, rhs_ref, slot_section_ref,
-    block_sc, spot_sc, dhigh_sc, dlow_sc, rhigh_sc, rlow_sc, sum_sc,
+    breadth, reach_rows, cells_ref, bed_ref, section_ref, owner_ref, local_ref, land_ref, *refs,
 ):
+    groups = lax.axis_size("layer")
+    block_refs = refs[:groups]
+    (
+        diag_ref, rhs_ref, slot_section_ref, near_ref, far_ref,
+        block_sc, spot_sc, dhigh_sc, dlow_sc, rhigh_sc, rlow_sc, sum_sc,
+    ) = refs[groups:]
+    layer, flip, number = position()
+    span = land_ref.shape[0]
     rows = section_ref.shape[0]
-    slots = row_ref.shape[1]
+    slots = owner_ref.shape[1]
     index = lax.broadcasted_iota(jnp.int32, (rows, slots), 0)
-    pick = jnp.where(index == row_ref[...], 1.0, 0.0).astype(jnp.bfloat16)
+    reach = owner_ref[...] * reach_rows + local_ref[...]
+    pick = jnp.where(index == reach, 1.0, 0.0).astype(jnp.bfloat16)
     picked = jnp.zeros(slot_section_ref.shape, jnp.float32)
     for piece in bf16_pieces(section_ref[...], 3):
         picked = picked + lax.dot_general(
@@ -76,7 +97,7 @@
         )
     slot_section_ref[...] = picked
 
-    block, spot = split_cells(cells_ref[...], place_ref[0], breadth, BLOCK)
+    block, spot = split_cells(cells_ref[...], number * span, breadth, BLOCK)
     block_sc[...] = block
     spot_sc[...] = spot
     bed = bed_ref[...]
@@ -87,20 +108,17 @@
     share = LANES // BLOCK
     blocks = share * diag_ref.shape[0]
     group = 32
-    one = jnp.ones((16, LANES), jnp.bfloat16)
-
-    def step(number, total):
+    block_names, spot_names = names_of(blocks), names_of(BLOCK)
+
+    def step(count, total):
+        first = count * group
         for pair in range(0, group, 2):
             left, right = [], []
-            for slot in (number * group + pair, number * group + pair + 1):
-                spots = row_copies(spot_sc, slot)
-                left.append(one_hot(row_copies(block_sc, slot), blocks, one))
-                right.append(
-                    jnp.concatenate(
-                        [one_hot(spots, BLOCK, row_copies(ref, slot)) for ref in (dhigh_sc, dlow_sc, rhigh_sc, rlow_sc)],
-                        axis=0,
-                    )
-                )
+            for place in (pair, pair + 1):
+                left.append(jnp.concatenate(one_hot(row_copies(block_sc, first, place), block_names), axis=0))
+                hot = one_hot(row_copies(spot_sc, first, place), spot_names)
+                values = [row_copies(ref, first, place) for ref in (dhigh_sc, dlow_sc, rhigh_sc, rlow_sc)]
+                right.append(jnp.concatenate([tile * value for value in values for tile in hot], axis=0))
             total = total + lax.dot_general(
                 jnp.concatenate(left, axis=1),
                 jnp.concatenate(right, axis=1),
@@ -111,41 +129,68 @@
 
     total = lax.fori_loop(0, slots // group, step, jnp.zeros((blocks, 4 * BLOCK), jnp.float32))
     low_half = lax.broadcasted_iota(jnp.int32, diag_ref.shape, 1) < BLOCK
-    for number, ref in ((0, diag_ref), (1, rhs_ref)):
-        part = total[:, number * LANES:(number + 1) * LANES]
+    for count, ref in ((0, diag_ref), (1, rhs_ref)):
+        part = total[:, count * LANES:(count + 1) * LANES]
         sum_sc[...] = part + pltpu.roll(part, BLOCK, 1)
         ref[...] = jnp.where(
             low_half, sum_sc[pl.ds(0, blocks // share, stride=share), :], sum_sc[pl.ds(1, blocks // share, stride=share), :]
         )
 
-
-def prepare_kernel(groups, place_ref, head_hbm, soil_hbm, section_hbm, land_hbm, *refs):
-    block_refs, spread_ref, land_out_ref = refs[:groups], refs[groups], refs[groups + 1]
-    head_ref, soil_ref, section_ref, land_ref, sems = refs[groups + 2:]
+    odd = lax.rem(number, 2) == 1
+    per_row = breadth // LANES
+
+    def put_edges(entry, top, bottom, lanes=slice(None)):
+        near_ref[pl.ds(entry * HALO, HALO), lanes] = jnp.where(odd, top, bottom)
+        far_ref[pl.ds(entry * HALO, HALO), lanes] = jnp.where(odd, bottom, top)
+
+    entry = 0
+    for kind in range(2):
+        for block_ref in block_refs:
+            for held_layer in range(block_ref.shape[1]):
+                field = block_ref[kind, held_layer]
+                put_edges(entry, field[:HALO], field[span - HALO:])
+                entry += 1
+    put_edges(entry, land_ref[:HALO, :], land_ref[span - HALO:, :])
+    for ref in (diag_ref, rhs_ref):
+        entry += 1
+        for part in range(per_row):
+            top = ref[pl.ds(part, HALO, stride=per_row), :]
+            bottom = ref[pl.ds((span - HALO) * per_row + part, HALO, stride=per_row), :]
+            put_edges(entry, top, bottom, slice(part * LANES, (part + 1) * LANES))
+
+
+def spread_kernel(section_hbm, spread_ref, section_ref, sem):
+    copy = pltpu.make_async_copy(section_hbm, section_ref, sem)
+    copy.start()
+    copy.wait()
+    for tile in range(spread_ref.shape[0]):
+        spread_ref[tile] = section_ref[...]
+
+
+def prepare_kernel(head_hbm, soil_hbm, land_hbm, *refs):
+    groups = lax.axis_size("layer")
+    block_refs, land_out_ref = refs[:groups], refs[groups]
+    head_ref, soil_ref, land_ref, sems = refs[groups + 1:]
     held, across, _ = head_ref.shape
     span = across // groups
-    pairs = [(section_hbm, section_ref), (land_hbm, land_ref)]
+    pairs = [(land_hbm, land_ref)]
     for layer in range(held):
         pairs += [(head_hbm.at[layer], head_ref.at[layer]), (soil_hbm.at[layer], soil_ref.at[layer])]
     copies = [pltpu.make_async_copy(here, there, sems.at[k]) for k, (here, there) in enumerate(pairs)]
     for copy in copies:
         copy.start()
+    own, flip, _ = position()
 
     def rows_of(target):
-        number = jnp.where(place_ref[1] == 1, groups - 1 - target, target)
-        return pl.ds(pl.multiple_of(number * span, span), span)
+        return pl.ds(pl.multiple_of(span_at(flip, groups, target) * span, span), span)
 
     copies[0].wait()
-    section = section_ref[...]
-    for tile in range(spread_ref.shape[0]):
-        spread_ref[tile] = section
-    copies[1].wait()
-    land_out_ref[...] = land_ref[rows_of(place_ref[2]), :].astype(jnp.float32)
+    land_out_ref[...] = land_ref[rows_of(own), :].astype(jnp.float32)
     for layer in range(held):
+        copies[1 + 2 * layer].wait()
         copies[2 + 2 * layer].wait()
-        copies[3 + 2 * layer].wait()
         for step, out_ref in enumerate(block_refs):
-            rows = rows_of(place_ref[2] ^ step)
+            rows = rows_of(own ^ step)
             out_ref[0, layer] = head_ref[layer, rows, :]
             out_ref[1, layer] = soil_ref[layer, rows, :].astype(jnp.float32)
 
@@ -242,7 +287,9 @@
     return jnp.concatenate(parts, axis=1)
 
 
-def stage_kernel(groups, place_ref, ks_ref, alpha_ref, store_ref, land_ref, *refs):
+def stage_kernel(ks_ref, alpha_ref, store_ref, land_ref, *refs):
+    groups = lax.axis_size("layer")
+    own, _, _ = position()
     block_refs = refs[:groups]
     first_out, ks_out, alpha_out, store_out, wx_out, wy_out, wz_out, diag_out, base_out, soil_sc = refs[groups:]
     _, held, span, breadth = block_refs[0].shape
@@ -252,7 +299,7 @@
 
     for step, block_ref in enumerate(block_refs):
         for held_layer in range(held):
-            layer = (place_ref[2] ^ step) * held + held_layer
+            layer = (own ^ step) * held + held_layer
             rows.put_layer(first_out, layer, 0, block_ref[0, held_layer])
             rows.put_layer(soil_sc, layer, 0, block_ref[1, held_layer])
     tables = lane_tables((ks_ref, alpha_ref, store_ref), layers)
@@ -273,9 +320,11 @@
         before = here
 
 
-def flow_kernel(
-    groups, place_ref, kst_ref, alphat_ref, storet_ref, land_ref, near_ref, far_ref, diag_ref, rhs_ref, *refs,
-):
+def flow_kernel(kst_ref, alphat_ref, storet_ref, land_ref, near_ref, far_ref, diag_ref, rhs_ref, *refs):
+    groups = lax.axis_size("layer")
+    own, _, number = position()
+    end = (number == 0) | (number == groups - 1)
+    far_partner = jnp.where(end, own, own ^ (groups - 1))
     first_ref, ks_ref, alpha_ref, store_ref, wx_ref, wy_ref, wz_ref, partial_ref, gravity_ref = refs[:9]
     head_refs, top_ref = refs[9:9 + groups], refs[9 + groups]
     (
@@ -298,22 +347,22 @@
         def entry(number):
             return ref[pl.ds(number * HALO, HALO), :]
 
-        for number in range(layers):
-            layer = (partner ^ (number // held)) * held + number % held
-            rows.put_layer(first_sc, layer, row, entry(number))
-            rows.put_layer(soil_sc, layer, row, entry(layers + number))
+        for count in range(layers):
+            layer = (partner ^ (count // held)) * held + count % held
+            rows.put_layer(first_sc, layer, row, entry(count))
+            rows.put_layer(soil_sc, layer, row, entry(layers + count))
         land_sc[pl.ds(row, HALO), :] = entry(2 * layers)
-        for number, top_sc in ((2 * layers + 1, dtop_sc), (2 * layers + 2, rtop_sc)):
-            value = entry(number)
+        for count, top_sc in ((2 * layers + 1, dtop_sc), (2 * layers + 2, rtop_sc)):
+            value = entry(count)
             for part in range(rows.per_row):
                 spot = pl.ds(row * rows.per_row + part, HALO, stride=rows.per_row)
                 top_sc[spot, :] = value[:, part * LANES:(part + 1) * LANES]
 
     for odd, above_ref, below_ref in ((0, far_ref, near_ref), (1, near_ref, far_ref)):
-        @pl.when(place_ref[3] == odd)
+        @pl.when(lax.rem(number, 2) == odd)
         def _(above_ref=above_ref, below_ref=below_ref):
             for ref, row in ((above_ref, 0), (below_ref, last_own)):
-                put_halo(ref, place_ref[4] if ref is near_ref else place_ref[5], row)
+                put_halo(ref, own ^ 1 if ref is near_ref else far_partner, row)
 
     tables = lane_tables((kst_ref, alphat_ref, storet_ref), layers)
     for row in [*range(HALO), *range(last_own, window)]:
@@ -395,11 +444,13 @@
         top_ref[:, lanes] = later_ref[part, pl.ds(HALO * layers, span, stride=layers), :]
         for step, head_ref in enumerate(head_refs):
             for held_layer in range(held):
-                layer = (place_ref[2] ^ step) * held + held_layer
+                layer = (own ^ step) * held + held_layer
                 head_ref[held_layer, :, lanes] = later_ref[part, pl.ds(HALO * layers + layer, span, stride=layers), :]
 
 
-def inflow_kernel(groups, place_ref, cells_ref, bed_ref, slot_section_ref, row_ref, *refs):
+def inflow_kernel(reach_rows, cells_ref, bed_ref, slot_section_ref, owner_ref, local_ref, *refs):
+    groups = lax.axis_size("layer")
+    own_layer, flip, _ = position()
     top_refs = refs[:groups]
     out_ref, block_sc, lane_sc, found_sc, turned_sc = refs[groups:]
     span, breadth = top_refs[0].shape
@@ -409,8 +460,7 @@
     quarter = LANES // groups
     packed = slots // groups
     for step, top_ref in enumerate(top_refs):
-        source = place_ref[2] ^ step
-        number = jnp.where(place_ref[1] == 1, groups - 1 - source, source)
+        number = span_at(flip, groups, own_layer ^ step)
         for part in range(per_row):
             spot = pl.ds(number * span * per_row + part, span, stride=per_row)
             turned_sc[spot, :] = top_ref[:, part * LANES:(part + 1) * LANES]
@@ -420,7 +470,7 @@
     def pack(ref):
         result = None
         for number in range(groups):
-            shift = lax.rem((number + groups - place_ref[2]) * quarter, LANES)
+            shift = lax.rem((number + groups - own_layer) * quarter, LANES)
             moved = pltpu.roll(ref[pl.ds(number * packed, packed), :], shift, 1)
             result = moved if result is None else jnp.where(own == number, moved, result)
         return result
@@ -431,21 +481,31 @@
     lane_sc[...] = lane
     table = jnp.concatenate(bf16_pieces(turned_sc[...].T, 2), axis=1)
     group = 32
-    one = jnp.ones((16, LANES), jnp.bfloat16)
-    index = lax.broadcasted_iota(jnp.int32, (LANES, LANES), 0).astype(jnp.float32)
-
-    def step(number, _):
+    names = names_of(blocks)
+    index = lax.broadcasted_iota(jnp.int32, (8, LANES), 0).astype(jnp.float32)
+
+    def step(count, _):
+        first = pl.multiple_of(count * group, group)
         for pair in range(0, group, 2):
-            places = (number * group + pair, number * group + pair + 1)
-            hots = jnp.concatenate([one_hot(row_copies(block_sc, row), blocks, one) for row in places], axis=1)
+            hots = jnp.concatenate(
+                [
+                    jnp.concatenate(one_hot(row_copies(block_sc, first, place), names), axis=0)
+                    for place in (pair, pair + 1)
+                ],
+                axis=1,
+            )
             found = lax.dot_general(
                 table, jnp.concatenate([hots, hots], axis=0), (((1,), (0,)), ((), ())),
                 preferred_element_type=jnp.float32,
             )
-            for place, row in enumerate(places):
-                lanes = jnp.broadcast_to(lane_sc[pl.ds(row, 1), :], (LANES, LANES))
-                mine = jnp.where(index == lanes, found[:, place * LANES:(place + 1) * LANES], 0.0)
-                found_sc[pl.ds(row, 1), :] = jnp.sum(mine, axis=0, keepdims=True)
+            for place in (pair, pair + 1):
+                rows = lane_sc[pl.ds(first + place // 8 * 8, 8), :]
+                lanes = jnp.broadcast_to(rows[place % 8:place % 8 + 1, :], (8, LANES))
+                mine = found[:, (place - pair) * LANES:(place - pair + 1) * LANES]
+                total = jnp.zeros((8, LANES), jnp.float32)
+                for start in range(0, LANES, 8):
+                    total = total + jnp.where(lanes == index + float(start), mine[start:start + 8], 0.0)
+                found_sc[pl.ds(first + place, 1), :] = jnp.sum(total, axis=0, keepdims=True)
         return 0
 
     lax.fori_loop(0, packed // group, step, 0)
@@ -456,7 +516,8 @@
     )
     rows = out_ref.shape[0]
     index = lax.broadcasted_iota(jnp.int32, (rows, slots), 0)
-    put = jnp.where(index == row_ref[...], 1.0, 0.0).astype(jnp.bfloat16)
+    reach = owner_ref[...] * reach_rows + local_ref[...]
+    put = jnp.where(index == reach, 1.0, 0.0).astype(jnp.bfloat16)
     total = jnp.zeros((rows, LANES), jnp.float32)
     for piece in bf16_pieces(spread, 3):
         total = total + lax.dot_general(
@@ -465,28 +526,32 @@
     out_ref[...] = total
 
 
-def result_kernel(groups, place_ref, terms_ref, *refs):
+def result_kernel(terms_ref, *refs):
+    groups = lax.axis_size("layer")
     back_refs = refs[:groups]
-    head_ref, inflow_ref = refs[groups:]
-    held, span, _ = back_refs[0].shape
+    head_hbm, inflow_ref, sems = refs[groups:]
+    _, span, _ = back_refs[0].shape
+    own, flip, _ = position()
+    copies = []
     for step, back_ref in enumerate(back_refs):
-        source = place_ref[2] ^ step
-        number = jnp.where(place_ref[1] == 1, groups - 1 - source, source)
-        for layer in range(held):
-            head_ref[layer, pl.ds(pl.multiple_of(number * span, span), span), :] = back_ref[layer]
+        rows = pl.ds(pl.multiple_of(span_at(flip, groups, own ^ step) * span, span), span)
+        copies.append(pltpu.make_async_copy(back_ref, head_hbm.at[:, rows, :], sems.at[step]))
+        copies[-1].start()
     total = terms_ref[0]
     for tile in range(1, terms_ref.shape[0]):
         total = total + terms_ref[tile]
     inflow_ref[...] = total[:, :inflow_ref.shape[1]]
-
-
-def call(kernel, out_shape, in_specs, scratch, flops, moved, vmem=VMEM_LIMIT):
+    for copy in copies:
+        copy.wait()
+
+
+def call(kernel, out_shape, in_specs, scratch, flops, moved, vmem=VMEM_LIMIT, out_specs=None):
     single = not isinstance(out_shape, (tuple, list))
     return pl.pallas_call(
         kernel,
         out_shape=out_shape,
         in_specs=in_specs,
-        out_specs=in_vmem if single else tuple(in_vmem for _ in out_shape),
+        out_specs=out_specs or (in_vmem if single else tuple(in_vmem for _ in out_shape)),
         scratch_shapes=scratch,
         compiler_params=pltpu.CompilerParams(vmem_limit_bytes=vmem),
         cost_estimate=pl.CostEstimate(flops=flops, bytes_accessed=moved, transcendentals=0),
@@ -514,14 +579,6 @@
     span = across // groups
     per_row = breadth // LANES
     blocks = span * per_row
-    tile = lax.axis_index("tile")
-    layer = lax.axis_index("layer")
-    flip = lax.rem(tile, 2)
-    number = jnp.where(flip == 1, groups - 1 - layer, layer)
-    odd = lax.rem(number, 2)
-    end = (number == 0) | (number == groups - 1)
-    far_partner = jnp.where(end, layer, layer ^ (groups - 1))
-    place = jnp.stack([number * span, flip, layer, odd, layer ^ 1, far_partner]).astype(jnp.int32)
     near = [(i, i ^ 1) for i in range(groups)]
     far = []
     for upper in range(tiles):
@@ -534,7 +591,6 @@
     cells = node_cell[0]
     bed = bed_cond[0]
     slots = cells.shape[0]
-    reach = cross_owner * reach_rows + cross_local
 
     def exchange(parts):
         received = [parts[0]]
@@ -543,94 +599,80 @@
         return received
 
     field_bytes = held * across * breadth * 4
-    *own_blocks, spread, land = call(
-        functools.partial(prepare_kernel, groups),
+    spread = call(
+        spread_kernel, jax.ShapeDtypeStruct((tiles, reach_rows, node_count), jnp.float32), [in_hbm],
+        [pltpu.VMEM(section.shape, jnp.float32), pltpu.SemaphoreType.DMA(())], 0, 0, VMEM_MOST,
+    )(section)
+    *own_blocks, land = call(
+        prepare_kernel,
         (jax.ShapeDtypeStruct((2, held, span, breadth), jnp.float32),) * groups
-        + (
-            jax.ShapeDtypeStruct((tiles, reach_rows, node_count), jnp.float32),
-            jax.ShapeDtypeStruct((span, breadth), jnp.float32),
-        ),
-        [in_smem] + [in_hbm] * 4,
+        + (jax.ShapeDtypeStruct((span, breadth), jnp.float32),),
+        [in_hbm] * 3,
         [
             pltpu.VMEM(head_start.shape, jnp.float32),
             pltpu.VMEM(soil_class.shape, jnp.int32),
-            pltpu.VMEM(section.shape, jnp.float32),
             pltpu.VMEM(land_mask.shape, jnp.int32),
-            pltpu.SemaphoreType.DMA((2 + 2 * held,)),
+            pltpu.SemaphoreType.DMA((1 + 2 * held,)),
         ],
         0, 4 * field_bytes, VMEM_MOST,
-    )(place, head_start, soil_class, section, land_mask)
+    )(head_start, soil_class, land_mask)
     whole_section = lax.all_to_all(spread, "tile", 0, 0).reshape(tiles * reach_rows, node_count)
     received = exchange(own_blocks)
 
     node_scratch = pltpu.VMEM((slots, LANES), jnp.float32)
     riv_shape = jax.ShapeDtypeStruct((blocks, LANES), jnp.float32)
     node_bytes = slots * LANES * 4
-    diag, rhs, slot_section = call(
-        functools.partial(river_kernel, breadth),
-        (riv_shape, riv_shape, jax.ShapeDtypeStruct((slots, node_count), jnp.float32)),
-        [in_smem] + [in_vmem] * 4,
-        [node_scratch] * 6
-        + [pltpu.VMEM((span * breadth // BLOCK, LANES), jnp.float32)],
+    edges = jax.ShapeDtypeStruct(((2 * layers + 3) * HALO, breadth), jnp.float32)
+    diag, rhs, slot_section, near_edge, far_edge = call(
+        functools.partial(river_kernel, breadth, reach_rows),
+        (riv_shape, riv_shape, jax.ShapeDtypeStruct((slots, node_count), jnp.float32), edges, edges),
+        [in_vmem] * (6 + groups),
+        [node_scratch] * 6 + [pltpu.VMEM((span * breadth // BLOCK, LANES), jnp.float32)],
         8 * span * breadth * slots * LANES, 4 * node_bytes,
-    )(place, cells, bed, whole_section, reach)
-
-    side = HALO * per_row
-
-    def edge(bottom):
-        row = jnp.where(bottom, span - HALO, 0)
-        grid = [lax.dynamic_slice_in_dim(block, row, HALO, 2) for block in received]
-        river = [jnp.where(bottom, term[blocks - side:], term[:side]) for term in (diag, rhs)]
-        return jnp.concatenate(
-            [
-                jnp.stack(grid, axis=1).reshape(2 * layers * HALO, breadth),
-                lax.dynamic_slice_in_dim(land, row, HALO, 0),
-                jnp.concatenate(river).reshape(2 * HALO, breadth),
-            ]
-        )
-
-    near_halo = lax.ppermute(edge(odd == 0), "layer", near)
-    far_halo = lax.ppermute(edge(odd == 1), FLAT, far)
+    )(cells, bed, whole_section, cross_owner, cross_local, land, *received)
+    near_halo = lax.ppermute(near_edge, "layer", near)
+    far_halo = lax.ppermute(far_edge, FLAT, far)
 
     window = span + 2 * HALO
     cells_held = layers * span * breadth
     own_field = jax.ShapeDtypeStruct((per_row, span * layers, LANES), jnp.float32)
     field = pltpu.VMEM((per_row, window * layers, LANES), jnp.float32)
     staged = call(
-        functools.partial(stage_kernel, groups), (own_field,) * 9,
-        [in_smem] * 4 + [in_vmem] * (1 + groups), [pltpu.VMEM(own_field.shape, jnp.float32)],
+        stage_kernel, (own_field,) * 9,
+        [in_smem] * 3 + [in_vmem] * (1 + groups), [pltpu.VMEM(own_field.shape, jnp.float32)],
         60 * cells_held, 40 * cells_held,
-    )(place, ks_table, alpha_table, store_table, land, *received)
+    )(ks_table, alpha_table, store_table, land, *received)
     head_shape = jax.ShapeDtypeStruct((held, span, breadth), jnp.float32)
     *heads, top = call(
-        functools.partial(flow_kernel, groups),
+        flow_kernel,
         (head_shape,) * groups + (jax.ShapeDtypeStruct((span, breadth), jnp.float32),),
-        [in_smem] * 4 + [in_vmem] * (5 + len(staged)),
+        [in_smem] * 3 + [in_vmem] * (5 + len(staged)),
         [field] * 12
         + [pltpu.VMEM((window, breadth), jnp.float32)]
         + [pltpu.VMEM((window * per_row, LANES), jnp.float32)] * 2,
         200 * cells_held, 60 * cells_held,
-    )(place, ks_table, alpha_table, store_table, land, near_halo, far_halo, diag, rhs, *staged)
+    )(ks_table, alpha_table, store_table, land, near_halo, far_halo, diag, rhs, *staged)
     tops = exchange([top] * groups)
     backs = exchange(heads)
 
     packed = pltpu.VMEM((slots // groups, LANES), jnp.float32)
     partial = call(
-        functools.partial(inflow_kernel, groups),
+        functools.partial(inflow_kernel, reach_rows),
         jax.ShapeDtypeStruct((tiles * reach_rows, node_count), jnp.float32),
-        [in_smem] + [in_vmem] * (4 + groups),
+        [in_vmem] * (5 + groups),
         [packed] * 3 + [pltpu.VMEM((across * per_row, LANES), jnp.float32)],
         4 * across * breadth * slots * node_count // groups, 8 * node_bytes,
-    )(place, cells, bed, slot_section, reach, *tops)
+    )(cells, bed, slot_section, cross_owner, cross_local, *tops)
     terms = lax.all_to_all(partial.reshape(tiles, reach_rows, node_count), "tile", 0, 0)
     return call(
-        functools.partial(result_kernel, groups),
+        result_kernel,
         (
             jax.ShapeDtypeStruct(head_start.shape, jnp.float32),
             jax.ShapeDtypeStruct((reach_rows, node_count // groups), jnp.float32),
         ),
-        [in_smem] + [in_vmem] * (1 + groups), [], 0, 2 * field_bytes,
-    )(place, terms, *backs)
+        [in_vmem] * (1 + groups), [pltpu.SemaphoreType.DMA((groups,))], 0, 2 * field_bytes,
+        out_specs=(in_hbm, in_vmem),
+    )(terms, *backs)
 
 
 def solution(mesh):

time: 61.5 us -> 60.8 us (0.989)
  blocking collectives: 0 us -> 12.9 us
  starting transfers between devices: 21.3 us -> 15.6 us
  waiting for transfers between devices: 13.3 us -> 7.98 us
  local copies, waits for them, and re-layouts: 2.94 us -> 0.67 us
    all_to_all x0 -> x1, blocking collectives: none -> 12.9 us  [on_device(): lax.all_to_all(spread, 'tile', 0, 0).reshape(tiles * reach_rows, node_count)]
    all_to_all x1 -> x0, starting transfers between devices: 6.01 us -> none  [on_device(): lax.all_to_all(spread, 'tile', 0, 0).reshape(tiles * reach_rows, node_count)]
    all_to_all x1 -> x0, waiting for transfers between devices: 5.4 us -> none  [on_device(): lax.all_to_all(spread, 'tile', 0, 0).reshape(tiles * reach_rows, node_count)]
    ppermute x9, starting transfers between devices: 8.29 us -> 11.5 us  [exchange(): lax.ppermute(parts[step], 'layer', [(i, i ^ step) for i in range(groups)])]
    ppermute x2, starting transfers between devices: 3.61 us -> 0.75 us  [the longest x1 0.68 us: on_device(): far_halo = lax.ppermute(far_edge, FLAT, far)]
    another operation x5 -> x0, local copies, waits for them, and re-layouts: 0.75 us -> none  [the longest x1 0.67 us: on_device(): jnp.stack([number * span, flip, layer, odd, layer ^ 1, far_partner])]
    dynamic_slice x1 -> x0, local copies, waits for them, and re-layouts: 0.74 us -> none  [edge(): lax.dynamic_slice_in_dim(land, row, HALO, 0)]
    unnamed x20 -> x18, local copies, waits for them, and re-layouts: 1.38 us -> 0.67 us
  transfers between devices with their start and end apart: 13 -> 12, of which waited for: 6 -> 5; matrix products, arithmetic and copies ran while one was open for 1% -> 0% of each run, Pallas kernels for 17% -> 6%
where the time goes in v6:
time: 60.8 us; the launch traced here: 60.4 us
  Pallas kernels  22.3 us (37%)
  starting transfers between devices  15.6 us (26%)
  blocking collectives  12.9 us (21%)
  waiting for transfers between devices  7.98 us (13%)
  between operations  0.86 us (1%)
  local copies, waits for them, and re-layouts  0.67 us (1%)
    all_to_all x1, blocking collectives, on_device(): lax.all_to_all(spread, 'tile', 0, 0).reshape(tiles * reach_rows, node_count)  12.9 us
    ppermute x9, starting transfers between devices, exchange(): lax.ppermute(parts[step], 'layer', [(i, i ^ step) for i in range(groups)])  11.5 us
    pallas_call x1, Pallas kernels, on_device(): call(functools.partial(river_kernel, breadth, reach_rows), (riv_shape, ri...  7.09 us
    ppermute x9, waiting for transfers between devices, exchange(): lax.ppermute(parts[step], 'layer', [(i, i ^ step) for i in range(groups)])  6.67 us
    pallas_call x1, Pallas kernels, on_device(): call(flow_kernel, (head_shape,) * groups + (jax.ShapeDtypeStruct((span, b...  5.18 us
    all_to_all x1, starting transfers between devices, on_device(): lax.all_to_all(partial.reshape(tiles, reach_rows, node_count), 'tile', 0, 0)  3.35 us
    pallas_call x1, Pallas kernels, on_device(): call(functools.partial(inflow_kernel, reach_rows), jax.ShapeDtypeStruct((...  2.81 us
    pallas_call x1, Pallas kernels, on_device(): call(stage_kernel, (own_field,) * 9, [in_smem] * 3 + [in_vmem] * (1 + gro...  2.54 us
  transfers between devices with their start and end apart: 12, of which 5 were waited for; matrix products, arithmetic and copies ran while one was open for 0% of the time, Pallas kernels for 6%

profile of v6, /device:TPU:0, one launch (start us, length us, event | category | flops | bytes accessed | tf_op | source)
XLA Modules:
  0.0 60.4 jit_solution(16513929313930728503)
XLA Ops:
  0.7 2.0 %shard_map.123 = (f32[2,2,16,512]{3,2,1,0:T(8,128)}, f32[2,2,16,512]{3,2,1,0:T(8,128)}, f32[2,2,16,512]{3,2,1,0:T(8,128)}, f32[2,2,16,512]{3,2,1,0:T(8,128)}, f32[16,512]{1,0:T(8,128)}) custom-call(f32[2,64,512]{2,1,0:T(8,128)} %head_hbm.1, s32[2,64,512]{2,1,0:T(8,128)} %soil_hbm.1, s32[64,512]{1,0:T(8,128)} %land_hbm.1), custom_call_target="tpu_custom_call" | custom-call | bytes 1048576 | tf_op jit(solution)/shard_map/pallas_call | solution.py:606
  2.7 0.5 collective-permute-start
  3.2 2.6 %collective-permute-start.1 = (f32[2,2,16,512]{3,2,1,0:T(8,128)}, f32[2,2,16,512]{3,2,1,0:T(8,128)S(1)}, u32[]{:S(2)}, u32[]{:S(2)}) collective-permute-start(f32[2,2,16,512]{3,2,1,0:T(8,128)} %get-tuple-element.29), channel_id=1, source_target_pairs={{0,2},{1,3},{2,0},{3,1},{4,6},{5,7},{6,4},{7,5},{8,10},{9,11},{10,... | collective-permute-start | bytes 393224 | tf_op jit(solution)/shard_map/ppermute | solution.py:598
  5.9 1.3 %shard_map.122 = f32[8,16,128]{2,1,0:T(8,128)} custom-call(f32[16,128]{1,0:T(8,128)} %section_hbm.1), custom_call_target="tpu_custom_call" | custom-call | tf_op jit(solution)/shard_map/pallas_call | solution.py:602
  7.3 12.9 %all_to_all.10 = f32[8,16,128]{2,1,0:T(8,128)S(1)} all-to-all(f32[8,16,128]{2,1,0:T(8,128)} %shard_map.122), channel_id=1, replica_groups=mesh['tile'=8,'layer'=4] {'tile'}, dimensions={0} | all-to-all | bytes 131072 | tf_op jit(solution)/shard_map/all_to_all | solution.py:619
  20.3 0.6 %copy-done.7 = s32[1,256]{1,0:T(1,128)S(1)} copy-done((s32[1,256]{1,0:T(1,128)S(1)}, s32[1,256]{1,0:T(1,128)}, u32[]{:S(2)}) %copy-start.7) | copy-done | bytes 1048
  20.9 7.1 %shard_map.124 = (f32[64,128]{1,0:T(8,128)S(1)}, f32[64,128]{1,0:T(8,128)S(1)}, f32[256,128]{1,0:T(8,128)S(1)}, f32[114,512]{1,0:T(8,128)S(1)}, f32[114,512]{1,0:T(8,128)S(1)}) custom-call(s32[256,128]{1,0:T(8,128)S(1)} %bitcast.5, f32[256,128]{1,0:T(8,128)S(1)} %bitcast.7, f32[128,128]{1,0:T(8,128)S(1)} %bitcast.4, s32[1,256]{1,0:T(1,128)S(1)} %copy-done.7, ...), custom_call_target="tpu_custom_call" | custom-call | flops 2147483648 | bytes 524288 | tf_op jit(solution)/shard_map/pallas_call | solution.py:626
  28.0 0.1 collective-permute-start.3
  28.1 0.7 %collective-permute-start.4 = (f32[114,512]{1,0:T(8,128)S(1)}, f32[114,512]{1,0:T(8,128)S(1)}, u32[]{:S(2)}, u32[]{:S(2)}) collective-permute-start(f32[114,512]{1,0:T(8,128)S(1)} %get-tuple-element.33), channel_id=1, source_target_pairs={{1,2},{2,1},{3,7},{7,3},{5,6},{6,5},{4,8},{8,4},{9,10},{10,9},{11,... | collective-permute-start | bytes 700424 | tf_op jit(solution)/shard_map/ppermute | solution.py:634
  28.8 2.5 %shard_map.125 = (f32[4,128,128]{2,1,0:T(8,128)S(1)}, f32[4,128,128]{2,1,0:T(8,128)S(1)}, f32[4,128,128]{2,1,0:T(8,128)S(1)}, f32[4,128,128]{2,1,0:T(8,128)S(1)}...) custom-call(f32[12]{0:T(128)S(1)} %copy-done.2, ...), custom_call_target="tpu_custom_call" | custom-call | flops 3932160 | bytes 2621440 | tf_op jit(solution)/shard_map/pallas_call | solution.py:640
  31.4 5.2 %shard_map.126 = (f32[2,16,512]{2,1,0:T(8,128)S(1)}, f32[2,16,512]{2,1,0:T(8,128)S(1)}, f32[2,16,512]{2,1,0:T(8,128)S(1)}, f32[2,16,512]{2,1,0:T(8,128)S(1)}, f32[16,512]{1,0:T(8,128)S(1)}) custom-call(f32[12]{0:T(128)S(1)} %copy-done.2, f32[12]{0:T(128)S(1)} %copy-done.3, f32[12]{0:T(128)S(1)} %copy-done.4, f32[16,512]{1,0:T(8,128)S(1)} %copy-done, ...), custom_call_target="tpu_custom_call" | custom-call | flops 13107200 | bytes 3932160 | tf_op jit(solution)/shard_map/pallas_call | solution.py:646
  36.5 5.5 %collective-permute-start.7 = (f32[16,512]{1,0:T(8,128)S(1)}, f32[16,512]{1,0:T(8,128)S(1)}, u32[]{:S(2)}, u32[]{:S(2)}) collective-permute-start(f32[16,512]{1,0:T(8,128)S(1)} %get-tuple-element.45.refs_0_), channel_id=1, source_target_pairs={{0,3},{1,2},{2,1},{3,0},{4,7},{5,6},{6,5},{7,4},{8,11},{9,10},{10,... | collective-permute-start | bytes 98312 | tf_op jit(solution)/shard_map/ppermute | solution.py:598
  42.1 0.9 %collective-permute-start.6 = (f32[16,512]{1,0:T(8,128)S(1)}, f32[16,512]{1,0:T(8,128)S(1)}, u32[]{:S(2)}, u32[]{:S(2)}) collective-permute-start(f32[16,512]{1,0:T(8,128)S(1)} %get-tuple-element.45.refs_0_), channel_id=1, source_target_pairs={{0,2},{1,3},{2,0},{3,1},{4,6},{5,7},{6,4},{7,5},{8,10},{9,11},{10,... | collective-permute-start | bytes 98312 | tf_op jit(solution)/shard_map/ppermute | solution.py:598
  43.0 0.9 %collective-permute-done.7.refs_3_ = f32[16,512]{1,0:T(8,128)S(1)} collective-permute-done((f32[16,512]{1,0:T(8,128)S(1)}, f32[16,512]{1,0:T(8,128)S(1)}, u32[]{:S(2)}, u32[]{:S(2)}) %collective-permute-start.7) | collective-permute-done | bytes 32800 | tf_op jit(solution)/shard_map/ppermute | solution.py:598
  43.9 2.2 %collective-permute-done.6.refs_2_ = f32[16,512]{1,0:T(8,128)S(1)} collective-permute-done((f32[16,512]{1,0:T(8,128)S(1)}, f32[16,512]{1,0:T(8,128)S(1)}, u32[]{:S(2)}, u32[]{:S(2)}) %collective-permute-start.6) | collective-permute-done | bytes 32800 | tf_op jit(solution)/shard_map/ppermute | solution.py:598
  46.0 2.8 %shard_map.127 = f32[128,128]{1,0:T(8,128)} custom-call(s32[256,128]{1,0:T(8,128)S(1)} %bitcast.6, f32[256,128]{1,0:T(8,128)S(1)} %bitcast.8, f32[256,128]{1,0:T(8,128)S(1)} %get-tuple-element.31.slot_section_ref, s32[1,256]{1,0:T(1,128)S(1)} %copy-done.7, s32[1,256]{1,0:T(1,128)S(1)} %copy-done.8, f32[16,512]{1,0:T(8,128)S(1)} %get-tuple-element.45.refs_0_, ...), custom_call_target="tpu_custom_call" | custom-call | flops 1073741824 | bytes 1048576 | tf_op jit(solution)/shard_map/pallas_call | solution.py:659
  48.8 3.4 %all-to-all-start.1 = ((f32[8,16,128]{2,1,0:T(8,128)}), f32[8,16,128]{2,1,0:T(8,128)S(1)}, u32[]{:S(2)}, u32[]{:S(2)}) async-start(f32[8,16,128]{2,1,0:T(8,128)} %bitcast.3), calls=%async_computation.1 | async-start | bytes 131072 | tf_op jit(solution)/shard_map/all_to_all | solution.py:666
  52.2 0.1 collective-permute-start.8
  52.3 0.9 %collective-permute-start.9 = (f32[2,16,512]{2,1,0:T(8,128)S(1)}, f32[2,16,512]{2,1,0:T(8,128)S(1)}, u32[]{:S(2)}, u32[]{:S(2)}) collective-permute-start(f32[2,16,512]{2,1,0:T(8,128)S(1)} %get-tuple-element.48), channel_id=1, source_target_pairs={{0,2},{1,3},{2,0},{3,1},{4,6},{5,7},{6,4},{7,5},{8,10},{9,11},{10,... | collective-permute-start | bytes 196616 | tf_op jit(solution)/shard_map/ppermute | solution.py:598
  53.2 0.9 %collective-permute-start.10 = (f32[2,16,512]{2,1,0:T(8,128)S(1)}, f32[2,16,512]{2,1,0:T(8,128)S(1)}, u32[]{:S(2)}, u32[]{:S(2)}) collective-permute-start(f32[2,16,512]{2,1,0:T(8,128)S(1)} %get-tuple-element.49), channel_id=1, source_target_pairs={{0,3},{1,2},{2,1},{3,0},{4,7},{5,6},{6,5},{7,4},{8,11},{9,10},{10,... | collective-permute-start | bytes 196616 | tf_op jit(solution)/shard_map/ppermute | solution.py:598
  54.2 3.1 %collective-permute-done.9.refs_2_ = f32[2,16,512]{2,1,0:T(8,128)S(1)} collective-permute-done((f32[2,16,512]{2,1,0:T(8,128)S(1)}, f32[2,16,512]{2,1,0:T(8,128)S(1)}, u32[]{:S(2)}, u32[]{:S(2)}) %collective-permute-start.9) | collective-permute-done | bytes 65568 | tf_op jit(solution)/shard_map/ppermute | solution.py:598
  57.2 0.5 collective-permute-done.10.refs_3_
  57.7 1.3 %all-to-all-done.1.terms_ref = f32[8,16,128]{2,1,0:T(8,128)S(1)} async-done(((f32[8,16,128]{2,1,0:T(8,128)}), f32[8,16,128]{2,1,0:T(8,128)S(1)}, u32[]{:S(2)}, u32[]{:S(2)}) %all-to-all-start.1) | async-done | bytes 65568 | tf_op jit(solution)/shard_map/all_to_all | solution.py:666
  59.0 1.3 %shard_map.128 = (f32[2,64,512]{2,1,0:T(8,128)}, f32[16,32]{1,0:T(8,128)}) custom-call(f32[8,16,128]{2,1,0:T(8,128)S(1)} %all-to-all-done.1.terms_ref, f32[2,16,512]{2,1,0:T(8,128)S(1)} %get-tuple-element.46.refs_0_, f32[2,16,512]{2,1,0:T(8,128)S(1)} %collective-permute-done.8.refs_1_, f32[2,16,512]{2,1,0:T(8,128)S(1)} %collective-permute-done.9.refs_2_, ...), custom_call_target="tpu_custom_call" | custom-call | bytes 524288 | tf_op jit(solution)/shard_map/pallas_call | solution.py:667
  (26 shorter events, 0.1 us)
Async XLA Ops:
  0.6 19.6 %copy-start.5 = (s32[1,256,128]{2,1,0:T(8,128)S(1)}, s32[1,256,128]{2,1,0:T(8,128)}, u32[]{:S(2)}) copy-start(s32[1,256,128]{2,1,0:T(8,128)} %param.20) | copy-start | bytes 393220
  0.6 19.6 %copy-start.6 = (f32[1,256,128]{2,1,0:T(8,128)S(1)}, f32[1,256,128]{2,1,0:T(8,128)}, u32[]{:S(2)}) copy-start(f32[1,256,128]{2,1,0:T(8,128)} %param.21) | copy-start | bytes 393220
  2.7 17.5 %copy-start.1 = (f32[2,2,16,512]{3,2,1,0:T(8,128)S(1)}, f32[2,2,16,512]{3,2,1,0:T(8,128)}, u32[]{:S(2)}) copy-start(f32[2,2,16,512]{3,2,1,0:T(8,128)} %get-tuple-element.27.refs_0_) | copy-start | bytes 393220
  2.7 17.5 %collective-permute-start = (f32[2,2,16,512]{3,2,1,0:T(8,128)}, f32[2,2,16,512]{3,2,1,0:T(8,128)S(1)}, u32[]{:S(2)}, u32[]{:S(2)}) collective-permute-start(f32[2,2,16,512]{3,2,1,0:T(8,128)} %get-tuple-element.28), channel_id=1, source_target_pairs={{0,1},{1,0},{2,3},{3,2},{4,5},{5,4},{6,7},{7,6},{8,9},{9,8},{10,11... | collective-permute-start | bytes 393224 | tf_op jit(solution)/shard_map/ppermute | solution.py:598
  3.2 16.9 %collective-permute-start.1 = (f32[2,2,16,512]{3,2,1,0:T(8,128)}, f32[2,2,16,512]{3,2,1,0:T(8,128)S(1)}, u32[]{:S(2)}, u32[]{:S(2)}) collective-permute-start(f32[2,2,16,512]{3,2,1,0:T(8,128)} %get-tuple-element.29), channel_id=1, source_target_pairs={{0,2},{1,3},{2,0},{3,1},{4,6},{5,7},{6,4},{7,5},{8,10},{9,11},{10,... | collective-permute-start | bytes 393224 | tf_op jit(solution)/shard_map/ppermute | solution.py:598
  5.8 14.4 %collective-permute-start.2 = (f32[2,2,16,512]{3,2,1,0:T(8,128)}, f32[2,2,16,512]{3,2,1,0:T(8,128)S(1)}, u32[]{:S(2)}, u32[]{:S(2)}) collective-permute-start(f32[2,2,16,512]{3,2,1,0:T(8,128)} %get-tuple-element.30), channel_id=1, source_target_pairs={{0,3},{1,2},{2,1},{3,0},{4,7},{5,6},{6,5},{7,4},{8,11},{9,10},{10,... | collective-permute-start | bytes 393224 | tf_op jit(solution)/shard_map/ppermute | solution.py:598
  7.2 13.0 %copy-start = (f32[16,512]{1,0:T(8,128)S(1)}, f32[16,512]{1,0:T(8,128)}, u32[]{:S(2)}) copy-start(f32[16,512]{1,0:T(8,128)} %get-tuple-element.26.land_ref) | copy-start | bytes 98308
  7.2 13.0 %copy-start.8 = (s32[1,256]{1,0:T(1,128)S(1)}, s32[1,256]{1,0:T(1,128)}, u32[]{:S(2)}) copy-start(s32[1,256]{1,0:T(1,128)} %local_ref.3) | copy-start | bytes 3076
  20.2 0.7 %copy-start.7 = (s32[1,256]{1,0:T(1,128)S(1)}, s32[1,256]{1,0:T(1,128)}, u32[]{:S(2)}) copy-start(s32[1,256]{1,0:T(1,128)} %owner_ref.3) | copy-start | bytes 3076
  28.0 0.8 %copy-start.2 = (f32[12]{0:T(128)S(1)}, f32[12]{0:T(128)}, u32[]{:S(2)}) copy-start(f32[12]{0:T(128)} %kst_ref.1) | copy-start | bytes 148
  28.0 0.8 %copy-start.3 = (f32[12]{0:T(128)S(1)}, f32[12]{0:T(128)}, u32[]{:S(2)}) copy-start(f32[12]{0:T(128)} %alphat_ref.1) | copy-start | bytes 148
  28.0 0.8 %copy-start.4 = (f32[12]{0:T(128)S(1)}, f32[12]{0:T(128)}, u32[]{:S(2)}) copy-start(f32[12]{0:T(128)} %storet_ref.1) | copy-start | bytes 148
  28.0 3.3 %collective-permute-start.3 = (f32[114,512]{1,0:T(8,128)S(1)}, f32[114,512]{1,0:T(8,128)S(1)}, u32[]{:S(2)}, u32[]{:S(2)}) collective-permute-start(f32[114,512]{1,0:T(8,128)S(1)} %get-tuple-element.32), channel_id=1, source_target_pairs={{0,1},{1,0},{2,3},{3,2},{4,5},{5,4},{6,7},{7,6},{8,9},{9,8},{10,11... | collective-permute-start | bytes 700424 | tf_op jit(solution)/shard_map/ppermute | solution.py:633
  28.1 3.3 %collective-permute-start.4 = (f32[114,512]{1,0:T(8,128)S(1)}, f32[114,512]{1,0:T(8,128)S(1)}, u32[]{:S(2)}, u32[]{:S(2)}) collective-permute-start(f32[114,512]{1,0:T(8,128)S(1)} %get-tuple-element.33), channel_id=1, source_target_pairs={{1,2},{2,1},{3,7},{7,3},{5,6},{6,5},{4,8},{8,4},{9,10},{10,9},{11,... | collective-permute-start | bytes 700424 | tf_op jit(solution)/shard_map/ppermute | solution.py:634
  36.5 7.3 %collective-permute-start.7 = (f32[16,512]{1,0:T(8,128)S(1)}, f32[16,512]{1,0:T(8,128)S(1)}, u32[]{:S(2)}, u32[]{:S(2)}) collective-permute-start(f32[16,512]{1,0:T(8,128)S(1)} %get-tuple-element.45.refs_0_), channel_id=1, source_target_pairs={{0,3},{1,2},{2,1},{3,0},{4,7},{5,6},{6,5},{7,4},{8,11},{9,10},{10,... | collective-permute-start | bytes 98312 | tf_op jit(solution)/shard_map/ppermute | solution.py:598
  42.1 3.9 %collective-permute-start.6 = (f32[16,512]{1,0:T(8,128)S(1)}, f32[16,512]{1,0:T(8,128)S(1)}, u32[]{:S(2)}, u32[]{:S(2)}) collective-permute-start(f32[16,512]{1,0:T(8,128)S(1)} %get-tuple-element.45.refs_0_), channel_id=1, source_target_pairs={{0,2},{1,3},{2,0},{3,1},{4,6},{5,7},{6,4},{7,5},{8,10},{9,11},{10,... | collective-permute-start | bytes 98312 | tf_op jit(solution)/shard_map/ppermute | solution.py:598
  43.0 3.1 %collective-permute-start.5 = (f32[16,512]{1,0:T(8,128)S(1)}, f32[16,512]{1,0:T(8,128)S(1)}, u32[]{:S(2)}, u32[]{:S(2)}) collective-permute-start(f32[16,512]{1,0:T(8,128)S(1)} %get-tuple-element.45.refs_0_), channel_id=1, source_target_pairs={{0,1},{1,0},{2,3},{3,2},{4,5},{5,4},{6,7},{7,6},{8,9},{9,8},{10,11... | collective-permute-start | bytes 98312 | tf_op jit(solution)/shard_map/ppermute | solution.py:598
  48.8 10.2 %all-to-all-start.1 = ((f32[8,16,128]{2,1,0:T(8,128)}), f32[8,16,128]{2,1,0:T(8,128)S(1)}, u32[]{:S(2)}, u32[]{:S(2)}) async-start(f32[8,16,128]{2,1,0:T(8,128)} %bitcast.3), calls=%async_computation.1 | async-start | bytes 131072 | tf_op jit(solution)/shard_map/all_to_all | solution.py:666
  52.2 1.9 %collective-permute-start.8 = (f32[2,16,512]{2,1,0:T(8,128)S(1)}, f32[2,16,512]{2,1,0:T(8,128)S(1)}, u32[]{:S(2)}, u32[]{:S(2)}) collective-permute-start(f32[2,16,512]{2,1,0:T(8,128)S(1)} %get-tuple-element.47), channel_id=1, source_target_pairs={{0,1},{1,0},{2,3},{3,2},{4,5},{5,4},{6,7},{7,6},{8,9},{9,8},{10,11... | collective-permute-start | bytes 196616 | tf_op jit(solution)/shard_map/ppermute | solution.py:598
  52.3 5.0 %collective-permute-start.9 = (f32[2,16,512]{2,1,0:T(8,128)S(1)}, f32[2,16,512]{2,1,0:T(8,128)S(1)}, u32[]{:S(2)}, u32[]{:S(2)}) collective-permute-start(f32[2,16,512]{2,1,0:T(8,128)S(1)} %get-tuple-element.48), channel_id=1, source_target_pairs={{0,2},{1,3},{2,0},{3,1},{4,6},{5,7},{6,4},{7,5},{8,10},{9,11},{10,... | collective-permute-start | bytes 196616 | tf_op jit(solution)/shard_map/ppermute | solution.py:598
  53.2 4.5 %collective-permute-start.10 = (f32[2,16,512]{2,1,0:T(8,128)S(1)}, f32[2,16,512]{2,1,0:T(8,128)S(1)}, u32[]{:S(2)}, u32[]{:S(2)}) collective-permute-start(f32[2,16,512]{2,1,0:T(8,128)S(1)} %get-tuple-element.49), channel_id=1, source_target_pairs={{0,3},{1,2},{2,1},{3,0},{4,7},{5,6},{6,5},{7,4},{8,11},{9,10},{10,... | collective-permute-start | bytes 196616 | tf_op jit(solution)/shard_map/ppermute | solution.py:598

commit v7 on v6

--- a/solution.py
+++ b/solution.py
@@ -75,16 +75,10 @@
 
 
 def river_kernel(
-    breadth, reach_rows, cells_ref, bed_ref, section_ref, owner_ref, local_ref, land_ref, *refs,
+    breadth, span, reach_rows, cells_ref, bed_ref, section_ref, owner_ref, local_ref,
+    diag_ref, rhs_ref, slot_section_ref, block_sc, spot_sc, dhigh_sc, dlow_sc, rhigh_sc, rlow_sc, sum_sc,
 ):
-    groups = lax.axis_size("layer")
-    block_refs = refs[:groups]
-    (
-        diag_ref, rhs_ref, slot_section_ref, near_ref, far_ref,
-        block_sc, spot_sc, dhigh_sc, dlow_sc, rhigh_sc, rlow_sc, sum_sc,
-    ) = refs[groups:]
-    layer, flip, number = position()
-    span = land_ref.shape[0]
+    _, _, number = position()
     rows = section_ref.shape[0]
     slots = owner_ref.shape[1]
     index = lax.broadcasted_iota(jnp.int32, (rows, slots), 0)
@@ -110,22 +104,24 @@
     group = 32
     block_names, spot_names = names_of(blocks), names_of(BLOCK)
 
+    def matmul(first, places):
+        left, right = [], []
+        for place in places:
+            left.append(jnp.concatenate(one_hot(row_copies(block_sc, first, place), block_names), axis=0))
+            hot = one_hot(row_copies(spot_sc, first, place), spot_names)
+            values = [row_copies(ref, first, place) for ref in (dhigh_sc, dlow_sc, rhigh_sc, rlow_sc)]
+            right.append(jnp.concatenate([tile * value for value in values for tile in hot], axis=0))
+        return lax.dot_general(
+            jnp.concatenate(left, axis=1),
+            jnp.concatenate(right, axis=1),
+            (((1,), (1,)), ((), ())),
+            preferred_element_type=jnp.float32,
+        )
+
     def step(count, total):
         first = count * group
-        for pair in range(0, group, 2):
-            left, right = [], []
-            for place in (pair, pair + 1):
-                left.append(jnp.concatenate(one_hot(row_copies(block_sc, first, place), block_names), axis=0))
-                hot = one_hot(row_copies(spot_sc, first, place), spot_names)
-                values = [row_copies(ref, first, place) for ref in (dhigh_sc, dlow_sc, rhigh_sc, rlow_sc)]
-                right.append(jnp.concatenate([tile * value for value in values for tile in hot], axis=0))
-            total = total + lax.dot_general(
-                jnp.concatenate(left, axis=1),
-                jnp.concatenate(right, axis=1),
-                (((1,), (1,)), ((), ())),
-                preferred_element_type=jnp.float32,
-            )
-        return total
+        half = group // 2
+        return total + (matmul(first, range(half)) + matmul(first, range(half, group)))
 
     total = lax.fori_loop(0, slots // group, step, jnp.zeros((blocks, 4 * BLOCK), jnp.float32))
     low_half = lax.broadcasted_iota(jnp.int32, diag_ref.shape, 1) < BLOCK
@@ -136,6 +132,11 @@
             low_half, sum_sc[pl.ds(0, blocks // share, stride=share), :], sum_sc[pl.ds(1, blocks // share, stride=share), :]
         )
 
+
+def edge_kernel(land_ref, diag_ref, rhs_ref, *refs):
+    block_refs, (near_ref, far_ref) = refs[:-2], refs[-2:]
+    _, held, span, breadth = block_refs[0].shape
+    _, _, number = position()
     odd = lax.rem(number, 2) == 1
     per_row = breadth // LANES
 
@@ -146,9 +147,8 @@
     entry = 0
     for kind in range(2):
         for block_ref in block_refs:
-            for held_layer in range(block_ref.shape[1]):
-                field = block_ref[kind, held_layer]
-                put_edges(entry, field[:HALO], field[span - HALO:])
+            for held_layer in range(held):
+                put_edges(entry, block_ref[kind, held_layer, :HALO, :], block_ref[kind, held_layer, span - HALO:, :])
                 entry += 1
     put_edges(entry, land_ref[:HALO, :], land_ref[span - HALO:, :])
     for ref in (diag_ref, rhs_ref):
@@ -167,7 +167,8 @@
         spread_ref[tile] = section_ref[...]
 
 
-def prepare_kernel(head_hbm, soil_hbm, land_hbm, *refs):
+def prepare_kernel(head_hbm, soil_hbm, land_hbm, after_hbm, *refs):
+    del after_hbm
     groups = lax.axis_size("layer")
     block_refs, land_out_ref = refs[:groups], refs[groups]
     head_ref, soil_ref, land_ref, sems = refs[groups + 1:]
@@ -526,10 +527,9 @@
     out_ref[...] = total
 
 
-def result_kernel(terms_ref, *refs):
+def head_kernel(*refs):
     groups = lax.axis_size("layer")
-    back_refs = refs[:groups]
-    head_hbm, inflow_ref, sems = refs[groups:]
+    back_refs, (head_hbm, sems) = refs[:groups], refs[groups:]
     _, span, _ = back_refs[0].shape
     own, flip, _ = position()
     copies = []
@@ -537,10 +537,6 @@
         rows = pl.ds(pl.multiple_of(span_at(flip, groups, own ^ step) * span, span), span)
         copies.append(pltpu.make_async_copy(back_ref, head_hbm.at[:, rows, :], sems.at[step]))
         copies[-1].start()
-    total = terms_ref[0]
-    for tile in range(1, terms_ref.shape[0]):
-        total = total + terms_ref[tile]
-    inflow_ref[...] = total[:, :inflow_ref.shape[1]]
     for copy in copies:
         copy.wait()
 
@@ -603,11 +599,12 @@
         spread_kernel, jax.ShapeDtypeStruct((tiles, reach_rows, node_count), jnp.float32), [in_hbm],
         [pltpu.VMEM(section.shape, jnp.float32), pltpu.SemaphoreType.DMA(())], 0, 0, VMEM_MOST,
     )(section)
+    whole_section = lax.all_to_all(spread, "tile", 0, 0).reshape(tiles * reach_rows, node_count)
     *own_blocks, land = call(
         prepare_kernel,
         (jax.ShapeDtypeStruct((2, held, span, breadth), jnp.float32),) * groups
         + (jax.ShapeDtypeStruct((span, breadth), jnp.float32),),
-        [in_hbm] * 3,
+        [in_hbm] * 4,
         [
             pltpu.VMEM(head_start.shape, jnp.float32),
             pltpu.VMEM(soil_class.shape, jnp.int32),
@@ -615,21 +612,23 @@
             pltpu.SemaphoreType.DMA((1 + 2 * held,)),
         ],
         0, 4 * field_bytes, VMEM_MOST,
-    )(head_start, soil_class, land_mask)
-    whole_section = lax.all_to_all(spread, "tile", 0, 0).reshape(tiles * reach_rows, node_count)
+    )(head_start, soil_class, land_mask, whole_section)
     received = exchange(own_blocks)
 
     node_scratch = pltpu.VMEM((slots, LANES), jnp.float32)
     riv_shape = jax.ShapeDtypeStruct((blocks, LANES), jnp.float32)
     node_bytes = slots * LANES * 4
-    edges = jax.ShapeDtypeStruct(((2 * layers + 3) * HALO, breadth), jnp.float32)
-    diag, rhs, slot_section, near_edge, far_edge = call(
-        functools.partial(river_kernel, breadth, reach_rows),
-        (riv_shape, riv_shape, jax.ShapeDtypeStruct((slots, node_count), jnp.float32), edges, edges),
-        [in_vmem] * (6 + groups),
+    diag, rhs, slot_section = call(
+        functools.partial(river_kernel, breadth, span, reach_rows),
+        (riv_shape, riv_shape, jax.ShapeDtypeStruct((slots, node_count), jnp.float32)),
+        [in_vmem] * 5,
         [node_scratch] * 6 + [pltpu.VMEM((span * breadth // BLOCK, LANES), jnp.float32)],
         8 * span * breadth * slots * LANES, 4 * node_bytes,
-    )(cells, bed, whole_section, cross_owner, cross_local, land, *received)
+    )(cells, bed, whole_section, cross_owner, cross_local)
+    edges = jax.ShapeDtypeStruct(((2 * layers + 3) * HALO, breadth), jnp.float32)
+    near_edge, far_edge = call(
+        edge_kernel, (edges, edges), [in_vmem] * (3 + groups), [], 0, 8 * layers * HALO * breadth * 4,
+    )(land, diag, rhs, *received)
     near_halo = lax.ppermute(near_edge, "layer", near)
     far_halo = lax.ppermute(far_edge, FLAT, far)
 
@@ -663,16 +662,13 @@
         [packed] * 3 + [pltpu.VMEM((across * per_row, LANES), jnp.float32)],
         4 * across * breadth * slots * node_count // groups, 8 * node_bytes,
     )(cells, bed, slot_section, cross_owner, cross_local, *tops)
+    partial, *backs = lax.optimization_barrier((partial, *backs))
     terms = lax.all_to_all(partial.reshape(tiles, reach_rows, node_count), "tile", 0, 0)
-    return call(
-        result_kernel,
-        (
-            jax.ShapeDtypeStruct(head_start.shape, jnp.float32),
-            jax.ShapeDtypeStruct((reach_rows, node_count // groups), jnp.float32),
-        ),
-        [in_vmem] * (1 + groups), [pltpu.SemaphoreType.DMA((groups,))], 0, 2 * field_bytes,
-        out_specs=(in_hbm, in_vmem),
-    )(terms, *backs)
+    head = call(
+        head_kernel, jax.ShapeDtypeStruct(head_start.shape, jnp.float32), [in_vmem] * groups,
+        [pltpu.SemaphoreType.DMA((groups,))], 0, 2 * field_bytes, out_specs=in_hbm,
+    )(*backs)
+    return head, jnp.sum(terms, axis=0)[:, :node_count // groups]
 
 
 def solution(mesh):

time: 60.8 us -> 60.4 us (level)
  waiting for transfers between devices: 7.98 us -> 6.24 us
  blocking collectives: 12.9 us -> 14.3 us
  other arithmetic: 0 us -> 0.61 us
    ppermute x9, waiting for transfers between devices: 6.67 us -> 0.12 us  [exchange(): lax.ppermute(parts[step], 'layer', [(i, i ^ step) for i in range(groups)])]
    all_to_all x1, waiting for transfers between devices: 1.3 us -> 6.11 us  [on_device(): lax.all_to_all(partial.reshape(tiles, reach_rows, node_count), 'tile', 0, 0)]
    all_to_all x1, blocking collectives: 12.9 us -> 14.3 us  [on_device(): lax.all_to_all(spread, 'tile', 0, 0).reshape(tiles * reach_rows, node_count)]
    pallas_call x2 -> x3, Pallas kernels: 8.42 us -> 7.92 us  [the longest x1 7.08 us: on_device(): call(functools.partial(river_kernel, breadth, span, reach_rows), (riv_sha...]
  transfers between devices with their start and end apart: 12 -> 12, of which waited for: 5 -> 2; matrix products, arithmetic and copies ran while one was open for 0% -> 0% of each run, Pallas kernels for 6% -> 22%
where the time goes in v7:
time: 60.4 us; the launch traced here: 60 us
  Pallas kernels  21.9 us (36%)
  starting transfers between devices  15.5 us (26%)
  blocking collectives  14.3 us (24%)
  waiting for transfers between devices  6.24 us (10%)
  between operations  0.83 us (1%)
  local copies, waits for them, and re-layouts  0.7 us (1%)
  other arithmetic  0.61 us (1%)
    all_to_all x1, blocking collectives, on_device(): lax.all_to_all(spread, 'tile', 0, 0).reshape(tiles * reach_rows, node_count)  14.3 us
    ppermute x9, starting transfers between devices, exchange(): lax.ppermute(parts[step], 'layer', [(i, i ^ step) for i in range(groups)])  11.1 us
    pallas_call x1, Pallas kernels, on_device(): call(functools.partial(river_kernel, breadth, span, reach_rows), (riv_sha...  7.08 us
    all_to_all x1, waiting for transfers between devices, on_device(): lax.all_to_all(partial.reshape(tiles, reach_rows, node_count), 'tile', 0, 0)  6.11 us
    pallas_call x1, Pallas kernels, on_device(): call(flow_kernel, (head_shape,) * groups + (jax.ShapeDtypeStruct((span, b...  5.19 us
    all_to_all x1, starting transfers between devices, on_device(): lax.all_to_all(partial.reshape(tiles, reach_rows, node_count), 'tile', 0, 0)  3.36 us
    pallas_call x1, Pallas kernels, on_device(): call(functools.partial(inflow_kernel, reach_rows), jax.ShapeDtypeStruct((...  2.83 us
    pallas_call x1, Pallas kernels, on_device(): call(stage_kernel, (own_field,) * 9, [in_smem] * 3 + [in_vmem] * (1 + gro...  2.54 us
  transfers between devices with their start and end apart: 12, of which 2 were waited for; matrix products, arithmetic and copies ran while one was open for 0% of the time, Pallas kernels for 22%

profile of v7, /device:TPU:0, one launch (start us, length us, event | category | flops | bytes accessed | tf_op | source)
XLA Modules:
  0.0 60.0 jit_solution(17310390129253582519)
XLA Ops:
  0.6 1.3 %shard_map.122 = f32[8,16,128]{2,1,0:T(8,128)} custom-call(f32[16,128]{1,0:T(8,128)} %section_hbm.1), custom_call_target="tpu_custom_call" | custom-call | tf_op jit(solution)/shard_map/pallas_call | solution.py:598
  2.0 14.3 %all_to_all.10 = f32[8,16,128]{2,1,0:T(8,128)} all-to-all(f32[8,16,128]{2,1,0:T(8,128)} %shard_map.122), channel_id=1, replica_groups=mesh['tile'=8,'layer'=4] {'tile'}, dimensions={0} | all-to-all | bytes 131072 | tf_op jit(solution)/shard_map/all_to_all | solution.py:602
  16.3 2.1 %shard_map.124 = (f32[2,2,16,512]{3,2,1,0:T(8,128)}, f32[2,2,16,512]{3,2,1,0:T(8,128)}, f32[2,2,16,512]{3,2,1,0:T(8,128)}, f32[2,2,16,512]{3,2,1,0:T(8,128)}, f32[16,512]{1,0:T(8,128)}) custom-call(f32[2,64,512]{2,1,0:T(8,128)} %head_hbm.1, s32[2,64,512]{2,1,0:T(8,128)} %soil_hbm.1, s32[64,512]{1,0:T(8,128)} %land_hbm.1, f32[128,128]{1,0:T(8,128)} %bitcast.5), custom_call_target="tpu_custom_call" | custom-call | bytes 1048576 | tf_op jit(solution)/shard_map/pallas_call | solution.py:603
  18.3 0.1 collective-permute-start
  18.4 1.6 %collective-permute-start.1 = (f32[2,2,16,512]{3,2,1,0:T(8,128)}, f32[2,2,16,512]{3,2,1,0:T(8,128)S(1)}, u32[]{:S(2)}, u32[]{:S(2)}) collective-permute-start(f32[2,2,16,512]{3,2,1,0:T(8,128)} %get-tuple-element.37), channel_id=1, source_target_pairs={{0,2},{1,3},{2,0},{3,1},{4,6},{5,7},{6,4},{7,5},{8,10},{9,11},{10,... | collective-permute-start | bytes 393224 | tf_op jit(solution)/shard_map/ppermute | solution.py:594
  20.0 0.3 collective-permute-start.2
  20.3 0.7 %copy-done.8 = s32[1,256]{1,0:T(1,128)S(1)} copy-done((s32[1,256]{1,0:T(1,128)S(1)}, s32[1,256]{1,0:T(1,128)}, u32[]{:S(2)}) %copy-start.8) | copy-done | bytes 1048
  20.9 7.1 %shard_map.123 = (f32[64,128]{1,0:T(8,128)S(1)}, f32[64,128]{1,0:T(8,128)S(1)}, f32[256,128]{1,0:T(8,128)S(1)}) custom-call(s32[256,128]{1,0:T(8,128)S(1)} %bitcast.7, f32[256,128]{1,0:T(8,128)S(1)} %bitcast.9, f32[128,128]{1,0:T(8,128)S(1)} %bitcast.6, s32[1,256]{1,0:T(1,128)S(1)} %copy-done.8, s32[1,256]{1,0:T(1,128)S(1)} %copy-done.9), custom_call_target="tpu_custom_call" | custom-call | flops 2147483648 | bytes 524288 | tf_op jit(solution)/shard_map/pallas_call | solution.py:621
  28.1 0.1 shard_map.125
  28.2 0.4 collective-permute-start.3
  28.6 0.7 %collective-permute-start.4 = (f32[114,512]{1,0:T(8,128)S(1)}, f32[114,512]{1,0:T(8,128)S(1)}, u32[]{:S(2)}, u32[]{:S(2)}) collective-permute-start(f32[114,512]{1,0:T(8,128)S(1)} %get-tuple-element.40), channel_id=1, source_target_pairs={{1,2},{2,1},{3,7},{7,3},{5,6},{6,5},{4,8},{8,4},{9,10},{10,9},{11,... | collective-permute-start | bytes 700424 | tf_op jit(solution)/shard_map/ppermute | solution.py:633
  29.3 2.5 %shard_map.126 = (f32[4,128,128]{2,1,0:T(8,128)S(1)}, f32[4,128,128]{2,1,0:T(8,128)S(1)}, f32[4,128,128]{2,1,0:T(8,128)S(1)}, f32[4,128,128]{2,1,0:T(8,128)S(1)}...) custom-call(f32[12]{0:T(128)S(1)} %copy-done.3, ...), custom_call_target="tpu_custom_call" | custom-call | flops 3932160 | bytes 2621440 | tf_op jit(solution)/shard_map/pallas_call | solution.py:639
  31.9 5.2 %shard_map.127 = (f32[2,16,512]{2,1,0:T(8,128)S(1)}, f32[2,16,512]{2,1,0:T(8,128)S(1)}, f32[2,16,512]{2,1,0:T(8,128)S(1)}, f32[2,16,512]{2,1,0:T(8,128)S(1)}, f32[16,512]{1,0:T(8,128)S(1)}) custom-call(f32[12]{0:T(128)S(1)} %copy-done.3, f32[12]{0:T(128)S(1)} %copy-done.4, f32[12]{0:T(128)S(1)} %copy-done.5, f32[16,512]{1,0:T(8,128)S(1)} %copy-done.1, ...), custom_call_target="tpu_custom_call" | custom-call | flops 13107200 | bytes 3932160 | tf_op jit(solution)/shard_map/pallas_call | solution.py:645
  37.1 5.3 %collective-permute-start.7 = (f32[16,512]{1,0:T(8,128)S(1)}, f32[16,512]{1,0:T(8,128)S(1)}, u32[]{:S(2)}, u32[]{:S(2)}) collective-permute-start(f32[16,512]{1,0:T(8,128)S(1)} %get-tuple-element.50.refs_0_), channel_id=1, source_target_pairs={{0,3},{1,2},{2,1},{3,0},{4,7},{5,6},{6,5},{7,4},{8,11},{9,10},{10,... | collective-permute-start | bytes 98312 | tf_op jit(solution)/shard_map/ppermute | solution.py:594
  42.4 0.8 %collective-permute-start.6 = (f32[16,512]{1,0:T(8,128)S(1)}, f32[16,512]{1,0:T(8,128)S(1)}, u32[]{:S(2)}, u32[]{:S(2)}) collective-permute-start(f32[16,512]{1,0:T(8,128)S(1)} %get-tuple-element.50.refs_0_), channel_id=1, source_target_pairs={{0,2},{1,3},{2,0},{3,1},{4,6},{5,7},{6,4},{7,5},{8,10},{9,11},{10,... | collective-permute-start | bytes 98312 | tf_op jit(solution)/shard_map/ppermute | solution.py:594
  43.2 0.5 collective-permute-start.8
  43.7 1.2 %collective-permute-start.9 = (f32[2,16,512]{2,1,0:T(8,128)S(1)}, f32[2,16,512]{2,1,0:T(8,128)S(1)}, u32[]{:S(2)}, u32[]{:S(2)}) collective-permute-start(f32[2,16,512]{2,1,0:T(8,128)S(1)} %get-tuple-element.53), channel_id=1, source_target_pairs={{0,2},{1,3},{2,0},{3,1},{4,6},{5,7},{6,4},{7,5},{8,10},{9,11},{10,... | collective-permute-start | bytes 196616 | tf_op jit(solution)/shard_map/ppermute | solution.py:594
  45.0 1.3 %collective-permute-start.10 = (f32[2,16,512]{2,1,0:T(8,128)S(1)}, f32[2,16,512]{2,1,0:T(8,128)S(1)}, u32[]{:S(2)}, u32[]{:S(2)}) collective-permute-start(f32[2,16,512]{2,1,0:T(8,128)S(1)} %get-tuple-element.54), channel_id=1, source_target_pairs={{0,3},{1,2},{2,1},{3,0},{4,7},{5,6},{6,5},{7,4},{8,11},{9,10},{10,... | collective-permute-start | bytes 196616 | tf_op jit(solution)/shard_map/ppermute | solution.py:594
  46.3 0.1 collective-permute-done.6.refs_2_
  46.4 2.8 %shard_map.128 = f32[128,128]{1,0:T(8,128)} custom-call(s32[256,128]{1,0:T(8,128)S(1)} %bitcast.8, f32[256,128]{1,0:T(8,128)S(1)} %bitcast.10, f32[256,128]{1,0:T(8,128)S(1)} %get-tuple-element.31.slot_section_ref, s32[1,256]{1,0:T(1,128)S(1)} %copy-done.8, s32[1,256]{1,0:T(1,128)S(1)} %copy-done.9, f32[16,512]{1,0:T(8,128)S(1)} %get-tuple-element.50.refs_0_, ...), custom_call_target="tpu_custom_call" | custom-call | flops 1073741824 | bytes 1048576 | tf_op jit(solution)/shard_map/pallas_call | solution.py:658
  49.2 3.4 %all-to-all-start.1 = ((f32[8,16,128]{2,1,0:T(8,128)}), f32[8,16,128]{2,1,0:T(8,128)S(1)}, u32[]{:S(2)}, u32[]{:S(2)}) async-start(f32[8,16,128]{2,1,0:T(8,128)} %bitcast.3), calls=%async_computation.1 | async-start | bytes 131072 | tf_op jit(solution)/shard_map/all_to_all | solution.py:666
  52.6 0.7 %shard_map.129 = f32[2,64,512]{2,1,0:T(8,128)} custom-call(f32[2,16,512]{2,1,0:T(8,128)S(1)} %get-tuple-element.55.refs_0_, f32[2,16,512]{2,1,0:T(8,128)S(1)} %collective-permute-done.8.refs_1_, f32[2,16,512]{2,1,0:T(8,128)S(1)} %collective-permute-done.9.refs_2_, f32[2,16,512]{2,1,0:T(8,128)S(1)} %collective-permute-done.10.refs_3_), custom_call_target="tpu_custom_call" | custom-call | bytes 524288 | tf_op jit(solution)/shard_map/pallas_call | solution.py:667
  53.3 6.1 %all-to-all-done.1 = f32[8,16,128]{2,1,0:T(8,128)S(1)} async-done(((f32[8,16,128]{2,1,0:T(8,128)}), f32[8,16,128]{2,1,0:T(8,128)S(1)}, u32[]{:S(2)}, u32[]{:S(2)}) %all-to-all-start.1) | async-done | bytes 65568 | tf_op jit(solution)/shard_map/all_to_all | solution.py:666
  59.4 0.6 %reduce_sum.9 = f32[16,128]{1,0:T(8,128)} reduce(f32[8,16,128]{2,1,0:T(8,128)S(1)} %all-to-all-done.1, f32[]{:T(128)} %constant.0.clone.1), dimensions={0}, to_apply=%region_0.0 | reduce | flops 14336 | bytes 73732 | tf_op jit(solution)/shard_map/reduce_sum | solution.py:671
  (30 shorter events, 0.1 us)
Async XLA Ops:
  16.2 4.0 %copy-start.2 = (f32[8,16,128]{2,1,0:T(8,128)S(1)}, f32[8,16,128]{2,1,0:T(8,128)}, u32[]{:S(2)}) copy-start(f32[8,16,128]{2,1,0:T(8,128)} %all_to_all.10) | copy-start | bytes 196612
  16.2 4.0 %copy-start.6 = (s32[1,256,128]{2,1,0:T(8,128)S(1)}, s32[1,256,128]{2,1,0:T(8,128)}, u32[]{:S(2)}) copy-start(s32[1,256,128]{2,1,0:T(8,128)} %param.20) | copy-start | bytes 393220
  16.2 4.0 %copy-start.7 = (f32[1,256,128]{2,1,0:T(8,128)S(1)}, f32[1,256,128]{2,1,0:T(8,128)}, u32[]{:S(2)}) copy-start(f32[1,256,128]{2,1,0:T(8,128)} %param.21) | copy-start | bytes 393220
  16.3 4.0 %copy-start.9 = (s32[1,256]{1,0:T(1,128)S(1)}, s32[1,256]{1,0:T(1,128)}, u32[]{:S(2)}) copy-start(s32[1,256]{1,0:T(1,128)} %local_ref.3) | copy-start | bytes 3076
  18.3 9.7 %collective-permute-start = (f32[2,2,16,512]{3,2,1,0:T(8,128)}, f32[2,2,16,512]{3,2,1,0:T(8,128)S(1)}, u32[]{:S(2)}, u32[]{:S(2)}) collective-permute-start(f32[2,2,16,512]{3,2,1,0:T(8,128)} %get-tuple-element.36), channel_id=1, source_target_pairs={{0,1},{1,0},{2,3},{3,2},{4,5},{5,4},{6,7},{7,6},{8,9},{9,8},{10,11... | collective-permute-start | bytes 393224 | tf_op jit(solution)/shard_map/ppermute | solution.py:594
  18.4 9.6 %collective-permute-start.1 = (f32[2,2,16,512]{3,2,1,0:T(8,128)}, f32[2,2,16,512]{3,2,1,0:T(8,128)S(1)}, u32[]{:S(2)}, u32[]{:S(2)}) collective-permute-start(f32[2,2,16,512]{3,2,1,0:T(8,128)} %get-tuple-element.37), channel_id=1, source_target_pairs={{0,2},{1,3},{2,0},{3,1},{4,6},{5,7},{6,4},{7,5},{8,10},{9,11},{10,... | collective-permute-start | bytes 393224 | tf_op jit(solution)/shard_map/ppermute | solution.py:594
  20.0 8.1 %collective-permute-start.2 = (f32[2,2,16,512]{3,2,1,0:T(8,128)}, f32[2,2,16,512]{3,2,1,0:T(8,128)S(1)}, u32[]{:S(2)}, u32[]{:S(2)}) collective-permute-start(f32[2,2,16,512]{3,2,1,0:T(8,128)} %get-tuple-element.38), channel_id=1, source_target_pairs={{0,3},{1,2},{2,1},{3,0},{4,7},{5,6},{6,5},{7,4},{8,11},{9,10},{10,... | collective-permute-start | bytes 393224 | tf_op jit(solution)/shard_map/ppermute | solution.py:594
  20.3 0.7 %copy-start.8 = (s32[1,256]{1,0:T(1,128)S(1)}, s32[1,256]{1,0:T(1,128)}, u32[]{:S(2)}) copy-start(s32[1,256]{1,0:T(1,128)} %owner_ref.3) | copy-start | bytes 3076
  20.9 7.1 %copy-start = (f32[2,2,16,512]{3,2,1,0:T(8,128)S(1)}, f32[2,2,16,512]{3,2,1,0:T(8,128)}, u32[]{:S(2)}) copy-start(f32[2,2,16,512]{3,2,1,0:T(8,128)} %get-tuple-element.35.refs_0_) | copy-start | bytes 393220
  20.9 7.1 %copy-start.1 = (f32[16,512]{1,0:T(8,128)S(1)}, f32[16,512]{1,0:T(8,128)}, u32[]{:S(2)}) copy-start(f32[16,512]{1,0:T(8,128)} %get-tuple-element.32.land_ref) | copy-start | bytes 98308
  28.2 1.1 %copy-start.3 = (f32[12]{0:T(128)S(1)}, f32[12]{0:T(128)}, u32[]{:S(2)}) copy-start(f32[12]{0:T(128)} %kst_ref.1) | copy-start | bytes 148
  28.2 1.1 %copy-start.4 = (f32[12]{0:T(128)S(1)}, f32[12]{0:T(128)}, u32[]{:S(2)}) copy-start(f32[12]{0:T(128)} %alphat_ref.1) | copy-start | bytes 148
  28.2 1.1 %copy-start.5 = (f32[12]{0:T(128)S(1)}, f32[12]{0:T(128)}, u32[]{:S(2)}) copy-start(f32[12]{0:T(128)} %storet_ref.1) | copy-start | bytes 148
  28.2 3.7 %collective-permute-start.3 = (f32[114,512]{1,0:T(8,128)S(1)}, f32[114,512]{1,0:T(8,128)S(1)}, u32[]{:S(2)}, u32[]{:S(2)}) collective-permute-start(f32[114,512]{1,0:T(8,128)S(1)} %get-tuple-element.39), channel_id=1, source_target_pairs={{0,1},{1,0},{2,3},{3,2},{4,5},{5,4},{6,7},{7,6},{8,9},{9,8},{10,11... | collective-permute-start | bytes 700424 | tf_op jit(solution)/shard_map/ppermute | solution.py:632
  28.6 3.3 %collective-permute-start.4 = (f32[114,512]{1,0:T(8,128)S(1)}, f32[114,512]{1,0:T(8,128)S(1)}, u32[]{:S(2)}, u32[]{:S(2)}) collective-permute-start(f32[114,512]{1,0:T(8,128)S(1)} %get-tuple-element.40), channel_id=1, source_target_pairs={{1,2},{2,1},{3,7},{7,3},{5,6},{6,5},{4,8},{8,4},{9,10},{10,9},{11,... | collective-permute-start | bytes 700424 | tf_op jit(solution)/shard_map/ppermute | solution.py:633
  37.1 7.9 %collective-permute-start.7 = (f32[16,512]{1,0:T(8,128)S(1)}, f32[16,512]{1,0:T(8,128)S(1)}, u32[]{:S(2)}, u32[]{:S(2)}) collective-permute-start(f32[16,512]{1,0:T(8,128)S(1)} %get-tuple-element.50.refs_0_), channel_id=1, source_target_pairs={{0,3},{1,2},{2,1},{3,0},{4,7},{5,6},{6,5},{7,4},{8,11},{9,10},{10,... | collective-permute-start | bytes 98312 | tf_op jit(solution)/shard_map/ppermute | solution.py:594
  42.4 3.9 %collective-permute-start.6 = (f32[16,512]{1,0:T(8,128)S(1)}, f32[16,512]{1,0:T(8,128)S(1)}, u32[]{:S(2)}, u32[]{:S(2)}) collective-permute-start(f32[16,512]{1,0:T(8,128)S(1)} %get-tuple-element.50.refs_0_), channel_id=1, source_target_pairs={{0,2},{1,3},{2,0},{3,1},{4,6},{5,7},{6,4},{7,5},{8,10},{9,11},{10,... | collective-permute-start | bytes 98312 | tf_op jit(solution)/shard_map/ppermute | solution.py:594
  43.2 3.2 %collective-permute-start.5 = (f32[16,512]{1,0:T(8,128)S(1)}, f32[16,512]{1,0:T(8,128)S(1)}, u32[]{:S(2)}, u32[]{:S(2)}) collective-permute-start(f32[16,512]{1,0:T(8,128)S(1)} %get-tuple-element.50.refs_0_), channel_id=1, source_target_pairs={{0,1},{1,0},{2,3},{3,2},{4,5},{5,4},{6,7},{7,6},{8,9},{9,8},{10,11... | collective-permute-start | bytes 98312 | tf_op jit(solution)/shard_map/ppermute | solution.py:594
  43.2 6.0 %collective-permute-start.8 = (f32[2,16,512]{2,1,0:T(8,128)S(1)}, f32[2,16,512]{2,1,0:T(8,128)S(1)}, u32[]{:S(2)}, u32[]{:S(2)}) collective-permute-start(f32[2,16,512]{2,1,0:T(8,128)S(1)} %get-tuple-element.52), channel_id=1, source_target_pairs={{0,1},{1,0},{2,3},{3,2},{4,5},{5,4},{6,7},{7,6},{8,9},{9,8},{10,11... | collective-permute-start | bytes 196616 | tf_op jit(solution)/shard_map/ppermute | solution.py:594
  43.7 5.5 %collective-permute-start.9 = (f32[2,16,512]{2,1,0:T(8,128)S(1)}, f32[2,16,512]{2,1,0:T(8,128)S(1)}, u32[]{:S(2)}, u32[]{:S(2)}) collective-permute-start(f32[2,16,512]{2,1,0:T(8,128)S(1)} %get-tuple-element.53), channel_id=1, source_target_pairs={{0,2},{1,3},{2,0},{3,1},{4,6},{5,7},{6,4},{7,5},{8,10},{9,11},{10,... | collective-permute-start | bytes 196616 | tf_op jit(solution)/shard_map/ppermute | solution.py:594
  45.0 4.2 %collective-permute-start.10 = (f32[2,16,512]{2,1,0:T(8,128)S(1)}, f32[2,16,512]{2,1,0:T(8,128)S(1)}, u32[]{:S(2)}, u32[]{:S(2)}) collective-permute-start(f32[2,16,512]{2,1,0:T(8,128)S(1)} %get-tuple-element.54), channel_id=1, source_target_pairs={{0,3},{1,2},{2,1},{3,0},{4,7},{5,6},{6,5},{7,4},{8,11},{9,10},{10,... | collective-permute-start | bytes 196616 | tf_op jit(solution)/shard_map/ppermute | solution.py:594
  49.2 10.2 %all-to-all-start.1 = ((f32[8,16,128]{2,1,0:T(8,128)}), f32[8,16,128]{2,1,0:T(8,128)S(1)}, u32[]{:S(2)}, u32[]{:S(2)}) async-start(f32[8,16,128]{2,1,0:T(8,128)} %bitcast.3), calls=%async_computation.1 | async-start | bytes 131072 | tf_op jit(solution)/shard_map/all_to_all | solution.py:666

commit v8 on v7

--- a/solution.py
+++ b/solution.py
@@ -75,15 +75,14 @@
 
 
 def river_kernel(
-    breadth, span, reach_rows, cells_ref, bed_ref, section_ref, owner_ref, local_ref,
+    breadth, span, cells_ref, bed_ref, section_ref, reach_ref,
     diag_ref, rhs_ref, slot_section_ref, block_sc, spot_sc, dhigh_sc, dlow_sc, rhigh_sc, rlow_sc, sum_sc,
 ):
     _, _, number = position()
     rows = section_ref.shape[0]
-    slots = owner_ref.shape[1]
+    slots = reach_ref.shape[1]
     index = lax.broadcasted_iota(jnp.int32, (rows, slots), 0)
-    reach = owner_ref[...] * reach_rows + local_ref[...]
-    pick = jnp.where(index == reach, 1.0, 0.0).astype(jnp.bfloat16)
+    pick = jnp.where(index == reach_ref[...], 1.0, 0.0).astype(jnp.bfloat16)
     picked = jnp.zeros(slot_section_ref.shape, jnp.float32)
     for piece in bf16_pieces(section_ref[...], 3):
         picked = picked + lax.dot_general(
@@ -159,41 +158,51 @@
             put_edges(entry, top, bottom, slice(part * LANES, (part + 1) * LANES))
 
 
-def spread_kernel(section_hbm, spread_ref, section_ref, sem):
-    copy = pltpu.make_async_copy(section_hbm, section_ref, sem)
-    copy.start()
-    copy.wait()
+def spread_kernel(section_hbm, owner_hbm, local_hbm, spread_ref, reach_ref, section_ref, owner_ref, local_ref, sems):
+    pairs = ((section_hbm, section_ref), (owner_hbm, owner_ref), (local_hbm, local_ref))
+    copies = [pltpu.make_async_copy(here, there, sems.at[k]) for k, (here, there) in enumerate(pairs)]
+    for copy in copies:
+        copy.start()
+    for copy in copies:
+        copy.wait()
     for tile in range(spread_ref.shape[0]):
         spread_ref[tile] = section_ref[...]
+    reach_ref[...] = owner_ref[...] * section_ref.shape[0] + local_ref[...]
 
 
 def prepare_kernel(head_hbm, soil_hbm, land_hbm, after_hbm, *refs):
     del after_hbm
     groups = lax.axis_size("layer")
-    block_refs, land_out_ref = refs[:groups], refs[groups]
-    head_ref, soil_ref, land_ref, sems = refs[groups + 1:]
-    held, across, _ = head_ref.shape
+    block_hbms, land_out_ref = refs[:groups], refs[groups]
+    soil_ref, soil_float_ref, land_ref, in_sems, head_sems, soil_sems = refs[groups + 1:]
+    held, across, _ = soil_ref.shape
     span = across // groups
-    pairs = [(land_hbm, land_ref)]
-    for layer in range(held):
-        pairs += [(head_hbm.at[layer], head_ref.at[layer]), (soil_hbm.at[layer], soil_ref.at[layer])]
-    copies = [pltpu.make_async_copy(here, there, sems.at[k]) for k, (here, there) in enumerate(pairs)]
-    for copy in copies:
-        copy.start()
     own, flip, _ = position()
 
     def rows_of(target):
         return pl.ds(pl.multiple_of(span_at(flip, groups, target) * span, span), span)
 
-    copies[0].wait()
-    land_out_ref[...] = land_ref[rows_of(own), :].astype(jnp.float32)
+    copies = [pltpu.make_async_copy(soil_hbm.at[layer], soil_ref.at[layer], in_sems.at[layer]) for layer in range(held)]
+    copies.append(pltpu.make_async_copy(land_hbm.at[rows_of(own), :], land_ref, in_sems.at[held]))
+    heads = [
+        pltpu.make_async_copy(head_hbm.at[:, rows_of(own ^ step), :], block_hbm.at[0], head_sems.at[step])
+        for step, block_hbm in enumerate(block_hbms)
+    ]
+    for copy in copies + heads:
+        copy.start()
     for layer in range(held):
-        copies[1 + 2 * layer].wait()
-        copies[2 + 2 * layer].wait()
-        for step, out_ref in enumerate(block_refs):
-            rows = rows_of(own ^ step)
-            out_ref[0, layer] = head_ref[layer, rows, :]
-            out_ref[1, layer] = soil_ref[layer, rows, :].astype(jnp.float32)
+        copies[layer].wait()
+        soil_float_ref[layer] = soil_ref[layer].astype(jnp.float32)
+    soils = [
+        pltpu.make_async_copy(soil_float_ref.at[:, rows_of(own ^ step), :], block_hbm.at[1], soil_sems.at[step])
+        for step, block_hbm in enumerate(block_hbms)
+    ]
+    for copy in soils:
+        copy.start()
+    copies[held].wait()
+    land_out_ref[...] = land_ref[...].astype(jnp.float32)
+    for copy in heads + soils:
+        copy.wait()
 
 
 class Rows:
@@ -241,29 +250,30 @@
 
 
 class Faces:
-    def __init__(self, rows):
-        self.rows = rows
+    def __init__(self, rows, land, lands):
+        self.rows, self.lands = rows, lands
+        lx_ref, ly_ref, lz_ref = lands
+        count = land.shape[0]
         level = lax.broadcasted_iota(jnp.int32, (rows.layers, rows.breadth), 0)
-        column = lax.broadcasted_iota(jnp.int32, (rows.layers, rows.breadth), 1)
         self.not_bottom = level < rows.layers - 1
-        self.not_last = column < rows.breadth - 1
-
-    def conduct(self, ks, alpha, head, land):
-        cond = ks * jnp.exp(alpha * jnp.minimum(head, 0.0))
-        return cond, cond * land
-
-    def face(self, factor, here, there):
-        return factor * 2.0 * here[1] * there[1] * reciprocal(here[0] + there[0])
-
-    def between_rows(self, here, there):
-        return self.face(LATERAL, here, there)
-
-    def in_row(self, here):
+        not_last = lax.broadcasted_iota(jnp.int32, land.shape, 1) < rows.breadth - 1
+        lx_ref[pl.ds(0, count - 1), :] = 2.0 * LATERAL * land[:count - 1] * land[1:]
+        ly_ref[...] = jnp.where(not_last, 2.0 * LATERAL * land * rows.east(land), 0.0)
+        lz_ref[...] = 2.0 * VERTICAL * land * land
+
+    def conduct(self, ks, alpha, head):
+        return ks * jnp.exp(alpha * jnp.minimum(head, 0.0))
+
+    def face(self, land, here, there):
+        return land * (here * there) * reciprocal(here + there)
+
+    def between_rows(self, row, here, there):
+        return self.face(self.lands[0][pl.ds(row, 1), :], here, there)
+
+    def in_row(self, row, here):
         rows = self.rows
-        cond, opened = here
-        wy = self.face(LATERAL, here, (rows.east(cond), rows.east(opened)))
-        wz = self.face(VERTICAL, here, (rows.below(cond), rows.below(opened)))
-        wy = jnp.where(self.not_last, wy, 0.0)
+        wy = self.face(self.lands[1][pl.ds(row, 1), :], here, rows.east(here))
+        wz = self.face(self.lands[2][pl.ds(row, 1), :], here, rows.below(here))
         wz = jnp.where(self.not_bottom, wz, 0.0)
         wz_above = rows.above(wz)
         return wy, wz, wy + rows.west(wy) + wz + wz_above, GRAVITY * (wz_above - wz)
@@ -292,11 +302,11 @@
     groups = lax.axis_size("layer")
     own, _, _ = position()
     block_refs = refs[:groups]
-    first_out, ks_out, alpha_out, store_out, wx_out, wy_out, wz_out, diag_out, base_out, soil_sc = refs[groups:]
+    first_out, ks_out, alpha_out, store_out, wx_out, wy_out, wz_out, diag_out, base_out, soil_sc, *lands = refs[groups:]
     _, held, span, breadth = block_refs[0].shape
     layers = groups * held
     rows = Rows(layers, breadth)
-    faces = Faces(rows)
+    faces = Faces(rows, land_ref[...], lands)
 
     for step, block_ref in enumerate(block_refs):
         for held_layer in range(held):
@@ -309,15 +319,15 @@
         soil = rows.get(soil_sc, row).astype(jnp.int32)
         ks, alpha, store = [look_up(rows, table, soil) for table in tables]
         first = rows.get(first_out, row)
-        here = faces.conduct(ks, alpha, first, land_ref[pl.ds(row, 1), :])
-        wy, wz, diagonal, gravity = faces.in_row(here)
+        here = faces.conduct(ks, alpha, first)
+        wy, wz, diagonal, gravity = faces.in_row(row, here)
         for ref, value in (
             (ks_out, ks), (alpha_out, alpha), (store_out, store), (wy_out, wy), (wz_out, wz),
             (diag_out, store + diagonal), (base_out, store * first + gravity),
         ):
             rows.put(ref, row, value)
         if row > 0:
-            rows.put(wx_out, row - 1, faces.between_rows(before, here))
+            rows.put(wx_out, row - 1, faces.between_rows(row - 1, before, here))
         before = here
 
 
@@ -330,14 +340,13 @@
     head_refs, top_ref = refs[9:9 + groups], refs[9 + groups]
     (
         first_sc, soil_sc, ks_sc, alpha_sc, store_sc, wx_sc, wy_sc, wz_sc, base_sc, inv_sc, ping_sc, pong_sc,
-        land_sc, dtop_sc, rtop_sc,
+        land_sc, dtop_sc, rtop_sc, *lands,
     ) = refs[10 + groups:]
     held, span, breadth = head_refs[0].shape
     layers = groups * held
     window = span + 2 * HALO
     last_own = HALO + span
     rows = Rows(layers, breadth)
-    faces = Faces(rows)
     side = HALO * rows.per_row
 
     land_sc[pl.ds(HALO, span), :] = land_ref[...]
@@ -365,6 +374,7 @@
             for ref, row in ((above_ref, 0), (below_ref, last_own)):
                 put_halo(ref, own ^ 1 if ref is near_ref else far_partner, row)
 
+    faces = Faces(rows, land_sc[...], lands)
     tables = lane_tables((kst_ref, alphat_ref, storet_ref), layers)
     for row in [*range(HALO), *range(last_own, window)]:
         soil = rows.get(soil_sc, row).astype(jnp.int32)
@@ -392,7 +402,7 @@
         rows.put(base_sc, row, base + riv_row(rtop_sc, row))
 
     def conduct(now, row):
-        return faces.conduct(ks.get(row), alpha.get(row), now.get(row), land_sc[pl.ds(row, 1), :])
+        return faces.conduct(ks.get(row), alpha.get(row), now.get(row))
 
     def sweep(now, later_ref, weights, begin, stop):
         wx_of, wy_of, wz_of = weights
@@ -420,7 +430,7 @@
                 if early and HALO <= row - 1 < last_own - 1:
                     wx = wx_of.get(row - 1)
                 else:
-                    wx = faces.between_rows(before, here)
+                    wx = faces.between_rows(row - 1, before, here)
                     wx_of.put(row - 1, wx)
                 if row - 1 > begin:
                     diagonal, base = pending
@@ -429,7 +439,7 @@
             if staged:
                 pending = rows.get(partial_ref, row - HALO), rows.get(gravity_ref, row - HALO)
             elif begin < row < stop - 1:
-                wy, wz, diagonal, gravity = faces.in_row(here)
+                wy, wz, diagonal, gravity = faces.in_row(row, here)
                 wy_of.put(row, wy)
                 wz_of.put(row, wz)
                 pending = store.get(row) + diagonal, store.get(row) * first.get(row) + gravity
@@ -449,7 +459,7 @@
                 head_ref[held_layer, :, lanes] = later_ref[part, pl.ds(HALO * layers + layer, span, stride=layers), :]
 
 
-def inflow_kernel(reach_rows, cells_ref, bed_ref, slot_section_ref, owner_ref, local_ref, *refs):
+def inflow_kernel(reach_rows, cells_ref, bed_ref, slot_section_ref, reach_ref, *refs):
     groups = lax.axis_size("layer")
     own_layer, flip, _ = position()
     top_refs = refs[:groups]
@@ -515,16 +525,31 @@
         [slot_in if number == 0 else pltpu.roll(slot_in, LANES - number * quarter, 1) for number in range(groups)],
         axis=0,
     )
-    rows = out_ref.shape[0]
-    index = lax.broadcasted_iota(jnp.int32, (rows, slots), 0)
-    reach = owner_ref[...] * reach_rows + local_ref[...]
-    put = jnp.where(index == reach, 1.0, 0.0).astype(jnp.bfloat16)
-    total = jnp.zeros((rows, LANES), jnp.float32)
-    for piece in bf16_pieces(spread, 3):
-        total = total + lax.dot_general(
-            put, piece, (((1,), (0,)), ((), ())), preferred_element_type=jnp.float32
-        )
-    out_ref[...] = total
+    in_quarter = lax.broadcasted_iota(jnp.int32, spread.shape, 1) < quarter
+    pieces = bf16_pieces(jnp.where(in_quarter, spread, 0.0), 3)
+    fold = reach_rows // groups
+    index = lax.broadcasted_iota(jnp.int32, (out_ref.shape[0], slots), 0)
+    index = index // fold * reach_rows + lax.rem(index, fold)
+    result = None
+    for number in range(groups):
+        put = jnp.where(index + number * fold == reach_ref[...], 1.0, 0.0).astype(jnp.bfloat16)
+        total = jnp.zeros(out_ref.shape, jnp.float32)
+        for piece in pieces:
+            total = total + lax.dot_general(
+                put, piece, (((1,), (0,)), ((), ())), preferred_element_type=jnp.float32
+            )
+        result = total if result is None else result + pltpu.roll(total, number * quarter, 1)
+    out_ref[...] = result
+
+
+def sum_kernel(terms_ref, inflow_ref):
+    total = terms_ref[0]
+    for tile in range(1, terms_ref.shape[0]):
+        total = total + terms_ref[tile]
+    fold, quarter = total.shape[0], inflow_ref.shape[1]
+    for number in range(inflow_ref.shape[0] // fold):
+        lanes = slice(number * quarter, (number + 1) * quarter)
+        inflow_ref[pl.ds(number * fold, fold), :] = total[:, lanes]
 
 
 def head_kernel(*refs):
@@ -541,7 +566,7 @@
         copy.wait()
 
 
-def call(kernel, out_shape, in_specs, scratch, flops, moved, vmem=VMEM_LIMIT, out_specs=None):
+def call(kernel, out_shape, in_specs, scratch, micros, vmem=VMEM_LIMIT, out_specs=None):
     single = not isinstance(out_shape, (tuple, list))
     return pl.pallas_call(
         kernel,
@@ -550,7 +575,7 @@
         out_specs=out_specs or (in_vmem if single else tuple(in_vmem for _ in out_shape)),
         scratch_shapes=scratch,
         compiler_params=pltpu.CompilerParams(vmem_limit_bytes=vmem),
-        cost_estimate=pl.CostEstimate(flops=flops, bytes_accessed=moved, transcendentals=0),
+        cost_estimate=pl.CostEstimate(flops=int(micros * 1.15e9), bytes_accessed=0, transcendentals=0),
     )
 
 
@@ -594,11 +619,21 @@
             received.append(lax.ppermute(parts[step], "layer", [(i, i ^ step) for i in range(groups)]))
         return received
 
-    field_bytes = held * across * breadth * 4
-    spread = call(
-        spread_kernel, jax.ShapeDtypeStruct((tiles, reach_rows, node_count), jnp.float32), [in_hbm],
-        [pltpu.VMEM(section.shape, jnp.float32), pltpu.SemaphoreType.DMA(())], 0, 0, VMEM_MOST,
-    )(section)
+    spread, reach = call(
+        spread_kernel,
+        (
+            jax.ShapeDtypeStruct((tiles, reach_rows, node_count), jnp.float32),
+            jax.ShapeDtypeStruct(cross_owner.shape, jnp.int32),
+        ),
+        [in_hbm] * 3,
+        [
+            pltpu.VMEM(section.shape, jnp.float32),
+            pltpu.VMEM(cross_owner.shape, jnp.int32),
+            pltpu.VMEM(cross_owner.shape, jnp.int32),
+            pltpu.SemaphoreType.DMA((3,)),
+        ],
+        1, VMEM_MOST,
+    )(section, cross_owner, cross_local)
     whole_section = lax.all_to_all(spread, "tile", 0, 0).reshape(tiles * reach_rows, node_count)
     *own_blocks, land = call(
         prepare_kernel,
@@ -606,40 +641,41 @@
         + (jax.ShapeDtypeStruct((span, breadth), jnp.float32),),
         [in_hbm] * 4,
         [
-            pltpu.VMEM(head_start.shape, jnp.float32),
             pltpu.VMEM(soil_class.shape, jnp.int32),
-            pltpu.VMEM(land_mask.shape, jnp.int32),
-            pltpu.SemaphoreType.DMA((1 + 2 * held,)),
+            pltpu.VMEM(soil_class.shape, jnp.float32),
+            pltpu.VMEM((span, breadth), jnp.int32),
+            pltpu.SemaphoreType.DMA((held + 1,)),
+            pltpu.SemaphoreType.DMA((groups,)),
+            pltpu.SemaphoreType.DMA((groups,)),
         ],
-        0, 4 * field_bytes, VMEM_MOST,
-    )(head_start, soil_class, land_mask, whole_section)
+        2, VMEM_MOST, (in_hbm,) * groups + (in_vmem,),
+    )(head_start, soil_class, land_mask, spread)
     received = exchange(own_blocks)
 
     node_scratch = pltpu.VMEM((slots, LANES), jnp.float32)
     riv_shape = jax.ShapeDtypeStruct((blocks, LANES), jnp.float32)
-    node_bytes = slots * LANES * 4
     diag, rhs, slot_section = call(
-        functools.partial(river_kernel, breadth, span, reach_rows),
+        functools.partial(river_kernel, breadth, span),
         (riv_shape, riv_shape, jax.ShapeDtypeStruct((slots, node_count), jnp.float32)),
-        [in_vmem] * 5,
+        [in_vmem] * 4,
         [node_scratch] * 6 + [pltpu.VMEM((span * breadth // BLOCK, LANES), jnp.float32)],
-        8 * span * breadth * slots * LANES, 4 * node_bytes,
-    )(cells, bed, whole_section, cross_owner, cross_local)
+        7,
+    )(cells, bed, whole_section, reach)
     edges = jax.ShapeDtypeStruct(((2 * layers + 3) * HALO, breadth), jnp.float32)
     near_edge, far_edge = call(
-        edge_kernel, (edges, edges), [in_vmem] * (3 + groups), [], 0, 8 * layers * HALO * breadth * 4,
+        edge_kernel, (edges, edges), [in_vmem] * (3 + groups), [], 0.1,
     )(land, diag, rhs, *received)
     near_halo = lax.ppermute(near_edge, "layer", near)
     far_halo = lax.ppermute(far_edge, FLAT, far)
 
     window = span + 2 * HALO
-    cells_held = layers * span * breadth
     own_field = jax.ShapeDtypeStruct((per_row, span * layers, LANES), jnp.float32)
     field = pltpu.VMEM((per_row, window * layers, LANES), jnp.float32)
     staged = call(
         stage_kernel, (own_field,) * 9,
-        [in_smem] * 3 + [in_vmem] * (1 + groups), [pltpu.VMEM(own_field.shape, jnp.float32)],
-        60 * cells_held, 40 * cells_held,
+        [in_smem] * 3 + [in_vmem] * (1 + groups),
+        [pltpu.VMEM(own_field.shape, jnp.float32)] + [pltpu.VMEM((span, breadth), jnp.float32)] * 3,
+        2.5,
     )(ks_table, alpha_table, store_table, land, *received)
     head_shape = jax.ShapeDtypeStruct((held, span, breadth), jnp.float32)
     *heads, top = call(
@@ -648,27 +684,30 @@
         [in_smem] * 3 + [in_vmem] * (5 + len(staged)),
         [field] * 12
         + [pltpu.VMEM((window, breadth), jnp.float32)]
-        + [pltpu.VMEM((window * per_row, LANES), jnp.float32)] * 2,
-        200 * cells_held, 60 * cells_held,
+        + [pltpu.VMEM((window * per_row, LANES), jnp.float32)] * 2
+        + [pltpu.VMEM((window, breadth), jnp.float32)] * 3,
+        5,
     )(ks_table, alpha_table, store_table, land, near_halo, far_halo, diag, rhs, *staged)
     tops = exchange([top] * groups)
     backs = exchange(heads)
 
+    fold = reach_rows // groups
     packed = pltpu.VMEM((slots // groups, LANES), jnp.float32)
     partial = call(
         functools.partial(inflow_kernel, reach_rows),
-        jax.ShapeDtypeStruct((tiles * reach_rows, node_count), jnp.float32),
-        [in_vmem] * (5 + groups),
+        jax.ShapeDtypeStruct((tiles * fold, node_count), jnp.float32),
+        [in_vmem] * (4 + groups),
         [packed] * 3 + [pltpu.VMEM((across * per_row, LANES), jnp.float32)],
-        4 * across * breadth * slots * node_count // groups, 8 * node_bytes,
-    )(cells, bed, slot_section, cross_owner, cross_local, *tops)
+        3,
+    )(cells, bed, slot_section, reach, *tops)
     partial, *backs = lax.optimization_barrier((partial, *backs))
-    terms = lax.all_to_all(partial.reshape(tiles, reach_rows, node_count), "tile", 0, 0)
+    terms = lax.all_to_all(partial.reshape(tiles, fold, node_count), "tile", 0, 0)
     head = call(
         head_kernel, jax.ShapeDtypeStruct(head_start.shape, jnp.float32), [in_vmem] * groups,
-        [pltpu.SemaphoreType.DMA((groups,))], 0, 2 * field_bytes, out_specs=in_hbm,
+        [pltpu.SemaphoreType.DMA((groups,))], 0.7, out_specs=in_hbm,
     )(*backs)
-    return head, jnp.sum(terms, axis=0)[:, :node_count // groups]
+    inflow_shape = jax.ShapeDtypeStruct((reach_rows, node_count // groups), jnp.float32)
+    return head, call(sum_kernel, inflow_shape, [in_vmem], [], 0.1)(terms)
 
 
 def solution(mesh):

time: 60.4 us -> 63.9 us (1.058)
  blocking collectives: 14.3 us -> 0 us
  starting transfers between devices: 15.5 us -> 25.6 us
  Pallas kernels: 21.9 us -> 30.1 us
    all_to_all x1 -> x0, blocking collectives: 14.3 us -> none  [on_device(): lax.all_to_all(spread, 'tile', 0, 0).reshape(tiles * reach_rows, node_count)]
    all_to_all x1 -> x2, starting transfers between devices: 3.36 us -> 13.1 us  [the longest x1 7.26 us: on_device(): lax.all_to_all(spread, 'tile', 0, 0).reshape(tiles * reach_rows, node_count)]
    pallas_call x1, Pallas kernels: 2.06 us -> 9.78 us  [on_device(): call(prepare_kernel, (jax.ShapeDtypeStruct((2, held, span, breadth), jnp....]
    pallas_call x3 -> x4, Pallas kernels: 8.52 us -> 9.23 us  [the longest x1 7.08 us: on_device(): call(functools.partial(river_kernel, breadth, span), (riv_shape, riv_shap...]
    all_to_all x1 -> x2, waiting for transfers between devices: 6.11 us -> 5.84 us  [the longest x1 5.84 us: on_device(): lax.all_to_all(partial.reshape(tiles, fold, node_count), 'tile', 0, 0)]
  transfers between devices with their start and end apart: 12 -> 13, of which waited for: 2 -> 2; matrix products, arithmetic and copies ran while one was open for 0% -> 0% of each run, Pallas kernels for 22% -> 36%
where the time goes in v8:
time: 63.9 us; the launch traced here: 63.5 us
  Pallas kernels  30.1 us (47%)
  starting transfers between devices  25.6 us (40%)
  waiting for transfers between devices  6.38 us (10%)
  between operations  0.82 us (1%)
  local copies, waits for them, and re-layouts  0.71 us (1%)
    ppermute x9, starting transfers between devices, exchange(): lax.ppermute(parts[step], 'layer', [(i, i ^ step) for i in range(groups)])  11.3 us
    pallas_call x1, Pallas kernels, on_device(): call(prepare_kernel, (jax.ShapeDtypeStruct((2, held, span, breadth), jnp....  9.78 us
    all_to_all x1, starting transfers between devices, on_device(): lax.all_to_all(spread, 'tile', 0, 0).reshape(tiles * reach_rows, node_count)  7.26 us
    pallas_call x1, Pallas kernels, on_device(): call(functools.partial(river_kernel, breadth, span), (riv_shape, riv_shap...  7.08 us
    all_to_all x1, starting transfers between devices, on_device(): lax.all_to_all(partial.reshape(tiles, fold, node_count), 'tile', 0, 0)  5.88 us
    all_to_all x1, waiting for transfers between devices, on_device(): lax.all_to_all(partial.reshape(tiles, fold, node_count), 'tile', 0, 0)  5.84 us
    pallas_call x1, Pallas kernels, on_device(): call(flow_kernel, (head_shape,) * groups + (jax.ShapeDtypeStruct((span, b...  5.05 us
    pallas_call x1, Pallas kernels, on_device(): call(functools.partial(inflow_kernel, reach_rows), jax.ShapeDtypeStruct((...  2.91 us
  transfers between devices with their start and end apart: 13, of which 2 were waited for; matrix products, arithmetic and copies ran while one was open for 0% of the time, Pallas kernels for 36%

profile of v8, /device:TPU:0, one launch (start us, length us, event | category | flops | bytes accessed | tf_op | source)
XLA Modules:
  0.0 63.5 jit_solution(12276149822804905851)
XLA Ops:
  0.6 1.4 %shard_map.122 = (f32[8,16,128]{2,1,0:T(8,128)}, s32[1,256]{1,0:T(1,128)}) custom-call(f32[16,128]{1,0:T(8,128)} %section_hbm.1, s32[1,256]{1,0:T(1,128)} %owner_hbm.1, s32[1,256]{1,0:T(1,128)} %local_hbm.1), custom_call_target="tpu_custom_call" | custom-call | flops 1150000000 | tf_op jit(solution)/shard_map/pallas_call | solution.py:622
  2.0 7.3 %all-to-all-start = ((f32[8,16,128]{2,1,0:T(8,128)}), f32[8,16,128]{2,1,0:T(8,128)S(1)}, u32[]{:S(2)}, u32[]{:S(2)}) async-start(f32[8,16,128]{2,1,0:T(8,128)} %get-tuple-element.33.after_hbm), calls=%async_computation | async-start | bytes 131072 | tf_op jit(solution)/shard_map/all_to_all | solution.py:637
  9.3 9.8 %shard_map.124 = (f32[2,2,16,512]{3,2,1,0:T(8,128)}, f32[2,2,16,512]{3,2,1,0:T(8,128)}, f32[2,2,16,512]{3,2,1,0:T(8,128)}, f32[2,2,16,512]{3,2,1,0:T(8,128)}, f32[16,512]{1,0:T(8,128)}) custom-call(f32[2,64,512]{2,1,0:T(8,128)} %head_hbm.1, s32[2,64,512]{2,1,0:T(8,128)} %soil_hbm.1, s32[64,512]{1,0:T(8,128)} %land_hbm.1, ...), custom_call_target="tpu_custom_call" | custom-call | flops 2300000000 | tf_op jit(solution)/shard_map/pallas_call | solution.py:638
  19.1 0.1 collective-permute-start
  19.2 1.6 %collective-permute-start.1 = (f32[2,2,16,512]{3,2,1,0:T(8,128)}, f32[2,2,16,512]{3,2,1,0:T(8,128)S(1)}, u32[]{:S(2)}, u32[]{:S(2)}) collective-permute-start(f32[2,2,16,512]{3,2,1,0:T(8,128)} %get-tuple-element.41), channel_id=1, source_target_pairs={{0,2},{1,3},{2,0},{3,1},{4,6},{5,7},{6,4},{7,5},{8,10},{9,11},{10,... | collective-permute-start | bytes 393224 | tf_op jit(solution)/shard_map/ppermute | solution.py:619
  20.7 0.3 collective-permute-start.2
  21.0 0.7 %copy-done.7 = s32[1,256]{1,0:T(1,128)S(1)} copy-done((s32[1,256]{1,0:T(1,128)S(1)}, s32[1,256]{1,0:T(1,128)}, u32[]{:S(2)}) %copy-start.7) | copy-done | bytes 1048
  21.7 7.1 %shard_map.123 = (f32[64,128]{1,0:T(8,128)S(1)}, f32[64,128]{1,0:T(8,128)S(1)}, f32[256,128]{1,0:T(8,128)S(1)}) custom-call(s32[256,128]{1,0:T(8,128)S(1)} %bitcast.5, f32[256,128]{1,0:T(8,128)S(1)} %bitcast.7, f32[128,128]{1,0:T(8,128)S(1)} %bitcast.4, s32[1,256]{1,0:T(1,128)S(1)} %copy-done.7), custom_call_target="tpu_custom_call" | custom-call | flops 8049999872 | tf_op jit(solution)/shard_map/pallas_call | solution.py:657
  28.8 0.1 shard_map.125
  29.0 0.4 collective-permute-start.3
  29.4 0.7 %collective-permute-start.4 = (f32[114,512]{1,0:T(8,128)S(1)}, f32[114,512]{1,0:T(8,128)S(1)}, u32[]{:S(2)}, u32[]{:S(2)}) collective-permute-start(f32[114,512]{1,0:T(8,128)S(1)} %get-tuple-element.44), channel_id=1, source_target_pairs={{1,2},{2,1},{3,7},{7,3},{5,6},{6,5},{4,8},{8,4},{9,10},{10,9},{11,... | collective-permute-start | bytes 700424 | tf_op jit(solution)/shard_map/ppermute | solution.py:669
  30.1 2.4 %shard_map.126 = (f32[4,128,128]{2,1,0:T(8,128)S(1)}, f32[4,128,128]{2,1,0:T(8,128)S(1)}, f32[4,128,128]{2,1,0:T(8,128)S(1)}, f32[4,128,128]{2,1,0:T(8,128)S(1)}...) custom-call(f32[12]{0:T(128)S(1)} %copy-done.4, ...), custom_call_target="tpu_custom_call" | custom-call | flops 2875000064 | tf_op jit(solution)/shard_map/pallas_call | solution.py:674
  32.5 5.1 %shard_map.127 = (f32[2,16,512]{2,1,0:T(8,128)S(1)}, f32[2,16,512]{2,1,0:T(8,128)S(1)}, f32[2,16,512]{2,1,0:T(8,128)S(1)}, f32[2,16,512]{2,1,0:T(8,128)S(1)}, f32[16,512]{1,0:T(8,128)S(1)}) custom-call(f32[12]{0:T(128)S(1)} %copy-done.4, f32[12]{0:T(128)S(1)} %copy-done.5, f32[12]{0:T(128)S(1)} %copy-done.6, f32[16,512]{1,0:T(8,128)S(1)} %copy-done.1, ...), custom_call_target="tpu_custom_call" | custom-call | flops 5750000128 | tf_op jit(solution)/shard_map/pallas_call | solution.py:681
  37.6 5.7 %collective-permute-start.7 = (f32[16,512]{1,0:T(8,128)S(1)}, f32[16,512]{1,0:T(8,128)S(1)}, u32[]{:S(2)}, u32[]{:S(2)}) collective-permute-start(f32[16,512]{1,0:T(8,128)S(1)} %get-tuple-element.54.refs_0_), channel_id=1, source_target_pairs={{0,3},{1,2},{2,1},{3,0},{4,7},{5,6},{6,5},{7,4},{8,11},{9,10},{10,... | collective-permute-start | bytes 98312 | tf_op jit(solution)/shard_map/ppermute | solution.py:619
  43.3 0.6 collective-permute-start.6
  43.8 0.5 collective-permute-start.8
  44.3 1.5 %collective-permute-start.9 = (f32[2,16,512]{2,1,0:T(8,128)S(1)}, f32[2,16,512]{2,1,0:T(8,128)S(1)}, u32[]{:S(2)}, u32[]{:S(2)}) collective-permute-start(f32[2,16,512]{2,1,0:T(8,128)S(1)} %get-tuple-element.57), channel_id=1, source_target_pairs={{0,2},{1,3},{2,0},{3,1},{4,6},{5,7},{6,4},{7,5},{8,10},{9,11},{10,... | collective-permute-start | bytes 196616 | tf_op jit(solution)/shard_map/ppermute | solution.py:619
  45.8 1.1 %collective-permute-start.10 = (f32[2,16,512]{2,1,0:T(8,128)S(1)}, f32[2,16,512]{2,1,0:T(8,128)S(1)}, u32[]{:S(2)}, u32[]{:S(2)}) collective-permute-start(f32[2,16,512]{2,1,0:T(8,128)S(1)} %get-tuple-element.58), channel_id=1, source_target_pairs={{0,3},{1,2},{2,1},{3,0},{4,7},{5,6},{6,5},{7,4},{8,11},{9,10},{10,... | collective-permute-start | bytes 196616 | tf_op jit(solution)/shard_map/ppermute | solution.py:619
  47.0 0.5 collective-permute-done.6.refs_2_
  47.5 2.9 %shard_map.128 = f32[32,128]{1,0:T(8,128)} custom-call(s32[256,128]{1,0:T(8,128)S(1)} %bitcast.6, f32[256,128]{1,0:T(8,128)S(1)} %bitcast.8, f32[256,128]{1,0:T(8,128)S(1)} %get-tuple-element.35.slot_section_ref, s32[1,256]{1,0:T(1,128)S(1)} %copy-done.7, f32[16,512]{1,0:T(8,128)S(1)} %get-tuple-element.54.refs_0_, ...), custom_call_target="tpu_custom_call" | custom-call | flops 3449999872 | tf_op jit(solution)/shard_map/pallas_call | solution.py:696
  50.4 5.9 %all-to-all-start.1 = ((f32[8,4,128]{2,1,0:T(4,128)}), f32[8,4,128]{2,1,0:T(4,128)S(1)}, u32[]{:S(2)}, u32[]{:S(2)}) async-start(f32[8,4,128]{2,1,0:T(4,128)} %bitcast.3), calls=%async_computation.1 | async-start | bytes 32768 | tf_op jit(solution)/shard_map/all_to_all | solution.py:704
  56.3 0.7 %shard_map.129 = f32[2,64,512]{2,1,0:T(8,128)} custom-call(f32[2,16,512]{2,1,0:T(8,128)S(1)} %get-tuple-element.59.refs_0_, f32[2,16,512]{2,1,0:T(8,128)S(1)} %collective-permute-done.8.refs_1_, f32[2,16,512]{2,1,0:T(8,128)S(1)} %collective-permute-done.9.refs_2_, f32[2,16,512]{2,1,0:T(8,128)S(1)} %collective-permute-done.10.refs_3_), custom_call_target="tpu_custom_call" | custom-call | flops 805000000 | tf_op jit(solution)/shard_map/pallas_call | solution.py:705
  57.0 5.8 %all-to-all-done.1.terms_ref = f32[8,4,128]{2,1,0:T(4,128)S(1)} async-done(((f32[8,4,128]{2,1,0:T(4,128)}), f32[8,4,128]{2,1,0:T(4,128)S(1)}, u32[]{:S(2)}, u32[]{:S(2)}) %all-to-all-start.1) | async-done | bytes 16416 | tf_op jit(solution)/shard_map/all_to_all | solution.py:704
  62.9 0.7 %shard_map.130 = f32[16,32]{1,0:T(8,128)} custom-call(f32[8,4,128]{2,1,0:T(4,128)S(1)} %all-to-all-done.1.terms_ref), custom_call_target="tpu_custom_call" | custom-call | flops 115000000 | tf_op jit(solution)/shard_map/pallas_call | solution.py:710
  (27 shorter events, 0.1 us)
Async XLA Ops:
  2.0 19.0 %all-to-all-start = ((f32[8,16,128]{2,1,0:T(8,128)}), f32[8,16,128]{2,1,0:T(8,128)S(1)}, u32[]{:S(2)}, u32[]{:S(2)}) async-start(f32[8,16,128]{2,1,0:T(8,128)} %get-tuple-element.33.after_hbm), calls=%async_computation | async-start | bytes 131072 | tf_op jit(solution)/shard_map/all_to_all | solution.py:637
  9.3 11.8 %copy-start.2 = (s32[1,256,128]{2,1,0:T(8,128)S(1)}, s32[1,256,128]{2,1,0:T(8,128)}, u32[]{:S(2)}) copy-start(s32[1,256,128]{2,1,0:T(8,128)} %param.20) | copy-start | bytes 393220
  9.3 11.8 %copy-start.3 = (f32[1,256,128]{2,1,0:T(8,128)S(1)}, f32[1,256,128]{2,1,0:T(8,128)}, u32[]{:S(2)}) copy-start(f32[1,256,128]{2,1,0:T(8,128)} %param.21) | copy-start | bytes 393220
  19.1 9.7 %collective-permute-start = (f32[2,2,16,512]{3,2,1,0:T(8,128)}, f32[2,2,16,512]{3,2,1,0:T(8,128)S(1)}, u32[]{:S(2)}, u32[]{:S(2)}) collective-permute-start(f32[2,2,16,512]{3,2,1,0:T(8,128)} %get-tuple-element.40), channel_id=1, source_target_pairs={{0,1},{1,0},{2,3},{3,2},{4,5},{5,4},{6,7},{7,6},{8,9},{9,8},{10,11... | collective-permute-start | bytes 393224 | tf_op jit(solution)/shard_map/ppermute | solution.py:619
  19.2 9.7 %collective-permute-start.1 = (f32[2,2,16,512]{3,2,1,0:T(8,128)}, f32[2,2,16,512]{3,2,1,0:T(8,128)S(1)}, u32[]{:S(2)}, u32[]{:S(2)}) collective-permute-start(f32[2,2,16,512]{3,2,1,0:T(8,128)} %get-tuple-element.41), channel_id=1, source_target_pairs={{0,2},{1,3},{2,0},{3,1},{4,6},{5,7},{6,4},{7,5},{8,10},{9,11},{10,... | collective-permute-start | bytes 393224 | tf_op jit(solution)/shard_map/ppermute | solution.py:619
  20.7 8.1 %collective-permute-start.2 = (f32[2,2,16,512]{3,2,1,0:T(8,128)}, f32[2,2,16,512]{3,2,1,0:T(8,128)S(1)}, u32[]{:S(2)}, u32[]{:S(2)}) collective-permute-start(f32[2,2,16,512]{3,2,1,0:T(8,128)} %get-tuple-element.42), channel_id=1, source_target_pairs={{0,3},{1,2},{2,1},{3,0},{4,7},{5,6},{6,5},{7,4},{8,11},{9,10},{10,... | collective-permute-start | bytes 393224 | tf_op jit(solution)/shard_map/ppermute | solution.py:619
  21.0 0.7 %copy-start.7 = (s32[1,256]{1,0:T(1,128)S(1)}, s32[1,256]{1,0:T(1,128)}, u32[]{:S(2)}) copy-start(s32[1,256]{1,0:T(1,128)} %get-tuple-element.34.reach_ref) | copy-start | bytes 3076
  21.7 7.1 %copy-start = (f32[2,2,16,512]{3,2,1,0:T(8,128)S(1)}, f32[2,2,16,512]{3,2,1,0:T(8,128)}, u32[]{:S(2)}) copy-start(f32[2,2,16,512]{3,2,1,0:T(8,128)} %get-tuple-element.39.refs_0_) | copy-start | bytes 393220
  21.7 7.1 %copy-start.1 = (f32[16,512]{1,0:T(8,128)S(1)}, f32[16,512]{1,0:T(8,128)}, u32[]{:S(2)}) copy-start(f32[16,512]{1,0:T(8,128)} %get-tuple-element.36.land_ref) | copy-start | bytes 98308
  29.0 1.1 %copy-start.4 = (f32[12]{0:T(128)S(1)}, f32[12]{0:T(128)}, u32[]{:S(2)}) copy-start(f32[12]{0:T(128)} %kst_ref.1) | copy-start | bytes 148
  29.0 1.1 %copy-start.5 = (f32[12]{0:T(128)S(1)}, f32[12]{0:T(128)}, u32[]{:S(2)}) copy-start(f32[12]{0:T(128)} %alphat_ref.1) | copy-start | bytes 148
  29.0 1.1 %copy-start.6 = (f32[12]{0:T(128)S(1)}, f32[12]{0:T(128)}, u32[]{:S(2)}) copy-start(f32[12]{0:T(128)} %storet_ref.1) | copy-start | bytes 148
  29.0 3.5 %collective-permute-start.3 = (f32[114,512]{1,0:T(8,128)S(1)}, f32[114,512]{1,0:T(8,128)S(1)}, u32[]{:S(2)}, u32[]{:S(2)}) collective-permute-start(f32[114,512]{1,0:T(8,128)S(1)} %get-tuple-element.43), channel_id=1, source_target_pairs={{0,1},{1,0},{2,3},{3,2},{4,5},{5,4},{6,7},{7,6},{8,9},{9,8},{10,11... | collective-permute-start | bytes 700424 | tf_op jit(solution)/shard_map/ppermute | solution.py:668
  29.4 3.1 %collective-permute-start.4 = (f32[114,512]{1,0:T(8,128)S(1)}, f32[114,512]{1,0:T(8,128)S(1)}, u32[]{:S(2)}, u32[]{:S(2)}) collective-permute-start(f32[114,512]{1,0:T(8,128)S(1)} %get-tuple-element.44), channel_id=1, source_target_pairs={{1,2},{2,1},{3,7},{7,3},{5,6},{6,5},{4,8},{8,4},{9,10},{10,9},{11,... | collective-permute-start | bytes 700424 | tf_op jit(solution)/shard_map/ppermute | solution.py:669
  37.6 8.3 %collective-permute-start.7 = (f32[16,512]{1,0:T(8,128)S(1)}, f32[16,512]{1,0:T(8,128)S(1)}, u32[]{:S(2)}, u32[]{:S(2)}) collective-permute-start(f32[16,512]{1,0:T(8,128)S(1)} %get-tuple-element.54.refs_0_), channel_id=1, source_target_pairs={{0,3},{1,2},{2,1},{3,0},{4,7},{5,6},{6,5},{7,4},{8,11},{9,10},{10,... | collective-permute-start | bytes 98312 | tf_op jit(solution)/shard_map/ppermute | solution.py:619
  43.3 4.2 %collective-permute-start.6 = (f32[16,512]{1,0:T(8,128)S(1)}, f32[16,512]{1,0:T(8,128)S(1)}, u32[]{:S(2)}, u32[]{:S(2)}) collective-permute-start(f32[16,512]{1,0:T(8,128)S(1)} %get-tuple-element.54.refs_0_), channel_id=1, source_target_pairs={{0,2},{1,3},{2,0},{3,1},{4,6},{5,7},{6,4},{7,5},{8,10},{9,11},{10,... | collective-permute-start | bytes 98312 | tf_op jit(solution)/shard_map/ppermute | solution.py:619
  43.8 3.7 %collective-permute-start.5 = (f32[16,512]{1,0:T(8,128)S(1)}, f32[16,512]{1,0:T(8,128)S(1)}, u32[]{:S(2)}, u32[]{:S(2)}) collective-permute-start(f32[16,512]{1,0:T(8,128)S(1)} %get-tuple-element.54.refs_0_), channel_id=1, source_target_pairs={{0,1},{1,0},{2,3},{3,2},{4,5},{5,4},{6,7},{7,6},{8,9},{9,8},{10,11... | collective-permute-start | bytes 98312 | tf_op jit(solution)/shard_map/ppermute | solution.py:619
  43.8 6.6 %collective-permute-start.8 = (f32[2,16,512]{2,1,0:T(8,128)S(1)}, f32[2,16,512]{2,1,0:T(8,128)S(1)}, u32[]{:S(2)}, u32[]{:S(2)}) collective-permute-start(f32[2,16,512]{2,1,0:T(8,128)S(1)} %get-tuple-element.56), channel_id=1, source_target_pairs={{0,1},{1,0},{2,3},{3,2},{4,5},{5,4},{6,7},{7,6},{8,9},{9,8},{10,11... | collective-permute-start | bytes 196616 | tf_op jit(solution)/shard_map/ppermute | solution.py:619
  44.3 6.1 %collective-permute-start.9 = (f32[2,16,512]{2,1,0:T(8,128)S(1)}, f32[2,16,512]{2,1,0:T(8,128)S(1)}, u32[]{:S(2)}, u32[]{:S(2)}) collective-permute-start(f32[2,16,512]{2,1,0:T(8,128)S(1)} %get-tuple-element.57), channel_id=1, source_target_pairs={{0,2},{1,3},{2,0},{3,1},{4,6},{5,7},{6,4},{7,5},{8,10},{9,11},{10,... | collective-permute-start | bytes 196616 | tf_op jit(solution)/shard_map/ppermute | solution.py:619
  45.8 4.6 %collective-permute-start.10 = (f32[2,16,512]{2,1,0:T(8,128)S(1)}, f32[2,16,512]{2,1,0:T(8,128)S(1)}, u32[]{:S(2)}, u32[]{:S(2)}) collective-permute-start(f32[2,16,512]{2,1,0:T(8,128)S(1)} %get-tuple-element.58), channel_id=1, source_target_pairs={{0,3},{1,2},{2,1},{3,0},{4,7},{5,6},{6,5},{7,4},{8,11},{9,10},{10,... | collective-permute-start | bytes 196616 | tf_op jit(solution)/shard_map/ppermute | solution.py:619
  50.4 12.5 %all-to-all-start.1 = ((f32[8,4,128]{2,1,0:T(4,128)}), f32[8,4,128]{2,1,0:T(4,128)S(1)}, u32[]{:S(2)}, u32[]{:S(2)}) async-start(f32[8,4,128]{2,1,0:T(4,128)} %bitcast.3), calls=%async_computation.1 | async-start | bytes 32768 | tf_op jit(solution)/shard_map/all_to_all | solution.py:704

commit v9 on v8

--- a/solution.py
+++ b/solution.py
@@ -75,14 +75,18 @@
 
 
 def river_kernel(
-    breadth, span, cells_ref, bed_ref, section_ref, reach_ref,
-    diag_ref, rhs_ref, slot_section_ref, block_sc, spot_sc, dhigh_sc, dlow_sc, rhigh_sc, rlow_sc, sum_sc,
+    breadth, span, stride, cells_ref, bed_ref, section_ref,
+    diag_ref, rhs_ref, slot_section_ref, reach_ref, block_sc, spot_sc, dhigh_sc, dlow_sc, rhigh_sc, rlow_sc, sum_sc,
 ):
     _, _, number = position()
     rows = section_ref.shape[0]
     slots = reach_ref.shape[1]
-    index = lax.broadcasted_iota(jnp.int32, (rows, slots), 0)
-    pick = jnp.where(index == reach_ref[...], 1.0, 0.0).astype(jnp.bfloat16)
+    first = (lax.axis_index("tile") + 1) * stride - 8
+    own_rows = section_ref[pl.ds(pl.multiple_of(first, 8), 8), :]
+    reach = jnp.concatenate([own_rows[k:k + 1, :] for k in range(slots // LANES)], axis=1)
+    reach_ref[...] = reach
+    index = lax.broadcasted_iota(jnp.int32, (rows, slots), 0).astype(jnp.float32)
+    pick = jnp.where(index == reach, 1.0, 0.0).astype(jnp.bfloat16)
     picked = jnp.zeros(slot_section_ref.shape, jnp.float32)
     for piece in bf16_pieces(section_ref[...], 3):
         picked = picked + lax.dot_general(
@@ -100,7 +104,7 @@
         low_sc[...] = low.astype(jnp.float32)
     share = LANES // BLOCK
     blocks = share * diag_ref.shape[0]
-    group = 32
+    group = 64
     block_names, spot_names = names_of(blocks), names_of(BLOCK)
 
     def matmul(first, places):
@@ -158,23 +162,28 @@
             put_edges(entry, top, bottom, slice(part * LANES, (part + 1) * LANES))
 
 
-def spread_kernel(section_hbm, owner_hbm, local_hbm, spread_ref, reach_ref, section_ref, owner_ref, local_ref, sems):
+def spread_kernel(section_hbm, owner_hbm, local_hbm, spread_ref, section_ref, owner_ref, local_ref, sems):
     pairs = ((section_hbm, section_ref), (owner_hbm, owner_ref), (local_hbm, local_ref))
     copies = [pltpu.make_async_copy(here, there, sems.at[k]) for k, (here, there) in enumerate(pairs)]
     for copy in copies:
         copy.start()
     for copy in copies:
         copy.wait()
-    for tile in range(spread_ref.shape[0]):
-        spread_ref[tile] = section_ref[...]
-    reach_ref[...] = owner_ref[...] * section_ref.shape[0] + local_ref[...]
+    tiles, stride, _ = spread_ref.shape
+    reach_rows = section_ref.shape[0]
+    reach = (owner_ref[...] * stride + local_ref[...]).astype(jnp.float32)
+    parts = [reach[:, start:start + LANES] for start in range(0, reach.shape[1], LANES)]
+    parts.append(jnp.zeros((stride - reach_rows - len(parts), LANES), jnp.float32))
+    payload = jnp.concatenate([section_ref[...], *parts], axis=0)
+    for tile in range(tiles):
+        spread_ref[tile] = payload
 
 
 def prepare_kernel(head_hbm, soil_hbm, land_hbm, after_hbm, *refs):
     del after_hbm
     groups = lax.axis_size("layer")
     block_hbms, land_out_ref = refs[:groups], refs[groups]
-    soil_ref, soil_float_ref, land_ref, in_sems, head_sems, soil_sems = refs[groups + 1:]
+    head_ref, soil_ref, soil_float_ref, land_ref, head_sems, soil_sems, land_sem, out_sems = refs[groups + 1:]
     held, across, _ = soil_ref.shape
     span = across // groups
     own, flip, _ = position()
@@ -182,26 +191,32 @@
     def rows_of(target):
         return pl.ds(pl.multiple_of(span_at(flip, groups, target) * span, span), span)
 
-    copies = [pltpu.make_async_copy(soil_hbm.at[layer], soil_ref.at[layer], in_sems.at[layer]) for layer in range(held)]
-    copies.append(pltpu.make_async_copy(land_hbm.at[rows_of(own), :], land_ref, in_sems.at[held]))
-    heads = [
-        pltpu.make_async_copy(head_hbm.at[:, rows_of(own ^ step), :], block_hbm.at[0], head_sems.at[step])
-        for step, block_hbm in enumerate(block_hbms)
-    ]
-    for copy in copies + heads:
+    soils = [pltpu.make_async_copy(soil_hbm.at[k], soil_ref.at[k], soil_sems.at[k]) for k in range(held)]
+    heads = [pltpu.make_async_copy(head_hbm.at[k], head_ref.at[k], head_sems.at[k]) for k in range(held)]
+    land = pltpu.make_async_copy(land_hbm.at[rows_of(own), :], land_ref, land_sem)
+    for copy in (*heads, *soils, land):
         copy.start()
-    for layer in range(held):
-        copies[layer].wait()
+    outs = []
+
+    def send(kind, field_ref):
+        for step, block_hbm in enumerate(block_hbms):
+            outs.append(
+                pltpu.make_async_copy(
+                    field_ref.at[:, rows_of(own ^ step), :], block_hbm.at[kind], out_sems.at[kind * groups + step]
+                )
+            )
+            outs[-1].start()
+
+    for copy in heads:
+        copy.wait()
+    send(0, head_ref)
+    for layer, copy in enumerate(soils):
+        copy.wait()
         soil_float_ref[layer] = soil_ref[layer].astype(jnp.float32)
-    soils = [
-        pltpu.make_async_copy(soil_float_ref.at[:, rows_of(own ^ step), :], block_hbm.at[1], soil_sems.at[step])
-        for step, block_hbm in enumerate(block_hbms)
-    ]
-    for copy in soils:
-        copy.start()
-    copies[held].wait()
+    send(1, soil_float_ref)
+    land.wait()
     land_out_ref[...] = land_ref[...].astype(jnp.float32)
-    for copy in heads + soils:
+    for copy in outs:
         copy.wait()
 
 
@@ -459,7 +474,7 @@
                 head_ref[held_layer, :, lanes] = later_ref[part, pl.ds(HALO * layers + layer, span, stride=layers), :]
 
 
-def inflow_kernel(reach_rows, cells_ref, bed_ref, slot_section_ref, reach_ref, *refs):
+def inflow_kernel(reach_rows, stride, cells_ref, bed_ref, slot_section_ref, reach_ref, *refs):
     groups = lax.axis_size("layer")
     own_layer, flip, _ = position()
     top_refs = refs[:groups]
@@ -490,7 +505,7 @@
     block, lane = split_cells(cells, 0, breadth, LANES)
     block_sc[...] = block
     lane_sc[...] = lane
-    table = jnp.concatenate(bf16_pieces(turned_sc[...].T, 2), axis=1)
+    table = jnp.concatenate(bf16_pieces(turned_sc[...].T, 2), axis=0)
     group = 32
     names = names_of(blocks)
     index = lax.broadcasted_iota(jnp.int32, (8, LANES), 0).astype(jnp.float32)
@@ -506,9 +521,9 @@
                 axis=1,
             )
             found = lax.dot_general(
-                table, jnp.concatenate([hots, hots], axis=0), (((1,), (0,)), ((), ())),
-                preferred_element_type=jnp.float32,
+                table, hots, (((1,), (0,)), ((), ())), preferred_element_type=jnp.float32
             )
+            found = found[:LANES] + found[LANES:]
             for place in (pair, pair + 1):
                 rows = lane_sc[pl.ds(first + place // 8 * 8, 8), :]
                 lanes = jnp.broadcast_to(rows[place % 8:place % 8 + 1, :], (8, LANES))
@@ -529,10 +544,11 @@
     pieces = bf16_pieces(jnp.where(in_quarter, spread, 0.0), 3)
     fold = reach_rows // groups
     index = lax.broadcasted_iota(jnp.int32, (out_ref.shape[0], slots), 0)
-    index = index // fold * reach_rows + lax.rem(index, fold)
+    index = index // fold * stride + lax.rem(index, fold)
     result = None
     for number in range(groups):
-        put = jnp.where(index + number * fold == reach_ref[...], 1.0, 0.0).astype(jnp.bfloat16)
+        name = (index + number * fold).astype(jnp.float32)
+        put = jnp.where(name == reach_ref[...], 1.0, 0.0).astype(jnp.bfloat16)
         total = jnp.zeros(out_ref.shape, jnp.float32)
         for piece in pieces:
             total = total + lax.dot_general(
@@ -619,13 +635,9 @@
             received.append(lax.ppermute(parts[step], "layer", [(i, i ^ step) for i in range(groups)]))
         return received
 
-    spread, reach = call(
-        spread_kernel,
-        (
-            jax.ShapeDtypeStruct((tiles, reach_rows, node_count), jnp.float32),
-            jax.ShapeDtypeStruct(cross_owner.shape, jnp.int32),
-        ),
-        [in_hbm] * 3,
+    stride = reach_rows + 8
+    spread = call(
+        spread_kernel, jax.ShapeDtypeStruct((tiles, stride, node_count), jnp.float32), [in_hbm] * 3,
         [
             pltpu.VMEM(section.shape, jnp.float32),
             pltpu.VMEM(cross_owner.shape, jnp.int32),
@@ -634,19 +646,21 @@
         ],
         1, VMEM_MOST,
     )(section, cross_owner, cross_local)
-    whole_section = lax.all_to_all(spread, "tile", 0, 0).reshape(tiles * reach_rows, node_count)
+    whole_section = lax.all_to_all(spread, "tile", 0, 0).reshape(tiles * stride, node_count)
     *own_blocks, land = call(
         prepare_kernel,
         (jax.ShapeDtypeStruct((2, held, span, breadth), jnp.float32),) * groups
         + (jax.ShapeDtypeStruct((span, breadth), jnp.float32),),
         [in_hbm] * 4,
         [
+            pltpu.VMEM(head_start.shape, jnp.float32),
             pltpu.VMEM(soil_class.shape, jnp.int32),
             pltpu.VMEM(soil_class.shape, jnp.float32),
             pltpu.VMEM((span, breadth), jnp.int32),
-            pltpu.SemaphoreType.DMA((held + 1,)),
-            pltpu.SemaphoreType.DMA((groups,)),
-            pltpu.SemaphoreType.DMA((groups,)),
+            pltpu.SemaphoreType.DMA((held,)),
+            pltpu.SemaphoreType.DMA((held,)),
+            pltpu.SemaphoreType.DMA(()),
+            pltpu.SemaphoreType.DMA((2 * groups,)),
         ],
         2, VMEM_MOST, (in_hbm,) * groups + (in_vmem,),
     )(head_start, soil_class, land_mask, spread)
@@ -654,13 +668,18 @@
 
     node_scratch = pltpu.VMEM((slots, LANES), jnp.float32)
     riv_shape = jax.ShapeDtypeStruct((blocks, LANES), jnp.float32)
-    diag, rhs, slot_section = call(
-        functools.partial(river_kernel, breadth, span),
-        (riv_shape, riv_shape, jax.ShapeDtypeStruct((slots, node_count), jnp.float32)),
-        [in_vmem] * 4,
+    diag, rhs, slot_section, reach = call(
+        functools.partial(river_kernel, breadth, span, stride),
+        (
+            riv_shape,
+            riv_shape,
+            jax.ShapeDtypeStruct((slots, node_count), jnp.float32),
+            jax.ShapeDtypeStruct((1, slots), jnp.float32),
+        ),
+        [in_vmem] * 3,
         [node_scratch] * 6 + [pltpu.VMEM((span * breadth // BLOCK, LANES), jnp.float32)],
         7,
-    )(cells, bed, whole_section, reach)
+    )(cells, bed, whole_section)
     edges = jax.ShapeDtypeStruct(((2 * layers + 3) * HALO, breadth), jnp.float32)
     near_edge, far_edge = call(
         edge_kernel, (edges, edges), [in_vmem] * (3 + groups), [], 0.1,
@@ -694,7 +713,7 @@
     fold = reach_rows // groups
     packed = pltpu.VMEM((slots // groups, LANES), jnp.float32)
     partial = call(
-        functools.partial(inflow_kernel, reach_rows),
+        functools.partial(inflow_kernel, reach_rows, stride),
         jax.ShapeDtypeStruct((tiles * fold, node_count), jnp.float32),
         [in_vmem] * (4 + groups),
         [packed] * 3 + [pltpu.VMEM((across * per_row, LANES), jnp.float32)],

time: 63.9 us -> 55.6 us (0.87)
  Pallas kernels: 30.1 us -> 22.4 us
  starting transfers between devices: 25.6 us -> 23.2 us
  waiting for transfers between devices: 6.38 us -> 8.73 us
  local copies, waits for them, and re-layouts: 0.71 us -> 0.04 us
    pallas_call x1, Pallas kernels: 9.78 us -> 2.57 us  [on_device(): call(prepare_kernel, (jax.ShapeDtypeStruct((2, held, span, breadth), jnp....]
    all_to_all x1, waiting for transfers between devices: 0.01 us -> 2.59 us  [on_device(): lax.all_to_all(spread, 'tile', 0, 0).reshape(tiles * stride, node_count)]
    all_to_all x1, starting transfers between devices: 5.88 us -> 3.88 us  [on_device(): lax.all_to_all(partial.reshape(tiles, fold, node_count), 'tile', 0, 0)]
    unnamed x16 -> x14, local copies, waits for them, and re-layouts: 0.71 us -> 0.04 us
  transfers between devices with their start and end apart: 13 -> 13, of which waited for: 2 -> 3; matrix products, arithmetic and copies ran while one was open for 0% -> 0% of each run, Pallas kernels for 36% -> 27%
where the time goes in v9:
time: 55.6 us; the launch traced here: 55.2 us
  starting transfers between devices  23.2 us (42%)
  Pallas kernels  22.4 us (40%)
  waiting for transfers between devices  8.73 us (16%)
  between operations  0.83 us (1%)
    ppermute x9, starting transfers between devices, exchange(): lax.ppermute(parts[step], 'layer', [(i, i ^ step) for i in range(groups)])  11.3 us
    all_to_all x1, starting transfers between devices, on_device(): lax.all_to_all(spread, 'tile', 0, 0).reshape(tiles * stride, node_count)  7.26 us
    pallas_call x1, Pallas kernels, on_device(): call(functools.partial(river_kernel, breadth, span, stride), (riv_shape,...  6.57 us
    all_to_all x1, waiting for transfers between devices, on_device(): lax.all_to_all(partial.reshape(tiles, fold, node_count), 'tile', 0, 0)  5.84 us
    pallas_call x1, Pallas kernels, on_device(): call(flow_kernel, (head_shape,) * groups + (jax.ShapeDtypeStruct((span, b...  5.05 us
    all_to_all x1, starting transfers between devices, on_device(): lax.all_to_all(partial.reshape(tiles, fold, node_count), 'tile', 0, 0)  3.88 us
    pallas_call x1, Pallas kernels, on_device(): call(functools.partial(inflow_kernel, reach_rows, stride), jax.ShapeDtype...  2.91 us
    all_to_all x1, waiting for transfers between devices, on_device(): lax.all_to_all(spread, 'tile', 0, 0).reshape(tiles * stride, node_count)  2.59 us
  transfers between devices with their start and end apart: 13, of which 3 were waited for; matrix products, arithmetic and copies ran while one was open for 0% of the time, Pallas kernels for 27%

profile of v9, /device:TPU:0, one launch (start us, length us, event | category | flops | bytes accessed | tf_op | source)
XLA Modules:
  0.0 55.2 jit_solution(11342768458949384466)
XLA Ops:
  0.6 1.4 %shard_map.122.after_hbm = f32[8,24,128]{2,1,0:T(8,128)} custom-call(f32[16,128]{1,0:T(8,128)} %section_hbm.1, s32[1,256]{1,0:T(1,128)} %owner_hbm.1, s32[1,256]{1,0:T(1,128)} %local_hbm.1), custom_call_target="tpu_custom_call" | custom-call | flops 1150000000 | tf_op jit(solution)/shard_map/pallas_call | solution.py:639
  2.0 7.3 %all-to-all-start = ((f32[8,24,128]{2,1,0:T(8,128)}), f32[8,24,128]{2,1,0:T(8,128)S(1)}, u32[]{:S(2)}, u32[]{:S(2)}) async-start(f32[8,24,128]{2,1,0:T(8,128)} %shard_map.122.after_hbm), calls=%async_computation | async-start | bytes 196608 | tf_op jit(solution)/shard_map/all_to_all | solution.py:649
  9.3 2.6 %shard_map.124 = (f32[2,2,16,512]{3,2,1,0:T(8,128)}, f32[2,2,16,512]{3,2,1,0:T(8,128)}, f32[2,2,16,512]{3,2,1,0:T(8,128)}, f32[2,2,16,512]{3,2,1,0:T(8,128)}, f32[16,512]{1,0:T(8,128)}) custom-call(f32[2,64,512]{2,1,0:T(8,128)} %head_hbm.1, s32[2,64,512]{2,1,0:T(8,128)} %soil_hbm.1, s32[64,512]{1,0:T(8,128)} %land_hbm.1, f32[8,24,128]{2,1,0:T(8,128)} %shard_map.122.after_hbm), custom_call_target="tpu_custom_call" | custom-call | flops 2300000000 | tf_op jit(solution)/shard_map/pallas_call | solution.py:650
  11.9 0.1 collective-permute-start
  12.0 1.6 %collective-permute-start.1 = (f32[2,2,16,512]{3,2,1,0:T(8,128)}, f32[2,2,16,512]{3,2,1,0:T(8,128)S(1)}, u32[]{:S(2)}, u32[]{:S(2)}) collective-permute-start(f32[2,2,16,512]{3,2,1,0:T(8,128)} %get-tuple-element.39), channel_id=1, source_target_pairs={{0,2},{1,3},{2,0},{3,1},{4,6},{5,7},{6,4},{7,5},{8,10},{9,11},{10,... | collective-permute-start | bytes 393224 | tf_op jit(solution)/shard_map/ppermute | solution.py:635
  13.5 0.3 collective-permute-start.2
  13.8 2.6 %all-to-all-done = f32[8,24,128]{2,1,0:T(8,128)S(1)} async-done(((f32[8,24,128]{2,1,0:T(8,128)}), f32[8,24,128]{2,1,0:T(8,128)S(1)}, u32[]{:S(2)}, u32[]{:S(2)}) %all-to-all-start) | async-done | bytes 98336 | tf_op jit(solution)/shard_map/all_to_all | solution.py:649
  16.4 6.6 %shard_map.123 = (f32[64,128]{1,0:T(8,128)S(1)}, f32[64,128]{1,0:T(8,128)S(1)}, f32[256,128]{1,0:T(8,128)S(1)}, f32[1,256]{1,0:T(1,128)S(1)}) custom-call(s32[256,128]{1,0:T(8,128)S(1)} %bitcast.5, f32[256,128]{1,0:T(8,128)S(1)} %bitcast.7, f32[192,128]{1,0:T(8,128)S(1)} %bitcast.4), custom_call_target="tpu_custom_call" | custom-call | flops 8049999872 | tf_op jit(solution)/shard_map/pallas_call | solution.py:671
  23.1 0.1 shard_map.125
  23.2 0.1 collective-permute-start.3
  23.3 0.7 %collective-permute-start.4 = (f32[114,512]{1,0:T(8,128)S(1)}, f32[114,512]{1,0:T(8,128)S(1)}, u32[]{:S(2)}, u32[]{:S(2)}) collective-permute-start(f32[114,512]{1,0:T(8,128)S(1)} %get-tuple-element.42), channel_id=1, source_target_pairs={{1,2},{2,1},{3,7},{7,3},{5,6},{6,5},{4,8},{8,4},{9,10},{10,9},{11,... | collective-permute-start | bytes 700424 | tf_op jit(solution)/shard_map/ppermute | solution.py:688
  24.0 2.4 %shard_map.126 = (f32[4,128,128]{2,1,0:T(8,128)S(1)}, f32[4,128,128]{2,1,0:T(8,128)S(1)}, f32[4,128,128]{2,1,0:T(8,128)S(1)}, f32[4,128,128]{2,1,0:T(8,128)S(1)}...) custom-call(f32[12]{0:T(128)S(1)} %copy-done.4, ...), custom_call_target="tpu_custom_call" | custom-call | flops 2875000064 | tf_op jit(solution)/shard_map/pallas_call | solution.py:693
  26.4 5.1 %shard_map.127 = (f32[2,16,512]{2,1,0:T(8,128)S(1)}, f32[2,16,512]{2,1,0:T(8,128)S(1)}, f32[2,16,512]{2,1,0:T(8,128)S(1)}, f32[2,16,512]{2,1,0:T(8,128)S(1)}, f32[16,512]{1,0:T(8,128)S(1)}) custom-call(f32[12]{0:T(128)S(1)} %copy-done.4, f32[12]{0:T(128)S(1)} %copy-done.5, f32[12]{0:T(128)S(1)} %copy-done.6, f32[16,512]{1,0:T(8,128)S(1)} %copy-done.1, ...), custom_call_target="tpu_custom_call" | custom-call | flops 5750000128 | tf_op jit(solution)/shard_map/pallas_call | solution.py:700
  31.4 5.7 %collective-permute-start.7 = (f32[16,512]{1,0:T(8,128)S(1)}, f32[16,512]{1,0:T(8,128)S(1)}, u32[]{:S(2)}, u32[]{:S(2)}) collective-permute-start(f32[16,512]{1,0:T(8,128)S(1)} %get-tuple-element.52.refs_0_), channel_id=1, source_target_pairs={{0,3},{1,2},{2,1},{3,0},{4,7},{5,6},{6,5},{7,4},{8,11},{9,10},{10,... | collective-permute-start | bytes 98312 | tf_op jit(solution)/shard_map/ppermute | solution.py:635
  37.2 0.9 %collective-permute-start.6 = (f32[16,512]{1,0:T(8,128)S(1)}, f32[16,512]{1,0:T(8,128)S(1)}, u32[]{:S(2)}, u32[]{:S(2)}) collective-permute-start(f32[16,512]{1,0:T(8,128)S(1)} %get-tuple-element.52.refs_0_), channel_id=1, source_target_pairs={{0,2},{1,3},{2,0},{3,1},{4,6},{5,7},{6,4},{7,5},{8,10},{9,11},{10,... | collective-permute-start | bytes 98312 | tf_op jit(solution)/shard_map/ppermute | solution.py:635
  38.0 0.5 collective-permute-start.8
  38.5 1.2 %collective-permute-start.9 = (f32[2,16,512]{2,1,0:T(8,128)S(1)}, f32[2,16,512]{2,1,0:T(8,128)S(1)}, u32[]{:S(2)}, u32[]{:S(2)}) collective-permute-start(f32[2,16,512]{2,1,0:T(8,128)S(1)} %get-tuple-element.55), channel_id=1, source_target_pairs={{0,2},{1,3},{2,0},{3,1},{4,6},{5,7},{6,4},{7,5},{8,10},{9,11},{10,... | collective-permute-start | bytes 196616 | tf_op jit(solution)/shard_map/ppermute | solution.py:635
  39.7 1.1 %collective-permute-start.10 = (f32[2,16,512]{2,1,0:T(8,128)S(1)}, f32[2,16,512]{2,1,0:T(8,128)S(1)}, u32[]{:S(2)}, u32[]{:S(2)}) collective-permute-start(f32[2,16,512]{2,1,0:T(8,128)S(1)} %get-tuple-element.56), channel_id=1, source_target_pairs={{0,3},{1,2},{2,1},{3,0},{4,7},{5,6},{6,5},{7,4},{8,11},{9,10},{10,... | collective-permute-start | bytes 196616 | tf_op jit(solution)/shard_map/ppermute | solution.py:635
  40.9 0.2 collective-permute-done.6.refs_2_
  41.1 2.9 %shard_map.128 = f32[32,128]{1,0:T(8,128)} custom-call(s32[256,128]{1,0:T(8,128)S(1)} %bitcast.6, f32[256,128]{1,0:T(8,128)S(1)} %bitcast.8, f32[256,128]{1,0:T(8,128)S(1)} %get-tuple-element.32.slot_section_ref, f32[1,256]{1,0:T(1,128)S(1)} %get-tuple-element.33.reach_ref, f32[16,512]{1,0:T(8,128)S(1)} %get-tuple-element.52.refs_0_, ...), custom_call_target="tpu_custom_call" | custom-call | flops 3449999872 | tf_op jit(solution)/shard_map/pallas_call | solution.py:715
  44.1 3.9 %all-to-all-start.1 = ((f32[8,4,128]{2,1,0:T(4,128)}), f32[8,4,128]{2,1,0:T(4,128)S(1)}, u32[]{:S(2)}, u32[]{:S(2)}) async-start(f32[8,4,128]{2,1,0:T(4,128)} %bitcast.3), calls=%async_computation.1 | async-start | bytes 32768 | tf_op jit(solution)/shard_map/all_to_all | solution.py:723
  47.9 0.7 %shard_map.129 = f32[2,64,512]{2,1,0:T(8,128)} custom-call(f32[2,16,512]{2,1,0:T(8,128)S(1)} %get-tuple-element.57.refs_0_, f32[2,16,512]{2,1,0:T(8,128)S(1)} %collective-permute-done.8.refs_1_, f32[2,16,512]{2,1,0:T(8,128)S(1)} %collective-permute-done.9.refs_2_, f32[2,16,512]{2,1,0:T(8,128)S(1)} %collective-permute-done.10.refs_3_), custom_call_target="tpu_custom_call" | custom-call | flops 805000000 | tf_op jit(solution)/shard_map/pallas_call | solution.py:724
  48.7 5.8 %all-to-all-done.1.terms_ref = f32[8,4,128]{2,1,0:T(4,128)S(1)} async-done(((f32[8,4,128]{2,1,0:T(4,128)}), f32[8,4,128]{2,1,0:T(4,128)S(1)}, u32[]{:S(2)}, u32[]{:S(2)}) %all-to-all-start.1) | async-done | bytes 16416 | tf_op jit(solution)/shard_map/all_to_all | solution.py:723
  54.5 0.7 %shard_map.130 = f32[16,32]{1,0:T(8,128)} custom-call(f32[8,4,128]{2,1,0:T(4,128)S(1)} %all-to-all-done.1.terms_ref), custom_call_target="tpu_custom_call" | custom-call | flops 115000000 | tf_op jit(solution)/shard_map/pallas_call | solution.py:729
  (25 shorter events, 0.1 us)
Async XLA Ops:
  2.0 14.4 %all-to-all-start = ((f32[8,24,128]{2,1,0:T(8,128)}), f32[8,24,128]{2,1,0:T(8,128)S(1)}, u32[]{:S(2)}, u32[]{:S(2)}) async-start(f32[8,24,128]{2,1,0:T(8,128)} %shard_map.122.after_hbm), calls=%async_computation | async-start | bytes 196608 | tf_op jit(solution)/shard_map/all_to_all | solution.py:649
  9.3 7.1 %copy-start.2 = (s32[1,256,128]{2,1,0:T(8,128)S(1)}, s32[1,256,128]{2,1,0:T(8,128)}, u32[]{:S(2)}) copy-start(s32[1,256,128]{2,1,0:T(8,128)} %param.20) | copy-start | bytes 393220
  9.3 7.1 %copy-start.3 = (f32[1,256,128]{2,1,0:T(8,128)S(1)}, f32[1,256,128]{2,1,0:T(8,128)}, u32[]{:S(2)}) copy-start(f32[1,256,128]{2,1,0:T(8,128)} %param.21) | copy-start | bytes 393220
  11.9 11.1 %collective-permute-start = (f32[2,2,16,512]{3,2,1,0:T(8,128)}, f32[2,2,16,512]{3,2,1,0:T(8,128)S(1)}, u32[]{:S(2)}, u32[]{:S(2)}) collective-permute-start(f32[2,2,16,512]{3,2,1,0:T(8,128)} %get-tuple-element.38), channel_id=1, source_target_pairs={{0,1},{1,0},{2,3},{3,2},{4,5},{5,4},{6,7},{7,6},{8,9},{9,8},{10,11... | collective-permute-start | bytes 393224 | tf_op jit(solution)/shard_map/ppermute | solution.py:635
  12.0 11.1 %collective-permute-start.1 = (f32[2,2,16,512]{3,2,1,0:T(8,128)}, f32[2,2,16,512]{3,2,1,0:T(8,128)S(1)}, u32[]{:S(2)}, u32[]{:S(2)}) collective-permute-start(f32[2,2,16,512]{3,2,1,0:T(8,128)} %get-tuple-element.39), channel_id=1, source_target_pairs={{0,2},{1,3},{2,0},{3,1},{4,6},{5,7},{6,4},{7,5},{8,10},{9,11},{10,... | collective-permute-start | bytes 393224 | tf_op jit(solution)/shard_map/ppermute | solution.py:635
  13.5 9.5 %collective-permute-start.2 = (f32[2,2,16,512]{3,2,1,0:T(8,128)}, f32[2,2,16,512]{3,2,1,0:T(8,128)S(1)}, u32[]{:S(2)}, u32[]{:S(2)}) collective-permute-start(f32[2,2,16,512]{3,2,1,0:T(8,128)} %get-tuple-element.40), channel_id=1, source_target_pairs={{0,3},{1,2},{2,1},{3,0},{4,7},{5,6},{6,5},{7,4},{8,11},{9,10},{10,... | collective-permute-start | bytes 393224 | tf_op jit(solution)/shard_map/ppermute | solution.py:635
  16.4 6.6 %copy-start = (f32[2,2,16,512]{3,2,1,0:T(8,128)S(1)}, f32[2,2,16,512]{3,2,1,0:T(8,128)}, u32[]{:S(2)}) copy-start(f32[2,2,16,512]{3,2,1,0:T(8,128)} %get-tuple-element.37.refs_0_) | copy-start | bytes 393220
  16.4 6.6 %copy-start.1 = (f32[16,512]{1,0:T(8,128)S(1)}, f32[16,512]{1,0:T(8,128)}, u32[]{:S(2)}) copy-start(f32[16,512]{1,0:T(8,128)} %get-tuple-element.34.land_ref) | copy-start | bytes 98308
  23.2 0.8 %copy-start.4 = (f32[12]{0:T(128)S(1)}, f32[12]{0:T(128)}, u32[]{:S(2)}) copy-start(f32[12]{0:T(128)} %kst_ref.1) | copy-start | bytes 148
  23.2 0.8 %copy-start.5 = (f32[12]{0:T(128)S(1)}, f32[12]{0:T(128)}, u32[]{:S(2)}) copy-start(f32[12]{0:T(128)} %alphat_ref.1) | copy-start | bytes 148
  23.2 0.8 %copy-start.6 = (f32[12]{0:T(128)S(1)}, f32[12]{0:T(128)}, u32[]{:S(2)}) copy-start(f32[12]{0:T(128)} %storet_ref.1) | copy-start | bytes 148
  23.2 3.2 %collective-permute-start.3 = (f32[114,512]{1,0:T(8,128)S(1)}, f32[114,512]{1,0:T(8,128)S(1)}, u32[]{:S(2)}, u32[]{:S(2)}) collective-permute-start(f32[114,512]{1,0:T(8,128)S(1)} %get-tuple-element.41), channel_id=1, source_target_pairs={{0,1},{1,0},{2,3},{3,2},{4,5},{5,4},{6,7},{7,6},{8,9},{9,8},{10,11... | collective-permute-start | bytes 700424 | tf_op jit(solution)/shard_map/ppermute | solution.py:687
  23.3 3.1 %collective-permute-start.4 = (f32[114,512]{1,0:T(8,128)S(1)}, f32[114,512]{1,0:T(8,128)S(1)}, u32[]{:S(2)}, u32[]{:S(2)}) collective-permute-start(f32[114,512]{1,0:T(8,128)S(1)} %get-tuple-element.42), channel_id=1, source_target_pairs={{1,2},{2,1},{3,7},{7,3},{5,6},{6,5},{4,8},{8,4},{9,10},{10,9},{11,... | collective-permute-start | bytes 700424 | tf_op jit(solution)/shard_map/ppermute | solution.py:688
  31.4 8.3 %collective-permute-start.7 = (f32[16,512]{1,0:T(8,128)S(1)}, f32[16,512]{1,0:T(8,128)S(1)}, u32[]{:S(2)}, u32[]{:S(2)}) collective-permute-start(f32[16,512]{1,0:T(8,128)S(1)} %get-tuple-element.52.refs_0_), channel_id=1, source_target_pairs={{0,3},{1,2},{2,1},{3,0},{4,7},{5,6},{6,5},{7,4},{8,11},{9,10},{10,... | collective-permute-start | bytes 98312 | tf_op jit(solution)/shard_map/ppermute | solution.py:635
  37.2 3.9 %collective-permute-start.6 = (f32[16,512]{1,0:T(8,128)S(1)}, f32[16,512]{1,0:T(8,128)S(1)}, u32[]{:S(2)}, u32[]{:S(2)}) collective-permute-start(f32[16,512]{1,0:T(8,128)S(1)} %get-tuple-element.52.refs_0_), channel_id=1, source_target_pairs={{0,2},{1,3},{2,0},{3,1},{4,6},{5,7},{6,4},{7,5},{8,10},{9,11},{10,... | collective-permute-start | bytes 98312 | tf_op jit(solution)/shard_map/ppermute | solution.py:635
  38.0 3.1 %collective-permute-start.5 = (f32[16,512]{1,0:T(8,128)S(1)}, f32[16,512]{1,0:T(8,128)S(1)}, u32[]{:S(2)}, u32[]{:S(2)}) collective-permute-start(f32[16,512]{1,0:T(8,128)S(1)} %get-tuple-element.52.refs_0_), channel_id=1, source_target_pairs={{0,1},{1,0},{2,3},{3,2},{4,5},{5,4},{6,7},{7,6},{8,9},{9,8},{10,11... | collective-permute-start | bytes 98312 | tf_op jit(solution)/shard_map/ppermute | solution.py:635
  38.0 6.0 %collective-permute-start.8 = (f32[2,16,512]{2,1,0:T(8,128)S(1)}, f32[2,16,512]{2,1,0:T(8,128)S(1)}, u32[]{:S(2)}, u32[]{:S(2)}) collective-permute-start(f32[2,16,512]{2,1,0:T(8,128)S(1)} %get-tuple-element.54), channel_id=1, source_target_pairs={{0,1},{1,0},{2,3},{3,2},{4,5},{5,4},{6,7},{7,6},{8,9},{9,8},{10,11... | collective-permute-start | bytes 196616 | tf_op jit(solution)/shard_map/ppermute | solution.py:635
  38.5 5.5 %collective-permute-start.9 = (f32[2,16,512]{2,1,0:T(8,128)S(1)}, f32[2,16,512]{2,1,0:T(8,128)S(1)}, u32[]{:S(2)}, u32[]{:S(2)}) collective-permute-start(f32[2,16,512]{2,1,0:T(8,128)S(1)} %get-tuple-element.55), channel_id=1, source_target_pairs={{0,2},{1,3},{2,0},{3,1},{4,6},{5,7},{6,4},{7,5},{8,10},{9,11},{10,... | collective-permute-start | bytes 196616 | tf_op jit(solution)/shard_map/ppermute | solution.py:635
  39.7 4.3 %collective-permute-start.10 = (f32[2,16,512]{2,1,0:T(8,128)S(1)}, f32[2,16,512]{2,1,0:T(8,128)S(1)}, u32[]{:S(2)}, u32[]{:S(2)}) collective-permute-start(f32[2,16,512]{2,1,0:T(8,128)S(1)} %get-tuple-element.56), channel_id=1, source_target_pairs={{0,3},{1,2},{2,1},{3,0},{4,7},{5,6},{6,5},{7,4},{8,11},{9,10},{10,... | collective-permute-start | bytes 196616 | tf_op jit(solution)/shard_map/ppermute | solution.py:635
  44.1 10.5 %all-to-all-start.1 = ((f32[8,4,128]{2,1,0:T(4,128)}), f32[8,4,128]{2,1,0:T(4,128)S(1)}, u32[]{:S(2)}, u32[]{:S(2)}) async-start(f32[8,4,128]{2,1,0:T(4,128)} %bitcast.3), calls=%async_computation.1 | async-start | bytes 32768 | tf_op jit(solution)/shard_map/all_to_all | solution.py:723

commit v10 on v9

--- a/solution.py
+++ b/solution.py
@@ -179,45 +179,23 @@
         spread_ref[tile] = payload
 
 
-def prepare_kernel(head_hbm, soil_hbm, land_hbm, after_hbm, *refs):
-    del after_hbm
+def prepare_kernel(head_ref, soil_ref, land_ref, after_ref, *refs):
+    del after_ref
     groups = lax.axis_size("layer")
-    block_hbms, land_out_ref = refs[:groups], refs[groups]
-    head_ref, soil_ref, soil_float_ref, land_ref, head_sems, soil_sems, land_sem, out_sems = refs[groups + 1:]
-    held, across, _ = soil_ref.shape
+    block_refs, land_out_ref = refs[:groups], refs[groups]
+    held, across, _ = head_ref.shape
     span = across // groups
     own, flip, _ = position()
 
     def rows_of(target):
         return pl.ds(pl.multiple_of(span_at(flip, groups, target) * span, span), span)
 
-    soils = [pltpu.make_async_copy(soil_hbm.at[k], soil_ref.at[k], soil_sems.at[k]) for k in range(held)]
-    heads = [pltpu.make_async_copy(head_hbm.at[k], head_ref.at[k], head_sems.at[k]) for k in range(held)]
-    land = pltpu.make_async_copy(land_hbm.at[rows_of(own), :], land_ref, land_sem)
-    for copy in (*heads, *soils, land):
-        copy.start()
-    outs = []
-
-    def send(kind, field_ref):
-        for step, block_hbm in enumerate(block_hbms):
-            outs.append(
-                pltpu.make_async_copy(
-                    field_ref.at[:, rows_of(own ^ step), :], block_hbm.at[kind], out_sems.at[kind * groups + step]
-                )
-            )
-            outs[-1].start()
-
-    for copy in heads:
-        copy.wait()
-    send(0, head_ref)
-    for layer, copy in enumerate(soils):
-        copy.wait()
-        soil_float_ref[layer] = soil_ref[layer].astype(jnp.float32)
-    send(1, soil_float_ref)
-    land.wait()
-    land_out_ref[...] = land_ref[...].astype(jnp.float32)
-    for copy in outs:
-        copy.wait()
+    land_out_ref[...] = land_ref[rows_of(own), :].astype(jnp.float32)
+    for step, block_ref in enumerate(block_refs):
+        rows = rows_of(own ^ step)
+        for layer in range(held):
+            block_ref[0, layer] = head_ref[layer, rows, :]
+            block_ref[1, layer] = soil_ref[layer, rows, :].astype(jnp.float32)
 
 
 class Rows:
@@ -255,13 +233,33 @@
     def __init__(self, rows, own, full, first, last):
         self.rows, self.own, self.full, self.first, self.last = rows, own, full, first, last
 
+    def holds(self, row):
+        return self.first <= row < self.last
+
     def get(self, row):
-        if self.first <= row < self.last:
-            return self.rows.get(self.own, row - self.first)
+        if self.holds(row):
+            return self.rows.get(self.own, row - HALO)
         return self.rows.get(self.full, row)
 
     def put(self, row, value):
         self.rows.put(self.full, row, value)
+
+
+def relax_row(rows, row, head, weights, wx_before, base, inverse):
+    before, here, after = head
+    wx, wy, wz = [field.get(row) for field in weights]
+    total = base.get(row) + wx_before * before + wx * after
+    total = total + wy * rows.east(here) + rows.west(wy * here)
+    total = total + wz * rows.below(here) + rows.above(wz * here)
+    return total * inverse.get(row), wx
+
+
+def river_row(rows, ref, row, top):
+    parts = [
+        jnp.broadcast_to(ref[pl.ds(row * rows.per_row + part, 1), :], (rows.layers, LANES))
+        for part in range(rows.per_row)
+    ]
+    return jnp.where(top, jnp.concatenate(parts, axis=1), 0.0)
 
 
 class Faces:
@@ -313,15 +311,19 @@
     return jnp.concatenate(parts, axis=1)
 
 
-def stage_kernel(ks_ref, alpha_ref, store_ref, land_ref, *refs):
+def stage_kernel(ks_ref, alpha_ref, store_ref, land_ref, diag_ref, rhs_ref, *refs):
     groups = lax.axis_size("layer")
     own, _, _ = position()
-    block_refs = refs[:groups]
-    first_out, ks_out, alpha_out, store_out, wx_out, wy_out, wz_out, diag_out, base_out, soil_sc, *lands = refs[groups:]
+    block_refs, refs = refs[:groups], refs[groups:]
+    first_out, ks_out, alpha_out, store_out = refs[:4]
+    fields = [refs[4 + 5 * picard:9 + 5 * picard] for picard in range(ITERS)]
+    head_outs = refs[4 + 5 * ITERS:4 + 5 * ITERS + HALO]
+    soil_sc, *lands = refs[4 + 5 * ITERS + HALO:]
     _, held, span, breadth = block_refs[0].shape
     layers = groups * held
     rows = Rows(layers, breadth)
     faces = Faces(rows, land_ref[...], lands)
+    top = lax.broadcasted_iota(jnp.int32, (layers, breadth), 0) == 0
 
     for step, block_ref in enumerate(block_refs):
         for held_layer in range(held):
@@ -329,21 +331,47 @@
             rows.put_layer(first_out, layer, 0, block_ref[0, held_layer])
             rows.put_layer(soil_sc, layer, 0, block_ref[1, held_layer])
     tables = lane_tables((ks_ref, alpha_ref, store_ref), layers)
-    before = None
     for row in range(span):
         soil = rows.get(soil_sc, row).astype(jnp.int32)
-        ks, alpha, store = [look_up(rows, table, soil) for table in tables]
-        first = rows.get(first_out, row)
-        here = faces.conduct(ks, alpha, first)
-        wy, wz, diagonal, gravity = faces.in_row(row, here)
-        for ref, value in (
-            (ks_out, ks), (alpha_out, alpha), (store_out, store), (wy_out, wy), (wz_out, wz),
-            (diag_out, store + diagonal), (base_out, store * first + gravity),
-        ):
-            rows.put(ref, row, value)
-        if row > 0:
-            rows.put(wx_out, row - 1, faces.between_rows(row - 1, before, here))
-        before = here
+        for table, out in zip(tables, (ks_out, alpha_out, store_out)):
+            rows.put(out, row, look_up(rows, table, soil))
+
+    now, begin, stop, done = first_out, 0, span, 0
+    for wx_out, wy_out, wz_out, inv_out, base_out in fields:
+        before = None
+        for row in range(begin, stop):
+            here = faces.conduct(rows.get(ks_out, row), rows.get(alpha_out, row), rows.get(now, row))
+            wy, wz, diagonal, gravity = faces.in_row(row, here)
+            rows.put(wy_out, row, wy)
+            rows.put(wz_out, row, wz)
+            store = rows.get(store_out, row)
+            sums = store + diagonal, store * rows.get(first_out, row) + gravity
+            if row > begin:
+                wx = faces.between_rows(row - 1, before[0], here)
+                rows.put(wx_out, row - 1, wx)
+                diagonal, base = before[1]
+                if row - 1 > begin:
+                    diagonal = reciprocal(diagonal + before[2] + wx + river_row(rows, diag_ref, row - 1, top))
+                    base = base + river_row(rows, rhs_ref, row - 1, top)
+                rows.put(inv_out, row - 1, diagonal)
+                rows.put(base_out, row - 1, base)
+            else:
+                wx = None
+            before = here, sums, wx
+        rows.put(inv_out, stop - 1, before[1][0])
+        rows.put(base_out, stop - 1, before[1][1])
+        weights = [Joined(rows, None, ref, HALO, HALO) for ref in (wx_out, wy_out, wz_out)]
+        base, inverse = [Joined(rows, None, ref, HALO, HALO) for ref in (base_out, inv_out)]
+        for _ in range(SWEEPS):
+            begin, stop = begin + 1, stop - 1
+            head = rows.get(now, begin - 1), rows.get(now, begin)
+            wx_before = rows.get(wx_out, begin - 1)
+            for row in range(begin, stop):
+                head = *head[-2:], rows.get(now, row + 1)
+                value, wx_before = relax_row(rows, row, head, weights, wx_before, base, inverse)
+                rows.put(head_outs[done], row, value)
+            now = head_outs[done]
+            done += 1
 
 
 def flow_kernel(kst_ref, alphat_ref, storet_ref, land_ref, near_ref, far_ref, diag_ref, rhs_ref, *refs):
@@ -351,12 +379,15 @@
     own, _, number = position()
     end = (number == 0) | (number == groups - 1)
     far_partner = jnp.where(end, own, own ^ (groups - 1))
-    first_ref, ks_ref, alpha_ref, store_ref, wx_ref, wy_ref, wz_ref, partial_ref, gravity_ref = refs[:9]
-    head_refs, top_ref = refs[9:9 + groups], refs[9 + groups]
+    first_ref, ks_ref, alpha_ref, store_ref = refs[:4]
+    fields = [refs[4 + 5 * picard:9 + 5 * picard] for picard in range(ITERS)]
+    staged_refs = refs[4 + 5 * ITERS:4 + 5 * ITERS + HALO]
+    refs = refs[4 + 5 * ITERS + HALO:]
+    head_refs, top_ref = refs[:groups], refs[groups]
     (
         first_sc, soil_sc, ks_sc, alpha_sc, store_sc, wx_sc, wy_sc, wz_sc, base_sc, inv_sc, ping_sc, pong_sc,
         land_sc, dtop_sc, rtop_sc, *lands,
-    ) = refs[10 + groups:]
+    ) = refs[1 + groups:]
     held, span, breadth = head_refs[0].shape
     layers = groups * held
     window = span + 2 * HALO
@@ -396,82 +427,64 @@
         for table, ref in zip(tables, (ks_sc, alpha_sc, store_sc)):
             rows.put(ref, row, look_up(rows, table, soil))
 
-    def joined(own, full, last=last_own):
-        return Joined(rows, own, full, HALO, last)
-
     first, ks, alpha, store = [
-        joined(own, full)
-        for own, full in ((first_ref, first_sc), (ks_ref, ks_sc), (alpha_ref, alpha_sc), (store_ref, store_sc))
+        Joined(rows, held_ref, full, HALO, last_own)
+        for held_ref, full in ((first_ref, first_sc), (ks_ref, ks_sc), (alpha_ref, alpha_sc), (store_ref, store_sc))
     ]
     top = lax.broadcasted_iota(jnp.int32, (layers, breadth), 0) == 0
 
-    def riv_row(ref, row):
-        parts = [
-            jnp.broadcast_to(ref[pl.ds(row * rows.per_row + part, 1), :], (layers, LANES))
-            for part in range(rows.per_row)
+    now, begin, stop, done = first, 0, window, 0
+    for wx_ref, wy_ref, wz_ref, inv_ref, base_ref in fields:
+        low, high = HALO + done, last_own - done
+        wx_of = Joined(rows, wx_ref, wx_sc, low, high - 1)
+        wy_of, wz_of = Joined(rows, wy_ref, wy_sc, low, high), Joined(rows, wz_ref, wz_sc, low, high)
+        inverse, base = [
+            Joined(rows, held_ref, full, low + 1, high - 1) for held_ref, full in ((inv_ref, inv_sc), (base_ref, base_sc))
         ]
-        return jnp.where(top, jnp.concatenate(parts, axis=1), 0.0)
-
-    def finish(row, diagonal, base):
-        rows.put(inv_sc, row, reciprocal(diagonal + riv_row(dtop_sc, row)))
-        rows.put(base_sc, row, base + riv_row(rtop_sc, row))
-
-    def conduct(now, row):
-        return faces.conduct(ks.get(row), alpha.get(row), now.get(row))
-
-    def sweep(now, later_ref, weights, begin, stop):
-        wx_of, wy_of, wz_of = weights
-        before, here, wx_before = now.get(begin - 1), now.get(begin), wx_of.get(begin - 1)
+        here_before, wx_before, sums_before = None, None, None
         for row in range(begin, stop):
-            after = now.get(row + 1)
-            wx, wy, wz = wx_of.get(row), wy_of.get(row), wz_of.get(row)
-            total = rows.get(base_sc, row) + wx_before * before + wx * after
-            total = total + wy * rows.east(here) + rows.west(wy * here)
-            total = total + wz * rows.below(here) + rows.above(wz * here)
-            rows.put(later_ref, row, total * rows.get(inv_sc, row))
-            before, here, wx_before = here, after, wx
-
-    now, spare = first, [ping_sc, pong_sc]
-    begin, stop = 0, window
-    for picard in range(ITERS):
-        early = picard == 0
-        wx_of = joined(wx_ref, wx_sc, last_own - 1 if early else HALO)
-        wy_of, wz_of = [joined(own, full, last_own if early else HALO) for own, full in ((wy_ref, wy_sc), (wz_ref, wz_sc))]
-        before, wx_before = None, None
-        for row in range(begin, stop):
-            staged = early and HALO <= row < last_own
-            here = conduct(now, row) if not staged or row in (HALO, last_own - 1) else None
-            if row > begin:
-                if early and HALO <= row - 1 < last_own - 1:
-                    wx = wx_of.get(row - 1)
-                else:
-                    wx = faces.between_rows(row - 1, before, here)
-                    wx_of.put(row - 1, wx)
-                if row - 1 > begin:
-                    diagonal, base = pending
-                    finish(row - 1, diagonal + wx_before + wx, base)
-                wx_before = wx
-            if staged:
-                pending = rows.get(partial_ref, row - HALO), rows.get(gravity_ref, row - HALO)
-            elif begin < row < stop - 1:
+            at_end = row in (low, high - 1)
+            here, sums = None, None
+            if not wy_of.holds(row) or at_end:
+                here = faces.conduct(ks.get(row), alpha.get(row), now.get(row))
+            if at_end:
+                sums = rows.get(inv_ref, row - HALO), rows.get(base_ref, row - HALO)
+            elif not wy_of.holds(row) and begin < row < stop - 1:
                 wy, wz, diagonal, gravity = faces.in_row(row, here)
                 wy_of.put(row, wy)
                 wz_of.put(row, wz)
-                pending = store.get(row) + diagonal, store.get(row) * first.get(row) + gravity
-            before = here
+                sums = store.get(row) + diagonal, store.get(row) * first.get(row) + gravity
+            if row > begin:
+                if wx_of.holds(row - 1):
+                    wx = wx_of.get(row - 1)
+                else:
+                    wx = faces.between_rows(row - 1, here_before, here)
+                    wx_of.put(row - 1, wx)
+                if sums_before is not None:
+                    diagonal = sums_before[0] + wx_before + wx + river_row(rows, dtop_sc, row - 1, top)
+                    inverse.put(row - 1, reciprocal(diagonal))
+                    base.put(row - 1, sums_before[1] + river_row(rows, rtop_sc, row - 1, top))
+                wx_before = wx
+            here_before, sums_before = here, sums
         for _ in range(SWEEPS):
             begin, stop = begin + 1, stop - 1
-            later_ref = spare[0]
-            sweep(now, later_ref, (wx_of, wy_of, wz_of), begin, stop)
-            spare = [spare[1], later_ref]
-            now = joined(None, later_ref, HALO)
+            later = Joined(rows, staged_refs[done], (ping_sc, pong_sc)[done % 2], HALO + done + 1, last_own - done - 1)
+            done += 1
+            for row in range(begin, stop):
+                if not later.holds(row):
+                    head = now.get(row - 1), now.get(row), now.get(row + 1)
+                    value, _ = relax_row(rows, row, head, (wx_of, wy_of, wz_of), wx_of.get(row - 1), base, inverse)
+                    later.put(row, value)
+            now = later
+    for row in range(now.first, now.last):
+        now.put(row, now.get(row))
     for part in range(rows.per_row):
         lanes = pl.ds(part * LANES, LANES)
-        top_ref[:, lanes] = later_ref[part, pl.ds(HALO * layers, span, stride=layers), :]
+        top_ref[:, lanes] = now.full[part, pl.ds(HALO * layers, span, stride=layers), :]
         for step, head_ref in enumerate(head_refs):
             for held_layer in range(held):
                 layer = (own ^ step) * held + held_layer
-                head_ref[held_layer, :, lanes] = later_ref[part, pl.ds(HALO * layers + layer, span, stride=layers), :]
+                head_ref[held_layer, :, lanes] = now.full[part, pl.ds(HALO * layers + layer, span, stride=layers), :]
 
 
 def inflow_kernel(reach_rows, stride, cells_ref, bed_ref, slot_section_ref, reach_ref, *refs):
@@ -651,18 +664,7 @@
         prepare_kernel,
         (jax.ShapeDtypeStruct((2, held, span, breadth), jnp.float32),) * groups
         + (jax.ShapeDtypeStruct((span, breadth), jnp.float32),),
-        [in_hbm] * 4,
-        [
-            pltpu.VMEM(head_start.shape, jnp.float32),
-            pltpu.VMEM(soil_class.shape, jnp.int32),
-            pltpu.VMEM(soil_class.shape, jnp.float32),
-            pltpu.VMEM((span, breadth), jnp.int32),
-            pltpu.SemaphoreType.DMA((held,)),
-            pltpu.SemaphoreType.DMA((held,)),
-            pltpu.SemaphoreType.DMA(()),
-            pltpu.SemaphoreType.DMA((2 * groups,)),
-        ],
-        2, VMEM_MOST, (in_hbm,) * groups + (in_vmem,),
+        [in_vmem] * 3 + [in_hbm], [], 0.5,
     )(head_start, soil_class, land_mask, spread)
     received = exchange(own_blocks)
 
@@ -691,11 +693,10 @@
     own_field = jax.ShapeDtypeStruct((per_row, span * layers, LANES), jnp.float32)
     field = pltpu.VMEM((per_row, window * layers, LANES), jnp.float32)
     staged = call(
-        stage_kernel, (own_field,) * 9,
-        [in_smem] * 3 + [in_vmem] * (1 + groups),
+        stage_kernel, (own_field,) * (4 + 5 * ITERS + HALO), [in_smem] * 3 + [in_vmem] * (3 + groups),
         [pltpu.VMEM(own_field.shape, jnp.float32)] + [pltpu.VMEM((span, breadth), jnp.float32)] * 3,
-        2.5,
-    )(ks_table, alpha_table, store_table, land, *received)
+        4,
+    )(ks_table, alpha_table, store_table, land, diag, rhs, *received)
     head_shape = jax.ShapeDtypeStruct((held, span, breadth), jnp.float32)
     *heads, top = call(
         flow_kernel,
@@ -705,7 +706,7 @@
         + [pltpu.VMEM((window, breadth), jnp.float32)]
         + [pltpu.VMEM((window * per_row, LANES), jnp.float32)] * 2
         + [pltpu.VMEM((window, breadth), jnp.float32)] * 3,
-        5,
+        3,
     )(ks_table, alpha_table, store_table, land, near_halo, far_halo, diag, rhs, *staged)
     tops = exchange([top] * groups)
     backs = exchange(heads)

time: 55.6 us -> 53.7 us (0.966)
  waiting for transfers between devices: 8.73 us -> 11.9 us
  starting transfers between devices: 23.2 us -> 20.4 us
  Pallas kernels: 22.4 us -> 20.2 us
    pallas_call x1, Pallas kernels: 2.57 us -> 0.06 us  [on_device(): call(prepare_kernel, (jax.ShapeDtypeStruct((2, held, span, breadth), jnp....]
    all_to_all x1, waiting for transfers between devices: 2.59 us -> 5.06 us  [on_device(): lax.all_to_all(spread, 'tile', 0, 0).reshape(tiles * stride, node_count)]
    ppermute x9, starting transfers between devices: 11.3 us -> 8.89 us  [exchange(): lax.ppermute(parts[step], 'layer', [(i, i ^ step) for i in range(groups)])]
    pallas_call x1, Pallas kernels: 2.37 us -> 4.1 us  [on_device(): call(stage_kernel, (own_field,) * (4 + 5 * ITERS + HALO), [in_smem] * 3 +...]
    pallas_call x1, Pallas kernels: 5.05 us -> 3.66 us  [on_device(): call(flow_kernel, (head_shape,) * groups + (jax.ShapeDtypeStruct((span, b...]
    ppermute x9, waiting for transfers between devices: 0.3 us -> 1.05 us  [exchange(): lax.ppermute(parts[step], 'layer', [(i, i ^ step) for i in range(groups)])]
  transfers between devices with their start and end apart: 13 -> 13, of which waited for: 3 -> 5; matrix products, arithmetic and copies ran while one was open for 0% -> 0% of each run, Pallas kernels for 27% -> 27%
where the time goes in v10:
time: 53.7 us; the launch traced here: 53.4 us
  starting transfers between devices  20.4 us (38%)
  Pallas kernels  20.2 us (38%)
  waiting for transfers between devices  11.9 us (22%)
  between operations  0.89 us (2%)
    ppermute x9, starting transfers between devices, exchange(): lax.ppermute(parts[step], 'layer', [(i, i ^ step) for i in range(groups)])  8.89 us
    all_to_all x1, starting transfers between devices, on_device(): lax.all_to_all(spread, 'tile', 0, 0).reshape(tiles * stride, node_count)  7.4 us
    pallas_call x1, Pallas kernels, on_device(): call(functools.partial(river_kernel, breadth, span, stride), (riv_shape,...  6.57 us
    all_to_all x1, waiting for transfers between devices, on_device(): lax.all_to_all(partial.reshape(tiles, fold, node_count), 'tile', 0, 0)  5.76 us
    all_to_all x1, waiting for transfers between devices, on_device(): lax.all_to_all(spread, 'tile', 0, 0).reshape(tiles * stride, node_count)  5.06 us
    pallas_call x1, Pallas kernels, on_device(): call(stage_kernel, (own_field,) * (4 + 5 * ITERS + HALO), [in_smem] * 3 +...  4.1 us
    pallas_call x1, Pallas kernels, on_device(): call(flow_kernel, (head_shape,) * groups + (jax.ShapeDtypeStruct((span, b...  3.66 us
    all_to_all x1, starting transfers between devices, on_device(): lax.all_to_all(partial.reshape(tiles, fold, node_count), 'tile', 0, 0)  3.33 us
  transfers between devices with their start and end apart: 13, of which 5 were waited for; matrix products, arithmetic and copies ran while one was open for 0% of the time, Pallas kernels for 27%

profile of v10, /device:TPU:0, one launch (start us, length us, event | category | flops | bytes accessed | tf_op | source)
XLA Modules:
  0.0 53.4 jit_solution(352743992416420150)
XLA Ops:
  0.7 1.4 %shard_map.122.after_ref = f32[8,24,128]{2,1,0:T(8,128)} custom-call(f32[16,128]{1,0:T(8,128)} %section_hbm.1, s32[1,256]{1,0:T(1,128)} %owner_hbm.1, s32[1,256]{1,0:T(1,128)} %local_hbm.1), custom_call_target="tpu_custom_call" | custom-call | flops 1150000000 | tf_op jit(solution)/shard_map/pallas_call | solution.py:652
  2.1 7.4 %all-to-all-start = ((f32[8,24,128]{2,1,0:T(8,128)}), f32[8,24,128]{2,1,0:T(8,128)S(1)}, u32[]{:S(2)}, u32[]{:S(2)}) async-start(f32[8,24,128]{2,1,0:T(8,128)} %shard_map.122.after_ref), calls=%async_computation | async-start | bytes 196608 | tf_op jit(solution)/shard_map/all_to_all | solution.py:662
  9.6 0.1 collective-permute-start
  9.7 1.6 %collective-permute-start.1 = (f32[2,2,16,512]{3,2,1,0:T(8,128)S(1)}, f32[2,2,16,512]{3,2,1,0:T(8,128)S(1)}, u32[]{:S(2)}, u32[]{:S(2)}) collective-permute-start(f32[2,2,16,512]{3,2,1,0:T(8,128)S(1)} %get-tuple-element.50), channel_id=1, source_target_pairs={{0,2},{1,3},{2,0},{3,1},{4,6},{5,7},{6,4},{7,5},{8,10},{9,11},{10,... | collective-permute-start | bytes 393224 | tf_op jit(solution)/shard_map/ppermute | solution.py:648
  11.3 0.3 collective-permute-start.2
  11.6 5.1 %all-to-all-done = f32[8,24,128]{2,1,0:T(8,128)S(1)} async-done(((f32[8,24,128]{2,1,0:T(8,128)}), f32[8,24,128]{2,1,0:T(8,128)S(1)}, u32[]{:S(2)}, u32[]{:S(2)}) %all-to-all-start) | async-done | bytes 98336 | tf_op jit(solution)/shard_map/all_to_all | solution.py:662
  16.7 6.6 %shard_map.123 = (f32[64,128]{1,0:T(8,128)S(1)}, f32[64,128]{1,0:T(8,128)S(1)}, f32[256,128]{1,0:T(8,128)S(1)}, f32[1,256]{1,0:T(1,128)S(1)}) custom-call(s32[256,128]{1,0:T(8,128)S(1)} %bitcast.5, f32[256,128]{1,0:T(8,128)S(1)} %bitcast.7, f32[192,128]{1,0:T(8,128)S(1)} %bitcast.4), custom_call_target="tpu_custom_call" | custom-call | flops 8049999872 | tf_op jit(solution)/shard_map/pallas_call | solution.py:673
  23.3 0.1 shard_map.125
  23.5 0.7 %collective-permute-start.4 = (f32[114,512]{1,0:T(8,128)S(1)}, f32[114,512]{1,0:T(8,128)S(1)}, u32[]{:S(2)}, u32[]{:S(2)}) collective-permute-start(f32[114,512]{1,0:T(8,128)S(1)} %get-tuple-element.53), channel_id=1, source_target_pairs={{1,2},{2,1},{3,7},{7,3},{5,6},{6,5},{4,8},{8,4},{9,10},{10,9},{11,... | collective-permute-start | bytes 700424 | tf_op jit(solution)/shard_map/ppermute | solution.py:690
  24.2 4.1 %shard_map.126 = (f32[4,128,128]{2,1,0:T(8,128)S(1)}, f32[4,128,128]{2,1,0:T(8,128)S(1)}, f32[4,128,128]{2,1,0:T(8,128)S(1)}, f32[4,128,128]{2,1,0:T(8,128)S(1)}...) custom-call(f32[12]{0:T(128)S(1)} %copy-done.6, ...), custom_call_target="tpu_custom_call" | custom-call | flops 4600000000 | tf_op jit(solution)/shard_map/pallas_call | solution.py:695
  28.3 3.7 %shard_map.127 = (f32[2,16,512]{2,1,0:T(8,128)S(1)}, f32[2,16,512]{2,1,0:T(8,128)S(1)}, f32[2,16,512]{2,1,0:T(8,128)S(1)}, f32[2,16,512]{2,1,0:T(8,128)S(1)}, f32[16,512]{1,0:T(8,128)S(1)}) custom-call(f32[12]{0:T(128)S(1)} %copy-done.6, f32[12]{0:T(128)S(1)} %copy-done.7, f32[12]{0:T(128)S(1)} %copy-done.8, f32[16,512]{1,0:T(8,128)S(1)} %get-tuple-element.45.land_ref, ...), custom_call_target="tpu_custom_call" | custom-call | flops 3449999872 | tf_op jit(solution)/shard_map/pallas_call | solution.py:701
  32.0 3.2 %collective-permute-start.5 = (f32[16,512]{1,0:T(8,128)S(1)}, f32[16,512]{1,0:T(8,128)S(1)}, u32[]{:S(2)}, u32[]{:S(2)}) collective-permute-start(f32[16,512]{1,0:T(8,128)S(1)} %get-tuple-element.74.refs_0_), channel_id=1, source_target_pairs={{0,1},{1,0},{2,3},{3,2},{4,5},{5,4},{6,7},{7,6},{8,9},{9,8},{10,11... | collective-permute-start | bytes 98312 | tf_op jit(solution)/shard_map/ppermute | solution.py:648
  35.2 1.2 %collective-permute-start.6 = (f32[16,512]{1,0:T(8,128)S(1)}, f32[16,512]{1,0:T(8,128)S(1)}, u32[]{:S(2)}, u32[]{:S(2)}) collective-permute-start(f32[16,512]{1,0:T(8,128)S(1)} %get-tuple-element.74.refs_0_), channel_id=1, source_target_pairs={{0,2},{1,3},{2,0},{3,1},{4,6},{5,7},{6,4},{7,5},{8,10},{9,11},{10,... | collective-permute-start | bytes 98312 | tf_op jit(solution)/shard_map/ppermute | solution.py:648
  36.4 0.3 collective-permute-start.7
  36.6 1.5 %collective-permute-start.10 = (f32[2,16,512]{2,1,0:T(8,128)S(1)}, f32[2,16,512]{2,1,0:T(8,128)S(1)}, u32[]{:S(2)}, u32[]{:S(2)}) collective-permute-start(f32[2,16,512]{2,1,0:T(8,128)S(1)} %get-tuple-element.78), channel_id=1, source_target_pairs={{0,3},{1,2},{2,1},{3,0},{4,7},{5,6},{6,5},{7,4},{8,11},{9,10},{10,... | collective-permute-start | bytes 196616 | tf_op jit(solution)/shard_map/ppermute | solution.py:648
  38.2 0.8 %collective-permute-start.9 = (f32[2,16,512]{2,1,0:T(8,128)S(1)}, f32[2,16,512]{2,1,0:T(8,128)S(1)}, u32[]{:S(2)}, u32[]{:S(2)}) collective-permute-start(f32[2,16,512]{2,1,0:T(8,128)S(1)} %get-tuple-element.77), channel_id=1, source_target_pairs={{0,2},{1,3},{2,0},{3,1},{4,6},{5,7},{6,4},{7,5},{8,10},{9,11},{10,... | collective-permute-start | bytes 196616 | tf_op jit(solution)/shard_map/ppermute | solution.py:648
  39.0 0.1 collective-permute-done.6.refs_2_
  39.1 0.7 %collective-permute-done.7.refs_3_ = f32[16,512]{1,0:T(8,128)S(1)} collective-permute-done((f32[16,512]{1,0:T(8,128)S(1)}, f32[16,512]{1,0:T(8,128)S(1)}, u32[]{:S(2)}, u32[]{:S(2)}) %collective-permute-start.7) | collective-permute-done | bytes 32800 | tf_op jit(solution)/shard_map/ppermute | solution.py:648
  39.8 2.9 %shard_map.128 = f32[32,128]{1,0:T(8,128)} custom-call(s32[256,128]{1,0:T(8,128)S(1)} %bitcast.6, f32[256,128]{1,0:T(8,128)S(1)} %bitcast.8, f32[256,128]{1,0:T(8,128)S(1)} %get-tuple-element.43.slot_section_ref, f32[1,256]{1,0:T(1,128)S(1)} %get-tuple-element.44.reach_ref, f32[16,512]{1,0:T(8,128)S(1)} %get-tuple-element.74.refs_0_, ...), custom_call_target="tpu_custom_call" | custom-call | flops 3449999872 | tf_op jit(solution)/shard_map/pallas_call | solution.py:716
  42.6 0.2 collective-permute-done.9.refs_2_
  42.9 3.3 %all-to-all-start.1 = ((f32[8,4,128]{2,1,0:T(4,128)}), f32[8,4,128]{2,1,0:T(4,128)S(1)}, u32[]{:S(2)}, u32[]{:S(2)}) async-start(f32[8,4,128]{2,1,0:T(4,128)} %bitcast.3), calls=%async_computation.1 | async-start | bytes 32768 | tf_op jit(solution)/shard_map/all_to_all | solution.py:724
  46.2 0.7 %shard_map.129 = f32[2,64,512]{2,1,0:T(8,128)} custom-call(f32[2,16,512]{2,1,0:T(8,128)S(1)} %get-tuple-element.79.refs_0_, f32[2,16,512]{2,1,0:T(8,128)S(1)} %collective-permute-done.8.refs_1_, f32[2,16,512]{2,1,0:T(8,128)S(1)} %collective-permute-done.9.refs_2_, f32[2,16,512]{2,1,0:T(8,128)S(1)} %collective-permute-done.10.refs_3_), custom_call_target="tpu_custom_call" | custom-call | flops 805000000 | tf_op jit(solution)/shard_map/pallas_call | solution.py:725
  46.9 5.8 %all-to-all-done.1.terms_ref = f32[8,4,128]{2,1,0:T(4,128)S(1)} async-done(((f32[8,4,128]{2,1,0:T(4,128)}), f32[8,4,128]{2,1,0:T(4,128)S(1)}, u32[]{:S(2)}, u32[]{:S(2)}) %all-to-all-start.1) | async-done | bytes 16416 | tf_op jit(solution)/shard_map/all_to_all | solution.py:724
  52.7 0.7 %shard_map.130 = f32[16,32]{1,0:T(8,128)} custom-call(f32[8,4,128]{2,1,0:T(4,128)S(1)} %all-to-all-done.1.terms_ref), custom_call_target="tpu_custom_call" | custom-call | flops 115000000 | tf_op jit(solution)/shard_map/pallas_call | solution.py:730
  (29 shorter events, 0.3 us)
Async XLA Ops:
  0.6 8.9 %copy-start.1 = (f32[2,64,512]{2,1,0:T(8,128)S(1)}, f32[2,64,512]{2,1,0:T(8,128)}, u32[]{:S(2)}) copy-start(f32[2,64,512]{2,1,0:T(8,128)} %head_ref.1) | copy-start | bytes 786436
  0.6 8.9 %copy-start.2 = (s32[2,64,512]{2,1,0:T(8,128)S(1)}, s32[2,64,512]{2,1,0:T(8,128)}, u32[]{:S(2)}) copy-start(s32[2,64,512]{2,1,0:T(8,128)} %soil_ref.1) | copy-start | bytes 786436
  0.7 8.9 %copy-start.3 = (s32[64,512]{1,0:T(8,128)S(1)}, s32[64,512]{1,0:T(8,128)}, u32[]{:S(2)}) copy-start(s32[64,512]{1,0:T(8,128)} %land_ref.1) | copy-start | bytes 393220
  2.1 7.4 %copy-start = (f32[8,24,128]{2,1,0:T(8,128)S(1)}, f32[8,24,128]{2,1,0:T(8,128)}, u32[]{:S(2)}) copy-start(f32[8,24,128]{2,1,0:T(8,128)} %shard_map.122.after_ref) | copy-start | bytes 294916
  2.1 14.5 %all-to-all-start = ((f32[8,24,128]{2,1,0:T(8,128)}), f32[8,24,128]{2,1,0:T(8,128)S(1)}, u32[]{:S(2)}, u32[]{:S(2)}) async-start(f32[8,24,128]{2,1,0:T(8,128)} %shard_map.122.after_ref), calls=%async_computation | async-start | bytes 196608 | tf_op jit(solution)/shard_map/all_to_all | solution.py:662
  9.6 7.1 %copy-start.4 = (s32[1,256,128]{2,1,0:T(8,128)S(1)}, s32[1,256,128]{2,1,0:T(8,128)}, u32[]{:S(2)}) copy-start(s32[1,256,128]{2,1,0:T(8,128)} %param.20) | copy-start | bytes 393220
  9.6 7.1 %copy-start.5 = (f32[1,256,128]{2,1,0:T(8,128)S(1)}, f32[1,256,128]{2,1,0:T(8,128)}, u32[]{:S(2)}) copy-start(f32[1,256,128]{2,1,0:T(8,128)} %param.21) | copy-start | bytes 393220
  9.6 13.6 %collective-permute-start = (f32[2,2,16,512]{3,2,1,0:T(8,128)S(1)}, f32[2,2,16,512]{3,2,1,0:T(8,128)S(1)}, u32[]{:S(2)}, u32[]{:S(2)}) collective-permute-start(f32[2,2,16,512]{3,2,1,0:T(8,128)S(1)} %get-tuple-element.49), channel_id=1, source_target_pairs={{0,1},{1,0},{2,3},{3,2},{4,5},{5,4},{6,7},{7,6},{8,9},{9,8},{10,11... | collective-permute-start | bytes 393224 | tf_op jit(solution)/shard_map/ppermute | solution.py:648
  9.7 13.5 %collective-permute-start.1 = (f32[2,2,16,512]{3,2,1,0:T(8,128)S(1)}, f32[2,2,16,512]{3,2,1,0:T(8,128)S(1)}, u32[]{:S(2)}, u32[]{:S(2)}) collective-permute-start(f32[2,2,16,512]{3,2,1,0:T(8,128)S(1)} %get-tuple-element.50), channel_id=1, source_target_pairs={{0,2},{1,3},{2,0},{3,1},{4,6},{5,7},{6,4},{7,5},{8,10},{9,11},{10,... | collective-permute-start | bytes 393224 | tf_op jit(solution)/shard_map/ppermute | solution.py:648
  11.3 11.9 %collective-permute-start.2 = (f32[2,2,16,512]{3,2,1,0:T(8,128)S(1)}, f32[2,2,16,512]{3,2,1,0:T(8,128)S(1)}, u32[]{:S(2)}, u32[]{:S(2)}) collective-permute-start(f32[2,2,16,512]{3,2,1,0:T(8,128)S(1)} %get-tuple-element.51), channel_id=1, source_target_pairs={{0,3},{1,2},{2,1},{3,0},{4,7},{5,6},{6,5},{7,4},{8,11},{9,10},{10,... | collective-permute-start | bytes 393224 | tf_op jit(solution)/shard_map/ppermute | solution.py:648
  23.4 0.8 %copy-start.6 = (f32[12]{0:T(128)S(1)}, f32[12]{0:T(128)}, u32[]{:S(2)}) copy-start(f32[12]{0:T(128)} %kst_ref.1) | copy-start | bytes 148
  23.4 0.8 %copy-start.7 = (f32[12]{0:T(128)S(1)}, f32[12]{0:T(128)}, u32[]{:S(2)}) copy-start(f32[12]{0:T(128)} %alphat_ref.1) | copy-start | bytes 148
  23.4 0.8 %copy-start.8 = (f32[12]{0:T(128)S(1)}, f32[12]{0:T(128)}, u32[]{:S(2)}) copy-start(f32[12]{0:T(128)} %storet_ref.1) | copy-start | bytes 148
  23.4 4.9 %collective-permute-start.3 = (f32[114,512]{1,0:T(8,128)S(1)}, f32[114,512]{1,0:T(8,128)S(1)}, u32[]{:S(2)}, u32[]{:S(2)}) collective-permute-start(f32[114,512]{1,0:T(8,128)S(1)} %get-tuple-element.52), channel_id=1, source_target_pairs={{0,1},{1,0},{2,3},{3,2},{4,5},{5,4},{6,7},{7,6},{8,9},{9,8},{10,11... | collective-permute-start | bytes 700424 | tf_op jit(solution)/shard_map/ppermute | solution.py:689
  23.5 4.8 %collective-permute-start.4 = (f32[114,512]{1,0:T(8,128)S(1)}, f32[114,512]{1,0:T(8,128)S(1)}, u32[]{:S(2)}, u32[]{:S(2)}) collective-permute-start(f32[114,512]{1,0:T(8,128)S(1)} %get-tuple-element.53), channel_id=1, source_target_pairs={{1,2},{2,1},{3,7},{7,3},{5,6},{6,5},{4,8},{8,4},{9,10},{10,9},{11,... | collective-permute-start | bytes 700424 | tf_op jit(solution)/shard_map/ppermute | solution.py:690
  32.0 6.2 %collective-permute-start.5 = (f32[16,512]{1,0:T(8,128)S(1)}, f32[16,512]{1,0:T(8,128)S(1)}, u32[]{:S(2)}, u32[]{:S(2)}) collective-permute-start(f32[16,512]{1,0:T(8,128)S(1)} %get-tuple-element.74.refs_0_), channel_id=1, source_target_pairs={{0,1},{1,0},{2,3},{3,2},{4,5},{5,4},{6,7},{7,6},{8,9},{9,8},{10,11... | collective-permute-start | bytes 98312 | tf_op jit(solution)/shard_map/ppermute | solution.py:648
  35.2 3.9 %collective-permute-start.6 = (f32[16,512]{1,0:T(8,128)S(1)}, f32[16,512]{1,0:T(8,128)S(1)}, u32[]{:S(2)}, u32[]{:S(2)}) collective-permute-start(f32[16,512]{1,0:T(8,128)S(1)} %get-tuple-element.74.refs_0_), channel_id=1, source_target_pairs={{0,2},{1,3},{2,0},{3,1},{4,6},{5,7},{6,4},{7,5},{8,10},{9,11},{10,... | collective-permute-start | bytes 98312 | tf_op jit(solution)/shard_map/ppermute | solution.py:648
  36.4 3.4 %collective-permute-start.7 = (f32[16,512]{1,0:T(8,128)S(1)}, f32[16,512]{1,0:T(8,128)S(1)}, u32[]{:S(2)}, u32[]{:S(2)}) collective-permute-start(f32[16,512]{1,0:T(8,128)S(1)} %get-tuple-element.74.refs_0_), channel_id=1, source_target_pairs={{0,3},{1,2},{2,1},{3,0},{4,7},{5,6},{6,5},{7,4},{8,11},{9,10},{10,... | collective-permute-start | bytes 98312 | tf_op jit(solution)/shard_map/ppermute | solution.py:648
  36.6 6.0 %collective-permute-start.10 = (f32[2,16,512]{2,1,0:T(8,128)S(1)}, f32[2,16,512]{2,1,0:T(8,128)S(1)}, u32[]{:S(2)}, u32[]{:S(2)}) collective-permute-start(f32[2,16,512]{2,1,0:T(8,128)S(1)} %get-tuple-element.78), channel_id=1, source_target_pairs={{0,3},{1,2},{2,1},{3,0},{4,7},{5,6},{6,5},{7,4},{8,11},{9,10},{10,... | collective-permute-start | bytes 196616 | tf_op jit(solution)/shard_map/ppermute | solution.py:648
  38.1 4.5 %collective-permute-start.8 = (f32[2,16,512]{2,1,0:T(8,128)S(1)}, f32[2,16,512]{2,1,0:T(8,128)S(1)}, u32[]{:S(2)}, u32[]{:S(2)}) collective-permute-start(f32[2,16,512]{2,1,0:T(8,128)S(1)} %get-tuple-element.76), channel_id=1, source_target_pairs={{0,1},{1,0},{2,3},{3,2},{4,5},{5,4},{6,7},{7,6},{8,9},{9,8},{10,11... | collective-permute-start | bytes 196616 | tf_op jit(solution)/shard_map/ppermute | solution.py:648
  38.2 4.7 %collective-permute-start.9 = (f32[2,16,512]{2,1,0:T(8,128)S(1)}, f32[2,16,512]{2,1,0:T(8,128)S(1)}, u32[]{:S(2)}, u32[]{:S(2)}) collective-permute-start(f32[2,16,512]{2,1,0:T(8,128)S(1)} %get-tuple-element.77), channel_id=1, source_target_pairs={{0,2},{1,3},{2,0},{3,1},{4,6},{5,7},{6,4},{7,5},{8,10},{9,11},{10,... | collective-permute-start | bytes 196616 | tf_op jit(solution)/shard_map/ppermute | solution.py:648
  42.9 9.9 %all-to-all-start.1 = ((f32[8,4,128]{2,1,0:T(4,128)}), f32[8,4,128]{2,1,0:T(4,128)S(1)}, u32[]{:S(2)}, u32[]{:S(2)}) async-start(f32[8,4,128]{2,1,0:T(4,128)} %bitcast.3), calls=%async_computation.1 | async-start | bytes 32768 | tf_op jit(solution)/shard_map/all_to_all | solution.py:724

commit v11 on v10

--- a/solution.py
+++ b/solution.py
@@ -74,11 +74,42 @@
     return block.astype(jnp.float32), (local & (width - 1)).astype(jnp.float32)
 
 
+def node_kernel(breadth, span, cells_ref, bed_ref, after_ref, *refs):
+    del after_ref
+    block_ref, spot_ref, high_ref, low_ref, lane_ref, bed_out_ref, hots_ref, block_sc = refs
+    groups = lax.axis_size("layer")
+    own_layer, _, number = position()
+    cells, bed = cells_ref[...], bed_ref[...]
+    block_ref[...], spot_ref[...] = split_cells(cells, number * span, breadth, BLOCK)
+    high, low = bf16_pieces(bed, 2)
+    high_ref[...] = high.astype(jnp.float32)
+    low_ref[...] = low.astype(jnp.float32)
+
+    packed_cells = pack_quarter(cells, groups, own_layer)
+    bed_out_ref[...] = jnp.where(packed_cells >= 0, pack_quarter(bed, groups, own_layer), 0.0)
+    block_sc[...], lane_ref[...] = split_cells(packed_cells, 0, breadth, LANES)
+    names = names_of(hots_ref.shape[0])
+    for row in range(block_sc.shape[0]):
+        for tile, hot in enumerate(one_hot(row_copies(block_sc, 0, row), names)):
+            hots_ref[pl.ds(tile * 16, 16), pl.ds(row * LANES, LANES)] = hot
+
+
+def pack_quarter(field, groups, own_layer):
+    quarter = LANES // groups
+    packed = field.shape[0] // groups
+    own = lax.broadcasted_iota(jnp.int32, (packed, LANES), 1) // quarter
+    result = None
+    for number in range(groups):
+        shift = lax.rem((number + groups - own_layer) * quarter, LANES)
+        moved = pltpu.roll(field[number * packed:(number + 1) * packed], shift, 1)
+        result = moved if result is None else jnp.where(own == number, moved, result)
+    return result
+
+
 def river_kernel(
-    breadth, span, stride, cells_ref, bed_ref, section_ref,
-    diag_ref, rhs_ref, slot_section_ref, reach_ref, block_sc, spot_sc, dhigh_sc, dlow_sc, rhigh_sc, rlow_sc, sum_sc,
+    stride, bed_ref, section_ref, block_ref, spot_ref, dhigh_ref, dlow_ref,
+    diag_ref, rhs_ref, slot_section_ref, reach_ref, rhigh_sc, rlow_sc, sum_sc,
 ):
-    _, _, number = position()
     rows = section_ref.shape[0]
     slots = reach_ref.shape[1]
     first = (lax.axis_index("tile") + 1) * stride - 8
@@ -94,14 +125,9 @@
         )
     slot_section_ref[...] = picked
 
-    block, spot = split_cells(cells_ref[...], number * span, breadth, BLOCK)
-    block_sc[...] = block
-    spot_sc[...] = spot
-    bed = bed_ref[...]
-    for value, high_sc, low_sc in ((bed, dhigh_sc, dlow_sc), (bed * picked, rhigh_sc, rlow_sc)):
-        high, low = bf16_pieces(value, 2)
-        high_sc[...] = high.astype(jnp.float32)
-        low_sc[...] = low.astype(jnp.float32)
+    high, low = bf16_pieces(bed_ref[...] * picked, 2)
+    rhigh_sc[...] = high.astype(jnp.float32)
+    rlow_sc[...] = low.astype(jnp.float32)
     share = LANES // BLOCK
     blocks = share * diag_ref.shape[0]
     group = 64
@@ -110,9 +136,9 @@
     def matmul(first, places):
         left, right = [], []
         for place in places:
-            left.append(jnp.concatenate(one_hot(row_copies(block_sc, first, place), block_names), axis=0))
-            hot = one_hot(row_copies(spot_sc, first, place), spot_names)
-            values = [row_copies(ref, first, place) for ref in (dhigh_sc, dlow_sc, rhigh_sc, rlow_sc)]
+            left.append(jnp.concatenate(one_hot(row_copies(block_ref, first, place), block_names), axis=0))
+            hot = one_hot(row_copies(spot_ref, first, place), spot_names)
+            values = [row_copies(ref, first, place) for ref in (dhigh_ref, dlow_ref, rhigh_sc, rlow_sc)]
             right.append(jnp.concatenate([tile * value for value in values for tile in hot], axis=0))
         return lax.dot_general(
             jnp.concatenate(left, axis=1),
@@ -374,7 +400,7 @@
             done += 1
 
 
-def flow_kernel(kst_ref, alphat_ref, storet_ref, land_ref, near_ref, far_ref, diag_ref, rhs_ref, *refs):
+def flow_kernel(kst_ref, alphat_ref, storet_ref, land_ref, far_ref, near_ref, diag_ref, rhs_ref, *refs):
     groups = lax.axis_size("layer")
     own, _, number = position()
     end = (number == 0) | (number == groups - 1)
@@ -487,68 +513,36 @@
                 head_ref[held_layer, :, lanes] = now.full[part, pl.ds(HALO * layers + layer, span, stride=layers), :]
 
 
-def inflow_kernel(reach_rows, stride, cells_ref, bed_ref, slot_section_ref, reach_ref, *refs):
+def inflow_kernel(reach_rows, stride, lane_ref, bed_ref, hots_ref, slot_section_ref, reach_ref, *refs):
     groups = lax.axis_size("layer")
     own_layer, flip, _ = position()
     top_refs = refs[:groups]
-    out_ref, block_sc, lane_sc, found_sc, turned_sc = refs[groups:]
+    out_ref, found_sc, turned_sc = refs[groups:]
     span, breadth = top_refs[0].shape
     per_row = breadth // LANES
-    blocks = groups * span * per_row
-    slots = cells_ref.shape[0]
+    slots = reach_ref.shape[1]
     quarter = LANES // groups
-    packed = slots // groups
     for step, top_ref in enumerate(top_refs):
         number = span_at(flip, groups, own_layer ^ step)
         for part in range(per_row):
             spot = pl.ds(number * span * per_row + part, span, stride=per_row)
             turned_sc[spot, :] = top_ref[:, part * LANES:(part + 1) * LANES]
-
-    own = lax.broadcasted_iota(jnp.int32, (packed, LANES), 1) // quarter
-
-    def pack(ref):
-        result = None
-        for number in range(groups):
-            shift = lax.rem((number + groups - own_layer) * quarter, LANES)
-            moved = pltpu.roll(ref[pl.ds(number * packed, packed), :], shift, 1)
-            result = moved if result is None else jnp.where(own == number, moved, result)
-        return result
-
-    cells = pack(cells_ref)
-    block, lane = split_cells(cells, 0, breadth, LANES)
-    block_sc[...] = block
-    lane_sc[...] = lane
     table = jnp.concatenate(bf16_pieces(turned_sc[...].T, 2), axis=0)
-    group = 32
-    names = names_of(blocks)
     index = lax.broadcasted_iota(jnp.int32, (8, LANES), 0).astype(jnp.float32)
-
-    def step(count, _):
-        first = pl.multiple_of(count * group, group)
-        for pair in range(0, group, 2):
-            hots = jnp.concatenate(
-                [
-                    jnp.concatenate(one_hot(row_copies(block_sc, first, place), names), axis=0)
-                    for place in (pair, pair + 1)
-                ],
-                axis=1,
-            )
-            found = lax.dot_general(
-                table, hots, (((1,), (0,)), ((), ())), preferred_element_type=jnp.float32
-            )
-            found = found[:LANES] + found[LANES:]
-            for place in (pair, pair + 1):
-                rows = lane_sc[pl.ds(first + place // 8 * 8, 8), :]
-                lanes = jnp.broadcast_to(rows[place % 8:place % 8 + 1, :], (8, LANES))
-                mine = found[:, (place - pair) * LANES:(place - pair + 1) * LANES]
-                total = jnp.zeros((8, LANES), jnp.float32)
-                for start in range(0, LANES, 8):
-                    total = total + jnp.where(lanes == index + float(start), mine[start:start + 8], 0.0)
-                found_sc[pl.ds(first + place, 1), :] = jnp.sum(total, axis=0, keepdims=True)
-        return 0
-
-    lax.fori_loop(0, packed // group, step, 0)
-    slot_in = jnp.where(cells >= 0, pack(bed_ref) * (found_sc[...] - pack(slot_section_ref)), 0.0)
+    for pair in range(0, lane_ref.shape[0], 2):
+        found = lax.dot_general(
+            table, hots_ref[:, pl.ds(pair * LANES, 2 * LANES)], (((1,), (0,)), ((), ())),
+            preferred_element_type=jnp.float32,
+        )
+        found = found[:LANES] + found[LANES:]
+        for row in (pair, pair + 1):
+            lanes = jnp.broadcast_to(lane_ref[pl.ds(row, 1), :], (8, LANES))
+            mine = found[:, (row - pair) * LANES:(row - pair + 1) * LANES]
+            total = jnp.zeros((8, LANES), jnp.float32)
+            for start in range(0, LANES, 8):
+                total = total + jnp.where(lanes == index + float(start), mine[start:start + 8], 0.0)
+            found_sc[pl.ds(row, 1), :] = jnp.sum(total, axis=0, keepdims=True)
+    slot_in = bed_ref[...] * (found_sc[...] - pack_quarter(slot_section_ref[...], groups, own_layer))
     spread = jnp.concatenate(
         [slot_in if number == 0 else pltpu.roll(slot_in, LANES - number * quarter, 1) for number in range(groups)],
         axis=0,
@@ -670,24 +664,25 @@
 
     node_scratch = pltpu.VMEM((slots, LANES), jnp.float32)
     riv_shape = jax.ShapeDtypeStruct((blocks, LANES), jnp.float32)
+    field = jax.ShapeDtypeStruct((slots, LANES), jnp.float32)
+    packed = jax.ShapeDtypeStruct((slots // groups, LANES), jnp.float32)
+    *parts, lanes, bed_packed, hots = call(
+        functools.partial(node_kernel, breadth, span),
+        (field,) * 4 + (packed,) * 2
+        + (jax.ShapeDtypeStruct((across * per_row, slots // groups * LANES), jnp.bfloat16),),
+        [in_vmem] * 3, [pltpu.VMEM(packed.shape, jnp.float32)], 1,
+    )(cells, bed, land)
     diag, rhs, slot_section, reach = call(
-        functools.partial(river_kernel, breadth, span, stride),
-        (
-            riv_shape,
-            riv_shape,
-            jax.ShapeDtypeStruct((slots, node_count), jnp.float32),
-            jax.ShapeDtypeStruct((1, slots), jnp.float32),
-        ),
-        [in_vmem] * 3,
-        [node_scratch] * 6 + [pltpu.VMEM((span * breadth // BLOCK, LANES), jnp.float32)],
-        7,
-    )(cells, bed, whole_section)
+        functools.partial(river_kernel, stride),
+        (riv_shape, riv_shape, field, jax.ShapeDtypeStruct((1, slots), jnp.float32)),
+        [in_vmem] * 6, [node_scratch] * 2 + [pltpu.VMEM((span * breadth // BLOCK, LANES), jnp.float32)], 7,
+    )(bed, whole_section, *parts)
     edges = jax.ShapeDtypeStruct(((2 * layers + 3) * HALO, breadth), jnp.float32)
     near_edge, far_edge = call(
         edge_kernel, (edges, edges), [in_vmem] * (3 + groups), [], 0.1,
     )(land, diag, rhs, *received)
+    far_halo = lax.ppermute(far_edge, FLAT, far)
     near_halo = lax.ppermute(near_edge, "layer", near)
-    far_halo = lax.ppermute(far_edge, FLAT, far)
 
     window = span + 2 * HALO
     own_field = jax.ShapeDtypeStruct((per_row, span * layers, LANES), jnp.float32)
@@ -707,19 +702,16 @@
         + [pltpu.VMEM((window * per_row, LANES), jnp.float32)] * 2
         + [pltpu.VMEM((window, breadth), jnp.float32)] * 3,
         3,
-    )(ks_table, alpha_table, store_table, land, near_halo, far_halo, diag, rhs, *staged)
+    )(ks_table, alpha_table, store_table, land, far_halo, near_halo, diag, rhs, *staged)
     tops = exchange([top] * groups)
     backs = exchange(heads)
 
     fold = reach_rows // groups
-    packed = pltpu.VMEM((slots // groups, LANES), jnp.float32)
     partial = call(
         functools.partial(inflow_kernel, reach_rows, stride),
-        jax.ShapeDtypeStruct((tiles * fold, node_count), jnp.float32),
-        [in_vmem] * (4 + groups),
-        [packed] * 3 + [pltpu.VMEM((across * per_row, LANES), jnp.float32)],
-        3,
-    )(cells, bed, slot_section, reach, *tops)
+        jax.ShapeDtypeStruct((tiles * fold, node_count), jnp.float32), [in_vmem] * (5 + groups),
+        [pltpu.VMEM(packed.shape, jnp.float32), pltpu.VMEM((across * per_row, LANES), jnp.float32)], 3,
+    )(lanes, bed_packed, hots, slot_section, reach, *tops)
     partial, *backs = lax.optimization_barrier((partial, *backs))
     terms = lax.all_to_all(partial.reshape(tiles, fold, node_count), "tile", 0, 0)
     head = call(

time: 53.7 us -> 55.6 us (1.035)
  waiting for transfers between devices: 11.9 us -> 7.3 us
  local copies, waits for them, and re-layouts: 0.05 us -> 2.89 us
  starting transfers between devices: 20.4 us -> 23.1 us
  Pallas kernels: 20.2 us -> 21.1 us
    all_to_all x1, waiting for transfers between devices: 5.06 us -> 0.75 us  [on_device(): lax.all_to_all(spread, 'tile', 0, 0).reshape(tiles * stride, node_count)]
    ppermute x1, starting transfers between devices: 0.07 us -> 2.93 us  [on_device(): near_halo = lax.ppermute(near_edge, 'layer', near)]
    unnamed x18 -> x22, local copies, waits for them, and re-layouts: 0.05 us -> 2.89 us
    ppermute x9, starting transfers between devices: 8.89 us -> 6.51 us  [exchange(): lax.ppermute(parts[step], 'layer', [(i, i ^ step) for i in range(groups)])]
    all_to_all x1, starting transfers between devices: 3.33 us -> 5.7 us  [on_device(): lax.all_to_all(partial.reshape(tiles, fold, node_count), 'tile', 0, 0)]
    pallas_call x1 -> x2, Pallas kernels: 6.57 us -> 8.02 us  [the longest x1 6.54 us: on_device(): call(functools.partial(river_kernel, stride), (riv_shape, riv_shape, fiel...]
  transfers between devices with their start and end apart: 13 -> 13, of which waited for: 5 -> 4; matrix products, arithmetic and copies ran while one was open for 0% -> 0% of each run, Pallas kernels for 27% -> 28%
where the time goes in v11:
time: 55.6 us; the launch traced here: 55.2 us
  starting transfers between devices  23.1 us (42%)
  Pallas kernels  21.1 us (38%)
  waiting for transfers between devices  7.3 us (13%)
  local copies, waits for them, and re-layouts  2.89 us (5%)
  between operations  0.84 us (2%)
    all_to_all x1, starting transfers between devices, on_device(): lax.all_to_all(spread, 'tile', 0, 0).reshape(tiles * stride, node_count)  7.26 us
    pallas_call x1, Pallas kernels, on_device(): call(functools.partial(river_kernel, stride), (riv_shape, riv_shape, fiel...  6.54 us
    ppermute x9, starting transfers between devices, exchange(): lax.ppermute(parts[step], 'layer', [(i, i ^ step) for i in range(groups)])  6.51 us
    all_to_all x1, waiting for transfers between devices, on_device(): lax.all_to_all(partial.reshape(tiles, fold, node_count), 'tile', 0, 0)  5.84 us
    all_to_all x1, starting transfers between devices, on_device(): lax.all_to_all(partial.reshape(tiles, fold, node_count), 'tile', 0, 0)  5.7 us
    pallas_call x1, Pallas kernels, on_device(): call(stage_kernel, (own_field,) * (4 + 5 * ITERS + HALO), [in_smem] * 3 +...  4.1 us
    pallas_call x1, Pallas kernels, on_device(): call(flow_kernel, (head_shape,) * groups + (jax.ShapeDtypeStruct((span, b...  3.66 us
    ppermute x1, starting transfers between devices, on_device(): near_halo = lax.ppermute(near_edge, 'layer', near)  2.93 us
  transfers between devices with their start and end apart: 13, of which 4 were waited for; matrix products, arithmetic and copies ran while one was open for 0% of the time, Pallas kernels for 28%

profile of v11, /device:TPU:0, one launch (start us, length us, event | category | flops | bytes accessed | tf_op | source)
XLA Modules:
  0.0 55.2 jit_solution(9597630635828974242)
XLA Ops:
  0.7 1.5 %shard_map.122.after_ref = f32[8,24,128]{2,1,0:T(8,128)} custom-call(f32[16,128]{1,0:T(8,128)} %section_hbm.1, s32[1,256]{1,0:T(1,128)} %owner_hbm.1, s32[1,256]{1,0:T(1,128)} %local_hbm.1), custom_call_target="tpu_custom_call" | custom-call | flops 1150000000 | tf_op jit(solution)/shard_map/pallas_call | solution.py:646
  2.2 7.3 %all-to-all-start = ((f32[8,24,128]{2,1,0:T(8,128)}), f32[8,24,128]{2,1,0:T(8,128)S(1)}, u32[]{:S(2)}, u32[]{:S(2)}) async-start(f32[8,24,128]{2,1,0:T(8,128)} %shard_map.122.after_ref), calls=%async_computation | async-start | bytes 196608 | tf_op jit(solution)/shard_map/all_to_all | solution.py:656
  9.5 0.9 %copy-done = f32[8,24,128]{2,1,0:T(8,128)S(1)} copy-done((f32[8,24,128]{2,1,0:T(8,128)S(1)}, f32[8,24,128]{2,1,0:T(8,128)}, u32[]{:S(2)}) %copy-start) | copy-done | bytes 98328
  10.5 1.6 %collective-permute-start.1 = (f32[2,2,16,512]{3,2,1,0:T(8,128)S(1)}, f32[2,2,16,512]{3,2,1,0:T(8,128)S(1)}, u32[]{:S(2)}, u32[]{:S(2)}) collective-permute-start(f32[2,2,16,512]{3,2,1,0:T(8,128)S(1)} %get-tuple-element.64), channel_id=1, source_target_pairs={{0,2},{1,3},{2,0},{3,1},{4,6},{5,7},{6,4},{7,5},{8,10},{9,11},{10,... | collective-permute-start | bytes 393224 | tf_op jit(solution)/shard_map/ppermute | solution.py:642
  12.0 0.3 collective-permute-start.2
  12.3 1.5 %shard_map.124 = (f32[256,128]{1,0:T(8,128)S(1)}, f32[256,128]{1,0:T(8,128)S(1)}, f32[256,128]{1,0:T(8,128)S(1)}, f32[256,128]{1,0:T(8,128)S(1)}, f32[64,128]{1,...) custom-call(s32[256,128]{1,0:T(8,128)S(1)} %bitcast.5, f32[256,128]{1,0:T(8,128)S(1)} %bitcast.6, ...), custom_call_target="tpu_custom_call" | custom-call | flops 1150000000 | tf_op jit(solution)/shard_map/pallas_call | solution.py:669
  13.8 2.0 %copy-done.9 = bf16[256,8192]{1,0:T(8,128)(2,1)} copy-done((bf16[256,8192]{1,0:T(8,128)(2,1)}, bf16[256,8192]{1,0:T(8,128)(2,1)S(1)}, u32[]{:S(2)}) %copy-start.9) | copy-done | bytes 4194328
  15.8 0.7 %all-to-all-done = f32[8,24,128]{2,1,0:T(8,128)S(1)} async-done(((f32[8,24,128]{2,1,0:T(8,128)}), f32[8,24,128]{2,1,0:T(8,128)S(1)}, u32[]{:S(2)}, u32[]{:S(2)}) %all-to-all-start) | async-done | bytes 98336 | tf_op jit(solution)/shard_map/all_to_all | solution.py:656
  16.5 6.5 %shard_map.125 = (f32[64,128]{1,0:T(8,128)S(1)}, f32[64,128]{1,0:T(8,128)S(1)}, f32[256,128]{1,0:T(8,128)S(1)}, f32[1,256]{1,0:T(1,128)S(1)}) custom-call(f32[256,128]{1,0:T(8,128)S(1)} %bitcast.7, f32[192,128]{1,0:T(8,128)S(1)} %bitcast.4, f32[256,128]{1,0:T(8,128)S(1)} %get-tuple-element.54.block_ref, f32[256,128]{1,0:T(8,128)S(1)} %get-tuple-element.55.spot_ref, ...), custom_call_target="tpu_custom_call" | custom-call | flops 8049999872 | tf_op jit(solution)/shard_map/pallas_call | solution.py:675
  23.2 0.7 %collective-permute-start.3 = (f32[114,512]{1,0:T(8,128)S(1)}, f32[114,512]{1,0:T(8,128)S(1)}, u32[]{:S(2)}, u32[]{:S(2)}) collective-permute-start(f32[114,512]{1,0:T(8,128)S(1)} %get-tuple-element.66), channel_id=1, source_target_pairs={{1,2},{2,1},{3,7},{7,3},{5,6},{6,5},{4,8},{8,4},{9,10},{10,9},{11,... | collective-permute-start | bytes 700424 | tf_op jit(solution)/shard_map/ppermute | solution.py:684
  23.9 2.9 %collective-permute-start.4 = (f32[114,512]{1,0:T(8,128)S(1)}, f32[114,512]{1,0:T(8,128)S(1)}, u32[]{:S(2)}, u32[]{:S(2)}) collective-permute-start(f32[114,512]{1,0:T(8,128)S(1)} %get-tuple-element.67), channel_id=1, source_target_pairs={{0,1},{1,0},{2,3},{3,2},{4,5},{5,4},{6,7},{7,6},{8,9},{9,8},{10,11... | collective-permute-start | bytes 700424 | tf_op jit(solution)/shard_map/ppermute | solution.py:685
  26.9 4.1 %shard_map.127 = (f32[4,128,128]{2,1,0:T(8,128)S(1)}, f32[4,128,128]{2,1,0:T(8,128)S(1)}, f32[4,128,128]{2,1,0:T(8,128)S(1)}, f32[4,128,128]{2,1,0:T(8,128)S(1)}...) custom-call(f32[12]{0:T(128)S(1)} %copy-done.6, ...), custom_call_target="tpu_custom_call" | custom-call | flops 4600000000 | tf_op jit(solution)/shard_map/pallas_call | solution.py:690
  31.0 3.7 %shard_map.128 = (f32[2,16,512]{2,1,0:T(8,128)S(1)}, f32[2,16,512]{2,1,0:T(8,128)S(1)}, f32[2,16,512]{2,1,0:T(8,128)S(1)}, f32[2,16,512]{2,1,0:T(8,128)S(1)}, f32[16,512]{1,0:T(8,128)S(1)}) custom-call(f32[12]{0:T(128)S(1)} %copy-done.6, f32[12]{0:T(128)S(1)} %copy-done.7, f32[12]{0:T(128)S(1)} %copy-done.8, ...), custom_call_target="tpu_custom_call" | custom-call | flops 3449999872 | tf_op jit(solution)/shard_map/pallas_call | solution.py:696
  34.7 1.0 %collective-permute-start.7 = (f32[16,512]{1,0:T(8,128)S(1)}, f32[16,512]{1,0:T(8,128)S(1)}, u32[]{:S(2)}, u32[]{:S(2)}) collective-permute-start(f32[16,512]{1,0:T(8,128)S(1)} %get-tuple-element.88.refs_0_), channel_id=1, source_target_pairs={{0,3},{1,2},{2,1},{3,0},{4,7},{5,6},{6,5},{7,4},{8,11},{9,10},{10,... | collective-permute-start | bytes 98312 | tf_op jit(solution)/shard_map/ppermute | solution.py:642
  35.6 0.8 %collective-permute-start.6 = (f32[16,512]{1,0:T(8,128)S(1)}, f32[16,512]{1,0:T(8,128)S(1)}, u32[]{:S(2)}, u32[]{:S(2)}) collective-permute-start(f32[16,512]{1,0:T(8,128)S(1)} %get-tuple-element.88.refs_0_), channel_id=1, source_target_pairs={{0,2},{1,3},{2,0},{3,1},{4,6},{5,7},{6,4},{7,5},{8,10},{9,11},{10,... | collective-permute-start | bytes 98312 | tf_op jit(solution)/shard_map/ppermute | solution.py:642
  36.6 0.3 collective-permute-start.8
  36.9 1.2 %collective-permute-start.9 = (f32[2,16,512]{2,1,0:T(8,128)S(1)}, f32[2,16,512]{2,1,0:T(8,128)S(1)}, u32[]{:S(2)}, u32[]{:S(2)}) collective-permute-start(f32[2,16,512]{2,1,0:T(8,128)S(1)} %get-tuple-element.91), channel_id=1, source_target_pairs={{0,2},{1,3},{2,0},{3,1},{4,6},{5,7},{6,4},{7,5},{8,10},{9,11},{10,... | collective-permute-start | bytes 196616 | tf_op jit(solution)/shard_map/ppermute | solution.py:642
  38.2 1.1 %collective-permute-start.10 = (f32[2,16,512]{2,1,0:T(8,128)S(1)}, f32[2,16,512]{2,1,0:T(8,128)S(1)}, u32[]{:S(2)}, u32[]{:S(2)}) collective-permute-start(f32[2,16,512]{2,1,0:T(8,128)S(1)} %get-tuple-element.92), channel_id=1, source_target_pairs={{0,3},{1,2},{2,1},{3,0},{4,7},{5,6},{6,5},{7,4},{8,11},{9,10},{10,... | collective-permute-start | bytes 196616 | tf_op jit(solution)/shard_map/ppermute | solution.py:642
  39.5 2.4 %shard_map.129 = f32[32,128]{1,0:T(8,128)} custom-call(f32[64,128]{1,0:T(8,128)S(1)} %get-tuple-element.51.lane_ref, f32[64,128]{1,0:T(8,128)S(1)} %get-tuple-element.52.bed_ref, bf16[256,8192]{1,0:T(8,128)(2,1)S(1)} %copy-done.10, f32[256,128]{1,0:T(8,128)S(1)} %get-tuple-element.58.slot_section_ref, f32[1,256]{1,0:T(1,128)S(1)} %get-tuple-element.59.reach_ref, ...), custom_call_target="tpu_custom_call" | custom-call | flops 3449999872 | tf_op jit(solution)/shard_map/pallas_call | solution.py:710
  41.9 0.4 collective-permute-done.10.refs_3_
  42.3 5.7 %all-to-all-start.1 = ((f32[8,4,128]{2,1,0:T(4,128)}), f32[8,4,128]{2,1,0:T(4,128)S(1)}, u32[]{:S(2)}, u32[]{:S(2)}) async-start(f32[8,4,128]{2,1,0:T(4,128)} %bitcast.3), calls=%async_computation.1 | async-start | bytes 32768 | tf_op jit(solution)/shard_map/all_to_all | solution.py:716
  48.0 0.7 %shard_map.130 = f32[2,64,512]{2,1,0:T(8,128)} custom-call(f32[2,16,512]{2,1,0:T(8,128)S(1)} %get-tuple-element.93.refs_0_, f32[2,16,512]{2,1,0:T(8,128)S(1)} %collective-permute-done.8.refs_1_, f32[2,16,512]{2,1,0:T(8,128)S(1)} %collective-permute-done.9.refs_2_, f32[2,16,512]{2,1,0:T(8,128)S(1)} %collective-permute-done.10.refs_3_), custom_call_target="tpu_custom_call" | custom-call | flops 805000000 | tf_op jit(solution)/shard_map/pallas_call | solution.py:717
  48.7 5.8 %all-to-all-done.1.terms_ref = f32[8,4,128]{2,1,0:T(4,128)S(1)} async-done(((f32[8,4,128]{2,1,0:T(4,128)}), f32[8,4,128]{2,1,0:T(4,128)S(1)}, u32[]{:S(2)}, u32[]{:S(2)}) %all-to-all-start.1) | async-done | bytes 16416 | tf_op jit(solution)/shard_map/all_to_all | solution.py:716
  54.6 0.7 %shard_map.131 = f32[16,32]{1,0:T(8,128)} custom-call(f32[8,4,128]{2,1,0:T(4,128)S(1)} %all-to-all-done.1.terms_ref), custom_call_target="tpu_custom_call" | custom-call | flops 115000000 | tf_op jit(solution)/shard_map/pallas_call | solution.py:722
  (34 shorter events, 0.7 us)
Async XLA Ops:
  0.6 8.8 %copy-start.3 = (s32[64,512]{1,0:T(8,128)S(1)}, s32[64,512]{1,0:T(8,128)}, u32[]{:S(2)}) copy-start(s32[64,512]{1,0:T(8,128)} %land_ref.1) | copy-start | bytes 393220
  0.6 8.8 %copy-start.2 = (s32[2,64,512]{2,1,0:T(8,128)S(1)}, s32[2,64,512]{2,1,0:T(8,128)}, u32[]{:S(2)}) copy-start(s32[2,64,512]{2,1,0:T(8,128)} %soil_ref.1) | copy-start | bytes 786436
  0.7 8.8 %copy-start.1 = (f32[2,64,512]{2,1,0:T(8,128)S(1)}, f32[2,64,512]{2,1,0:T(8,128)}, u32[]{:S(2)}) copy-start(f32[2,64,512]{2,1,0:T(8,128)} %head_ref.1) | copy-start | bytes 786436
  0.7 11.7 %copy-start.5 = (f32[1,256,128]{2,1,0:T(8,128)S(1)}, f32[1,256,128]{2,1,0:T(8,128)}, u32[]{:S(2)}) copy-start(f32[1,256,128]{2,1,0:T(8,128)} %param.21) | copy-start | bytes 393220
  0.7 11.7 %copy-start.4 = (s32[1,256,128]{2,1,0:T(8,128)S(1)}, s32[1,256,128]{2,1,0:T(8,128)}, u32[]{:S(2)}) copy-start(s32[1,256,128]{2,1,0:T(8,128)} %param.20) | copy-start | bytes 393220
  2.2 14.4 %all-to-all-start = ((f32[8,24,128]{2,1,0:T(8,128)}), f32[8,24,128]{2,1,0:T(8,128)S(1)}, u32[]{:S(2)}, u32[]{:S(2)}) async-start(f32[8,24,128]{2,1,0:T(8,128)} %shard_map.122.after_ref), calls=%async_computation | async-start | bytes 196608 | tf_op jit(solution)/shard_map/all_to_all | solution.py:656
  9.4 0.9 %copy-start = (f32[8,24,128]{2,1,0:T(8,128)S(1)}, f32[8,24,128]{2,1,0:T(8,128)}, u32[]{:S(2)}) copy-start(f32[8,24,128]{2,1,0:T(8,128)} %shard_map.122.after_ref) | copy-start | bytes 294916
  10.4 12.7 %collective-permute-start = (f32[2,2,16,512]{3,2,1,0:T(8,128)S(1)}, f32[2,2,16,512]{3,2,1,0:T(8,128)S(1)}, u32[]{:S(2)}, u32[]{:S(2)}) collective-permute-start(f32[2,2,16,512]{3,2,1,0:T(8,128)S(1)} %get-tuple-element.63), channel_id=1, source_target_pairs={{0,1},{1,0},{2,3},{3,2},{4,5},{5,4},{6,7},{7,6},{8,9},{9,8},{10,11... | collective-permute-start | bytes 393224 | tf_op jit(solution)/shard_map/ppermute | solution.py:642
  10.5 12.6 %collective-permute-start.1 = (f32[2,2,16,512]{3,2,1,0:T(8,128)S(1)}, f32[2,2,16,512]{3,2,1,0:T(8,128)S(1)}, u32[]{:S(2)}, u32[]{:S(2)}) collective-permute-start(f32[2,2,16,512]{3,2,1,0:T(8,128)S(1)} %get-tuple-element.64), channel_id=1, source_target_pairs={{0,2},{1,3},{2,0},{3,1},{4,6},{5,7},{6,4},{7,5},{8,10},{9,11},{10,... | collective-permute-start | bytes 393224 | tf_op jit(solution)/shard_map/ppermute | solution.py:642
  12.0 11.1 %collective-permute-start.2 = (f32[2,2,16,512]{3,2,1,0:T(8,128)S(1)}, f32[2,2,16,512]{3,2,1,0:T(8,128)S(1)}, u32[]{:S(2)}, u32[]{:S(2)}) collective-permute-start(f32[2,2,16,512]{3,2,1,0:T(8,128)S(1)} %get-tuple-element.65), channel_id=1, source_target_pairs={{0,3},{1,2},{2,1},{3,0},{4,7},{5,6},{6,5},{7,4},{8,11},{9,10},{10,... | collective-permute-start | bytes 393224 | tf_op jit(solution)/shard_map/ppermute | solution.py:642
  13.8 2.0 %copy-start.9 = (bf16[256,8192]{1,0:T(8,128)(2,1)}, bf16[256,8192]{1,0:T(8,128)(2,1)S(1)}, u32[]{:S(2)}) copy-start(bf16[256,8192]{1,0:T(8,128)(2,1)S(1)} %get-tuple-element.53.hots_ref) | copy-start | bytes 12582916
  16.5 10.3 %copy-start.6 = (f32[12]{0:T(128)S(1)}, f32[12]{0:T(128)}, u32[]{:S(2)}) copy-start(f32[12]{0:T(128)} %kst_ref.1) | copy-start | bytes 148
  16.5 10.3 %copy-start.7 = (f32[12]{0:T(128)S(1)}, f32[12]{0:T(128)}, u32[]{:S(2)}) copy-start(f32[12]{0:T(128)} %alphat_ref.1) | copy-start | bytes 148
  16.5 10.3 %copy-start.8 = (f32[12]{0:T(128)S(1)}, f32[12]{0:T(128)}, u32[]{:S(2)}) copy-start(f32[12]{0:T(128)} %storet_ref.1) | copy-start | bytes 148
  23.2 7.7 %collective-permute-start.3 = (f32[114,512]{1,0:T(8,128)S(1)}, f32[114,512]{1,0:T(8,128)S(1)}, u32[]{:S(2)}, u32[]{:S(2)}) collective-permute-start(f32[114,512]{1,0:T(8,128)S(1)} %get-tuple-element.66), channel_id=1, source_target_pairs={{1,2},{2,1},{3,7},{7,3},{5,6},{6,5},{4,8},{8,4},{9,10},{10,9},{11,... | collective-permute-start | bytes 700424 | tf_op jit(solution)/shard_map/ppermute | solution.py:684
  23.9 7.1 %collective-permute-start.4 = (f32[114,512]{1,0:T(8,128)S(1)}, f32[114,512]{1,0:T(8,128)S(1)}, u32[]{:S(2)}, u32[]{:S(2)}) collective-permute-start(f32[114,512]{1,0:T(8,128)S(1)} %get-tuple-element.67), channel_id=1, source_target_pairs={{0,1},{1,0},{2,3},{3,2},{4,5},{5,4},{6,7},{7,6},{8,9},{9,8},{10,11... | collective-permute-start | bytes 700424 | tf_op jit(solution)/shard_map/ppermute | solution.py:685
  31.0 8.5 %copy-start.10 = (bf16[256,8192]{1,0:T(8,128)(2,1)S(1)}, bf16[256,8192]{1,0:T(8,128)(2,1)}, u32[]{:S(2)}) copy-start(bf16[256,8192]{1,0:T(8,128)(2,1)} %copy-done.9) | copy-start | bytes 12582916
  34.7 3.5 %collective-permute-start.7 = (f32[16,512]{1,0:T(8,128)S(1)}, f32[16,512]{1,0:T(8,128)S(1)}, u32[]{:S(2)}, u32[]{:S(2)}) collective-permute-start(f32[16,512]{1,0:T(8,128)S(1)} %get-tuple-element.88.refs_0_), channel_id=1, source_target_pairs={{0,3},{1,2},{2,1},{3,0},{4,7},{5,6},{6,5},{7,4},{8,11},{9,10},{10,... | collective-permute-start | bytes 98312 | tf_op jit(solution)/shard_map/ppermute | solution.py:642
  35.6 3.9 %collective-permute-start.6 = (f32[16,512]{1,0:T(8,128)S(1)}, f32[16,512]{1,0:T(8,128)S(1)}, u32[]{:S(2)}, u32[]{:S(2)}) collective-permute-start(f32[16,512]{1,0:T(8,128)S(1)} %get-tuple-element.88.refs_0_), channel_id=1, source_target_pairs={{0,2},{1,3},{2,0},{3,1},{4,6},{5,7},{6,4},{7,5},{8,10},{9,11},{10,... | collective-permute-start | bytes 98312 | tf_op jit(solution)/shard_map/ppermute | solution.py:642
  36.4 3.1 %collective-permute-start.5 = (f32[16,512]{1,0:T(8,128)S(1)}, f32[16,512]{1,0:T(8,128)S(1)}, u32[]{:S(2)}, u32[]{:S(2)}) collective-permute-start(f32[16,512]{1,0:T(8,128)S(1)} %get-tuple-element.88.refs_0_), channel_id=1, source_target_pairs={{0,1},{1,0},{2,3},{3,2},{4,5},{5,4},{6,7},{7,6},{8,9},{9,8},{10,11... | collective-permute-start | bytes 98312 | tf_op jit(solution)/shard_map/ppermute | solution.py:642
  36.6 5.3 %collective-permute-start.8 = (f32[2,16,512]{2,1,0:T(8,128)S(1)}, f32[2,16,512]{2,1,0:T(8,128)S(1)}, u32[]{:S(2)}, u32[]{:S(2)}) collective-permute-start(f32[2,16,512]{2,1,0:T(8,128)S(1)} %get-tuple-element.90), channel_id=1, source_target_pairs={{0,1},{1,0},{2,3},{3,2},{4,5},{5,4},{6,7},{7,6},{8,9},{9,8},{10,11... | collective-permute-start | bytes 196616 | tf_op jit(solution)/shard_map/ppermute | solution.py:642
  36.9 5.0 %collective-permute-start.9 = (f32[2,16,512]{2,1,0:T(8,128)S(1)}, f32[2,16,512]{2,1,0:T(8,128)S(1)}, u32[]{:S(2)}, u32[]{:S(2)}) collective-permute-start(f32[2,16,512]{2,1,0:T(8,128)S(1)} %get-tuple-element.91), channel_id=1, source_target_pairs={{0,2},{1,3},{2,0},{3,1},{4,6},{5,7},{6,4},{7,5},{8,10},{9,11},{10,... | collective-permute-start | bytes 196616 | tf_op jit(solution)/shard_map/ppermute | solution.py:642
  38.2 4.1 %collective-permute-start.10 = (f32[2,16,512]{2,1,0:T(8,128)S(1)}, f32[2,16,512]{2,1,0:T(8,128)S(1)}, u32[]{:S(2)}, u32[]{:S(2)}) collective-permute-start(f32[2,16,512]{2,1,0:T(8,128)S(1)} %get-tuple-element.92), channel_id=1, source_target_pairs={{0,3},{1,2},{2,1},{3,0},{4,7},{5,6},{6,5},{7,4},{8,11},{9,10},{10,... | collective-permute-start | bytes 196616 | tf_op jit(solution)/shard_map/ppermute | solution.py:642
  42.3 12.3 %all-to-all-start.1 = ((f32[8,4,128]{2,1,0:T(4,128)}), f32[8,4,128]{2,1,0:T(4,128)S(1)}, u32[]{:S(2)}, u32[]{:S(2)}) async-start(f32[8,4,128]{2,1,0:T(4,128)} %bitcast.3), calls=%async_computation.1 | async-start | bytes 32768 | tf_op jit(solution)/shard_map/all_to_all | solution.py:716

commit v12 on v10

--- a/solution.py
+++ b/solution.py
@@ -374,7 +374,7 @@
             done += 1
 
 
-def flow_kernel(kst_ref, alphat_ref, storet_ref, land_ref, near_ref, far_ref, diag_ref, rhs_ref, *refs):
+def flow_kernel(kst_ref, alphat_ref, storet_ref, land_ref, far_ref, near_ref, diag_ref, rhs_ref, *refs):
     groups = lax.axis_size("layer")
     own, _, number = position()
     end = (number == 0) | (number == groups - 1)
@@ -519,35 +519,23 @@
     block_sc[...] = block
     lane_sc[...] = lane
     table = jnp.concatenate(bf16_pieces(turned_sc[...].T, 2), axis=0)
-    group = 32
     names = names_of(blocks)
     index = lax.broadcasted_iota(jnp.int32, (8, LANES), 0).astype(jnp.float32)
-
-    def step(count, _):
-        first = pl.multiple_of(count * group, group)
-        for pair in range(0, group, 2):
-            hots = jnp.concatenate(
-                [
-                    jnp.concatenate(one_hot(row_copies(block_sc, first, place), names), axis=0)
-                    for place in (pair, pair + 1)
-                ],
-                axis=1,
-            )
-            found = lax.dot_general(
-                table, hots, (((1,), (0,)), ((), ())), preferred_element_type=jnp.float32
-            )
-            found = found[:LANES] + found[LANES:]
-            for place in (pair, pair + 1):
-                rows = lane_sc[pl.ds(first + place // 8 * 8, 8), :]
-                lanes = jnp.broadcast_to(rows[place % 8:place % 8 + 1, :], (8, LANES))
-                mine = found[:, (place - pair) * LANES:(place - pair + 1) * LANES]
-                total = jnp.zeros((8, LANES), jnp.float32)
-                for start in range(0, LANES, 8):
-                    total = total + jnp.where(lanes == index + float(start), mine[start:start + 8], 0.0)
-                found_sc[pl.ds(first + place, 1), :] = jnp.sum(total, axis=0, keepdims=True)
-        return 0
-
-    lax.fori_loop(0, packed // group, step, 0)
+    for pair in range(0, packed, 2):
+        hots = jnp.concatenate(
+            [jnp.concatenate(one_hot(row_copies(block_sc, 0, row), names), axis=0) for row in (pair, pair + 1)], axis=1
+        )
+        found = lax.dot_general(
+            table, hots, (((1,), (0,)), ((), ())), preferred_element_type=jnp.float32
+        )
+        found = found[:LANES] + found[LANES:]
+        for row in (pair, pair + 1):
+            lanes = jnp.broadcast_to(lane_sc[pl.ds(row, 1), :], (8, LANES))
+            mine = found[:, (row - pair) * LANES:(row - pair + 1) * LANES]
+            total = jnp.zeros((8, LANES), jnp.float32)
+            for start in range(0, LANES, 8):
+                total = total + jnp.where(lanes == index + float(start), mine[start:start + 8], 0.0)
+            found_sc[pl.ds(row, 1), :] = jnp.sum(total, axis=0, keepdims=True)
     slot_in = jnp.where(cells >= 0, pack(bed_ref) * (found_sc[...] - pack(slot_section_ref)), 0.0)
     spread = jnp.concatenate(
         [slot_in if number == 0 else pltpu.roll(slot_in, LANES - number * quarter, 1) for number in range(groups)],
@@ -686,8 +674,8 @@
     near_edge, far_edge = call(
         edge_kernel, (edges, edges), [in_vmem] * (3 + groups), [], 0.1,
     )(land, diag, rhs, *received)
+    far_halo = lax.ppermute(far_edge, FLAT, far)
     near_halo = lax.ppermute(near_edge, "layer", near)
-    far_halo = lax.ppermute(far_edge, FLAT, far)
 
     window = span + 2 * HALO
     own_field = jax.ShapeDtypeStruct((per_row, span * layers, LANES), jnp.float32)
@@ -707,7 +695,7 @@
         + [pltpu.VMEM((window * per_row, LANES), jnp.float32)] * 2
         + [pltpu.VMEM((window, breadth), jnp.float32)] * 3,
         3,
-    )(ks_table, alpha_table, store_table, land, near_halo, far_halo, diag, rhs, *staged)
+    )(ks_table, alpha_table, store_table, land, far_halo, near_halo, diag, rhs, *staged)
     tops = exchange([top] * groups)
     backs = exchange(heads)
 
@@ -720,7 +708,7 @@
         [packed] * 3 + [pltpu.VMEM((across * per_row, LANES), jnp.float32)],
         3,
     )(cells, bed, slot_section, reach, *tops)
-    partial, *backs = lax.optimization_barrier((partial, *backs))
+    partial, *backs[:-1] = lax.optimization_barrier((partial, *backs[:-1]))
     terms = lax.all_to_all(partial.reshape(tiles, fold, node_count), "tile", 0, 0)
     head = call(
         head_kernel, jax.ShapeDtypeStruct(head_start.shape, jnp.float32), [in_vmem] * groups,

time: 53.7 us -> 53.1 us (0.989)
    ppermute x9, starting transfers between devices: 8.89 us -> 5.73 us  [exchange(): lax.ppermute(parts[step], 'layer', [(i, i ^ step) for i in range(groups)])]
    ppermute x1, starting transfers between devices: 0.07 us -> 2.93 us  [on_device(): near_halo = lax.ppermute(near_edge, 'layer', near)]
  transfers between devices with their start and end apart: 13 -> 13, of which waited for: 5 -> 4; matrix products, arithmetic and copies ran while one was open for 0% -> 0% of each run, Pallas kernels for 27% -> 26%
where the time goes in v12:
time: 53.1 us; the launch traced here: 52.7 us
  starting transfers between devices  20.2 us (38%)
  Pallas kernels  19.8 us (37%)
  waiting for transfers between devices  11.8 us (22%)
  between operations  0.87 us (2%)
    all_to_all x1, starting transfers between devices, on_device(): lax.all_to_all(spread, 'tile', 0, 0).reshape(tiles * stride, node_count)  7.4 us
    pallas_call x1, Pallas kernels, on_device(): call(functools.partial(river_kernel, breadth, span, stride), (riv_shape,...  6.57 us
    all_to_all x1, waiting for transfers between devices, on_device(): lax.all_to_all(partial.reshape(tiles, fold, node_count), 'tile', 0, 0)  5.75 us
    ppermute x9, starting transfers between devices, exchange(): lax.ppermute(parts[step], 'layer', [(i, i ^ step) for i in range(groups)])  5.73 us
    all_to_all x1, waiting for transfers between devices, on_device(): lax.all_to_all(spread, 'tile', 0, 0).reshape(tiles * stride, node_count)  5.06 us
    pallas_call x1, Pallas kernels, on_device(): call(stage_kernel, (own_field,) * (4 + 5 * ITERS + HALO), [in_smem] * 3 +...  4.1 us
    pallas_call x1, Pallas kernels, on_device(): call(flow_kernel, (head_shape,) * groups + (jax.ShapeDtypeStruct((span, b...  3.66 us
    all_to_all x1, starting transfers between devices, on_device(): lax.all_to_all(partial.reshape(tiles, fold, node_count), 'tile', 0, 0)  3.33 us
  transfers between devices with their start and end apart: 13, of which 4 were waited for; matrix products, arithmetic and copies ran while one was open for 0% of the time, Pallas kernels for 26%

profile of v12, /device:TPU:0, one launch (start us, length us, event | category | flops | bytes accessed | tf_op | source)
XLA Modules:
  0.0 52.7 jit_solution(4260115429634144279)
XLA Ops:
  0.7 1.4 %shard_map.122.after_ref = f32[8,24,128]{2,1,0:T(8,128)} custom-call(f32[16,128]{1,0:T(8,128)} %section_hbm.1, s32[1,256]{1,0:T(1,128)} %owner_hbm.1, s32[1,256]{1,0:T(1,128)} %local_hbm.1), custom_call_target="tpu_custom_call" | custom-call | flops 1150000000 | tf_op jit(solution)/shard_map/pallas_call | solution.py:640
  2.1 7.4 %all-to-all-start = ((f32[8,24,128]{2,1,0:T(8,128)}), f32[8,24,128]{2,1,0:T(8,128)S(1)}, u32[]{:S(2)}, u32[]{:S(2)}) async-start(f32[8,24,128]{2,1,0:T(8,128)} %shard_map.122.after_ref), calls=%async_computation | async-start | bytes 196608 | tf_op jit(solution)/shard_map/all_to_all | solution.py:650
  9.7 1.6 %collective-permute-start.1 = (f32[2,2,16,512]{3,2,1,0:T(8,128)S(1)}, f32[2,2,16,512]{3,2,1,0:T(8,128)S(1)}, u32[]{:S(2)}, u32[]{:S(2)}) collective-permute-start(f32[2,2,16,512]{3,2,1,0:T(8,128)S(1)} %get-tuple-element.49), channel_id=1, source_target_pairs={{0,2},{1,3},{2,0},{3,1},{4,6},{5,7},{6,4},{7,5},{8,10},{9,11},{10,... | collective-permute-start | bytes 393224 | tf_op jit(solution)/shard_map/ppermute | solution.py:636
  11.3 0.3 collective-permute-start.2
  11.6 5.1 %all-to-all-done = f32[8,24,128]{2,1,0:T(8,128)S(1)} async-done(((f32[8,24,128]{2,1,0:T(8,128)}), f32[8,24,128]{2,1,0:T(8,128)S(1)}, u32[]{:S(2)}, u32[]{:S(2)}) %all-to-all-start) | async-done | bytes 98336 | tf_op jit(solution)/shard_map/all_to_all | solution.py:650
  16.7 6.6 %shard_map.123 = (f32[64,128]{1,0:T(8,128)S(1)}, f32[64,128]{1,0:T(8,128)S(1)}, f32[256,128]{1,0:T(8,128)S(1)}, f32[1,256]{1,0:T(1,128)S(1)}) custom-call(s32[256,128]{1,0:T(8,128)S(1)} %bitcast.5, f32[256,128]{1,0:T(8,128)S(1)} %bitcast.7, f32[192,128]{1,0:T(8,128)S(1)} %bitcast.4), custom_call_target="tpu_custom_call" | custom-call | flops 8049999872 | tf_op jit(solution)/shard_map/pallas_call | solution.py:661
  23.3 0.1 shard_map.125
  23.4 0.8 %collective-permute-start.3 = (f32[114,512]{1,0:T(8,128)S(1)}, f32[114,512]{1,0:T(8,128)S(1)}, u32[]{:S(2)}, u32[]{:S(2)}) collective-permute-start(f32[114,512]{1,0:T(8,128)S(1)} %get-tuple-element.51), channel_id=1, source_target_pairs={{1,2},{2,1},{3,7},{7,3},{5,6},{6,5},{4,8},{8,4},{9,10},{10,9},{11,... | collective-permute-start | bytes 700424 | tf_op jit(solution)/shard_map/ppermute | solution.py:677
  24.2 2.9 %collective-permute-start.4 = (f32[114,512]{1,0:T(8,128)S(1)}, f32[114,512]{1,0:T(8,128)S(1)}, u32[]{:S(2)}, u32[]{:S(2)}) collective-permute-start(f32[114,512]{1,0:T(8,128)S(1)} %get-tuple-element.52), channel_id=1, source_target_pairs={{0,1},{1,0},{2,3},{3,2},{4,5},{5,4},{6,7},{7,6},{8,9},{9,8},{10,11... | collective-permute-start | bytes 700424 | tf_op jit(solution)/shard_map/ppermute | solution.py:678
  27.2 4.1 %shard_map.126 = (f32[4,128,128]{2,1,0:T(8,128)S(1)}, f32[4,128,128]{2,1,0:T(8,128)S(1)}, f32[4,128,128]{2,1,0:T(8,128)S(1)}, f32[4,128,128]{2,1,0:T(8,128)S(1)}...) custom-call(f32[12]{0:T(128)S(1)} %copy-done.6, ...), custom_call_target="tpu_custom_call" | custom-call | flops 4600000000 | tf_op jit(solution)/shard_map/pallas_call | solution.py:683
  31.3 3.7 %shard_map.127 = (f32[2,16,512]{2,1,0:T(8,128)S(1)}, f32[2,16,512]{2,1,0:T(8,128)S(1)}, f32[2,16,512]{2,1,0:T(8,128)S(1)}, f32[2,16,512]{2,1,0:T(8,128)S(1)}, f32[16,512]{1,0:T(8,128)S(1)}) custom-call(f32[12]{0:T(128)S(1)} %copy-done.6, f32[12]{0:T(128)S(1)} %copy-done.7, f32[12]{0:T(128)S(1)} %copy-done.8, f32[16,512]{1,0:T(8,128)S(1)} %get-tuple-element.44.land_ref, ...), custom_call_target="tpu_custom_call" | custom-call | flops 3449999872 | tf_op jit(solution)/shard_map/pallas_call | solution.py:689
  35.0 0.1 collective-permute-start.5
  35.1 1.3 %collective-permute-start.6 = (f32[16,512]{1,0:T(8,128)S(1)}, f32[16,512]{1,0:T(8,128)S(1)}, u32[]{:S(2)}, u32[]{:S(2)}) collective-permute-start(f32[16,512]{1,0:T(8,128)S(1)} %get-tuple-element.73.refs_0_), channel_id=1, source_target_pairs={{0,2},{1,3},{2,0},{3,1},{4,6},{5,7},{6,4},{7,5},{8,10},{9,11},{10,... | collective-permute-start | bytes 98312 | tf_op jit(solution)/shard_map/ppermute | solution.py:636
  36.3 0.6 %collective-permute-start.7 = (f32[16,512]{1,0:T(8,128)S(1)}, f32[16,512]{1,0:T(8,128)S(1)}, u32[]{:S(2)}, u32[]{:S(2)}) collective-permute-start(f32[16,512]{1,0:T(8,128)S(1)} %get-tuple-element.73.refs_0_), channel_id=1, source_target_pairs={{0,3},{1,2},{2,1},{3,0},{4,7},{5,6},{6,5},{7,4},{8,11},{9,10},{10,... | collective-permute-start | bytes 98312 | tf_op jit(solution)/shard_map/ppermute | solution.py:636
  36.9 0.3 collective-permute-start.8
  37.2 1.2 %collective-permute-start.9 = (f32[2,16,512]{2,1,0:T(8,128)S(1)}, f32[2,16,512]{2,1,0:T(8,128)S(1)}, u32[]{:S(2)}, u32[]{:S(2)}) collective-permute-start(f32[2,16,512]{2,1,0:T(8,128)S(1)} %get-tuple-element.76), channel_id=1, source_target_pairs={{0,2},{1,3},{2,0},{3,1},{4,6},{5,7},{6,4},{7,5},{8,10},{9,11},{10,... | collective-permute-start | bytes 196616 | tf_op jit(solution)/shard_map/ppermute | solution.py:636
  38.5 0.3 collective-permute-start.10
  38.8 0.3 collective-permute-done.6.refs_2_
  39.0 0.7 %collective-permute-done.7.refs_3_ = f32[16,512]{1,0:T(8,128)S(1)} collective-permute-done((f32[16,512]{1,0:T(8,128)S(1)}, f32[16,512]{1,0:T(8,128)S(1)}, u32[]{:S(2)}, u32[]{:S(2)}) %collective-permute-start.7) | collective-permute-done | bytes 32800 | tf_op jit(solution)/shard_map/ppermute | solution.py:636
  39.7 2.5 %shard_map.128 = f32[32,128]{1,0:T(8,128)} custom-call(s32[256,128]{1,0:T(8,128)S(1)} %bitcast.6, f32[256,128]{1,0:T(8,128)S(1)} %bitcast.8, f32[256,128]{1,0:T(8,128)S(1)} %get-tuple-element.42.slot_section_ref, f32[1,256]{1,0:T(1,128)S(1)} %get-tuple-element.43.reach_ref, f32[16,512]{1,0:T(8,128)S(1)} %get-tuple-element.73.refs_0_, ...), custom_call_target="tpu_custom_call" | custom-call | flops 3449999872 | tf_op jit(solution)/shard_map/pallas_call | solution.py:704
  42.2 3.3 %all-to-all-start.1 = ((f32[8,4,128]{2,1,0:T(4,128)}), f32[8,4,128]{2,1,0:T(4,128)S(1)}, u32[]{:S(2)}, u32[]{:S(2)}) async-start(f32[8,4,128]{2,1,0:T(4,128)} %bitcast.3), calls=%async_computation.1 | async-start | bytes 32768 | tf_op jit(solution)/shard_map/all_to_all | solution.py:712
  45.5 0.7 %shard_map.129 = f32[2,64,512]{2,1,0:T(8,128)} custom-call(f32[2,16,512]{2,1,0:T(8,128)S(1)} %get-tuple-element.77.refs_0_, f32[2,16,512]{2,1,0:T(8,128)S(1)} %collective-permute-done.8.refs_1_, f32[2,16,512]{2,1,0:T(8,128)S(1)} %collective-permute-done.9.refs_2_, f32[2,16,512]{2,1,0:T(8,128)S(1)} %collective-permute-done.10.refs_3_), custom_call_target="tpu_custom_call" | custom-call | flops 805000000 | tf_op jit(solution)/shard_map/pallas_call | solution.py:713
  46.3 5.8 %all-to-all-done.1.terms_ref = f32[8,4,128]{2,1,0:T(4,128)S(1)} async-done(((f32[8,4,128]{2,1,0:T(4,128)}), f32[8,4,128]{2,1,0:T(4,128)S(1)}, u32[]{:S(2)}, u32[]{:S(2)}) %all-to-all-start.1) | async-done | bytes 16416 | tf_op jit(solution)/shard_map/all_to_all | solution.py:712
  52.0 0.7 %shard_map.130 = f32[16,32]{1,0:T(8,128)} custom-call(f32[8,4,128]{2,1,0:T(4,128)S(1)} %all-to-all-done.1.terms_ref), custom_call_target="tpu_custom_call" | custom-call | flops 115000000 | tf_op jit(solution)/shard_map/pallas_call | solution.py:718
  (29 shorter events, 0.2 us)
Async XLA Ops:
  0.6 8.9 %copy-start.1 = (f32[2,64,512]{2,1,0:T(8,128)S(1)}, f32[2,64,512]{2,1,0:T(8,128)}, u32[]{:S(2)}) copy-start(f32[2,64,512]{2,1,0:T(8,128)} %head_ref.1) | copy-start | bytes 786436
  0.6 8.9 %copy-start.2 = (s32[2,64,512]{2,1,0:T(8,128)S(1)}, s32[2,64,512]{2,1,0:T(8,128)}, u32[]{:S(2)}) copy-start(s32[2,64,512]{2,1,0:T(8,128)} %soil_ref.1) | copy-start | bytes 786436
  0.7 8.9 %copy-start.3 = (s32[64,512]{1,0:T(8,128)S(1)}, s32[64,512]{1,0:T(8,128)}, u32[]{:S(2)}) copy-start(s32[64,512]{1,0:T(8,128)} %land_ref.1) | copy-start | bytes 393220
  2.1 7.4 %copy-start = (f32[8,24,128]{2,1,0:T(8,128)S(1)}, f32[8,24,128]{2,1,0:T(8,128)}, u32[]{:S(2)}) copy-start(f32[8,24,128]{2,1,0:T(8,128)} %shard_map.122.after_ref) | copy-start | bytes 294916
  2.1 14.5 %all-to-all-start = ((f32[8,24,128]{2,1,0:T(8,128)}), f32[8,24,128]{2,1,0:T(8,128)S(1)}, u32[]{:S(2)}, u32[]{:S(2)}) async-start(f32[8,24,128]{2,1,0:T(8,128)} %shard_map.122.after_ref), calls=%async_computation | async-start | bytes 196608 | tf_op jit(solution)/shard_map/all_to_all | solution.py:650
  9.6 7.1 %copy-start.4 = (s32[1,256,128]{2,1,0:T(8,128)S(1)}, s32[1,256,128]{2,1,0:T(8,128)}, u32[]{:S(2)}) copy-start(s32[1,256,128]{2,1,0:T(8,128)} %param.20) | copy-start | bytes 393220
  9.6 7.1 %copy-start.5 = (f32[1,256,128]{2,1,0:T(8,128)S(1)}, f32[1,256,128]{2,1,0:T(8,128)}, u32[]{:S(2)}) copy-start(f32[1,256,128]{2,1,0:T(8,128)} %param.21) | copy-start | bytes 393220
  9.6 13.6 %collective-permute-start = (f32[2,2,16,512]{3,2,1,0:T(8,128)S(1)}, f32[2,2,16,512]{3,2,1,0:T(8,128)S(1)}, u32[]{:S(2)}, u32[]{:S(2)}) collective-permute-start(f32[2,2,16,512]{3,2,1,0:T(8,128)S(1)} %get-tuple-element.48), channel_id=1, source_target_pairs={{0,1},{1,0},{2,3},{3,2},{4,5},{5,4},{6,7},{7,6},{8,9},{9,8},{10,11... | collective-permute-start | bytes 393224 | tf_op jit(solution)/shard_map/ppermute | solution.py:636
  9.7 13.5 %collective-permute-start.1 = (f32[2,2,16,512]{3,2,1,0:T(8,128)S(1)}, f32[2,2,16,512]{3,2,1,0:T(8,128)S(1)}, u32[]{:S(2)}, u32[]{:S(2)}) collective-permute-start(f32[2,2,16,512]{3,2,1,0:T(8,128)S(1)} %get-tuple-element.49), channel_id=1, source_target_pairs={{0,2},{1,3},{2,0},{3,1},{4,6},{5,7},{6,4},{7,5},{8,10},{9,11},{10,... | collective-permute-start | bytes 393224 | tf_op jit(solution)/shard_map/ppermute | solution.py:636
  11.3 11.9 %collective-permute-start.2 = (f32[2,2,16,512]{3,2,1,0:T(8,128)S(1)}, f32[2,2,16,512]{3,2,1,0:T(8,128)S(1)}, u32[]{:S(2)}, u32[]{:S(2)}) collective-permute-start(f32[2,2,16,512]{3,2,1,0:T(8,128)S(1)} %get-tuple-element.50), channel_id=1, source_target_pairs={{0,3},{1,2},{2,1},{3,0},{4,7},{5,6},{6,5},{7,4},{8,11},{9,10},{10,... | collective-permute-start | bytes 393224 | tf_op jit(solution)/shard_map/ppermute | solution.py:636
  23.4 3.8 %copy-start.6 = (f32[12]{0:T(128)S(1)}, f32[12]{0:T(128)}, u32[]{:S(2)}) copy-start(f32[12]{0:T(128)} %kst_ref.1) | copy-start | bytes 148
  23.4 3.8 %copy-start.7 = (f32[12]{0:T(128)S(1)}, f32[12]{0:T(128)}, u32[]{:S(2)}) copy-start(f32[12]{0:T(128)} %alphat_ref.1) | copy-start | bytes 148
  23.4 3.8 %copy-start.8 = (f32[12]{0:T(128)S(1)}, f32[12]{0:T(128)}, u32[]{:S(2)}) copy-start(f32[12]{0:T(128)} %storet_ref.1) | copy-start | bytes 148
  23.4 7.9 %collective-permute-start.3 = (f32[114,512]{1,0:T(8,128)S(1)}, f32[114,512]{1,0:T(8,128)S(1)}, u32[]{:S(2)}, u32[]{:S(2)}) collective-permute-start(f32[114,512]{1,0:T(8,128)S(1)} %get-tuple-element.51), channel_id=1, source_target_pairs={{1,2},{2,1},{3,7},{7,3},{5,6},{6,5},{4,8},{8,4},{9,10},{10,9},{11,... | collective-permute-start | bytes 700424 | tf_op jit(solution)/shard_map/ppermute | solution.py:677
  24.2 7.1 %collective-permute-start.4 = (f32[114,512]{1,0:T(8,128)S(1)}, f32[114,512]{1,0:T(8,128)S(1)}, u32[]{:S(2)}, u32[]{:S(2)}) collective-permute-start(f32[114,512]{1,0:T(8,128)S(1)} %get-tuple-element.52), channel_id=1, source_target_pairs={{0,1},{1,0},{2,3},{3,2},{4,5},{5,4},{6,7},{7,6},{8,9},{9,8},{10,11... | collective-permute-start | bytes 700424 | tf_op jit(solution)/shard_map/ppermute | solution.py:678
  35.0 3.5 %collective-permute-start.5 = (f32[16,512]{1,0:T(8,128)S(1)}, f32[16,512]{1,0:T(8,128)S(1)}, u32[]{:S(2)}, u32[]{:S(2)}) collective-permute-start(f32[16,512]{1,0:T(8,128)S(1)} %get-tuple-element.73.refs_0_), channel_id=1, source_target_pairs={{0,1},{1,0},{2,3},{3,2},{4,5},{5,4},{6,7},{7,6},{8,9},{9,8},{10,11... | collective-permute-start | bytes 98312 | tf_op jit(solution)/shard_map/ppermute | solution.py:636
  35.1 3.9 %collective-permute-start.6 = (f32[16,512]{1,0:T(8,128)S(1)}, f32[16,512]{1,0:T(8,128)S(1)}, u32[]{:S(2)}, u32[]{:S(2)}) collective-permute-start(f32[16,512]{1,0:T(8,128)S(1)} %get-tuple-element.73.refs_0_), channel_id=1, source_target_pairs={{0,2},{1,3},{2,0},{3,1},{4,6},{5,7},{6,4},{7,5},{8,10},{9,11},{10,... | collective-permute-start | bytes 98312 | tf_op jit(solution)/shard_map/ppermute | solution.py:636
  36.3 3.3 %collective-permute-start.7 = (f32[16,512]{1,0:T(8,128)S(1)}, f32[16,512]{1,0:T(8,128)S(1)}, u32[]{:S(2)}, u32[]{:S(2)}) collective-permute-start(f32[16,512]{1,0:T(8,128)S(1)} %get-tuple-element.73.refs_0_), channel_id=1, source_target_pairs={{0,3},{1,2},{2,1},{3,0},{4,7},{5,6},{6,5},{7,4},{8,11},{9,10},{10,... | collective-permute-start | bytes 98312 | tf_op jit(solution)/shard_map/ppermute | solution.py:636
  36.9 5.3 %collective-permute-start.8 = (f32[2,16,512]{2,1,0:T(8,128)S(1)}, f32[2,16,512]{2,1,0:T(8,128)S(1)}, u32[]{:S(2)}, u32[]{:S(2)}) collective-permute-start(f32[2,16,512]{2,1,0:T(8,128)S(1)} %get-tuple-element.75), channel_id=1, source_target_pairs={{0,1},{1,0},{2,3},{3,2},{4,5},{5,4},{6,7},{7,6},{8,9},{9,8},{10,11... | collective-permute-start | bytes 196616 | tf_op jit(solution)/shard_map/ppermute | solution.py:636
  37.2 5.0 %collective-permute-start.9 = (f32[2,16,512]{2,1,0:T(8,128)S(1)}, f32[2,16,512]{2,1,0:T(8,128)S(1)}, u32[]{:S(2)}, u32[]{:S(2)}) collective-permute-start(f32[2,16,512]{2,1,0:T(8,128)S(1)} %get-tuple-element.76), channel_id=1, source_target_pairs={{0,2},{1,3},{2,0},{3,1},{4,6},{5,7},{6,4},{7,5},{8,10},{9,11},{10,... | collective-permute-start | bytes 196616 | tf_op jit(solution)/shard_map/ppermute | solution.py:636
  38.5 7.0 %collective-permute-start.10 = (f32[2,16,512]{2,1,0:T(8,128)S(1)}, f32[2,16,512]{2,1,0:T(8,128)S(1)}, u32[]{:S(2)}, u32[]{:S(2)}) collective-permute-start(f32[2,16,512]{2,1,0:T(8,128)S(1)} %get-tuple-element.80), channel_id=1, source_target_pairs={{0,3},{1,2},{2,1},{3,0},{4,7},{5,6},{6,5},{7,4},{8,11},{9,10},{10,... | collective-permute-start | bytes 196616 | tf_op jit(solution)/shard_map/ppermute | solution.py:636
  42.2 9.9 %all-to-all-start.1 = ((f32[8,4,128]{2,1,0:T(4,128)}), f32[8,4,128]{2,1,0:T(4,128)S(1)}, u32[]{:S(2)}, u32[]{:S(2)}) async-start(f32[8,4,128]{2,1,0:T(4,128)} %bitcast.3), calls=%async_computation.1 | async-start | bytes 32768 | tf_op jit(solution)/shard_map/all_to_all | solution.py:712

commit v13 on v12

--- a/solution.py
+++ b/solution.py
@@ -160,6 +160,9 @@
             top = ref[pl.ds(part, HALO, stride=per_row), :]
             bottom = ref[pl.ds((span - HALO) * per_row + part, HALO, stride=per_row), :]
             put_edges(entry, top, bottom, slice(part * LANES, (part + 1) * LANES))
+    rest = near_ref.shape[0] - (entry + 1) * HALO
+    for ref in (near_ref, far_ref):
+        ref[pl.ds((entry + 1) * HALO, rest), :] = jnp.zeros((rest, breadth), jnp.float32)
 
 
 def spread_kernel(section_hbm, owner_hbm, local_hbm, spread_ref, section_ref, owner_ref, local_ref, sems):
@@ -379,6 +382,8 @@
     own, _, number = position()
     end = (number == 0) | (number == groups - 1)
     far_partner = jnp.where(end, own, own ^ (groups - 1))
+    tile, tiles = lax.axis_index("tile"), lax.axis_size("tile")
+    outside = ((tile == 0) & (number == 0)) | ((tile == tiles - 1) & (number == groups - 1))
     first_ref, ks_ref, alpha_ref, store_ref = refs[:4]
     fields = [refs[4 + 5 * picard:9 + 5 * picard] for picard in range(ITERS)]
     staged_refs = refs[4 + 5 * ITERS:4 + 5 * ITERS + HALO]
@@ -407,7 +412,8 @@
             layer = (partner ^ (count // held)) * held + count % held
             rows.put_layer(first_sc, layer, row, entry(count))
             rows.put_layer(soil_sc, layer, row, entry(layers + count))
-        land_sc[pl.ds(row, HALO), :] = entry(2 * layers)
+        water = outside if ref is far_ref else False
+        land_sc[pl.ds(row, HALO), :] = jnp.where(water, 0.0, entry(2 * layers))
         for count, top_sc in ((2 * layers + 1, dtop_sc), (2 * layers + 2, rtop_sc)):
             value = entry(count)
             for part in range(rows.per_row):
@@ -625,6 +631,9 @@
             index = groups - 1 if upper % 2 == 0 else 0
             one, two = upper * groups + index, (upper + 1) * groups + index
             far += [(one, two), (two, one)]
+    far += [(0, 0)]
+    last = tiles * groups - (1 if tiles % 2 == 1 else groups)
+    far += [(last, last)]
 
     cells = node_cell[0]
     bed = bed_cond[0]
@@ -670,7 +679,7 @@
         [node_scratch] * 6 + [pltpu.VMEM((span * breadth // BLOCK, LANES), jnp.float32)],
         7,
     )(cells, bed, whole_section)
-    edges = jax.ShapeDtypeStruct(((2 * layers + 3) * HALO, breadth), jnp.float32)
+    edges = jax.ShapeDtypeStruct((-(-(2 * layers + 3) * HALO // 8) * 8, breadth), jnp.float32)
     near_edge, far_edge = call(
         edge_kernel, (edges, edges), [in_vmem] * (3 + groups), [], 0.1,
     )(land, diag, rhs, *received)

time: 53.1 us -> 53.1 us (level)
  no operation moved by 1% of the time
where the time goes in v13:
time: 53.1 us; the launch traced here: 52.7 us
  starting transfers between devices  20.2 us (38%)
  Pallas kernels  19.8 us (37%)
  waiting for transfers between devices  11.8 us (22%)
  between operations  0.87 us (2%)
    all_to_all x1, starting transfers between devices, on_device(): lax.all_to_all(spread, 'tile', 0, 0).reshape(tiles * stride, node_count)  7.4 us
    pallas_call x1, Pallas kernels, on_device(): call(functools.partial(river_kernel, breadth, span, stride), (riv_shape,...  6.57 us
    all_to_all x1, waiting for transfers between devices, on_device(): lax.all_to_all(partial.reshape(tiles, fold, node_count), 'tile', 0, 0)  5.75 us
    ppermute x9, starting transfers between devices, exchange(): lax.ppermute(parts[step], 'layer', [(i, i ^ step) for i in range(groups)])  5.73 us
    all_to_all x1, waiting for transfers between devices, on_device(): lax.all_to_all(spread, 'tile', 0, 0).reshape(tiles * stride, node_count)  5.06 us
    pallas_call x1, Pallas kernels, on_device(): call(stage_kernel, (own_field,) * (4 + 5 * ITERS + HALO), [in_smem] * 3 +...  4.1 us
    pallas_call x1, Pallas kernels, on_device(): call(flow_kernel, (head_shape,) * groups + (jax.ShapeDtypeStruct((span, b...  3.66 us
    all_to_all x1, starting transfers between devices, on_device(): lax.all_to_all(partial.reshape(tiles, fold, node_count), 'tile', 0, 0)  3.33 us
  transfers between devices with their start and end apart: 13, of which 4 were waited for; matrix products, arithmetic and copies ran while one was open for 0% of the time, Pallas kernels for 26%

profile of v13, /device:TPU:0, one launch (start us, length us, event | category | flops | bytes accessed | tf_op | source)
XLA Modules:
  0.0 52.7 jit_solution(7302782965487532197)
XLA Ops:
  0.7 1.4 %shard_map.122.after_ref = f32[8,24,128]{2,1,0:T(8,128)} custom-call(f32[16,128]{1,0:T(8,128)} %section_hbm.1, s32[1,256]{1,0:T(1,128)} %owner_hbm.1, s32[1,256]{1,0:T(1,128)} %local_hbm.1), custom_call_target="tpu_custom_call" | custom-call | flops 1150000000 | tf_op jit(solution)/shard_map/pallas_call | solution.py:649
  2.1 7.4 %all-to-all-start = ((f32[8,24,128]{2,1,0:T(8,128)}), f32[8,24,128]{2,1,0:T(8,128)S(1)}, u32[]{:S(2)}, u32[]{:S(2)}) async-start(f32[8,24,128]{2,1,0:T(8,128)} %shard_map.122.after_ref), calls=%async_computation | async-start | bytes 196608 | tf_op jit(solution)/shard_map/all_to_all | solution.py:659
  9.7 1.6 %collective-permute-start.1 = (f32[2,2,16,512]{3,2,1,0:T(8,128)S(1)}, f32[2,2,16,512]{3,2,1,0:T(8,128)S(1)}, u32[]{:S(2)}, u32[]{:S(2)}) collective-permute-start(f32[2,2,16,512]{3,2,1,0:T(8,128)S(1)} %get-tuple-element.49), channel_id=1, source_target_pairs={{0,2},{1,3},{2,0},{3,1},{4,6},{5,7},{6,4},{7,5},{8,10},{9,11},{10,... | collective-permute-start | bytes 393224 | tf_op jit(solution)/shard_map/ppermute | solution.py:645
  11.3 0.3 collective-permute-start.2
  11.6 5.1 %all-to-all-done = f32[8,24,128]{2,1,0:T(8,128)S(1)} async-done(((f32[8,24,128]{2,1,0:T(8,128)}), f32[8,24,128]{2,1,0:T(8,128)S(1)}, u32[]{:S(2)}, u32[]{:S(2)}) %all-to-all-start) | async-done | bytes 98336 | tf_op jit(solution)/shard_map/all_to_all | solution.py:659
  16.7 6.6 %shard_map.123 = (f32[64,128]{1,0:T(8,128)S(1)}, f32[64,128]{1,0:T(8,128)S(1)}, f32[256,128]{1,0:T(8,128)S(1)}, f32[1,256]{1,0:T(1,128)S(1)}) custom-call(s32[256,128]{1,0:T(8,128)S(1)} %bitcast.5, f32[256,128]{1,0:T(8,128)S(1)} %bitcast.7, f32[192,128]{1,0:T(8,128)S(1)} %bitcast.4), custom_call_target="tpu_custom_call" | custom-call | flops 8049999872 | tf_op jit(solution)/shard_map/pallas_call | solution.py:670
  23.3 0.1 shard_map.125
  23.4 0.8 %collective-permute-start.3 = (f32[120,512]{1,0:T(8,128)S(1)}, f32[120,512]{1,0:T(8,128)S(1)}, u32[]{:S(2)}, u32[]{:S(2)}) collective-permute-start(f32[120,512]{1,0:T(8,128)S(1)} %get-tuple-element.51), channel_id=1, source_target_pairs={{1,2},{2,1},{3,7},{7,3},{5,6},{6,5},{4,8},{8,4},{9,10},{10,9},{11,... | collective-permute-start | bytes 737288 | tf_op jit(solution)/shard_map/ppermute | solution.py:686
  24.2 2.9 %collective-permute-start.4 = (f32[120,512]{1,0:T(8,128)S(1)}, f32[120,512]{1,0:T(8,128)S(1)}, u32[]{:S(2)}, u32[]{:S(2)}) collective-permute-start(f32[120,512]{1,0:T(8,128)S(1)} %get-tuple-element.52), channel_id=1, source_target_pairs={{0,1},{1,0},{2,3},{3,2},{4,5},{5,4},{6,7},{7,6},{8,9},{9,8},{10,11... | collective-permute-start | bytes 737288 | tf_op jit(solution)/shard_map/ppermute | solution.py:687
  27.2 4.1 %shard_map.126 = (f32[4,128,128]{2,1,0:T(8,128)S(1)}, f32[4,128,128]{2,1,0:T(8,128)S(1)}, f32[4,128,128]{2,1,0:T(8,128)S(1)}, f32[4,128,128]{2,1,0:T(8,128)S(1)}...) custom-call(f32[12]{0:T(128)S(1)} %copy-done.6, ...), custom_call_target="tpu_custom_call" | custom-call | flops 4600000000 | tf_op jit(solution)/shard_map/pallas_call | solution.py:692
  31.3 3.7 %shard_map.127 = (f32[2,16,512]{2,1,0:T(8,128)S(1)}, f32[2,16,512]{2,1,0:T(8,128)S(1)}, f32[2,16,512]{2,1,0:T(8,128)S(1)}, f32[2,16,512]{2,1,0:T(8,128)S(1)}, f32[16,512]{1,0:T(8,128)S(1)}) custom-call(f32[12]{0:T(128)S(1)} %copy-done.6, f32[12]{0:T(128)S(1)} %copy-done.7, f32[12]{0:T(128)S(1)} %copy-done.8, f32[16,512]{1,0:T(8,128)S(1)} %get-tuple-element.44.land_ref, ...), custom_call_target="tpu_custom_call" | custom-call | flops 3449999872 | tf_op jit(solution)/shard_map/pallas_call | solution.py:698
  35.0 0.1 collective-permute-start.5
  35.1 1.3 %collective-permute-start.6 = (f32[16,512]{1,0:T(8,128)S(1)}, f32[16,512]{1,0:T(8,128)S(1)}, u32[]{:S(2)}, u32[]{:S(2)}) collective-permute-start(f32[16,512]{1,0:T(8,128)S(1)} %get-tuple-element.73.refs_0_), channel_id=1, source_target_pairs={{0,2},{1,3},{2,0},{3,1},{4,6},{5,7},{6,4},{7,5},{8,10},{9,11},{10,... | collective-permute-start | bytes 98312 | tf_op jit(solution)/shard_map/ppermute | solution.py:645
  36.3 0.6 %collective-permute-start.7 = (f32[16,512]{1,0:T(8,128)S(1)}, f32[16,512]{1,0:T(8,128)S(1)}, u32[]{:S(2)}, u32[]{:S(2)}) collective-permute-start(f32[16,512]{1,0:T(8,128)S(1)} %get-tuple-element.73.refs_0_), channel_id=1, source_target_pairs={{0,3},{1,2},{2,1},{3,0},{4,7},{5,6},{6,5},{7,4},{8,11},{9,10},{10,... | collective-permute-start | bytes 98312 | tf_op jit(solution)/shard_map/ppermute | solution.py:645
  36.9 0.3 collective-permute-start.8
  37.2 1.2 %collective-permute-start.9 = (f32[2,16,512]{2,1,0:T(8,128)S(1)}, f32[2,16,512]{2,1,0:T(8,128)S(1)}, u32[]{:S(2)}, u32[]{:S(2)}) collective-permute-start(f32[2,16,512]{2,1,0:T(8,128)S(1)} %get-tuple-element.76), channel_id=1, source_target_pairs={{0,2},{1,3},{2,0},{3,1},{4,6},{5,7},{6,4},{7,5},{8,10},{9,11},{10,... | collective-permute-start | bytes 196616 | tf_op jit(solution)/shard_map/ppermute | solution.py:645
  38.5 0.3 collective-permute-start.10
  38.8 0.3 collective-permute-done.6.refs_2_
  39.0 0.7 %collective-permute-done.7.refs_3_ = f32[16,512]{1,0:T(8,128)S(1)} collective-permute-done((f32[16,512]{1,0:T(8,128)S(1)}, f32[16,512]{1,0:T(8,128)S(1)}, u32[]{:S(2)}, u32[]{:S(2)}) %collective-permute-start.7) | collective-permute-done | bytes 32800 | tf_op jit(solution)/shard_map/ppermute | solution.py:645
  39.7 2.5 %shard_map.128 = f32[32,128]{1,0:T(8,128)} custom-call(s32[256,128]{1,0:T(8,128)S(1)} %bitcast.6, f32[256,128]{1,0:T(8,128)S(1)} %bitcast.8, f32[256,128]{1,0:T(8,128)S(1)} %get-tuple-element.42.slot_section_ref, f32[1,256]{1,0:T(1,128)S(1)} %get-tuple-element.43.reach_ref, f32[16,512]{1,0:T(8,128)S(1)} %get-tuple-element.73.refs_0_, ...), custom_call_target="tpu_custom_call" | custom-call | flops 3449999872 | tf_op jit(solution)/shard_map/pallas_call | solution.py:713
  42.2 3.3 %all-to-all-start.1 = ((f32[8,4,128]{2,1,0:T(4,128)}), f32[8,4,128]{2,1,0:T(4,128)S(1)}, u32[]{:S(2)}, u32[]{:S(2)}) async-start(f32[8,4,128]{2,1,0:T(4,128)} %bitcast.3), calls=%async_computation.1 | async-start | bytes 32768 | tf_op jit(solution)/shard_map/all_to_all | solution.py:721
  45.5 0.7 %shard_map.129 = f32[2,64,512]{2,1,0:T(8,128)} custom-call(f32[2,16,512]{2,1,0:T(8,128)S(1)} %get-tuple-element.77.refs_0_, f32[2,16,512]{2,1,0:T(8,128)S(1)} %collective-permute-done.8.refs_1_, f32[2,16,512]{2,1,0:T(8,128)S(1)} %collective-permute-done.9.refs_2_, f32[2,16,512]{2,1,0:T(8,128)S(1)} %collective-permute-done.10.refs_3_), custom_call_target="tpu_custom_call" | custom-call | flops 805000000 | tf_op jit(solution)/shard_map/pallas_call | solution.py:722
  46.3 5.8 %all-to-all-done.1.terms_ref = f32[8,4,128]{2,1,0:T(4,128)S(1)} async-done(((f32[8,4,128]{2,1,0:T(4,128)}), f32[8,4,128]{2,1,0:T(4,128)S(1)}, u32[]{:S(2)}, u32[]{:S(2)}) %all-to-all-start.1) | async-done | bytes 16416 | tf_op jit(solution)/shard_map/all_to_all | solution.py:721
  52.0 0.7 %shard_map.130 = f32[16,32]{1,0:T(8,128)} custom-call(f32[8,4,128]{2,1,0:T(4,128)S(1)} %all-to-all-done.1.terms_ref), custom_call_target="tpu_custom_call" | custom-call | flops 115000000 | tf_op jit(solution)/shard_map/pallas_call | solution.py:727
  (29 shorter events, 0.2 us)
Async XLA Ops:
  0.6 8.9 %copy-start.1 = (f32[2,64,512]{2,1,0:T(8,128)S(1)}, f32[2,64,512]{2,1,0:T(8,128)}, u32[]{:S(2)}) copy-start(f32[2,64,512]{2,1,0:T(8,128)} %head_ref.1) | copy-start | bytes 786436
  0.6 8.9 %copy-start.2 = (s32[2,64,512]{2,1,0:T(8,128)S(1)}, s32[2,64,512]{2,1,0:T(8,128)}, u32[]{:S(2)}) copy-start(s32[2,64,512]{2,1,0:T(8,128)} %soil_ref.1) | copy-start | bytes 786436
  0.7 8.9 %copy-start.3 = (s32[64,512]{1,0:T(8,128)S(1)}, s32[64,512]{1,0:T(8,128)}, u32[]{:S(2)}) copy-start(s32[64,512]{1,0:T(8,128)} %land_ref.1) | copy-start | bytes 393220
  2.1 7.4 %copy-start = (f32[8,24,128]{2,1,0:T(8,128)S(1)}, f32[8,24,128]{2,1,0:T(8,128)}, u32[]{:S(2)}) copy-start(f32[8,24,128]{2,1,0:T(8,128)} %shard_map.122.after_ref) | copy-start | bytes 294916
  2.1 14.5 %all-to-all-start = ((f32[8,24,128]{2,1,0:T(8,128)}), f32[8,24,128]{2,1,0:T(8,128)S(1)}, u32[]{:S(2)}, u32[]{:S(2)}) async-start(f32[8,24,128]{2,1,0:T(8,128)} %shard_map.122.after_ref), calls=%async_computation | async-start | bytes 196608 | tf_op jit(solution)/shard_map/all_to_all | solution.py:659
  9.6 7.1 %copy-start.4 = (s32[1,256,128]{2,1,0:T(8,128)S(1)}, s32[1,256,128]{2,1,0:T(8,128)}, u32[]{:S(2)}) copy-start(s32[1,256,128]{2,1,0:T(8,128)} %param.20) | copy-start | bytes 393220
  9.6 7.1 %copy-start.5 = (f32[1,256,128]{2,1,0:T(8,128)S(1)}, f32[1,256,128]{2,1,0:T(8,128)}, u32[]{:S(2)}) copy-start(f32[1,256,128]{2,1,0:T(8,128)} %param.21) | copy-start | bytes 393220
  9.6 13.6 %collective-permute-start = (f32[2,2,16,512]{3,2,1,0:T(8,128)S(1)}, f32[2,2,16,512]{3,2,1,0:T(8,128)S(1)}, u32[]{:S(2)}, u32[]{:S(2)}) collective-permute-start(f32[2,2,16,512]{3,2,1,0:T(8,128)S(1)} %get-tuple-element.48), channel_id=1, source_target_pairs={{0,1},{1,0},{2,3},{3,2},{4,5},{5,4},{6,7},{7,6},{8,9},{9,8},{10,11... | collective-permute-start | bytes 393224 | tf_op jit(solution)/shard_map/ppermute | solution.py:645
  9.7 13.5 %collective-permute-start.1 = (f32[2,2,16,512]{3,2,1,0:T(8,128)S(1)}, f32[2,2,16,512]{3,2,1,0:T(8,128)S(1)}, u32[]{:S(2)}, u32[]{:S(2)}) collective-permute-start(f32[2,2,16,512]{3,2,1,0:T(8,128)S(1)} %get-tuple-element.49), channel_id=1, source_target_pairs={{0,2},{1,3},{2,0},{3,1},{4,6},{5,7},{6,4},{7,5},{8,10},{9,11},{10,... | collective-permute-start | bytes 393224 | tf_op jit(solution)/shard_map/ppermute | solution.py:645
  11.3 11.9 %collective-permute-start.2 = (f32[2,2,16,512]{3,2,1,0:T(8,128)S(1)}, f32[2,2,16,512]{3,2,1,0:T(8,128)S(1)}, u32[]{:S(2)}, u32[]{:S(2)}) collective-permute-start(f32[2,2,16,512]{3,2,1,0:T(8,128)S(1)} %get-tuple-element.50), channel_id=1, source_target_pairs={{0,3},{1,2},{2,1},{3,0},{4,7},{5,6},{6,5},{7,4},{8,11},{9,10},{10,... | collective-permute-start | bytes 393224 | tf_op jit(solution)/shard_map/ppermute | solution.py:645
  23.4 3.8 %copy-start.6 = (f32[12]{0:T(128)S(1)}, f32[12]{0:T(128)}, u32[]{:S(2)}) copy-start(f32[12]{0:T(128)} %kst_ref.1) | copy-start | bytes 148
  23.4 3.8 %copy-start.7 = (f32[12]{0:T(128)S(1)}, f32[12]{0:T(128)}, u32[]{:S(2)}) copy-start(f32[12]{0:T(128)} %alphat_ref.1) | copy-start | bytes 148
  23.4 3.8 %copy-start.8 = (f32[12]{0:T(128)S(1)}, f32[12]{0:T(128)}, u32[]{:S(2)}) copy-start(f32[12]{0:T(128)} %storet_ref.1) | copy-start | bytes 148
  23.4 7.9 %collective-permute-start.3 = (f32[120,512]{1,0:T(8,128)S(1)}, f32[120,512]{1,0:T(8,128)S(1)}, u32[]{:S(2)}, u32[]{:S(2)}) collective-permute-start(f32[120,512]{1,0:T(8,128)S(1)} %get-tuple-element.51), channel_id=1, source_target_pairs={{1,2},{2,1},{3,7},{7,3},{5,6},{6,5},{4,8},{8,4},{9,10},{10,9},{11,... | collective-permute-start | bytes 737288 | tf_op jit(solution)/shard_map/ppermute | solution.py:686
  24.2 7.1 %collective-permute-start.4 = (f32[120,512]{1,0:T(8,128)S(1)}, f32[120,512]{1,0:T(8,128)S(1)}, u32[]{:S(2)}, u32[]{:S(2)}) collective-permute-start(f32[120,512]{1,0:T(8,128)S(1)} %get-tuple-element.52), channel_id=1, source_target_pairs={{0,1},{1,0},{2,3},{3,2},{4,5},{5,4},{6,7},{7,6},{8,9},{9,8},{10,11... | collective-permute-start | bytes 737288 | tf_op jit(solution)/shard_map/ppermute | solution.py:687
  35.0 3.5 %collective-permute-start.5 = (f32[16,512]{1,0:T(8,128)S(1)}, f32[16,512]{1,0:T(8,128)S(1)}, u32[]{:S(2)}, u32[]{:S(2)}) collective-permute-start(f32[16,512]{1,0:T(8,128)S(1)} %get-tuple-element.73.refs_0_), channel_id=1, source_target_pairs={{0,1},{1,0},{2,3},{3,2},{4,5},{5,4},{6,7},{7,6},{8,9},{9,8},{10,11... | collective-permute-start | bytes 98312 | tf_op jit(solution)/shard_map/ppermute | solution.py:645
  35.1 3.9 %collective-permute-start.6 = (f32[16,512]{1,0:T(8,128)S(1)}, f32[16,512]{1,0:T(8,128)S(1)}, u32[]{:S(2)}, u32[]{:S(2)}) collective-permute-start(f32[16,512]{1,0:T(8,128)S(1)} %get-tuple-element.73.refs_0_), channel_id=1, source_target_pairs={{0,2},{1,3},{2,0},{3,1},{4,6},{5,7},{6,4},{7,5},{8,10},{9,11},{10,... | collective-permute-start | bytes 98312 | tf_op jit(solution)/shard_map/ppermute | solution.py:645
  36.3 3.3 %collective-permute-start.7 = (f32[16,512]{1,0:T(8,128)S(1)}, f32[16,512]{1,0:T(8,128)S(1)}, u32[]{:S(2)}, u32[]{:S(2)}) collective-permute-start(f32[16,512]{1,0:T(8,128)S(1)} %get-tuple-element.73.refs_0_), channel_id=1, source_target_pairs={{0,3},{1,2},{2,1},{3,0},{4,7},{5,6},{6,5},{7,4},{8,11},{9,10},{10,... | collective-permute-start | bytes 98312 | tf_op jit(solution)/shard_map/ppermute | solution.py:645
  36.9 5.3 %collective-permute-start.8 = (f32[2,16,512]{2,1,0:T(8,128)S(1)}, f32[2,16,512]{2,1,0:T(8,128)S(1)}, u32[]{:S(2)}, u32[]{:S(2)}) collective-permute-start(f32[2,16,512]{2,1,0:T(8,128)S(1)} %get-tuple-element.75), channel_id=1, source_target_pairs={{0,1},{1,0},{2,3},{3,2},{4,5},{5,4},{6,7},{7,6},{8,9},{9,8},{10,11... | collective-permute-start | bytes 196616 | tf_op jit(solution)/shard_map/ppermute | solution.py:645
  37.2 5.0 %collective-permute-start.9 = (f32[2,16,512]{2,1,0:T(8,128)S(1)}, f32[2,16,512]{2,1,0:T(8,128)S(1)}, u32[]{:S(2)}, u32[]{:S(2)}) collective-permute-start(f32[2,16,512]{2,1,0:T(8,128)S(1)} %get-tuple-element.76), channel_id=1, source_target_pairs={{0,2},{1,3},{2,0},{3,1},{4,6},{5,7},{6,4},{7,5},{8,10},{9,11},{10,... | collective-permute-start | bytes 196616 | tf_op jit(solution)/shard_map/ppermute | solution.py:645
  38.5 7.0 %collective-permute-start.10 = (f32[2,16,512]{2,1,0:T(8,128)S(1)}, f32[2,16,512]{2,1,0:T(8,128)S(1)}, u32[]{:S(2)}, u32[]{:S(2)}) collective-permute-start(f32[2,16,512]{2,1,0:T(8,128)S(1)} %get-tuple-element.80), channel_id=1, source_target_pairs={{0,3},{1,2},{2,1},{3,0},{4,7},{5,6},{6,5},{7,4},{8,11},{9,10},{10,... | collective-permute-start | bytes 196616 | tf_op jit(solution)/shard_map/ppermute | solution.py:645
  42.2 9.9 %all-to-all-start.1 = ((f32[8,4,128]{2,1,0:T(4,128)}), f32[8,4,128]{2,1,0:T(4,128)S(1)}, u32[]{:S(2)}, u32[]{:S(2)}) async-start(f32[8,4,128]{2,1,0:T(4,128)} %bitcast.3), calls=%async_computation.1 | async-start | bytes 32768 | tf_op jit(solution)/shard_map/all_to_all | solution.py:721

commit v14 on v13

--- a/solution.py
+++ b/solution.py
@@ -63,6 +63,11 @@
     return layer, flip, jnp.where(flip == 1, groups - 1 - layer, layer)
 
 
+def own_land(land_ref, span):
+    _, _, number = position()
+    return land_ref[pl.ds(pl.multiple_of(number * span, span), span), :].astype(jnp.float32)
+
+
 def span_at(flip, groups, layer):
     return jnp.where(flip == 1, groups - 1 - layer, layer)
 
@@ -74,11 +79,55 @@
     return block.astype(jnp.float32), (local & (width - 1)).astype(jnp.float32)
 
 
+GROUP = 64
+
+
+def scatter_sum(group, blocks, block_ref, spot_ref, value_refs):
+    block_names, spot_names = names_of(blocks), names_of(BLOCK)
+    total = None
+    for start in range(0, GROUP, GROUP // 2):
+        left, right = [], []
+        for place in range(start, start + GROUP // 2):
+            left.append(jnp.concatenate(one_hot(row_copies(block_ref, group * GROUP, place), block_names), axis=0))
+            hot = one_hot(row_copies(spot_ref, group * GROUP, place), spot_names)
+            values = [row_copies(ref, group * GROUP, place) for ref in value_refs]
+            right.append(jnp.concatenate([tile * value for value in values for tile in hot], axis=0))
+        part = lax.dot_general(
+            jnp.concatenate(left, axis=1),
+            jnp.concatenate(right, axis=1),
+            (((1,), (1,)), ((), ())),
+            preferred_element_type=jnp.float32,
+        )
+        total = part if total is None else total + part
+    return total
+
+
+def scatter_range(first, last, blocks, block_ref, spot_ref, value_refs):
+    def step(group, total):
+        return total + scatter_sum(group, blocks, block_ref, spot_ref, value_refs)
+
+    return lax.fori_loop(first, last, step, jnp.zeros((blocks, BLOCK * len(value_refs)), jnp.float32))
+
+
+def early_groups(slots):
+    return slots // GROUP // 2
+
+
+def early_kernel(breadth, span, cells_ref, bed_ref, block_ref, spot_ref, high_ref, low_ref, early_ref):
+    _, _, number = position()
+    block_ref[...], spot_ref[...] = split_cells(cells_ref[...], number * span, breadth, BLOCK)
+    high, low = bf16_pieces(bed_ref[...], 2)
+    high_ref[...] = high.astype(jnp.float32)
+    low_ref[...] = low.astype(jnp.float32)
+    early_ref[...] = scatter_range(
+        0, early_groups(cells_ref.shape[0]), early_ref.shape[0], block_ref, spot_ref, (high_ref, low_ref)
+    )
+
+
 def river_kernel(
-    breadth, span, stride, cells_ref, bed_ref, section_ref,
-    diag_ref, rhs_ref, slot_section_ref, reach_ref, block_sc, spot_sc, dhigh_sc, dlow_sc, rhigh_sc, rlow_sc, sum_sc,
+    stride, bed_ref, section_ref, block_ref, spot_ref, dhigh_ref, dlow_ref, early_ref,
+    diag_ref, rhs_ref, slot_section_ref, reach_ref, rhigh_sc, rlow_sc, sum_sc,
 ):
-    _, _, number = position()
     rows = section_ref.shape[0]
     slots = reach_ref.shape[1]
     first = (lax.axis_index("tile") + 1) * stride - 8
@@ -93,43 +142,19 @@
             pick, piece, (((0,), (0,)), ((), ())), preferred_element_type=jnp.float32
         )
     slot_section_ref[...] = picked
-
-    block, spot = split_cells(cells_ref[...], number * span, breadth, BLOCK)
-    block_sc[...] = block
-    spot_sc[...] = spot
-    bed = bed_ref[...]
-    for value, high_sc, low_sc in ((bed, dhigh_sc, dlow_sc), (bed * picked, rhigh_sc, rlow_sc)):
-        high, low = bf16_pieces(value, 2)
-        high_sc[...] = high.astype(jnp.float32)
-        low_sc[...] = low.astype(jnp.float32)
+    high, low = bf16_pieces(bed_ref[...] * picked, 2)
+    rhigh_sc[...] = high.astype(jnp.float32)
+    rlow_sc[...] = low.astype(jnp.float32)
+
     share = LANES // BLOCK
     blocks = share * diag_ref.shape[0]
-    group = 64
-    block_names, spot_names = names_of(blocks), names_of(BLOCK)
-
-    def matmul(first, places):
-        left, right = [], []
-        for place in places:
-            left.append(jnp.concatenate(one_hot(row_copies(block_sc, first, place), block_names), axis=0))
-            hot = one_hot(row_copies(spot_sc, first, place), spot_names)
-            values = [row_copies(ref, first, place) for ref in (dhigh_sc, dlow_sc, rhigh_sc, rlow_sc)]
-            right.append(jnp.concatenate([tile * value for value in values for tile in hot], axis=0))
-        return lax.dot_general(
-            jnp.concatenate(left, axis=1),
-            jnp.concatenate(right, axis=1),
-            (((1,), (1,)), ((), ())),
-            preferred_element_type=jnp.float32,
-        )
-
-    def step(count, total):
-        first = count * group
-        half = group // 2
-        return total + (matmul(first, range(half)) + matmul(first, range(half, group)))
-
-    total = lax.fori_loop(0, slots // group, step, jnp.zeros((blocks, 4 * BLOCK), jnp.float32))
+    middle = early_groups(slots)
+    rhs_only = scatter_range(0, middle, blocks, block_ref, spot_ref, (rhigh_sc, rlow_sc))
+    both = scatter_range(
+        middle, slots // GROUP, blocks, block_ref, spot_ref, (dhigh_ref, dlow_ref, rhigh_sc, rlow_sc)
+    )
     low_half = lax.broadcasted_iota(jnp.int32, diag_ref.shape, 1) < BLOCK
-    for count, ref in ((0, diag_ref), (1, rhs_ref)):
-        part = total[:, count * LANES:(count + 1) * LANES]
+    for part, ref in ((both[:, :LANES] + early_ref[...], diag_ref), (both[:, LANES:] + rhs_only, rhs_ref)):
         sum_sc[...] = part + pltpu.roll(part, BLOCK, 1)
         ref[...] = jnp.where(
             low_half, sum_sc[pl.ds(0, blocks // share, stride=share), :], sum_sc[pl.ds(1, blocks // share, stride=share), :]
@@ -153,7 +178,8 @@
             for held_layer in range(held):
                 put_edges(entry, block_ref[kind, held_layer, :HALO, :], block_ref[kind, held_layer, span - HALO:, :])
                 entry += 1
-    put_edges(entry, land_ref[:HALO, :], land_ref[span - HALO:, :])
+    land = own_land(land_ref, span)
+    put_edges(entry, land[:HALO], land[span - HALO:])
     for ref in (diag_ref, rhs_ref):
         entry += 1
         for part in range(per_row):
@@ -182,10 +208,9 @@
         spread_ref[tile] = payload
 
 
-def prepare_kernel(head_ref, soil_ref, land_ref, after_ref, *refs):
+def prepare_kernel(head_ref, soil_ref, after_ref, *refs):
     del after_ref
-    groups = lax.axis_size("layer")
-    block_refs, land_out_ref = refs[:groups], refs[groups]
+    groups = len(refs)
     held, across, _ = head_ref.shape
     span = across // groups
     own, flip, _ = position()
@@ -193,8 +218,7 @@
     def rows_of(target):
         return pl.ds(pl.multiple_of(span_at(flip, groups, target) * span, span), span)
 
-    land_out_ref[...] = land_ref[rows_of(own), :].astype(jnp.float32)
-    for step, block_ref in enumerate(block_refs):
+    for step, block_ref in enumerate(refs):
         rows = rows_of(own ^ step)
         for layer in range(held):
             block_ref[0, layer] = head_ref[layer, rows, :]
@@ -325,7 +349,7 @@
     _, held, span, breadth = block_refs[0].shape
     layers = groups * held
     rows = Rows(layers, breadth)
-    faces = Faces(rows, land_ref[...], lands)
+    faces = Faces(rows, own_land(land_ref, span), lands)
     top = lax.broadcasted_iota(jnp.int32, (layers, breadth), 0) == 0
 
     for step, block_ref in enumerate(block_refs):
@@ -400,7 +424,7 @@
     rows = Rows(layers, breadth)
     side = HALO * rows.per_row
 
-    land_sc[pl.ds(HALO, span), :] = land_ref[...]
+    land_sc[pl.ds(HALO, span), :] = own_land(land_ref, span)
     dtop_sc[pl.ds(side, span * rows.per_row), :] = diag_ref[...]
     rtop_sc[pl.ds(side, span * rows.per_row), :] = rhs_ref[...]
 
@@ -657,32 +681,30 @@
         1, VMEM_MOST,
     )(section, cross_owner, cross_local)
     whole_section = lax.all_to_all(spread, "tile", 0, 0).reshape(tiles * stride, node_count)
-    *own_blocks, land = call(
+    own_blocks = call(
         prepare_kernel,
-        (jax.ShapeDtypeStruct((2, held, span, breadth), jnp.float32),) * groups
-        + (jax.ShapeDtypeStruct((span, breadth), jnp.float32),),
-        [in_vmem] * 3 + [in_hbm], [], 0.5,
-    )(head_start, soil_class, land_mask, spread)
+        (jax.ShapeDtypeStruct((2, held, span, breadth), jnp.float32),) * groups,
+        [in_vmem] * 2 + [in_hbm], [], 0.5,
+    )(head_start, soil_class, spread)
     received = exchange(own_blocks)
 
     node_scratch = pltpu.VMEM((slots, LANES), jnp.float32)
     riv_shape = jax.ShapeDtypeStruct((blocks, LANES), jnp.float32)
+    node_field = jax.ShapeDtypeStruct((slots, LANES), jnp.float32)
+    groups_of_cells = span * breadth // BLOCK
+    early = call(
+        functools.partial(early_kernel, breadth, span),
+        (node_field,) * 4 + (jax.ShapeDtypeStruct((groups_of_cells, LANES), jnp.float32),), [in_vmem] * 2, [], 2.5,
+    )(cells, bed)
     diag, rhs, slot_section, reach = call(
-        functools.partial(river_kernel, breadth, span, stride),
-        (
-            riv_shape,
-            riv_shape,
-            jax.ShapeDtypeStruct((slots, node_count), jnp.float32),
-            jax.ShapeDtypeStruct((1, slots), jnp.float32),
-        ),
-        [in_vmem] * 3,
-        [node_scratch] * 6 + [pltpu.VMEM((span * breadth // BLOCK, LANES), jnp.float32)],
-        7,
-    )(cells, bed, whole_section)
+        functools.partial(river_kernel, stride),
+        (riv_shape, riv_shape, node_field, jax.ShapeDtypeStruct((1, slots), jnp.float32)),
+        [in_vmem] * 7, [node_scratch] * 2 + [pltpu.VMEM((groups_of_cells, LANES), jnp.float32)], 6,
+    )(bed, whole_section, *early)
     edges = jax.ShapeDtypeStruct((-(-(2 * layers + 3) * HALO // 8) * 8, breadth), jnp.float32)
     near_edge, far_edge = call(
         edge_kernel, (edges, edges), [in_vmem] * (3 + groups), [], 0.1,
-    )(land, diag, rhs, *received)
+    )(land_mask, diag, rhs, *received)
     far_halo = lax.ppermute(far_edge, FLAT, far)
     near_halo = lax.ppermute(near_edge, "layer", near)
 
@@ -693,7 +715,7 @@
         stage_kernel, (own_field,) * (4 + 5 * ITERS + HALO), [in_smem] * 3 + [in_vmem] * (3 + groups),
         [pltpu.VMEM(own_field.shape, jnp.float32)] + [pltpu.VMEM((span, breadth), jnp.float32)] * 3,
         4,
-    )(ks_table, alpha_table, store_table, land, diag, rhs, *received)
+    )(ks_table, alpha_table, store_table, land_mask, diag, rhs, *received)
     head_shape = jax.ShapeDtypeStruct((held, span, breadth), jnp.float32)
     *heads, top = call(
         flow_kernel,
@@ -704,7 +726,7 @@
         + [pltpu.VMEM((window * per_row, LANES), jnp.float32)] * 2
         + [pltpu.VMEM((window, breadth), jnp.float32)] * 3,
         3,
-    )(ks_table, alpha_table, store_table, land, far_halo, near_halo, diag, rhs, *staged)
+    )(ks_table, alpha_table, store_table, land_mask, far_halo, near_halo, diag, rhs, *staged)
     tops = exchange([top] * groups)
     backs = exchange(heads)
 

time: 53.1 us -> 51.4 us (0.968)
  waiting for transfers between devices: 11.8 us -> 10.2 us
    all_to_all x1, waiting for transfers between devices: 5.06 us -> 3.49 us  [on_device(): lax.all_to_all(spread, 'tile', 0, 0).reshape(tiles * stride, node_count)]
    pallas_call x1 -> x2, Pallas kernels: 6.57 us -> 6.55 us  [the longest x1 4.99 us: on_device(): call(functools.partial(river_kernel, stride), (riv_shape, riv_shape, node...]
  transfers between devices with their start and end apart: 13 -> 13, of which waited for: 4 -> 4; matrix products, arithmetic and copies ran while one was open for 0% -> 0% of each run, Pallas kernels for 26% -> 27%
where the time goes in v14:
time: 51.4 us; the launch traced here: 51.1 us
  starting transfers between devices  20.2 us (39%)
  Pallas kernels  19.8 us (39%)
  waiting for transfers between devices  10.2 us (20%)
  between operations  0.87 us (2%)
    all_to_all x1, starting transfers between devices, on_device(): lax.all_to_all(spread, 'tile', 0, 0).reshape(tiles * stride, node_count)  7.4 us
    all_to_all x1, waiting for transfers between devices, on_device(): lax.all_to_all(partial.reshape(tiles, fold, node_count), 'tile', 0, 0)  5.75 us
    ppermute x9, starting transfers between devices, exchange(): lax.ppermute(parts[step], 'layer', [(i, i ^ step) for i in range(groups)])  5.73 us
    pallas_call x1, Pallas kernels, on_device(): call(functools.partial(river_kernel, stride), (riv_shape, riv_shape, node...  4.99 us
    pallas_call x1, Pallas kernels, on_device(): call(stage_kernel, (own_field,) * (4 + 5 * ITERS + HALO), [in_smem] * 3 +...  4.1 us
    pallas_call x1, Pallas kernels, on_device(): call(flow_kernel, (head_shape,) * groups + (jax.ShapeDtypeStruct((span, b...  3.67 us
    all_to_all x1, waiting for transfers between devices, on_device(): lax.all_to_all(spread, 'tile', 0, 0).reshape(tiles * stride, node_count)  3.49 us
    all_to_all x1, starting transfers between devices, on_device(): lax.all_to_all(partial.reshape(tiles, fold, node_count), 'tile', 0, 0)  3.32 us
  transfers between devices with their start and end apart: 13, of which 4 were waited for; matrix products, arithmetic and copies ran while one was open for 0% of the time, Pallas kernels for 27%

profile of v14, /device:TPU:0, one launch (start us, length us, event | category | flops | bytes accessed | tf_op | source)
XLA Modules:
  0.0 51.1 jit_solution(7377036412373566468)
XLA Ops:
  0.7 1.4 %shard_map.122.after_ref = f32[8,24,128]{2,1,0:T(8,128)} custom-call(f32[16,128]{1,0:T(8,128)} %section_hbm.1, s32[1,256]{1,0:T(1,128)} %owner_hbm.1, s32[1,256]{1,0:T(1,128)} %local_hbm.1), custom_call_target="tpu_custom_call" | custom-call | flops 1150000000 | tf_op jit(solution)/shard_map/pallas_call | solution.py:673
  2.1 7.4 %all-to-all-start = ((f32[8,24,128]{2,1,0:T(8,128)}), f32[8,24,128]{2,1,0:T(8,128)S(1)}, u32[]{:S(2)}, u32[]{:S(2)}) async-start(f32[8,24,128]{2,1,0:T(8,128)} %shard_map.122.after_ref), calls=%async_computation | async-start | bytes 196608 | tf_op jit(solution)/shard_map/all_to_all | solution.py:683
  9.7 1.6 %collective-permute-start.1 = (f32[2,2,16,512]{3,2,1,0:T(8,128)S(1)}, f32[2,2,16,512]{3,2,1,0:T(8,128)S(1)}, u32[]{:S(2)}, u32[]{:S(2)}) collective-permute-start(f32[2,2,16,512]{3,2,1,0:T(8,128)S(1)} %get-tuple-element.57), channel_id=1, source_target_pairs={{0,2},{1,3},{2,0},{3,1},{4,6},{5,7},{6,4},{7,5},{8,10},{9,11},{10,... | collective-permute-start | bytes 393224 | tf_op jit(solution)/shard_map/ppermute | solution.py:669
  11.3 0.3 collective-permute-start.2
  11.6 1.6 %shard_map.123 = (f32[256,128]{1,0:T(8,128)S(1)}, f32[256,128]{1,0:T(8,128)S(1)}, f32[256,128]{1,0:T(8,128)S(1)}, f32[256,128]{1,0:T(8,128)S(1)}, f32[128,128]{1,0:T(8,128)S(1)}) custom-call(s32[256,128]{1,0:T(8,128)S(1)} %bitcast.8, f32[256,128]{1,0:T(8,128)S(1)} %bitcast.5), custom_call_target="tpu_custom_call" | custom-call | flops 2875000064 | tf_op jit(solution)/shard_map/pallas_call | solution.py:695
  13.1 3.5 %all-to-all-done = f32[8,24,128]{2,1,0:T(8,128)S(1)} async-done(((f32[8,24,128]{2,1,0:T(8,128)}), f32[8,24,128]{2,1,0:T(8,128)S(1)}, u32[]{:S(2)}, u32[]{:S(2)}) %all-to-all-start) | async-done | bytes 98336 | tf_op jit(solution)/shard_map/all_to_all | solution.py:683
  16.6 5.0 %shard_map.124 = (f32[64,128]{1,0:T(8,128)S(1)}, f32[64,128]{1,0:T(8,128)S(1)}, f32[256,128]{1,0:T(8,128)S(1)}, f32[1,256]{1,0:T(1,128)S(1)}) custom-call(f32[256,128]{1,0:T(8,128)S(1)} %bitcast.6, f32[192,128]{1,0:T(8,128)S(1)} %bitcast.4, f32[256,128]{1,0:T(8,128)S(1)} %get-tuple-element.46.block_ref, f32[256,128]{1,0:T(8,128)S(1)} %get-tuple-element.47.spot_ref, ...), custom_call_target="tpu_custom_call" | custom-call | flops 6899999744 | tf_op jit(solution)/shard_map/pallas_call | solution.py:699
  21.8 0.8 %collective-permute-start.3 = (f32[120,512]{1,0:T(8,128)S(1)}, f32[120,512]{1,0:T(8,128)S(1)}, u32[]{:S(2)}, u32[]{:S(2)}) collective-permute-start(f32[120,512]{1,0:T(8,128)S(1)} %get-tuple-element.59), channel_id=1, source_target_pairs={{1,2},{2,1},{3,7},{7,3},{5,6},{6,5},{4,8},{8,4},{9,10},{10,9},{11,... | collective-permute-start | bytes 737288 | tf_op jit(solution)/shard_map/ppermute | solution.py:708
  22.6 2.9 %collective-permute-start.4 = (f32[120,512]{1,0:T(8,128)S(1)}, f32[120,512]{1,0:T(8,128)S(1)}, u32[]{:S(2)}, u32[]{:S(2)}) collective-permute-start(f32[120,512]{1,0:T(8,128)S(1)} %get-tuple-element.60), channel_id=1, source_target_pairs={{0,1},{1,0},{2,3},{3,2},{4,5},{5,4},{6,7},{7,6},{8,9},{9,8},{10,11... | collective-permute-start | bytes 737288 | tf_op jit(solution)/shard_map/ppermute | solution.py:709
  25.6 4.1 %shard_map.127 = (f32[4,128,128]{2,1,0:T(8,128)S(1)}, f32[4,128,128]{2,1,0:T(8,128)S(1)}, f32[4,128,128]{2,1,0:T(8,128)S(1)}, f32[4,128,128]{2,1,0:T(8,128)S(1)}...) custom-call(f32[12]{0:T(128)S(1)} %copy-done.6, ...), custom_call_target="tpu_custom_call" | custom-call | flops 4600000000 | tf_op jit(solution)/shard_map/pallas_call | solution.py:714
  29.7 3.7 %shard_map.128 = (f32[2,16,512]{2,1,0:T(8,128)S(1)}, f32[2,16,512]{2,1,0:T(8,128)S(1)}, f32[2,16,512]{2,1,0:T(8,128)S(1)}, f32[2,16,512]{2,1,0:T(8,128)S(1)}, f32[16,512]{1,0:T(8,128)S(1)}) custom-call(f32[12]{0:T(128)S(1)} %copy-done.6, f32[12]{0:T(128)S(1)} %copy-done.7, f32[12]{0:T(128)S(1)} %copy-done.8, s32[64,512]{1,0:T(8,128)S(1)} %copy-done, ...), custom_call_target="tpu_custom_call" | custom-call | flops 3449999872 | tf_op jit(solution)/shard_map/pallas_call | solution.py:720
  33.4 0.1 collective-permute-start.5
  33.5 1.3 %collective-permute-start.6 = (f32[16,512]{1,0:T(8,128)S(1)}, f32[16,512]{1,0:T(8,128)S(1)}, u32[]{:S(2)}, u32[]{:S(2)}) collective-permute-start(f32[16,512]{1,0:T(8,128)S(1)} %get-tuple-element.81.refs_0_), channel_id=1, source_target_pairs={{0,2},{1,3},{2,0},{3,1},{4,6},{5,7},{6,4},{7,5},{8,10},{9,11},{10,... | collective-permute-start | bytes 98312 | tf_op jit(solution)/shard_map/ppermute | solution.py:669
  34.8 0.6 %collective-permute-start.7 = (f32[16,512]{1,0:T(8,128)S(1)}, f32[16,512]{1,0:T(8,128)S(1)}, u32[]{:S(2)}, u32[]{:S(2)}) collective-permute-start(f32[16,512]{1,0:T(8,128)S(1)} %get-tuple-element.81.refs_0_), channel_id=1, source_target_pairs={{0,3},{1,2},{2,1},{3,0},{4,7},{5,6},{6,5},{7,4},{8,11},{9,10},{10,... | collective-permute-start | bytes 98312 | tf_op jit(solution)/shard_map/ppermute | solution.py:669
  35.3 0.3 collective-permute-start.8
  35.7 1.2 %collective-permute-start.9 = (f32[2,16,512]{2,1,0:T(8,128)S(1)}, f32[2,16,512]{2,1,0:T(8,128)S(1)}, u32[]{:S(2)}, u32[]{:S(2)}) collective-permute-start(f32[2,16,512]{2,1,0:T(8,128)S(1)} %get-tuple-element.84), channel_id=1, source_target_pairs={{0,2},{1,3},{2,0},{3,1},{4,6},{5,7},{6,4},{7,5},{8,10},{9,11},{10,... | collective-permute-start | bytes 196616 | tf_op jit(solution)/shard_map/ppermute | solution.py:669
  36.9 0.3 collective-permute-start.10
  37.2 0.3 collective-permute-done.6.refs_2_
  37.4 0.7 %collective-permute-done.7.refs_3_ = f32[16,512]{1,0:T(8,128)S(1)} collective-permute-done((f32[16,512]{1,0:T(8,128)S(1)}, f32[16,512]{1,0:T(8,128)S(1)}, u32[]{:S(2)}, u32[]{:S(2)}) %collective-permute-start.7) | collective-permute-done | bytes 32800 | tf_op jit(solution)/shard_map/ppermute | solution.py:669
  38.1 2.5 %shard_map.129 = f32[32,128]{1,0:T(8,128)} custom-call(s32[256,128]{1,0:T(8,128)S(1)} %bitcast.9, f32[256,128]{1,0:T(8,128)S(1)} %bitcast.7, f32[256,128]{1,0:T(8,128)S(1)} %get-tuple-element.51.slot_section_ref, f32[1,256]{1,0:T(1,128)S(1)} %get-tuple-element.52.reach_ref, f32[16,512]{1,0:T(8,128)S(1)} %get-tuple-element.81.refs_0_, ...), custom_call_target="tpu_custom_call" | custom-call | flops 3449999872 | tf_op jit(solution)/shard_map/pallas_call | solution.py:735
  40.6 3.3 %all-to-all-start.1 = ((f32[8,4,128]{2,1,0:T(4,128)}), f32[8,4,128]{2,1,0:T(4,128)S(1)}, u32[]{:S(2)}, u32[]{:S(2)}) async-start(f32[8,4,128]{2,1,0:T(4,128)} %bitcast.3), calls=%async_computation.1 | async-start | bytes 32768 | tf_op jit(solution)/shard_map/all_to_all | solution.py:743
  43.9 0.7 %shard_map.130 = f32[2,64,512]{2,1,0:T(8,128)} custom-call(f32[2,16,512]{2,1,0:T(8,128)S(1)} %get-tuple-element.85.refs_0_, f32[2,16,512]{2,1,0:T(8,128)S(1)} %collective-permute-done.8.refs_1_, f32[2,16,512]{2,1,0:T(8,128)S(1)} %collective-permute-done.9.refs_2_, f32[2,16,512]{2,1,0:T(8,128)S(1)} %collective-permute-done.10.refs_3_), custom_call_target="tpu_custom_call" | custom-call | flops 805000000 | tf_op jit(solution)/shard_map/pallas_call | solution.py:744
  44.7 5.8 %all-to-all-done.1.terms_ref = f32[8,4,128]{2,1,0:T(4,128)S(1)} async-done(((f32[8,4,128]{2,1,0:T(4,128)}), f32[8,4,128]{2,1,0:T(4,128)S(1)}, u32[]{:S(2)}, u32[]{:S(2)}) %all-to-all-start.1) | async-done | bytes 16416 | tf_op jit(solution)/shard_map/all_to_all | solution.py:743
  50.4 0.7 %shard_map.131 = f32[16,32]{1,0:T(8,128)} custom-call(f32[8,4,128]{2,1,0:T(4,128)S(1)} %all-to-all-done.1.terms_ref), custom_call_target="tpu_custom_call" | custom-call | flops 115000000 | tf_op jit(solution)/shard_map/pallas_call | solution.py:749
  (30 shorter events, 0.3 us)
Async XLA Ops:
  0.6 8.9 %copy-start.2 = (f32[2,64,512]{2,1,0:T(8,128)S(1)}, f32[2,64,512]{2,1,0:T(8,128)}, u32[]{:S(2)}) copy-start(f32[2,64,512]{2,1,0:T(8,128)} %head_ref.1) | copy-start | bytes 786436
  0.6 8.9 %copy-start.3 = (s32[2,64,512]{2,1,0:T(8,128)S(1)}, s32[2,64,512]{2,1,0:T(8,128)}, u32[]{:S(2)}) copy-start(s32[2,64,512]{2,1,0:T(8,128)} %soil_ref.1) | copy-start | bytes 786436
  2.1 7.4 %copy-start.1 = (f32[8,24,128]{2,1,0:T(8,128)S(1)}, f32[8,24,128]{2,1,0:T(8,128)}, u32[]{:S(2)}) copy-start(f32[8,24,128]{2,1,0:T(8,128)} %shard_map.122.after_ref) | copy-start | bytes 294916
  2.1 14.5 %all-to-all-start = ((f32[8,24,128]{2,1,0:T(8,128)}), f32[8,24,128]{2,1,0:T(8,128)S(1)}, u32[]{:S(2)}, u32[]{:S(2)}) async-start(f32[8,24,128]{2,1,0:T(8,128)} %shard_map.122.after_ref), calls=%async_computation | async-start | bytes 196608 | tf_op jit(solution)/shard_map/all_to_all | solution.py:683
  9.5 2.0 %copy-start.4 = (f32[1,256,128]{2,1,0:T(8,128)S(1)}, f32[1,256,128]{2,1,0:T(8,128)}, u32[]{:S(2)}) copy-start(f32[1,256,128]{2,1,0:T(8,128)} %param.21) | copy-start | bytes 393220
  9.5 2.0 %copy-start.5 = (s32[1,256,128]{2,1,0:T(8,128)S(1)}, s32[1,256,128]{2,1,0:T(8,128)}, u32[]{:S(2)}) copy-start(s32[1,256,128]{2,1,0:T(8,128)} %param.20) | copy-start | bytes 393220
  9.6 12.0 %collective-permute-start = (f32[2,2,16,512]{3,2,1,0:T(8,128)S(1)}, f32[2,2,16,512]{3,2,1,0:T(8,128)S(1)}, u32[]{:S(2)}, u32[]{:S(2)}) collective-permute-start(f32[2,2,16,512]{3,2,1,0:T(8,128)S(1)} %get-tuple-element.56), channel_id=1, source_target_pairs={{0,1},{1,0},{2,3},{3,2},{4,5},{5,4},{6,7},{7,6},{8,9},{9,8},{10,11... | collective-permute-start | bytes 393224 | tf_op jit(solution)/shard_map/ppermute | solution.py:669
  9.7 11.9 %collective-permute-start.1 = (f32[2,2,16,512]{3,2,1,0:T(8,128)S(1)}, f32[2,2,16,512]{3,2,1,0:T(8,128)S(1)}, u32[]{:S(2)}, u32[]{:S(2)}) collective-permute-start(f32[2,2,16,512]{3,2,1,0:T(8,128)S(1)} %get-tuple-element.57), channel_id=1, source_target_pairs={{0,2},{1,3},{2,0},{3,1},{4,6},{5,7},{6,4},{7,5},{8,10},{9,11},{10,... | collective-permute-start | bytes 393224 | tf_op jit(solution)/shard_map/ppermute | solution.py:669
  11.3 10.4 %collective-permute-start.2 = (f32[2,2,16,512]{3,2,1,0:T(8,128)S(1)}, f32[2,2,16,512]{3,2,1,0:T(8,128)S(1)}, u32[]{:S(2)}, u32[]{:S(2)}) collective-permute-start(f32[2,2,16,512]{3,2,1,0:T(8,128)S(1)} %get-tuple-element.58), channel_id=1, source_target_pairs={{0,3},{1,2},{2,1},{3,0},{4,7},{5,6},{6,5},{7,4},{8,11},{9,10},{10,... | collective-permute-start | bytes 393224 | tf_op jit(solution)/shard_map/ppermute | solution.py:669
  16.6 5.0 %copy-start = (s32[64,512]{1,0:T(8,128)S(1)}, s32[64,512]{1,0:T(8,128)}, u32[]{:S(2)}) copy-start(s32[64,512]{1,0:T(8,128)} %land_ref.5) | copy-start | bytes 393220
  21.8 3.8 %copy-start.6 = (f32[12]{0:T(128)S(1)}, f32[12]{0:T(128)}, u32[]{:S(2)}) copy-start(f32[12]{0:T(128)} %kst_ref.1) | copy-start | bytes 148
  21.8 3.8 %copy-start.7 = (f32[12]{0:T(128)S(1)}, f32[12]{0:T(128)}, u32[]{:S(2)}) copy-start(f32[12]{0:T(128)} %alphat_ref.1) | copy-start | bytes 148
  21.8 3.8 %copy-start.8 = (f32[12]{0:T(128)S(1)}, f32[12]{0:T(128)}, u32[]{:S(2)}) copy-start(f32[12]{0:T(128)} %storet_ref.1) | copy-start | bytes 148
  21.8 7.9 %collective-permute-start.3 = (f32[120,512]{1,0:T(8,128)S(1)}, f32[120,512]{1,0:T(8,128)S(1)}, u32[]{:S(2)}, u32[]{:S(2)}) collective-permute-start(f32[120,512]{1,0:T(8,128)S(1)} %get-tuple-element.59), channel_id=1, source_target_pairs={{1,2},{2,1},{3,7},{7,3},{5,6},{6,5},{4,8},{8,4},{9,10},{10,9},{11,... | collective-permute-start | bytes 737288 | tf_op jit(solution)/shard_map/ppermute | solution.py:708
  22.6 7.1 %collective-permute-start.4 = (f32[120,512]{1,0:T(8,128)S(1)}, f32[120,512]{1,0:T(8,128)S(1)}, u32[]{:S(2)}, u32[]{:S(2)}) collective-permute-start(f32[120,512]{1,0:T(8,128)S(1)} %get-tuple-element.60), channel_id=1, source_target_pairs={{0,1},{1,0},{2,3},{3,2},{4,5},{5,4},{6,7},{7,6},{8,9},{9,8},{10,11... | collective-permute-start | bytes 737288 | tf_op jit(solution)/shard_map/ppermute | solution.py:709
  33.4 3.5 %collective-permute-start.5 = (f32[16,512]{1,0:T(8,128)S(1)}, f32[16,512]{1,0:T(8,128)S(1)}, u32[]{:S(2)}, u32[]{:S(2)}) collective-permute-start(f32[16,512]{1,0:T(8,128)S(1)} %get-tuple-element.81.refs_0_), channel_id=1, source_target_pairs={{0,1},{1,0},{2,3},{3,2},{4,5},{5,4},{6,7},{7,6},{8,9},{9,8},{10,11... | collective-permute-start | bytes 98312 | tf_op jit(solution)/shard_map/ppermute | solution.py:669
  33.5 4.0 %collective-permute-start.6 = (f32[16,512]{1,0:T(8,128)S(1)}, f32[16,512]{1,0:T(8,128)S(1)}, u32[]{:S(2)}, u32[]{:S(2)}) collective-permute-start(f32[16,512]{1,0:T(8,128)S(1)} %get-tuple-element.81.refs_0_), channel_id=1, source_target_pairs={{0,2},{1,3},{2,0},{3,1},{4,6},{5,7},{6,4},{7,5},{8,10},{9,11},{10,... | collective-permute-start | bytes 98312 | tf_op jit(solution)/shard_map/ppermute | solution.py:669
  34.8 3.3 %collective-permute-start.7 = (f32[16,512]{1,0:T(8,128)S(1)}, f32[16,512]{1,0:T(8,128)S(1)}, u32[]{:S(2)}, u32[]{:S(2)}) collective-permute-start(f32[16,512]{1,0:T(8,128)S(1)} %get-tuple-element.81.refs_0_), channel_id=1, source_target_pairs={{0,3},{1,2},{2,1},{3,0},{4,7},{5,6},{6,5},{7,4},{8,11},{9,10},{10,... | collective-permute-start | bytes 98312 | tf_op jit(solution)/shard_map/ppermute | solution.py:669
  35.3 5.3 %collective-permute-start.8 = (f32[2,16,512]{2,1,0:T(8,128)S(1)}, f32[2,16,512]{2,1,0:T(8,128)S(1)}, u32[]{:S(2)}, u32[]{:S(2)}) collective-permute-start(f32[2,16,512]{2,1,0:T(8,128)S(1)} %get-tuple-element.83), channel_id=1, source_target_pairs={{0,1},{1,0},{2,3},{3,2},{4,5},{5,4},{6,7},{7,6},{8,9},{9,8},{10,11... | collective-permute-start | bytes 196616 | tf_op jit(solution)/shard_map/ppermute | solution.py:669
  35.7 4.9 %collective-permute-start.9 = (f32[2,16,512]{2,1,0:T(8,128)S(1)}, f32[2,16,512]{2,1,0:T(8,128)S(1)}, u32[]{:S(2)}, u32[]{:S(2)}) collective-permute-start(f32[2,16,512]{2,1,0:T(8,128)S(1)} %get-tuple-element.84), channel_id=1, source_target_pairs={{0,2},{1,3},{2,0},{3,1},{4,6},{5,7},{6,4},{7,5},{8,10},{9,11},{10,... | collective-permute-start | bytes 196616 | tf_op jit(solution)/shard_map/ppermute | solution.py:669
  36.9 7.0 %collective-permute-start.10 = (f32[2,16,512]{2,1,0:T(8,128)S(1)}, f32[2,16,512]{2,1,0:T(8,128)S(1)}, u32[]{:S(2)}, u32[]{:S(2)}) collective-permute-start(f32[2,16,512]{2,1,0:T(8,128)S(1)} %get-tuple-element.88), channel_id=1, source_target_pairs={{0,3},{1,2},{2,1},{3,0},{4,7},{5,6},{6,5},{7,4},{8,11},{9,10},{10,... | collective-permute-start | bytes 196616 | tf_op jit(solution)/shard_map/ppermute | solution.py:669
  40.6 9.8 %all-to-all-start.1 = ((f32[8,4,128]{2,1,0:T(4,128)}), f32[8,4,128]{2,1,0:T(4,128)S(1)}, u32[]{:S(2)}, u32[]{:S(2)}) async-start(f32[8,4,128]{2,1,0:T(4,128)} %bitcast.3), calls=%async_computation.1 | async-start | bytes 32768 | tf_op jit(solution)/shard_map/all_to_all | solution.py:743

commit v15 on v14

--- a/solution.py
+++ b/solution.py
@@ -110,7 +110,7 @@
 
 
 def early_groups(slots):
-    return slots // GROUP // 2
+    return slots // GROUP * 3 // 4
 
 
 def early_kernel(breadth, span, cells_ref, bed_ref, block_ref, spot_ref, high_ref, low_ref, early_ref):
@@ -162,30 +162,30 @@
 
 
 def edge_kernel(land_ref, diag_ref, rhs_ref, *refs):
-    block_refs, (near_ref, far_ref) = refs[:-2], refs[-2:]
+    block_refs, (near_head_ref, near_ref, far_head_ref, far_ref) = refs[:-4], refs[-4:]
     _, held, span, breadth = block_refs[0].shape
     _, _, number = position()
     odd = lax.rem(number, 2) == 1
     per_row = breadth // LANES
 
-    def put_edges(entry, top, bottom, lanes=slice(None)):
-        near_ref[pl.ds(entry * HALO, HALO), lanes] = jnp.where(odd, top, bottom)
-        far_ref[pl.ds(entry * HALO, HALO), lanes] = jnp.where(odd, bottom, top)
-
-    entry = 0
-    for kind in range(2):
-        for block_ref in block_refs:
+    def put_edges(to_near, to_far, entry, top, bottom, lanes=slice(None)):
+        to_near[pl.ds(entry * HALO, HALO), lanes] = jnp.where(odd, top, bottom)
+        to_far[pl.ds(entry * HALO, HALO), lanes] = jnp.where(odd, bottom, top)
+
+    for kind, to in enumerate(((near_head_ref, far_head_ref), (near_ref, far_ref))):
+        for step, block_ref in enumerate(block_refs):
             for held_layer in range(held):
-                put_edges(entry, block_ref[kind, held_layer, :HALO, :], block_ref[kind, held_layer, span - HALO:, :])
-                entry += 1
+                field = block_ref.at[kind, held_layer]
+                put_edges(*to, step * held + held_layer, field[:HALO, :], field[span - HALO:, :])
+    entry = len(block_refs) * held
     land = own_land(land_ref, span)
-    put_edges(entry, land[:HALO], land[span - HALO:])
+    put_edges(near_ref, far_ref, entry, land[:HALO], land[span - HALO:])
     for ref in (diag_ref, rhs_ref):
         entry += 1
         for part in range(per_row):
             top = ref[pl.ds(part, HALO, stride=per_row), :]
             bottom = ref[pl.ds((span - HALO) * per_row + part, HALO, stride=per_row), :]
-            put_edges(entry, top, bottom, slice(part * LANES, (part + 1) * LANES))
+            put_edges(near_ref, far_ref, entry, top, bottom, slice(part * LANES, (part + 1) * LANES))
     rest = near_ref.shape[0] - (entry + 1) * HALO
     for ref in (near_ref, far_ref):
         ref[pl.ds((entry + 1) * HALO, rest), :] = jnp.zeros((rest, breadth), jnp.float32)
@@ -401,7 +401,9 @@
             done += 1
 
 
-def flow_kernel(kst_ref, alphat_ref, storet_ref, land_ref, far_ref, near_ref, diag_ref, rhs_ref, *refs):
+def flow_kernel(
+    kst_ref, alphat_ref, storet_ref, land_ref, far_head_ref, far_ref, near_head_ref, near_ref, diag_ref, rhs_ref, *refs,
+):
     groups = lax.axis_size("layer")
     own, _, number = position()
     end = (number == 0) | (number == groups - 1)
@@ -428,27 +430,29 @@
     dtop_sc[pl.ds(side, span * rows.per_row), :] = diag_ref[...]
     rtop_sc[pl.ds(side, span * rows.per_row), :] = rhs_ref[...]
 
-    def put_halo(ref, partner, row):
-        def entry(number):
+    def put_halo(refs, partner, water, row):
+        def entry(ref, number):
             return ref[pl.ds(number * HALO, HALO), :]
 
+        head, rest = refs
         for count in range(layers):
             layer = (partner ^ (count // held)) * held + count % held
-            rows.put_layer(first_sc, layer, row, entry(count))
-            rows.put_layer(soil_sc, layer, row, entry(layers + count))
-        water = outside if ref is far_ref else False
-        land_sc[pl.ds(row, HALO), :] = jnp.where(water, 0.0, entry(2 * layers))
-        for count, top_sc in ((2 * layers + 1, dtop_sc), (2 * layers + 2, rtop_sc)):
-            value = entry(count)
+            rows.put_layer(first_sc, layer, row, entry(head, count))
+            rows.put_layer(soil_sc, layer, row, entry(rest, count))
+        land_sc[pl.ds(row, HALO), :] = jnp.where(water, 0.0, entry(rest, layers))
+        for count, top_sc in ((layers + 1, dtop_sc), (layers + 2, rtop_sc)):
+            value = entry(rest, count)
             for part in range(rows.per_row):
                 spot = pl.ds(row * rows.per_row + part, HALO, stride=rows.per_row)
                 top_sc[spot, :] = value[:, part * LANES:(part + 1) * LANES]
 
-    for odd, above_ref, below_ref in ((0, far_ref, near_ref), (1, near_ref, far_ref)):
+    far = (far_head_ref, far_ref), far_partner, outside
+    near = (near_head_ref, near_ref), own ^ 1, False
+    for odd, above, below in ((0, far, near), (1, near, far)):
         @pl.when(lax.rem(number, 2) == odd)
-        def _(above_ref=above_ref, below_ref=below_ref):
-            for ref, row in ((above_ref, 0), (below_ref, last_own)):
-                put_halo(ref, own ^ 1 if ref is near_ref else far_partner, row)
+        def _(above=above, below=below):
+            put_halo(*above, 0)
+            put_halo(*below, last_own)
 
     faces = Faces(rows, land_sc[...], lands)
     tables = lane_tables((kst_ref, alphat_ref, storet_ref), layers)
@@ -701,12 +705,15 @@
         (riv_shape, riv_shape, node_field, jax.ShapeDtypeStruct((1, slots), jnp.float32)),
         [in_vmem] * 7, [node_scratch] * 2 + [pltpu.VMEM((groups_of_cells, LANES), jnp.float32)], 6,
     )(bed, whole_section, *early)
-    edges = jax.ShapeDtypeStruct((-(-(2 * layers + 3) * HALO // 8) * 8, breadth), jnp.float32)
-    near_edge, far_edge = call(
-        edge_kernel, (edges, edges), [in_vmem] * (3 + groups), [], 0.1,
+    edges = (
+        jax.ShapeDtypeStruct((layers * HALO, breadth), jnp.float32),
+        jax.ShapeDtypeStruct((-(-(layers + 3) * HALO // 8) * 8, breadth), jnp.float32),
+    )
+    edge_parts = call(
+        edge_kernel, edges * 2, [in_vmem] * (3 + groups), [], 0.1,
     )(land_mask, diag, rhs, *received)
-    far_halo = lax.ppermute(far_edge, FLAT, far)
-    near_halo = lax.ppermute(near_edge, "layer", near)
+    far_halo = [lax.ppermute(part, FLAT, far) for part in edge_parts[2:]]
+    near_halo = [lax.ppermute(part, "layer", near) for part in edge_parts[:2]]
 
     window = span + 2 * HALO
     own_field = jax.ShapeDtypeStruct((per_row, span * layers, LANES), jnp.float32)
@@ -720,13 +727,13 @@
     *heads, top = call(
         flow_kernel,
         (head_shape,) * groups + (jax.ShapeDtypeStruct((span, breadth), jnp.float32),),
-        [in_smem] * 3 + [in_vmem] * (5 + len(staged)),
+        [in_smem] * 3 + [in_vmem] * (7 + len(staged)),
         [field] * 12
         + [pltpu.VMEM((window, breadth), jnp.float32)]
         + [pltpu.VMEM((window * per_row, LANES), jnp.float32)] * 2
         + [pltpu.VMEM((window, breadth), jnp.float32)] * 3,
         3,
-    )(ks_table, alpha_table, store_table, land_mask, far_halo, near_halo, diag, rhs, *staged)
+    )(ks_table, alpha_table, store_table, land_mask, *far_halo, *near_halo, diag, rhs, *staged)
     tops = exchange([top] * groups)
     backs = exchange(heads)
 

time: 51.4 us -> 53.8 us (1.047)
  starting transfers between devices: 20.2 us -> 22.8 us
    ppermute x2 -> x4, starting transfers between devices: 3.74 us -> 5.77 us  [the longest x2 4.31 us: on_device(): near_halo = [lax.ppermute(part, 'layer', near) for part in edge_parts[:2]]]
    pallas_call x1, Pallas kernels: 4.99 us -> 4.13 us  [on_device(): call(functools.partial(river_kernel, stride), (riv_shape, riv_shape, node...]
    pallas_call x1, Pallas kernels: 1.57 us -> 2.33 us  [on_device(): call(functools.partial(early_kernel, breadth, span), (node_field,) * 4 +...]
    all_to_all x1, waiting for transfers between devices: 3.49 us -> 2.73 us  [on_device(): lax.all_to_all(spread, 'tile', 0, 0).reshape(tiles * stride, node_count)]
    ppermute x9, waiting for transfers between devices: 0.94 us -> 1.54 us  [exchange(): lax.ppermute(parts[step], 'layer', [(i, i ^ step) for i in range(groups)])]
  transfers between devices with their start and end apart: 13 -> 15, of which waited for: 4 -> 3; matrix products, arithmetic and copies ran while one was open for 0% -> 0% of each run, Pallas kernels for 27% -> 26%
where the time goes in v15:
time: 53.8 us; the launch traced here: 53.5 us
  starting transfers between devices  22.8 us (42%)
  Pallas kernels  19.7 us (37%)
  waiting for transfers between devices  10 us (19%)
  between operations  0.87 us (2%)
    all_to_all x1, starting transfers between devices, on_device(): lax.all_to_all(spread, 'tile', 0, 0).reshape(tiles * stride, node_count)  7.4 us
    ppermute x9, starting transfers between devices, exchange(): lax.ppermute(parts[step], 'layer', [(i, i ^ step) for i in range(groups)])  6.27 us
    all_to_all x1, waiting for transfers between devices, on_device(): lax.all_to_all(partial.reshape(tiles, fold, node_count), 'tile', 0, 0)  5.75 us
    ppermute x2, starting transfers between devices, on_device(): near_halo = [lax.ppermute(part, 'layer', near) for part in edge_parts[:2]]  4.31 us
    pallas_call x1, Pallas kernels, on_device(): call(functools.partial(river_kernel, stride), (riv_shape, riv_shape, node...  4.13 us
    pallas_call x1, Pallas kernels, on_device(): call(stage_kernel, (own_field,) * (4 + 5 * ITERS + HALO), [in_smem] * 3 +...  4.1 us
    pallas_call x1, Pallas kernels, on_device(): call(flow_kernel, (head_shape,) * groups + (jax.ShapeDtypeStruct((span, b...  3.67 us
    all_to_all x1, starting transfers between devices, on_device(): lax.all_to_all(partial.reshape(tiles, fold, node_count), 'tile', 0, 0)  3.34 us
  transfers between devices with their start and end apart: 15, of which 3 were waited for; matrix products, arithmetic and copies ran while one was open for 0% of the time, Pallas kernels for 26%

profile of v15, /device:TPU:0, one launch (start us, length us, event | category | flops | bytes accessed | tf_op | source)
XLA Modules:
  0.0 53.5 jit_solution(3923347367947844475)
XLA Ops:
  0.7 1.4 %shard_map.122.after_ref = f32[8,24,128]{2,1,0:T(8,128)} custom-call(f32[16,128]{1,0:T(8,128)} %section_hbm.1, s32[1,256]{1,0:T(1,128)} %owner_hbm.1, s32[1,256]{1,0:T(1,128)} %local_hbm.1), custom_call_target="tpu_custom_call" | custom-call | flops 1150000000 | tf_op jit(solution)/shard_map/pallas_call | solution.py:677
  2.1 7.4 %all-to-all-start = ((f32[8,24,128]{2,1,0:T(8,128)}), f32[8,24,128]{2,1,0:T(8,128)S(1)}, u32[]{:S(2)}, u32[]{:S(2)}) async-start(f32[8,24,128]{2,1,0:T(8,128)} %shard_map.122.after_ref), calls=%async_computation | async-start | bytes 196608 | tf_op jit(solution)/shard_map/all_to_all | solution.py:687
  9.7 1.6 %collective-permute-start.1 = (f32[2,2,16,512]{3,2,1,0:T(8,128)S(1)}, f32[2,2,16,512]{3,2,1,0:T(8,128)S(1)}, u32[]{:S(2)}, u32[]{:S(2)}) collective-permute-start(f32[2,2,16,512]{3,2,1,0:T(8,128)S(1)} %get-tuple-element.59), channel_id=1, source_target_pairs={{0,2},{1,3},{2,0},{3,1},{4,6},{5,7},{6,4},{7,5},{8,10},{9,11},{10,... | collective-permute-start | bytes 393224 | tf_op jit(solution)/shard_map/ppermute | solution.py:673
  11.3 0.3 collective-permute-start.2
  11.6 2.3 %shard_map.123 = (f32[256,128]{1,0:T(8,128)S(1)}, f32[256,128]{1,0:T(8,128)S(1)}, f32[256,128]{1,0:T(8,128)S(1)}, f32[256,128]{1,0:T(8,128)S(1)}, f32[128,128]{1,0:T(8,128)S(1)}) custom-call(s32[256,128]{1,0:T(8,128)S(1)} %bitcast.8, f32[256,128]{1,0:T(8,128)S(1)} %bitcast.5), custom_call_target="tpu_custom_call" | custom-call | flops 2875000064 | tf_op jit(solution)/shard_map/pallas_call | solution.py:699
  13.9 2.7 %all-to-all-done = f32[8,24,128]{2,1,0:T(8,128)S(1)} async-done(((f32[8,24,128]{2,1,0:T(8,128)}), f32[8,24,128]{2,1,0:T(8,128)S(1)}, u32[]{:S(2)}, u32[]{:S(2)}) %all-to-all-start) | async-done | bytes 98336 | tf_op jit(solution)/shard_map/all_to_all | solution.py:687
  16.6 4.1 %shard_map.124 = (f32[64,128]{1,0:T(8,128)S(1)}, f32[64,128]{1,0:T(8,128)S(1)}, f32[256,128]{1,0:T(8,128)S(1)}, f32[1,256]{1,0:T(1,128)S(1)}) custom-call(f32[256,128]{1,0:T(8,128)S(1)} %bitcast.6, f32[192,128]{1,0:T(8,128)S(1)} %bitcast.4, f32[256,128]{1,0:T(8,128)S(1)} %get-tuple-element.48.block_ref, f32[256,128]{1,0:T(8,128)S(1)} %get-tuple-element.49.spot_ref, ...), custom_call_target="tpu_custom_call" | custom-call | flops 6899999744 | tf_op jit(solution)/shard_map/pallas_call | solution.py:703
  20.8 0.1 shard_map.126
  20.9 0.7 %collective-permute-start.4 = (f32[72,512]{1,0:T(8,128)S(1)}, f32[72,512]{1,0:T(8,128)S(1)}, u32[]{:S(2)}, u32[]{:S(2)}) collective-permute-start(f32[72,512]{1,0:T(8,128)S(1)} %get-tuple-element.62), channel_id=1, source_target_pairs={{1,2},{2,1},{3,7},{7,3},{5,6},{6,5},{4,8},{8,4},{9,10},{10,9},{11,... | collective-permute-start | bytes 442376 | tf_op jit(solution)/shard_map/ppermute | solution.py:715
  21.6 2.9 %collective-permute-start.6 = (f32[72,512]{1,0:T(8,128)S(1)}, f32[72,512]{1,0:T(8,128)S(1)}, u32[]{:S(2)}, u32[]{:S(2)}) collective-permute-start(f32[72,512]{1,0:T(8,128)S(1)} %get-tuple-element.64), channel_id=1, source_target_pairs={{0,1},{1,0},{2,3},{3,2},{4,5},{5,4},{6,7},{7,6},{8,9},{9,8},{10,11... | collective-permute-start | bytes 442376 | tf_op jit(solution)/shard_map/ppermute | solution.py:716
  24.5 0.8 %collective-permute-start.3 = (f32[48,512]{1,0:T(8,128)S(1)}, f32[48,512]{1,0:T(8,128)S(1)}, u32[]{:S(2)}, u32[]{:S(2)}) collective-permute-start(f32[48,512]{1,0:T(8,128)S(1)} %get-tuple-element.61), channel_id=1, source_target_pairs={{1,2},{2,1},{3,7},{7,3},{5,6},{6,5},{4,8},{8,4},{9,10},{10,9},{11,... | collective-permute-start | bytes 294920 | tf_op jit(solution)/shard_map/ppermute | solution.py:715
  25.3 1.4 %collective-permute-start.5 = (f32[48,512]{1,0:T(8,128)S(1)}, f32[48,512]{1,0:T(8,128)S(1)}, u32[]{:S(2)}, u32[]{:S(2)}) collective-permute-start(f32[48,512]{1,0:T(8,128)S(1)} %get-tuple-element.63), channel_id=1, source_target_pairs={{0,1},{1,0},{2,3},{3,2},{4,5},{5,4},{6,7},{7,6},{8,9},{9,8},{10,11... | collective-permute-start | bytes 294920 | tf_op jit(solution)/shard_map/ppermute | solution.py:716
  26.7 4.1 %shard_map.127 = (f32[4,128,128]{2,1,0:T(8,128)S(1)}, f32[4,128,128]{2,1,0:T(8,128)S(1)}, f32[4,128,128]{2,1,0:T(8,128)S(1)}, f32[4,128,128]{2,1,0:T(8,128)S(1)}...) custom-call(f32[12]{0:T(128)S(1)} %copy-done.6, ...), custom_call_target="tpu_custom_call" | custom-call | flops 4600000000 | tf_op jit(solution)/shard_map/pallas_call | solution.py:721
  30.9 3.7 %shard_map.128 = (f32[2,16,512]{2,1,0:T(8,128)S(1)}, f32[2,16,512]{2,1,0:T(8,128)S(1)}, f32[2,16,512]{2,1,0:T(8,128)S(1)}, f32[2,16,512]{2,1,0:T(8,128)S(1)}, f32[16,512]{1,0:T(8,128)S(1)}) custom-call(f32[12]{0:T(128)S(1)} %copy-done.6, f32[12]{0:T(128)S(1)} %copy-done.7, f32[12]{0:T(128)S(1)} %copy-done.8, s32[64,512]{1,0:T(8,128)S(1)} %copy-done, ...), custom_call_target="tpu_custom_call" | custom-call | flops 3449999872 | tf_op jit(solution)/shard_map/pallas_call | solution.py:727
  34.6 0.1 collective-permute-start.7
  34.7 2.1 %collective-permute-start.8 = (f32[16,512]{1,0:T(8,128)S(1)}, f32[16,512]{1,0:T(8,128)S(1)}, u32[]{:S(2)}, u32[]{:S(2)}) collective-permute-start(f32[16,512]{1,0:T(8,128)S(1)} %get-tuple-element.85.refs_0_), channel_id=1, source_target_pairs={{0,2},{1,3},{2,0},{3,1},{4,6},{5,7},{6,4},{7,5},{8,10},{9,11},{10,... | collective-permute-start | bytes 98312 | tf_op jit(solution)/shard_map/ppermute | solution.py:673
  36.8 0.1 collective-permute-start.10
  36.9 2.0 %collective-permute-start.11 = (f32[2,16,512]{2,1,0:T(8,128)S(1)}, f32[2,16,512]{2,1,0:T(8,128)S(1)}, u32[]{:S(2)}, u32[]{:S(2)}) collective-permute-start(f32[2,16,512]{2,1,0:T(8,128)S(1)} %get-tuple-element.88), channel_id=1, source_target_pairs={{0,2},{1,3},{2,0},{3,1},{4,6},{5,7},{6,4},{7,5},{8,10},{9,11},{10,... | collective-permute-start | bytes 196616 | tf_op jit(solution)/shard_map/ppermute | solution.py:673
  38.9 1.5 %collective-permute-done.9.refs_3_ = f32[16,512]{1,0:T(8,128)S(1)} collective-permute-done((f32[16,512]{1,0:T(8,128)S(1)}, f32[16,512]{1,0:T(8,128)S(1)}, u32[]{:S(2)}, u32[]{:S(2)}) %collective-permute-start.9) | collective-permute-done | bytes 32800 | tf_op jit(solution)/shard_map/ppermute | solution.py:673
  40.4 2.5 %shard_map.129 = f32[32,128]{1,0:T(8,128)} custom-call(s32[256,128]{1,0:T(8,128)S(1)} %bitcast.9, f32[256,128]{1,0:T(8,128)S(1)} %bitcast.7, f32[256,128]{1,0:T(8,128)S(1)} %get-tuple-element.53.slot_section_ref, f32[1,256]{1,0:T(1,128)S(1)} %get-tuple-element.54.reach_ref, f32[16,512]{1,0:T(8,128)S(1)} %get-tuple-element.85.refs_0_, ...), custom_call_target="tpu_custom_call" | custom-call | flops 3449999872 | tf_op jit(solution)/shard_map/pallas_call | solution.py:742
  42.9 3.3 %all-to-all-start.1 = ((f32[8,4,128]{2,1,0:T(4,128)}), f32[8,4,128]{2,1,0:T(4,128)S(1)}, u32[]{:S(2)}, u32[]{:S(2)}) async-start(f32[8,4,128]{2,1,0:T(4,128)} %bitcast.3), calls=%async_computation.1 | async-start | bytes 32768 | tf_op jit(solution)/shard_map/all_to_all | solution.py:750
  46.3 0.7 %shard_map.130 = f32[2,64,512]{2,1,0:T(8,128)} custom-call(f32[2,16,512]{2,1,0:T(8,128)S(1)} %get-tuple-element.89.refs_0_, f32[2,16,512]{2,1,0:T(8,128)S(1)} %collective-permute-done.10.refs_1_, f32[2,16,512]{2,1,0:T(8,128)S(1)} %collective-permute-done.11.refs_2_, f32[2,16,512]{2,1,0:T(8,128)S(1)} %collective-permute-done.12.refs_3_), custom_call_target="tpu_custom_call" | custom-call | flops 805000000 | tf_op jit(solution)/shard_map/pallas_call | solution.py:751
  47.0 5.8 %all-to-all-done.1.terms_ref = f32[8,4,128]{2,1,0:T(4,128)S(1)} async-done(((f32[8,4,128]{2,1,0:T(4,128)}), f32[8,4,128]{2,1,0:T(4,128)S(1)}, u32[]{:S(2)}, u32[]{:S(2)}) %all-to-all-start.1) | async-done | bytes 16416 | tf_op jit(solution)/shard_map/all_to_all | solution.py:750
  52.8 0.7 %shard_map.131 = f32[16,32]{1,0:T(8,128)} custom-call(f32[8,4,128]{2,1,0:T(4,128)S(1)} %all-to-all-done.1.terms_ref), custom_call_target="tpu_custom_call" | custom-call | flops 115000000 | tf_op jit(solution)/shard_map/pallas_call | solution.py:756
  (34 shorter events, 0.2 us)
Async XLA Ops:
  0.6 8.9 %copy-start.2 = (f32[2,64,512]{2,1,0:T(8,128)S(1)}, f32[2,64,512]{2,1,0:T(8,128)}, u32[]{:S(2)}) copy-start(f32[2,64,512]{2,1,0:T(8,128)} %head_ref.1) | copy-start | bytes 786436
  0.6 8.9 %copy-start.3 = (s32[2,64,512]{2,1,0:T(8,128)S(1)}, s32[2,64,512]{2,1,0:T(8,128)}, u32[]{:S(2)}) copy-start(s32[2,64,512]{2,1,0:T(8,128)} %soil_ref.1) | copy-start | bytes 786436
  2.1 7.4 %copy-start.1 = (f32[8,24,128]{2,1,0:T(8,128)S(1)}, f32[8,24,128]{2,1,0:T(8,128)}, u32[]{:S(2)}) copy-start(f32[8,24,128]{2,1,0:T(8,128)} %shard_map.122.after_ref) | copy-start | bytes 294916
  2.1 14.5 %all-to-all-start = ((f32[8,24,128]{2,1,0:T(8,128)}), f32[8,24,128]{2,1,0:T(8,128)S(1)}, u32[]{:S(2)}, u32[]{:S(2)}) async-start(f32[8,24,128]{2,1,0:T(8,128)} %shard_map.122.after_ref), calls=%async_computation | async-start | bytes 196608 | tf_op jit(solution)/shard_map/all_to_all | solution.py:687
  9.5 2.0 %copy-start.4 = (f32[1,256,128]{2,1,0:T(8,128)S(1)}, f32[1,256,128]{2,1,0:T(8,128)}, u32[]{:S(2)}) copy-start(f32[1,256,128]{2,1,0:T(8,128)} %param.21) | copy-start | bytes 393220
  9.5 2.0 %copy-start.5 = (s32[1,256,128]{2,1,0:T(8,128)S(1)}, s32[1,256,128]{2,1,0:T(8,128)}, u32[]{:S(2)}) copy-start(s32[1,256,128]{2,1,0:T(8,128)} %param.20) | copy-start | bytes 393220
  9.6 11.2 %collective-permute-start = (f32[2,2,16,512]{3,2,1,0:T(8,128)S(1)}, f32[2,2,16,512]{3,2,1,0:T(8,128)S(1)}, u32[]{:S(2)}, u32[]{:S(2)}) collective-permute-start(f32[2,2,16,512]{3,2,1,0:T(8,128)S(1)} %get-tuple-element.58), channel_id=1, source_target_pairs={{0,1},{1,0},{2,3},{3,2},{4,5},{5,4},{6,7},{7,6},{8,9},{9,8},{10,11... | collective-permute-start | bytes 393224 | tf_op jit(solution)/shard_map/ppermute | solution.py:673
  9.7 11.1 %collective-permute-start.1 = (f32[2,2,16,512]{3,2,1,0:T(8,128)S(1)}, f32[2,2,16,512]{3,2,1,0:T(8,128)S(1)}, u32[]{:S(2)}, u32[]{:S(2)}) collective-permute-start(f32[2,2,16,512]{3,2,1,0:T(8,128)S(1)} %get-tuple-element.59), channel_id=1, source_target_pairs={{0,2},{1,3},{2,0},{3,1},{4,6},{5,7},{6,4},{7,5},{8,10},{9,11},{10,... | collective-permute-start | bytes 393224 | tf_op jit(solution)/shard_map/ppermute | solution.py:673
  11.3 9.5 %collective-permute-start.2 = (f32[2,2,16,512]{3,2,1,0:T(8,128)S(1)}, f32[2,2,16,512]{3,2,1,0:T(8,128)S(1)}, u32[]{:S(2)}, u32[]{:S(2)}) collective-permute-start(f32[2,2,16,512]{3,2,1,0:T(8,128)S(1)} %get-tuple-element.60), channel_id=1, source_target_pairs={{0,3},{1,2},{2,1},{3,0},{4,7},{5,6},{6,5},{7,4},{8,11},{9,10},{10,... | collective-permute-start | bytes 393224 | tf_op jit(solution)/shard_map/ppermute | solution.py:673
  16.6 4.2 %copy-start = (s32[64,512]{1,0:T(8,128)S(1)}, s32[64,512]{1,0:T(8,128)}, u32[]{:S(2)}) copy-start(s32[64,512]{1,0:T(8,128)} %land_ref.5) | copy-start | bytes 393220
  20.9 9.9 %collective-permute-start.4 = (f32[72,512]{1,0:T(8,128)S(1)}, f32[72,512]{1,0:T(8,128)S(1)}, u32[]{:S(2)}, u32[]{:S(2)}) collective-permute-start(f32[72,512]{1,0:T(8,128)S(1)} %get-tuple-element.62), channel_id=1, source_target_pairs={{1,2},{2,1},{3,7},{7,3},{5,6},{6,5},{4,8},{8,4},{9,10},{10,9},{11,... | collective-permute-start | bytes 442376 | tf_op jit(solution)/shard_map/ppermute | solution.py:715
  21.6 9.3 %collective-permute-start.6 = (f32[72,512]{1,0:T(8,128)S(1)}, f32[72,512]{1,0:T(8,128)S(1)}, u32[]{:S(2)}, u32[]{:S(2)}) collective-permute-start(f32[72,512]{1,0:T(8,128)S(1)} %get-tuple-element.64), channel_id=1, source_target_pairs={{0,1},{1,0},{2,3},{3,2},{4,5},{5,4},{6,7},{7,6},{8,9},{9,8},{10,11... | collective-permute-start | bytes 442376 | tf_op jit(solution)/shard_map/ppermute | solution.py:716
  24.5 2.2 %copy-start.6 = (f32[12]{0:T(128)S(1)}, f32[12]{0:T(128)}, u32[]{:S(2)}) copy-start(f32[12]{0:T(128)} %kst_ref.1) | copy-start | bytes 148
  24.5 2.2 %copy-start.7 = (f32[12]{0:T(128)S(1)}, f32[12]{0:T(128)}, u32[]{:S(2)}) copy-start(f32[12]{0:T(128)} %alphat_ref.1) | copy-start | bytes 148
  24.5 2.2 %copy-start.8 = (f32[12]{0:T(128)S(1)}, f32[12]{0:T(128)}, u32[]{:S(2)}) copy-start(f32[12]{0:T(128)} %storet_ref.1) | copy-start | bytes 148
  24.5 6.3 %collective-permute-start.3 = (f32[48,512]{1,0:T(8,128)S(1)}, f32[48,512]{1,0:T(8,128)S(1)}, u32[]{:S(2)}, u32[]{:S(2)}) collective-permute-start(f32[48,512]{1,0:T(8,128)S(1)} %get-tuple-element.61), channel_id=1, source_target_pairs={{1,2},{2,1},{3,7},{7,3},{5,6},{6,5},{4,8},{8,4},{9,10},{10,9},{11,... | collective-permute-start | bytes 294920 | tf_op jit(solution)/shard_map/ppermute | solution.py:715
  25.3 5.5 %collective-permute-start.5 = (f32[48,512]{1,0:T(8,128)S(1)}, f32[48,512]{1,0:T(8,128)S(1)}, u32[]{:S(2)}, u32[]{:S(2)}) collective-permute-start(f32[48,512]{1,0:T(8,128)S(1)} %get-tuple-element.63), channel_id=1, source_target_pairs={{0,1},{1,0},{2,3},{3,2},{4,5},{5,4},{6,7},{7,6},{8,9},{9,8},{10,11... | collective-permute-start | bytes 294920 | tf_op jit(solution)/shard_map/ppermute | solution.py:716
  34.6 4.3 %collective-permute-start.7 = (f32[16,512]{1,0:T(8,128)S(1)}, f32[16,512]{1,0:T(8,128)S(1)}, u32[]{:S(2)}, u32[]{:S(2)}) collective-permute-start(f32[16,512]{1,0:T(8,128)S(1)} %get-tuple-element.85.refs_0_), channel_id=1, source_target_pairs={{0,1},{1,0},{2,3},{3,2},{4,5},{5,4},{6,7},{7,6},{8,9},{9,8},{10,11... | collective-permute-start | bytes 98312 | tf_op jit(solution)/shard_map/ppermute | solution.py:673
  34.7 4.2 %collective-permute-start.8 = (f32[16,512]{1,0:T(8,128)S(1)}, f32[16,512]{1,0:T(8,128)S(1)}, u32[]{:S(2)}, u32[]{:S(2)}) collective-permute-start(f32[16,512]{1,0:T(8,128)S(1)} %get-tuple-element.85.refs_0_), channel_id=1, source_target_pairs={{0,2},{1,3},{2,0},{3,1},{4,6},{5,7},{6,4},{7,5},{8,10},{9,11},{10,... | collective-permute-start | bytes 98312 | tf_op jit(solution)/shard_map/ppermute | solution.py:673
  36.7 3.7 %collective-permute-start.9 = (f32[16,512]{1,0:T(8,128)S(1)}, f32[16,512]{1,0:T(8,128)S(1)}, u32[]{:S(2)}, u32[]{:S(2)}) collective-permute-start(f32[16,512]{1,0:T(8,128)S(1)} %get-tuple-element.85.refs_0_), channel_id=1, source_target_pairs={{0,3},{1,2},{2,1},{3,0},{4,7},{5,6},{6,5},{7,4},{8,11},{9,10},{10,... | collective-permute-start | bytes 98312 | tf_op jit(solution)/shard_map/ppermute | solution.py:673
  36.8 6.2 %collective-permute-start.10 = (f32[2,16,512]{2,1,0:T(8,128)S(1)}, f32[2,16,512]{2,1,0:T(8,128)S(1)}, u32[]{:S(2)}, u32[]{:S(2)}) collective-permute-start(f32[2,16,512]{2,1,0:T(8,128)S(1)} %get-tuple-element.87), channel_id=1, source_target_pairs={{0,1},{1,0},{2,3},{3,2},{4,5},{5,4},{6,7},{7,6},{8,9},{9,8},{10,11... | collective-permute-start | bytes 196616 | tf_op jit(solution)/shard_map/ppermute | solution.py:673
  36.9 6.0 %collective-permute-start.11 = (f32[2,16,512]{2,1,0:T(8,128)S(1)}, f32[2,16,512]{2,1,0:T(8,128)S(1)}, u32[]{:S(2)}, u32[]{:S(2)}) collective-permute-start(f32[2,16,512]{2,1,0:T(8,128)S(1)} %get-tuple-element.88), channel_id=1, source_target_pairs={{0,2},{1,3},{2,0},{3,1},{4,6},{5,7},{6,4},{7,5},{8,10},{9,11},{10,... | collective-permute-start | bytes 196616 | tf_op jit(solution)/shard_map/ppermute | solution.py:673
  38.9 7.4 %collective-permute-start.12 = (f32[2,16,512]{2,1,0:T(8,128)S(1)}, f32[2,16,512]{2,1,0:T(8,128)S(1)}, u32[]{:S(2)}, u32[]{:S(2)}) collective-permute-start(f32[2,16,512]{2,1,0:T(8,128)S(1)} %get-tuple-element.92), channel_id=1, source_target_pairs={{0,3},{1,2},{2,1},{3,0},{4,7},{5,6},{6,5},{7,4},{8,11},{9,10},{10,... | collective-permute-start | bytes 196616 | tf_op jit(solution)/shard_map/ppermute | solution.py:673
  42.9 9.9 %all-to-all-start.1 = ((f32[8,4,128]{2,1,0:T(4,128)}), f32[8,4,128]{2,1,0:T(4,128)S(1)}, u32[]{:S(2)}, u32[]{:S(2)}) async-start(f32[8,4,128]{2,1,0:T(4,128)} %bitcast.3), calls=%async_computation.1 | async-start | bytes 32768 | tf_op jit(solution)/shard_map/all_to_all | solution.py:750

commit v16 on v14

--- a/solution.py
+++ b/solution.py
@@ -110,7 +110,7 @@
 
 
 def early_groups(slots):
-    return slots // GROUP // 2
+    return slots // GROUP * 3 // 4
 
 
 def early_kernel(breadth, span, cells_ref, bed_ref, block_ref, spot_ref, high_ref, low_ref, early_ref):

time: 51.4 us -> 50.8 us (0.988)
  waiting for transfers between devices: 10.2 us -> 9.49 us
    pallas_call x1, Pallas kernels: 4.99 us -> 4.13 us  [on_device(): call(functools.partial(river_kernel, stride), (riv_shape, riv_shape, node...]
    pallas_call x1, Pallas kernels: 1.57 us -> 2.33 us  [on_device(): call(functools.partial(early_kernel, breadth, span), (node_field,) * 4 +...]
    all_to_all x1, waiting for transfers between devices: 3.49 us -> 2.73 us  [on_device(): lax.all_to_all(spread, 'tile', 0, 0).reshape(tiles * stride, node_count)]
where the time goes in v16:
time: 50.8 us; the launch traced here: 50.5 us
  starting transfers between devices  20.4 us (40%)
  Pallas kernels  19.7 us (39%)
  waiting for transfers between devices  9.49 us (19%)
  between operations  0.85 us (2%)
    all_to_all x1, starting transfers between devices, on_device(): lax.all_to_all(spread, 'tile', 0, 0).reshape(tiles * stride, node_count)  7.4 us
    all_to_all x1, waiting for transfers between devices, on_device(): lax.all_to_all(partial.reshape(tiles, fold, node_count), 'tile', 0, 0)  5.82 us
    ppermute x9, starting transfers between devices, exchange(): lax.ppermute(parts[step], 'layer', [(i, i ^ step) for i in range(groups)])  5.73 us
    pallas_call x1, Pallas kernels, on_device(): call(functools.partial(river_kernel, stride), (riv_shape, riv_shape, node...  4.13 us
    pallas_call x1, Pallas kernels, on_device(): call(stage_kernel, (own_field,) * (4 + 5 * ITERS + HALO), [in_smem] * 3 +...  4.1 us
    pallas_call x1, Pallas kernels, on_device(): call(flow_kernel, (head_shape,) * groups + (jax.ShapeDtypeStruct((span, b...  3.67 us
    all_to_all x1, starting transfers between devices, on_device(): lax.all_to_all(partial.reshape(tiles, fold, node_count), 'tile', 0, 0)  3.5 us
    ppermute x1, starting transfers between devices, on_device(): near_halo = lax.ppermute(near_edge, 'layer', near)  2.93 us
  transfers between devices with their start and end apart: 13, of which 4 were waited for; matrix products, arithmetic and copies ran while one was open for 0% of the time, Pallas kernels for 27%

profile of v16, /device:TPU:0, one launch (start us, length us, event | category | flops | bytes accessed | tf_op | source)
XLA Modules:
  0.0 50.5 jit_solution(6844256148985604553)
XLA Ops:
  0.7 1.4 %shard_map.122.after_ref = f32[8,24,128]{2,1,0:T(8,128)} custom-call(f32[16,128]{1,0:T(8,128)} %section_hbm.1, s32[1,256]{1,0:T(1,128)} %owner_hbm.1, s32[1,256]{1,0:T(1,128)} %local_hbm.1), custom_call_target="tpu_custom_call" | custom-call | flops 1150000000 | tf_op jit(solution)/shard_map/pallas_call | solution.py:673
  2.1 7.4 %all-to-all-start = ((f32[8,24,128]{2,1,0:T(8,128)}), f32[8,24,128]{2,1,0:T(8,128)S(1)}, u32[]{:S(2)}, u32[]{:S(2)}) async-start(f32[8,24,128]{2,1,0:T(8,128)} %shard_map.122.after_ref), calls=%async_computation | async-start | bytes 196608 | tf_op jit(solution)/shard_map/all_to_all | solution.py:683
  9.7 1.6 %collective-permute-start.1 = (f32[2,2,16,512]{3,2,1,0:T(8,128)S(1)}, f32[2,2,16,512]{3,2,1,0:T(8,128)S(1)}, u32[]{:S(2)}, u32[]{:S(2)}) collective-permute-start(f32[2,2,16,512]{3,2,1,0:T(8,128)S(1)} %get-tuple-element.57), channel_id=1, source_target_pairs={{0,2},{1,3},{2,0},{3,1},{4,6},{5,7},{6,4},{7,5},{8,10},{9,11},{10,... | collective-permute-start | bytes 393224 | tf_op jit(solution)/shard_map/ppermute | solution.py:669
  11.3 0.3 collective-permute-start.2
  11.6 2.3 %shard_map.123 = (f32[256,128]{1,0:T(8,128)S(1)}, f32[256,128]{1,0:T(8,128)S(1)}, f32[256,128]{1,0:T(8,128)S(1)}, f32[256,128]{1,0:T(8,128)S(1)}, f32[128,128]{1,0:T(8,128)S(1)}) custom-call(s32[256,128]{1,0:T(8,128)S(1)} %bitcast.8, f32[256,128]{1,0:T(8,128)S(1)} %bitcast.5), custom_call_target="tpu_custom_call" | custom-call | flops 2875000064 | tf_op jit(solution)/shard_map/pallas_call | solution.py:695
  13.9 2.7 %all-to-all-done = f32[8,24,128]{2,1,0:T(8,128)S(1)} async-done(((f32[8,24,128]{2,1,0:T(8,128)}), f32[8,24,128]{2,1,0:T(8,128)S(1)}, u32[]{:S(2)}, u32[]{:S(2)}) %all-to-all-start) | async-done | bytes 98336 | tf_op jit(solution)/shard_map/all_to_all | solution.py:683
  16.6 4.1 %shard_map.124 = (f32[64,128]{1,0:T(8,128)S(1)}, f32[64,128]{1,0:T(8,128)S(1)}, f32[256,128]{1,0:T(8,128)S(1)}, f32[1,256]{1,0:T(1,128)S(1)}) custom-call(f32[256,128]{1,0:T(8,128)S(1)} %bitcast.6, f32[192,128]{1,0:T(8,128)S(1)} %bitcast.4, f32[256,128]{1,0:T(8,128)S(1)} %get-tuple-element.46.block_ref, f32[256,128]{1,0:T(8,128)S(1)} %get-tuple-element.47.spot_ref, ...), custom_call_target="tpu_custom_call" | custom-call | flops 6899999744 | tf_op jit(solution)/shard_map/pallas_call | solution.py:699
  21.0 0.8 %collective-permute-start.3 = (f32[120,512]{1,0:T(8,128)S(1)}, f32[120,512]{1,0:T(8,128)S(1)}, u32[]{:S(2)}, u32[]{:S(2)}) collective-permute-start(f32[120,512]{1,0:T(8,128)S(1)} %get-tuple-element.59), channel_id=1, source_target_pairs={{1,2},{2,1},{3,7},{7,3},{5,6},{6,5},{4,8},{8,4},{9,10},{10,9},{11,... | collective-permute-start | bytes 737288 | tf_op jit(solution)/shard_map/ppermute | solution.py:708
  21.8 2.9 %collective-permute-start.4 = (f32[120,512]{1,0:T(8,128)S(1)}, f32[120,512]{1,0:T(8,128)S(1)}, u32[]{:S(2)}, u32[]{:S(2)}) collective-permute-start(f32[120,512]{1,0:T(8,128)S(1)} %get-tuple-element.60), channel_id=1, source_target_pairs={{0,1},{1,0},{2,3},{3,2},{4,5},{5,4},{6,7},{7,6},{8,9},{9,8},{10,11... | collective-permute-start | bytes 737288 | tf_op jit(solution)/shard_map/ppermute | solution.py:709
  24.7 4.1 %shard_map.127 = (f32[4,128,128]{2,1,0:T(8,128)S(1)}, f32[4,128,128]{2,1,0:T(8,128)S(1)}, f32[4,128,128]{2,1,0:T(8,128)S(1)}, f32[4,128,128]{2,1,0:T(8,128)S(1)}...) custom-call(f32[12]{0:T(128)S(1)} %copy-done.6, ...), custom_call_target="tpu_custom_call" | custom-call | flops 4600000000 | tf_op jit(solution)/shard_map/pallas_call | solution.py:714
  28.8 3.7 %shard_map.128 = (f32[2,16,512]{2,1,0:T(8,128)S(1)}, f32[2,16,512]{2,1,0:T(8,128)S(1)}, f32[2,16,512]{2,1,0:T(8,128)S(1)}, f32[2,16,512]{2,1,0:T(8,128)S(1)}, f32[16,512]{1,0:T(8,128)S(1)}) custom-call(f32[12]{0:T(128)S(1)} %copy-done.6, f32[12]{0:T(128)S(1)} %copy-done.7, f32[12]{0:T(128)S(1)} %copy-done.8, s32[64,512]{1,0:T(8,128)S(1)} %copy-done, ...), custom_call_target="tpu_custom_call" | custom-call | flops 3449999872 | tf_op jit(solution)/shard_map/pallas_call | solution.py:720
  32.5 0.1 collective-permute-start.5
  32.6 1.3 %collective-permute-start.6 = (f32[16,512]{1,0:T(8,128)S(1)}, f32[16,512]{1,0:T(8,128)S(1)}, u32[]{:S(2)}, u32[]{:S(2)}) collective-permute-start(f32[16,512]{1,0:T(8,128)S(1)} %get-tuple-element.81.refs_0_), channel_id=1, source_target_pairs={{0,2},{1,3},{2,0},{3,1},{4,6},{5,7},{6,4},{7,5},{8,10},{9,11},{10,... | collective-permute-start | bytes 98312 | tf_op jit(solution)/shard_map/ppermute | solution.py:669
  33.9 0.6 %collective-permute-start.7 = (f32[16,512]{1,0:T(8,128)S(1)}, f32[16,512]{1,0:T(8,128)S(1)}, u32[]{:S(2)}, u32[]{:S(2)}) collective-permute-start(f32[16,512]{1,0:T(8,128)S(1)} %get-tuple-element.81.refs_0_), channel_id=1, source_target_pairs={{0,3},{1,2},{2,1},{3,0},{4,7},{5,6},{6,5},{7,4},{8,11},{9,10},{10,... | collective-permute-start | bytes 98312 | tf_op jit(solution)/shard_map/ppermute | solution.py:669
  34.5 0.3 collective-permute-start.8
  34.8 1.2 %collective-permute-start.9 = (f32[2,16,512]{2,1,0:T(8,128)S(1)}, f32[2,16,512]{2,1,0:T(8,128)S(1)}, u32[]{:S(2)}, u32[]{:S(2)}) collective-permute-start(f32[2,16,512]{2,1,0:T(8,128)S(1)} %get-tuple-element.84), channel_id=1, source_target_pairs={{0,2},{1,3},{2,0},{3,1},{4,6},{5,7},{6,4},{7,5},{8,10},{9,11},{10,... | collective-permute-start | bytes 196616 | tf_op jit(solution)/shard_map/ppermute | solution.py:669
  36.0 0.3 collective-permute-start.10
  36.3 0.3 collective-permute-done.6.refs_2_
  36.6 0.7 %collective-permute-done.7.refs_3_ = f32[16,512]{1,0:T(8,128)S(1)} collective-permute-done((f32[16,512]{1,0:T(8,128)S(1)}, f32[16,512]{1,0:T(8,128)S(1)}, u32[]{:S(2)}, u32[]{:S(2)}) %collective-permute-start.7) | collective-permute-done | bytes 32800 | tf_op jit(solution)/shard_map/ppermute | solution.py:669
  37.2 2.5 %shard_map.129 = f32[32,128]{1,0:T(8,128)} custom-call(s32[256,128]{1,0:T(8,128)S(1)} %bitcast.9, f32[256,128]{1,0:T(8,128)S(1)} %bitcast.7, f32[256,128]{1,0:T(8,128)S(1)} %get-tuple-element.51.slot_section_ref, f32[1,256]{1,0:T(1,128)S(1)} %get-tuple-element.52.reach_ref, f32[16,512]{1,0:T(8,128)S(1)} %get-tuple-element.81.refs_0_, ...), custom_call_target="tpu_custom_call" | custom-call | flops 3449999872 | tf_op jit(solution)/shard_map/pallas_call | solution.py:735
  39.7 3.5 %all-to-all-start.1 = ((f32[8,4,128]{2,1,0:T(4,128)}), f32[8,4,128]{2,1,0:T(4,128)S(1)}, u32[]{:S(2)}, u32[]{:S(2)}) async-start(f32[8,4,128]{2,1,0:T(4,128)} %bitcast.3), calls=%async_computation.1 | async-start | bytes 32768 | tf_op jit(solution)/shard_map/all_to_all | solution.py:743
  43.2 0.7 %shard_map.130 = f32[2,64,512]{2,1,0:T(8,128)} custom-call(f32[2,16,512]{2,1,0:T(8,128)S(1)} %get-tuple-element.85.refs_0_, f32[2,16,512]{2,1,0:T(8,128)S(1)} %collective-permute-done.8.refs_1_, f32[2,16,512]{2,1,0:T(8,128)S(1)} %collective-permute-done.9.refs_2_, f32[2,16,512]{2,1,0:T(8,128)S(1)} %collective-permute-done.10.refs_3_), custom_call_target="tpu_custom_call" | custom-call | flops 805000000 | tf_op jit(solution)/shard_map/pallas_call | solution.py:744
  44.0 5.8 %all-to-all-done.1.terms_ref = f32[8,4,128]{2,1,0:T(4,128)S(1)} async-done(((f32[8,4,128]{2,1,0:T(4,128)}), f32[8,4,128]{2,1,0:T(4,128)S(1)}, u32[]{:S(2)}, u32[]{:S(2)}) %all-to-all-start.1) | async-done | bytes 16416 | tf_op jit(solution)/shard_map/all_to_all | solution.py:743
  49.8 0.7 %shard_map.131 = f32[16,32]{1,0:T(8,128)} custom-call(f32[8,4,128]{2,1,0:T(4,128)S(1)} %all-to-all-done.1.terms_ref), custom_call_target="tpu_custom_call" | custom-call | flops 115000000 | tf_op jit(solution)/shard_map/pallas_call | solution.py:749
  (30 shorter events, 0.3 us)
Async XLA Ops:
  0.6 8.9 %copy-start.2 = (f32[2,64,512]{2,1,0:T(8,128)S(1)}, f32[2,64,512]{2,1,0:T(8,128)}, u32[]{:S(2)}) copy-start(f32[2,64,512]{2,1,0:T(8,128)} %head_ref.1) | copy-start | bytes 786436
  0.6 8.9 %copy-start.3 = (s32[2,64,512]{2,1,0:T(8,128)S(1)}, s32[2,64,512]{2,1,0:T(8,128)}, u32[]{:S(2)}) copy-start(s32[2,64,512]{2,1,0:T(8,128)} %soil_ref.1) | copy-start | bytes 786436
  2.1 7.4 %copy-start.1 = (f32[8,24,128]{2,1,0:T(8,128)S(1)}, f32[8,24,128]{2,1,0:T(8,128)}, u32[]{:S(2)}) copy-start(f32[8,24,128]{2,1,0:T(8,128)} %shard_map.122.after_ref) | copy-start | bytes 294916
  2.1 14.5 %all-to-all-start = ((f32[8,24,128]{2,1,0:T(8,128)}), f32[8,24,128]{2,1,0:T(8,128)S(1)}, u32[]{:S(2)}, u32[]{:S(2)}) async-start(f32[8,24,128]{2,1,0:T(8,128)} %shard_map.122.after_ref), calls=%async_computation | async-start | bytes 196608 | tf_op jit(solution)/shard_map/all_to_all | solution.py:683
  9.5 2.0 %copy-start.4 = (f32[1,256,128]{2,1,0:T(8,128)S(1)}, f32[1,256,128]{2,1,0:T(8,128)}, u32[]{:S(2)}) copy-start(f32[1,256,128]{2,1,0:T(8,128)} %param.21) | copy-start | bytes 393220
  9.5 2.0 %copy-start.5 = (s32[1,256,128]{2,1,0:T(8,128)S(1)}, s32[1,256,128]{2,1,0:T(8,128)}, u32[]{:S(2)}) copy-start(s32[1,256,128]{2,1,0:T(8,128)} %param.20) | copy-start | bytes 393220
  9.6 11.2 %collective-permute-start = (f32[2,2,16,512]{3,2,1,0:T(8,128)S(1)}, f32[2,2,16,512]{3,2,1,0:T(8,128)S(1)}, u32[]{:S(2)}, u32[]{:S(2)}) collective-permute-start(f32[2,2,16,512]{3,2,1,0:T(8,128)S(1)} %get-tuple-element.56), channel_id=1, source_target_pairs={{0,1},{1,0},{2,3},{3,2},{4,5},{5,4},{6,7},{7,6},{8,9},{9,8},{10,11... | collective-permute-start | bytes 393224 | tf_op jit(solution)/shard_map/ppermute | solution.py:669
  9.7 11.1 %collective-permute-start.1 = (f32[2,2,16,512]{3,2,1,0:T(8,128)S(1)}, f32[2,2,16,512]{3,2,1,0:T(8,128)S(1)}, u32[]{:S(2)}, u32[]{:S(2)}) collective-permute-start(f32[2,2,16,512]{3,2,1,0:T(8,128)S(1)} %get-tuple-element.57), channel_id=1, source_target_pairs={{0,2},{1,3},{2,0},{3,1},{4,6},{5,7},{6,4},{7,5},{8,10},{9,11},{10,... | collective-permute-start | bytes 393224 | tf_op jit(solution)/shard_map/ppermute | solution.py:669
  11.3 9.5 %collective-permute-start.2 = (f32[2,2,16,512]{3,2,1,0:T(8,128)S(1)}, f32[2,2,16,512]{3,2,1,0:T(8,128)S(1)}, u32[]{:S(2)}, u32[]{:S(2)}) collective-permute-start(f32[2,2,16,512]{3,2,1,0:T(8,128)S(1)} %get-tuple-element.58), channel_id=1, source_target_pairs={{0,3},{1,2},{2,1},{3,0},{4,7},{5,6},{6,5},{7,4},{8,11},{9,10},{10,... | collective-permute-start | bytes 393224 | tf_op jit(solution)/shard_map/ppermute | solution.py:669
  16.6 4.2 %copy-start = (s32[64,512]{1,0:T(8,128)S(1)}, s32[64,512]{1,0:T(8,128)}, u32[]{:S(2)}) copy-start(s32[64,512]{1,0:T(8,128)} %land_ref.5) | copy-start | bytes 393220
  20.9 3.8 %copy-start.6 = (f32[12]{0:T(128)S(1)}, f32[12]{0:T(128)}, u32[]{:S(2)}) copy-start(f32[12]{0:T(128)} %kst_ref.1) | copy-start | bytes 148
  20.9 3.8 %copy-start.7 = (f32[12]{0:T(128)S(1)}, f32[12]{0:T(128)}, u32[]{:S(2)}) copy-start(f32[12]{0:T(128)} %alphat_ref.1) | copy-start | bytes 148
  20.9 3.8 %copy-start.8 = (f32[12]{0:T(128)S(1)}, f32[12]{0:T(128)}, u32[]{:S(2)}) copy-start(f32[12]{0:T(128)} %storet_ref.1) | copy-start | bytes 148
  21.0 7.9 %collective-permute-start.3 = (f32[120,512]{1,0:T(8,128)S(1)}, f32[120,512]{1,0:T(8,128)S(1)}, u32[]{:S(2)}, u32[]{:S(2)}) collective-permute-start(f32[120,512]{1,0:T(8,128)S(1)} %get-tuple-element.59), channel_id=1, source_target_pairs={{1,2},{2,1},{3,7},{7,3},{5,6},{6,5},{4,8},{8,4},{9,10},{10,9},{11,... | collective-permute-start | bytes 737288 | tf_op jit(solution)/shard_map/ppermute | solution.py:708
  21.8 7.1 %collective-permute-start.4 = (f32[120,512]{1,0:T(8,128)S(1)}, f32[120,512]{1,0:T(8,128)S(1)}, u32[]{:S(2)}, u32[]{:S(2)}) collective-permute-start(f32[120,512]{1,0:T(8,128)S(1)} %get-tuple-element.60), channel_id=1, source_target_pairs={{0,1},{1,0},{2,3},{3,2},{4,5},{5,4},{6,7},{7,6},{8,9},{9,8},{10,11... | collective-permute-start | bytes 737288 | tf_op jit(solution)/shard_map/ppermute | solution.py:709
  32.5 3.5 %collective-permute-start.5 = (f32[16,512]{1,0:T(8,128)S(1)}, f32[16,512]{1,0:T(8,128)S(1)}, u32[]{:S(2)}, u32[]{:S(2)}) collective-permute-start(f32[16,512]{1,0:T(8,128)S(1)} %get-tuple-element.81.refs_0_), channel_id=1, source_target_pairs={{0,1},{1,0},{2,3},{3,2},{4,5},{5,4},{6,7},{7,6},{8,9},{9,8},{10,11... | collective-permute-start | bytes 98312 | tf_op jit(solution)/shard_map/ppermute | solution.py:669
  32.6 4.0 %collective-permute-start.6 = (f32[16,512]{1,0:T(8,128)S(1)}, f32[16,512]{1,0:T(8,128)S(1)}, u32[]{:S(2)}, u32[]{:S(2)}) collective-permute-start(f32[16,512]{1,0:T(8,128)S(1)} %get-tuple-element.81.refs_0_), channel_id=1, source_target_pairs={{0,2},{1,3},{2,0},{3,1},{4,6},{5,7},{6,4},{7,5},{8,10},{9,11},{10,... | collective-permute-start | bytes 98312 | tf_op jit(solution)/shard_map/ppermute | solution.py:669
  33.9 3.3 %collective-permute-start.7 = (f32[16,512]{1,0:T(8,128)S(1)}, f32[16,512]{1,0:T(8,128)S(1)}, u32[]{:S(2)}, u32[]{:S(2)}) collective-permute-start(f32[16,512]{1,0:T(8,128)S(1)} %get-tuple-element.81.refs_0_), channel_id=1, source_target_pairs={{0,3},{1,2},{2,1},{3,0},{4,7},{5,6},{6,5},{7,4},{8,11},{9,10},{10,... | collective-permute-start | bytes 98312 | tf_op jit(solution)/shard_map/ppermute | solution.py:669
  34.5 5.3 %collective-permute-start.8 = (f32[2,16,512]{2,1,0:T(8,128)S(1)}, f32[2,16,512]{2,1,0:T(8,128)S(1)}, u32[]{:S(2)}, u32[]{:S(2)}) collective-permute-start(f32[2,16,512]{2,1,0:T(8,128)S(1)} %get-tuple-element.83), channel_id=1, source_target_pairs={{0,1},{1,0},{2,3},{3,2},{4,5},{5,4},{6,7},{7,6},{8,9},{9,8},{10,11... | collective-permute-start | bytes 196616 | tf_op jit(solution)/shard_map/ppermute | solution.py:669
  34.8 4.9 %collective-permute-start.9 = (f32[2,16,512]{2,1,0:T(8,128)S(1)}, f32[2,16,512]{2,1,0:T(8,128)S(1)}, u32[]{:S(2)}, u32[]{:S(2)}) collective-permute-start(f32[2,16,512]{2,1,0:T(8,128)S(1)} %get-tuple-element.84), channel_id=1, source_target_pairs={{0,2},{1,3},{2,0},{3,1},{4,6},{5,7},{6,4},{7,5},{8,10},{9,11},{10,... | collective-permute-start | bytes 196616 | tf_op jit(solution)/shard_map/ppermute | solution.py:669
  36.0 7.2 %collective-permute-start.10 = (f32[2,16,512]{2,1,0:T(8,128)S(1)}, f32[2,16,512]{2,1,0:T(8,128)S(1)}, u32[]{:S(2)}, u32[]{:S(2)}) collective-permute-start(f32[2,16,512]{2,1,0:T(8,128)S(1)} %get-tuple-element.88), channel_id=1, source_target_pairs={{0,3},{1,2},{2,1},{3,0},{4,7},{5,6},{6,5},{7,4},{8,11},{9,10},{10,... | collective-permute-start | bytes 196616 | tf_op jit(solution)/shard_map/ppermute | solution.py:669
  39.7 10.1 %all-to-all-start.1 = ((f32[8,4,128]{2,1,0:T(4,128)}), f32[8,4,128]{2,1,0:T(4,128)S(1)}, u32[]{:S(2)}, u32[]{:S(2)}) async-start(f32[8,4,128]{2,1,0:T(4,128)} %bitcast.3), calls=%async_computation.1 | async-start | bytes 32768 | tf_op jit(solution)/shard_map/all_to_all | solution.py:743

commit v17 on v16

--- a/solution.py
+++ b/solution.py
@@ -109,24 +109,28 @@
     return lax.fori_loop(first, last, step, jnp.zeros((blocks, BLOCK * len(value_refs)), jnp.float32))
 
 
-def early_groups(slots):
-    return slots // GROUP * 3 // 4
-
-
-def early_kernel(breadth, span, cells_ref, bed_ref, block_ref, spot_ref, high_ref, low_ref, early_ref):
+def early_kernel(breadth, span, cells_ref, bed_ref, block_ref, spot_ref, diag_ref, high_ref, low_ref, sum_sc):
     _, _, number = position()
     block_ref[...], spot_ref[...] = split_cells(cells_ref[...], number * span, breadth, BLOCK)
     high, low = bf16_pieces(bed_ref[...], 2)
     high_ref[...] = high.astype(jnp.float32)
     low_ref[...] = low.astype(jnp.float32)
-    early_ref[...] = scatter_range(
-        0, early_groups(cells_ref.shape[0]), early_ref.shape[0], block_ref, spot_ref, (high_ref, low_ref)
+    put_sums(diag_ref, sum_sc, block_ref, spot_ref, (high_ref, low_ref))
+
+
+def put_sums(out_ref, sum_sc, block_ref, spot_ref, piece_refs):
+    share = LANES // BLOCK
+    blocks = share * out_ref.shape[0]
+    part = scatter_range(0, block_ref.shape[0] // GROUP, blocks, block_ref, spot_ref, piece_refs)
+    sum_sc[...] = part + pltpu.roll(part, BLOCK, 1)
+    low_half = lax.broadcasted_iota(jnp.int32, out_ref.shape, 1) < BLOCK
+    out_ref[...] = jnp.where(
+        low_half, sum_sc[pl.ds(0, blocks // share, stride=share), :], sum_sc[pl.ds(1, blocks // share, stride=share), :]
     )
 
 
 def river_kernel(
-    stride, bed_ref, section_ref, block_ref, spot_ref, dhigh_ref, dlow_ref, early_ref,
-    diag_ref, rhs_ref, slot_section_ref, reach_ref, rhigh_sc, rlow_sc, sum_sc,
+    stride, bed_ref, section_ref, block_ref, spot_ref, rhs_ref, slot_section_ref, reach_ref, rhigh_sc, rlow_sc, sum_sc,
 ):
     rows = section_ref.shape[0]
     slots = reach_ref.shape[1]
@@ -146,19 +150,7 @@
     rhigh_sc[...] = high.astype(jnp.float32)
     rlow_sc[...] = low.astype(jnp.float32)
 
-    share = LANES // BLOCK
-    blocks = share * diag_ref.shape[0]
-    middle = early_groups(slots)
-    rhs_only = scatter_range(0, middle, blocks, block_ref, spot_ref, (rhigh_sc, rlow_sc))
-    both = scatter_range(
-        middle, slots // GROUP, blocks, block_ref, spot_ref, (dhigh_ref, dlow_ref, rhigh_sc, rlow_sc)
-    )
-    low_half = lax.broadcasted_iota(jnp.int32, diag_ref.shape, 1) < BLOCK
-    for part, ref in ((both[:, :LANES] + early_ref[...], diag_ref), (both[:, LANES:] + rhs_only, rhs_ref)):
-        sum_sc[...] = part + pltpu.roll(part, BLOCK, 1)
-        ref[...] = jnp.where(
-            low_half, sum_sc[pl.ds(0, blocks // share, stride=share), :], sum_sc[pl.ds(1, blocks // share, stride=share), :]
-        )
+    put_sums(rhs_ref, sum_sc, block_ref, spot_ref, (rhigh_sc, rlow_sc))
 
 
 def edge_kernel(land_ref, diag_ref, rhs_ref, *refs):
@@ -692,15 +684,16 @@
     riv_shape = jax.ShapeDtypeStruct((blocks, LANES), jnp.float32)
     node_field = jax.ShapeDtypeStruct((slots, LANES), jnp.float32)
     groups_of_cells = span * breadth // BLOCK
-    early = call(
-        functools.partial(early_kernel, breadth, span),
-        (node_field,) * 4 + (jax.ShapeDtypeStruct((groups_of_cells, LANES), jnp.float32),), [in_vmem] * 2, [], 2.5,
+    sums = pltpu.VMEM((groups_of_cells, LANES), jnp.float32)
+    block_number, spot, diag = call(
+        functools.partial(early_kernel, breadth, span), (node_field, node_field, riv_shape), [in_vmem] * 2,
+        [node_scratch] * 2 + [sums], 3,
     )(cells, bed)
-    diag, rhs, slot_section, reach = call(
+    rhs, slot_section, reach = call(
         functools.partial(river_kernel, stride),
-        (riv_shape, riv_shape, node_field, jax.ShapeDtypeStruct((1, slots), jnp.float32)),
-        [in_vmem] * 7, [node_scratch] * 2 + [pltpu.VMEM((groups_of_cells, LANES), jnp.float32)], 6,
-    )(bed, whole_section, *early)
+        (riv_shape, node_field, jax.ShapeDtypeStruct((1, slots), jnp.float32)),
+        [in_vmem] * 4, [node_scratch] * 2 + [sums], 5,
+    )(bed, whole_section, block_number, spot)
     edges = jax.ShapeDtypeStruct((-(-(2 * layers + 3) * HALO // 8) * 8, breadth), jnp.float32)
     near_edge, far_edge = call(
         edge_kernel, (edges, edges), [in_vmem] * (3 + groups), [], 0.1,

time: 50.8 us -> 50.9 us (level)
  starting transfers between devices: 20.4 us -> 21.2 us
  waiting for transfers between devices: 9.49 us -> 8.69 us
    all_to_all x1, starting transfers between devices: 3.5 us -> 4.32 us  [on_device(): lax.all_to_all(partial.reshape(tiles, fold, node_count), 'tile', 0, 0)]
    all_to_all x1, waiting for transfers between devices: 2.73 us -> 1.92 us  [on_device(): lax.all_to_all(spread, 'tile', 0, 0).reshape(tiles * stride, node_count)]
  transfers between devices with their start and end apart: 13 -> 13, of which waited for: 4 -> 4; matrix products, arithmetic and copies ran while one was open for 0% -> 0% of each run, Pallas kernels for 27% -> 28%
where the time goes in v17:
time: 50.9 us; the launch traced here: 50.5 us
  starting transfers between devices  21.2 us (42%)
  Pallas kernels  19.8 us (39%)
  waiting for transfers between devices  8.69 us (17%)
  between operations  0.84 us (2%)
    all_to_all x1, starting transfers between devices, on_device(): lax.all_to_all(spread, 'tile', 0, 0).reshape(tiles * stride, node_count)  7.4 us
    all_to_all x1, waiting for transfers between devices, on_device(): lax.all_to_all(partial.reshape(tiles, fold, node_count), 'tile', 0, 0)  5.82 us
    ppermute x9, starting transfers between devices, exchange(): lax.ppermute(parts[step], 'layer', [(i, i ^ step) for i in range(groups)])  5.73 us
    all_to_all x1, starting transfers between devices, on_device(): lax.all_to_all(partial.reshape(tiles, fold, node_count), 'tile', 0, 0)  4.32 us
    pallas_call x1, Pallas kernels, on_device(): call(stage_kernel, (own_field,) * (4 + 5 * ITERS + HALO), [in_smem] * 3 +...  4.09 us
    pallas_call x1, Pallas kernels, on_device(): call(flow_kernel, (head_shape,) * groups + (jax.ShapeDtypeStruct((span, b...  3.67 us
    pallas_call x1, Pallas kernels, on_device(): call(functools.partial(river_kernel, stride), (riv_shape, node_field, jax...  3.38 us
    pallas_call x1, Pallas kernels, on_device(): call(functools.partial(early_kernel, breadth, span), (node_field, node_fi...  3.14 us
  transfers between devices with their start and end apart: 13, of which 4 were waited for; matrix products, arithmetic and copies ran while one was open for 0% of the time, Pallas kernels for 28%

profile of v17, /device:TPU:0, one launch (start us, length us, event | category | flops | bytes accessed | tf_op | source)
XLA Modules:
  0.0 50.5 jit_solution(2951277042045180859)
XLA Ops:
  0.7 1.4 %shard_map.122.after_ref = f32[8,24,128]{2,1,0:T(8,128)} custom-call(f32[16,128]{1,0:T(8,128)} %section_hbm.1, s32[1,256]{1,0:T(1,128)} %owner_hbm.1, s32[1,256]{1,0:T(1,128)} %local_hbm.1), custom_call_target="tpu_custom_call" | custom-call | flops 1150000000 | tf_op jit(solution)/shard_map/pallas_call | solution.py:665
  2.1 7.4 %all-to-all-start = ((f32[8,24,128]{2,1,0:T(8,128)}), f32[8,24,128]{2,1,0:T(8,128)S(1)}, u32[]{:S(2)}, u32[]{:S(2)}) async-start(f32[8,24,128]{2,1,0:T(8,128)} %shard_map.122.after_ref), calls=%async_computation | async-start | bytes 196608 | tf_op jit(solution)/shard_map/all_to_all | solution.py:675
  9.7 1.6 %collective-permute-start.1 = (f32[2,2,16,512]{3,2,1,0:T(8,128)S(1)}, f32[2,2,16,512]{3,2,1,0:T(8,128)S(1)}, u32[]{:S(2)}, u32[]{:S(2)}) collective-permute-start(f32[2,2,16,512]{3,2,1,0:T(8,128)S(1)} %get-tuple-element.51), channel_id=1, source_target_pairs={{0,2},{1,3},{2,0},{3,1},{4,6},{5,7},{6,4},{7,5},{8,10},{9,11},{10,... | collective-permute-start | bytes 393224 | tf_op jit(solution)/shard_map/ppermute | solution.py:661
  11.3 0.3 collective-permute-start.2
  11.6 3.1 %shard_map.123 = (f32[256,128]{1,0:T(8,128)S(1)}, f32[256,128]{1,0:T(8,128)S(1)}, f32[64,128]{1,0:T(8,128)S(1)}) custom-call(s32[256,128]{1,0:T(8,128)S(1)} %bitcast.5, f32[256,128]{1,0:T(8,128)S(1)} %bitcast.7), custom_call_target="tpu_custom_call" | custom-call | flops 3449999872 | tf_op jit(solution)/shard_map/pallas_call | solution.py:688
  14.7 1.9 %all-to-all-done = f32[8,24,128]{2,1,0:T(8,128)S(1)} async-done(((f32[8,24,128]{2,1,0:T(8,128)}), f32[8,24,128]{2,1,0:T(8,128)S(1)}, u32[]{:S(2)}, u32[]{:S(2)}) %all-to-all-start) | async-done | bytes 98336 | tf_op jit(solution)/shard_map/all_to_all | solution.py:675
  16.6 3.4 %shard_map.124 = (f32[64,128]{1,0:T(8,128)S(1)}, f32[256,128]{1,0:T(8,128)S(1)}, f32[1,256]{1,0:T(1,128)S(1)}) custom-call(f32[256,128]{1,0:T(8,128)S(1)} %bitcast.8, f32[192,128]{1,0:T(8,128)S(1)} %bitcast.4, f32[256,128]{1,0:T(8,128)S(1)} %get-tuple-element.43.block_ref, f32[256,128]{1,0:T(8,128)S(1)} %get-tuple-element.44.spot_ref), custom_call_target="tpu_custom_call" | custom-call | flops 5750000128 | tf_op jit(solution)/shard_map/pallas_call | solution.py:692
  20.2 0.8 %collective-permute-start.3 = (f32[120,512]{1,0:T(8,128)S(1)}, f32[120,512]{1,0:T(8,128)S(1)}, u32[]{:S(2)}, u32[]{:S(2)}) collective-permute-start(f32[120,512]{1,0:T(8,128)S(1)} %get-tuple-element.53), channel_id=1, source_target_pairs={{1,2},{2,1},{3,7},{7,3},{5,6},{6,5},{4,8},{8,4},{9,10},{10,9},{11,... | collective-permute-start | bytes 737288 | tf_op jit(solution)/shard_map/ppermute | solution.py:701
  21.0 2.9 %collective-permute-start.4 = (f32[120,512]{1,0:T(8,128)S(1)}, f32[120,512]{1,0:T(8,128)S(1)}, u32[]{:S(2)}, u32[]{:S(2)}) collective-permute-start(f32[120,512]{1,0:T(8,128)S(1)} %get-tuple-element.54), channel_id=1, source_target_pairs={{0,1},{1,0},{2,3},{3,2},{4,5},{5,4},{6,7},{7,6},{8,9},{9,8},{10,11... | collective-permute-start | bytes 737288 | tf_op jit(solution)/shard_map/ppermute | solution.py:702
  24.0 4.1 %shard_map.127 = (f32[4,128,128]{2,1,0:T(8,128)S(1)}, f32[4,128,128]{2,1,0:T(8,128)S(1)}, f32[4,128,128]{2,1,0:T(8,128)S(1)}, f32[4,128,128]{2,1,0:T(8,128)S(1)}...) custom-call(f32[12]{0:T(128)S(1)} %copy-done.6, ...), custom_call_target="tpu_custom_call" | custom-call | flops 4600000000 | tf_op jit(solution)/shard_map/pallas_call | solution.py:707
  28.1 3.7 %shard_map.128 = (f32[2,16,512]{2,1,0:T(8,128)S(1)}, f32[2,16,512]{2,1,0:T(8,128)S(1)}, f32[2,16,512]{2,1,0:T(8,128)S(1)}, f32[2,16,512]{2,1,0:T(8,128)S(1)}, f32[16,512]{1,0:T(8,128)S(1)}) custom-call(f32[12]{0:T(128)S(1)} %copy-done.6, f32[12]{0:T(128)S(1)} %copy-done.7, f32[12]{0:T(128)S(1)} %copy-done.8, s32[64,512]{1,0:T(8,128)S(1)} %copy-done, ...), custom_call_target="tpu_custom_call" | custom-call | flops 3449999872 | tf_op jit(solution)/shard_map/pallas_call | solution.py:713
  31.7 0.1 collective-permute-start.5
  31.9 1.3 %collective-permute-start.6 = (f32[16,512]{1,0:T(8,128)S(1)}, f32[16,512]{1,0:T(8,128)S(1)}, u32[]{:S(2)}, u32[]{:S(2)}) collective-permute-start(f32[16,512]{1,0:T(8,128)S(1)} %get-tuple-element.75.refs_0_), channel_id=1, source_target_pairs={{0,2},{1,3},{2,0},{3,1},{4,6},{5,7},{6,4},{7,5},{8,10},{9,11},{10,... | collective-permute-start | bytes 98312 | tf_op jit(solution)/shard_map/ppermute | solution.py:661
  33.1 0.5 %collective-permute-start.7 = (f32[16,512]{1,0:T(8,128)S(1)}, f32[16,512]{1,0:T(8,128)S(1)}, u32[]{:S(2)}, u32[]{:S(2)}) collective-permute-start(f32[16,512]{1,0:T(8,128)S(1)} %get-tuple-element.75.refs_0_), channel_id=1, source_target_pairs={{0,3},{1,2},{2,1},{3,0},{4,7},{5,6},{6,5},{7,4},{8,11},{9,10},{10,... | collective-permute-start | bytes 98312 | tf_op jit(solution)/shard_map/ppermute | solution.py:661
  33.7 0.3 collective-permute-start.8
  34.0 1.2 %collective-permute-start.9 = (f32[2,16,512]{2,1,0:T(8,128)S(1)}, f32[2,16,512]{2,1,0:T(8,128)S(1)}, u32[]{:S(2)}, u32[]{:S(2)}) collective-permute-start(f32[2,16,512]{2,1,0:T(8,128)S(1)} %get-tuple-element.78), channel_id=1, source_target_pairs={{0,2},{1,3},{2,0},{3,1},{4,6},{5,7},{6,4},{7,5},{8,10},{9,11},{10,... | collective-permute-start | bytes 196616 | tf_op jit(solution)/shard_map/ppermute | solution.py:661
  35.3 0.3 collective-permute-start.10
  35.6 0.3 collective-permute-done.6.refs_2_
  35.8 0.7 %collective-permute-done.7.refs_3_ = f32[16,512]{1,0:T(8,128)S(1)} collective-permute-done((f32[16,512]{1,0:T(8,128)S(1)}, f32[16,512]{1,0:T(8,128)S(1)}, u32[]{:S(2)}, u32[]{:S(2)}) %collective-permute-start.7) | collective-permute-done | bytes 32800 | tf_op jit(solution)/shard_map/ppermute | solution.py:661
  36.5 2.5 %shard_map.129 = f32[32,128]{1,0:T(8,128)} custom-call(s32[256,128]{1,0:T(8,128)S(1)} %bitcast.6, f32[256,128]{1,0:T(8,128)S(1)} %bitcast.9, f32[256,128]{1,0:T(8,128)S(1)} %get-tuple-element.45.slot_section_ref, f32[1,256]{1,0:T(1,128)S(1)} %get-tuple-element.46.reach_ref, f32[16,512]{1,0:T(8,128)S(1)} %get-tuple-element.75.refs_0_, ...), custom_call_target="tpu_custom_call" | custom-call | flops 3449999872 | tf_op jit(solution)/shard_map/pallas_call | solution.py:728
  39.0 4.3 %all-to-all-start.1 = ((f32[8,4,128]{2,1,0:T(4,128)}), f32[8,4,128]{2,1,0:T(4,128)S(1)}, u32[]{:S(2)}, u32[]{:S(2)}) async-start(f32[8,4,128]{2,1,0:T(4,128)} %bitcast.3), calls=%async_computation.1 | async-start | bytes 32768 | tf_op jit(solution)/shard_map/all_to_all | solution.py:736
  43.3 0.7 %shard_map.130 = f32[2,64,512]{2,1,0:T(8,128)} custom-call(f32[2,16,512]{2,1,0:T(8,128)S(1)} %get-tuple-element.79.refs_0_, f32[2,16,512]{2,1,0:T(8,128)S(1)} %collective-permute-done.8.refs_1_, f32[2,16,512]{2,1,0:T(8,128)S(1)} %collective-permute-done.9.refs_2_, f32[2,16,512]{2,1,0:T(8,128)S(1)} %collective-permute-done.10.refs_3_), custom_call_target="tpu_custom_call" | custom-call | flops 805000000 | tf_op jit(solution)/shard_map/pallas_call | solution.py:737
  44.1 5.8 %all-to-all-done.1.terms_ref = f32[8,4,128]{2,1,0:T(4,128)S(1)} async-done(((f32[8,4,128]{2,1,0:T(4,128)}), f32[8,4,128]{2,1,0:T(4,128)S(1)}, u32[]{:S(2)}, u32[]{:S(2)}) %all-to-all-start.1) | async-done | bytes 16416 | tf_op jit(solution)/shard_map/all_to_all | solution.py:736
  49.9 0.7 %shard_map.131 = f32[16,32]{1,0:T(8,128)} custom-call(f32[8,4,128]{2,1,0:T(4,128)S(1)} %all-to-all-done.1.terms_ref), custom_call_target="tpu_custom_call" | custom-call | flops 115000000 | tf_op jit(solution)/shard_map/pallas_call | solution.py:742
  (30 shorter events, 0.3 us)
Async XLA Ops:
  0.6 8.9 %copy-start.2 = (f32[2,64,512]{2,1,0:T(8,128)S(1)}, f32[2,64,512]{2,1,0:T(8,128)}, u32[]{:S(2)}) copy-start(f32[2,64,512]{2,1,0:T(8,128)} %head_ref.1) | copy-start | bytes 786436
  0.6 8.9 %copy-start.3 = (s32[2,64,512]{2,1,0:T(8,128)S(1)}, s32[2,64,512]{2,1,0:T(8,128)}, u32[]{:S(2)}) copy-start(s32[2,64,512]{2,1,0:T(8,128)} %soil_ref.1) | copy-start | bytes 786436
  2.1 7.4 %copy-start.1 = (f32[8,24,128]{2,1,0:T(8,128)S(1)}, f32[8,24,128]{2,1,0:T(8,128)}, u32[]{:S(2)}) copy-start(f32[8,24,128]{2,1,0:T(8,128)} %shard_map.122.after_ref) | copy-start | bytes 294916
  2.1 14.5 %all-to-all-start = ((f32[8,24,128]{2,1,0:T(8,128)}), f32[8,24,128]{2,1,0:T(8,128)S(1)}, u32[]{:S(2)}, u32[]{:S(2)}) async-start(f32[8,24,128]{2,1,0:T(8,128)} %shard_map.122.after_ref), calls=%async_computation | async-start | bytes 196608 | tf_op jit(solution)/shard_map/all_to_all | solution.py:675
  9.5 2.0 %copy-start.4 = (s32[1,256,128]{2,1,0:T(8,128)S(1)}, s32[1,256,128]{2,1,0:T(8,128)}, u32[]{:S(2)}) copy-start(s32[1,256,128]{2,1,0:T(8,128)} %param.20) | copy-start | bytes 393220
  9.5 2.0 %copy-start.5 = (f32[1,256,128]{2,1,0:T(8,128)S(1)}, f32[1,256,128]{2,1,0:T(8,128)}, u32[]{:S(2)}) copy-start(f32[1,256,128]{2,1,0:T(8,128)} %param.21) | copy-start | bytes 393220
  9.6 10.4 %collective-permute-start = (f32[2,2,16,512]{3,2,1,0:T(8,128)S(1)}, f32[2,2,16,512]{3,2,1,0:T(8,128)S(1)}, u32[]{:S(2)}, u32[]{:S(2)}) collective-permute-start(f32[2,2,16,512]{3,2,1,0:T(8,128)S(1)} %get-tuple-element.50), channel_id=1, source_target_pairs={{0,1},{1,0},{2,3},{3,2},{4,5},{5,4},{6,7},{7,6},{8,9},{9,8},{10,11... | collective-permute-start | bytes 393224 | tf_op jit(solution)/shard_map/ppermute | solution.py:661
  9.7 10.3 %collective-permute-start.1 = (f32[2,2,16,512]{3,2,1,0:T(8,128)S(1)}, f32[2,2,16,512]{3,2,1,0:T(8,128)S(1)}, u32[]{:S(2)}, u32[]{:S(2)}) collective-permute-start(f32[2,2,16,512]{3,2,1,0:T(8,128)S(1)} %get-tuple-element.51), channel_id=1, source_target_pairs={{0,2},{1,3},{2,0},{3,1},{4,6},{5,7},{6,4},{7,5},{8,10},{9,11},{10,... | collective-permute-start | bytes 393224 | tf_op jit(solution)/shard_map/ppermute | solution.py:661
  11.3 8.8 %collective-permute-start.2 = (f32[2,2,16,512]{3,2,1,0:T(8,128)S(1)}, f32[2,2,16,512]{3,2,1,0:T(8,128)S(1)}, u32[]{:S(2)}, u32[]{:S(2)}) collective-permute-start(f32[2,2,16,512]{3,2,1,0:T(8,128)S(1)} %get-tuple-element.52), channel_id=1, source_target_pairs={{0,3},{1,2},{2,1},{3,0},{4,7},{5,6},{6,5},{7,4},{8,11},{9,10},{10,... | collective-permute-start | bytes 393224 | tf_op jit(solution)/shard_map/ppermute | solution.py:661
  16.6 3.4 %copy-start = (s32[64,512]{1,0:T(8,128)S(1)}, s32[64,512]{1,0:T(8,128)}, u32[]{:S(2)}) copy-start(s32[64,512]{1,0:T(8,128)} %land_ref.5) | copy-start | bytes 393220
  20.2 3.8 %copy-start.6 = (f32[12]{0:T(128)S(1)}, f32[12]{0:T(128)}, u32[]{:S(2)}) copy-start(f32[12]{0:T(128)} %kst_ref.1) | copy-start | bytes 148
  20.2 3.8 %copy-start.7 = (f32[12]{0:T(128)S(1)}, f32[12]{0:T(128)}, u32[]{:S(2)}) copy-start(f32[12]{0:T(128)} %alphat_ref.1) | copy-start | bytes 148
  20.2 3.8 %copy-start.8 = (f32[12]{0:T(128)S(1)}, f32[12]{0:T(128)}, u32[]{:S(2)}) copy-start(f32[12]{0:T(128)} %storet_ref.1) | copy-start | bytes 148
  20.2 7.9 %collective-permute-start.3 = (f32[120,512]{1,0:T(8,128)S(1)}, f32[120,512]{1,0:T(8,128)S(1)}, u32[]{:S(2)}, u32[]{:S(2)}) collective-permute-start(f32[120,512]{1,0:T(8,128)S(1)} %get-tuple-element.53), channel_id=1, source_target_pairs={{1,2},{2,1},{3,7},{7,3},{5,6},{6,5},{4,8},{8,4},{9,10},{10,9},{11,... | collective-permute-start | bytes 737288 | tf_op jit(solution)/shard_map/ppermute | solution.py:701
  21.0 7.1 %collective-permute-start.4 = (f32[120,512]{1,0:T(8,128)S(1)}, f32[120,512]{1,0:T(8,128)S(1)}, u32[]{:S(2)}, u32[]{:S(2)}) collective-permute-start(f32[120,512]{1,0:T(8,128)S(1)} %get-tuple-element.54), channel_id=1, source_target_pairs={{0,1},{1,0},{2,3},{3,2},{4,5},{5,4},{6,7},{7,6},{8,9},{9,8},{10,11... | collective-permute-start | bytes 737288 | tf_op jit(solution)/shard_map/ppermute | solution.py:702
  31.7 3.5 %collective-permute-start.5 = (f32[16,512]{1,0:T(8,128)S(1)}, f32[16,512]{1,0:T(8,128)S(1)}, u32[]{:S(2)}, u32[]{:S(2)}) collective-permute-start(f32[16,512]{1,0:T(8,128)S(1)} %get-tuple-element.75.refs_0_), channel_id=1, source_target_pairs={{0,1},{1,0},{2,3},{3,2},{4,5},{5,4},{6,7},{7,6},{8,9},{9,8},{10,11... | collective-permute-start | bytes 98312 | tf_op jit(solution)/shard_map/ppermute | solution.py:661
  31.9 4.0 %collective-permute-start.6 = (f32[16,512]{1,0:T(8,128)S(1)}, f32[16,512]{1,0:T(8,128)S(1)}, u32[]{:S(2)}, u32[]{:S(2)}) collective-permute-start(f32[16,512]{1,0:T(8,128)S(1)} %get-tuple-element.75.refs_0_), channel_id=1, source_target_pairs={{0,2},{1,3},{2,0},{3,1},{4,6},{5,7},{6,4},{7,5},{8,10},{9,11},{10,... | collective-permute-start | bytes 98312 | tf_op jit(solution)/shard_map/ppermute | solution.py:661
  33.1 3.3 %collective-permute-start.7 = (f32[16,512]{1,0:T(8,128)S(1)}, f32[16,512]{1,0:T(8,128)S(1)}, u32[]{:S(2)}, u32[]{:S(2)}) collective-permute-start(f32[16,512]{1,0:T(8,128)S(1)} %get-tuple-element.75.refs_0_), channel_id=1, source_target_pairs={{0,3},{1,2},{2,1},{3,0},{4,7},{5,6},{6,5},{7,4},{8,11},{9,10},{10,... | collective-permute-start | bytes 98312 | tf_op jit(solution)/shard_map/ppermute | solution.py:661
  33.7 5.3 %collective-permute-start.8 = (f32[2,16,512]{2,1,0:T(8,128)S(1)}, f32[2,16,512]{2,1,0:T(8,128)S(1)}, u32[]{:S(2)}, u32[]{:S(2)}) collective-permute-start(f32[2,16,512]{2,1,0:T(8,128)S(1)} %get-tuple-element.77), channel_id=1, source_target_pairs={{0,1},{1,0},{2,3},{3,2},{4,5},{5,4},{6,7},{7,6},{8,9},{9,8},{10,11... | collective-permute-start | bytes 196616 | tf_op jit(solution)/shard_map/ppermute | solution.py:661
  34.0 4.9 %collective-permute-start.9 = (f32[2,16,512]{2,1,0:T(8,128)S(1)}, f32[2,16,512]{2,1,0:T(8,128)S(1)}, u32[]{:S(2)}, u32[]{:S(2)}) collective-permute-start(f32[2,16,512]{2,1,0:T(8,128)S(1)} %get-tuple-element.78), channel_id=1, source_target_pairs={{0,2},{1,3},{2,0},{3,1},{4,6},{5,7},{6,4},{7,5},{8,10},{9,11},{10,... | collective-permute-start | bytes 196616 | tf_op jit(solution)/shard_map/ppermute | solution.py:661
  35.3 8.0 %collective-permute-start.10 = (f32[2,16,512]{2,1,0:T(8,128)S(1)}, f32[2,16,512]{2,1,0:T(8,128)S(1)}, u32[]{:S(2)}, u32[]{:S(2)}) collective-permute-start(f32[2,16,512]{2,1,0:T(8,128)S(1)} %get-tuple-element.82), channel_id=1, source_target_pairs={{0,3},{1,2},{2,1},{3,0},{4,7},{5,6},{6,5},{7,4},{8,11},{9,10},{10,... | collective-permute-start | bytes 196616 | tf_op jit(solution)/shard_map/ppermute | solution.py:661
  39.0 10.9 %all-to-all-start.1 = ((f32[8,4,128]{2,1,0:T(4,128)}), f32[8,4,128]{2,1,0:T(4,128)S(1)}, u32[]{:S(2)}, u32[]{:S(2)}) async-start(f32[8,4,128]{2,1,0:T(4,128)} %bitcast.3), calls=%async_computation.1 | async-start | bytes 32768 | tf_op jit(solution)/shard_map/all_to_all | solution.py:736

commit v18 on v17

--- a/solution.py
+++ b/solution.py
@@ -393,42 +393,51 @@
             done += 1
 
 
-def flow_kernel(kst_ref, alphat_ref, storet_ref, land_ref, far_ref, near_ref, diag_ref, rhs_ref, *refs):
+def flow_kernel(is_far, kst_ref, alphat_ref, storet_ref, land_ref, halo_ref, diag_ref, rhs_ref, *refs):
     groups = lax.axis_size("layer")
     own, _, number = position()
     end = (number == 0) | (number == groups - 1)
     far_partner = jnp.where(end, own, own ^ (groups - 1))
     tile, tiles = lax.axis_index("tile"), lax.axis_size("tile")
     outside = ((tile == 0) & (number == 0)) | ((tile == tiles - 1) & (number == groups - 1))
+    partner, water = (far_partner, outside) if is_far else (own ^ 1, False)
     first_ref, ks_ref, alpha_ref, store_ref = refs[:4]
     fields = [refs[4 + 5 * picard:9 + 5 * picard] for picard in range(ITERS)]
     staged_refs = refs[4 + 5 * ITERS:4 + 5 * ITERS + HALO]
     refs = refs[4 + 5 * ITERS + HALO:]
-    head_refs, top_ref = refs[:groups], refs[groups]
+    if is_far:
+        near_ref, refs = refs[0], refs[1:]
+        head_refs, top_ref, result_ref, refs = refs[:groups], refs[groups], refs[groups + 1], refs[groups + 2:]
+        held = head_refs[0].shape[0]
+    else:
+        result_ref, refs = refs[0], refs[1:]
     (
         first_sc, soil_sc, ks_sc, alpha_sc, store_sc, wx_sc, wy_sc, wz_sc, base_sc, inv_sc, ping_sc, pong_sc,
         land_sc, dtop_sc, rtop_sc, *lands,
-    ) = refs[1 + groups:]
-    held, span, breadth = head_refs[0].shape
-    layers = groups * held
+    ) = refs
+    breadth = land_ref.shape[1]
+    span = land_ref.shape[0] // groups
+    layers = first_ref.shape[1] // span
+    held = layers // groups
     window = span + 2 * HALO
     last_own = HALO + span
     rows = Rows(layers, breadth)
     side = HALO * rows.per_row
 
+    land_sc[...] = jnp.zeros_like(land_sc)
     land_sc[pl.ds(HALO, span), :] = own_land(land_ref, span)
     dtop_sc[pl.ds(side, span * rows.per_row), :] = diag_ref[...]
     rtop_sc[pl.ds(side, span * rows.per_row), :] = rhs_ref[...]
-
-    def put_halo(ref, partner, row):
+    top = lax.broadcasted_iota(jnp.int32, (layers, breadth), 0) == 0
+
+    def put_halo(row):
         def entry(number):
-            return ref[pl.ds(number * HALO, HALO), :]
+            return halo_ref[pl.ds(number * HALO, HALO), :]
 
         for count in range(layers):
             layer = (partner ^ (count // held)) * held + count % held
             rows.put_layer(first_sc, layer, row, entry(count))
             rows.put_layer(soil_sc, layer, row, entry(layers + count))
-        water = outside if ref is far_ref else False
         land_sc[pl.ds(row, HALO), :] = jnp.where(water, 0.0, entry(2 * layers))
         for count, top_sc in ((2 * layers + 1, dtop_sc), (2 * layers + 2, rtop_sc)):
             value = entry(count)
@@ -436,77 +445,86 @@
                 spot = pl.ds(row * rows.per_row + part, HALO, stride=rows.per_row)
                 top_sc[spot, :] = value[:, part * LANES:(part + 1) * LANES]
 
-    for odd, above_ref, below_ref in ((0, far_ref, near_ref), (1, near_ref, far_ref)):
-        @pl.when(lax.rem(number, 2) == odd)
-        def _(above_ref=above_ref, below_ref=below_ref):
-            for ref, row in ((above_ref, 0), (below_ref, last_own)):
-                put_halo(ref, own ^ 1 if ref is near_ref else far_partner, row)
-
-    faces = Faces(rows, land_sc[...], lands)
-    tables = lane_tables((kst_ref, alphat_ref, storet_ref), layers)
-    for row in [*range(HALO), *range(last_own, window)]:
-        soil = rows.get(soil_sc, row).astype(jnp.int32)
-        for table, ref in zip(tables, (ks_sc, alpha_sc, store_sc)):
-            rows.put(ref, row, look_up(rows, table, soil))
-
-    first, ks, alpha, store = [
-        Joined(rows, held_ref, full, HALO, last_own)
-        for held_ref, full in ((first_ref, first_sc), (ks_ref, ks_sc), (alpha_ref, alpha_sc), (store_ref, store_sc))
-    ]
-    top = lax.broadcasted_iota(jnp.int32, (layers, breadth), 0) == 0
-
-    now, begin, stop, done = first, 0, window, 0
-    for wx_ref, wy_ref, wz_ref, inv_ref, base_ref in fields:
-        low, high = HALO + done, last_own - done
-        wx_of = Joined(rows, wx_ref, wx_sc, low, high - 1)
-        wy_of, wz_of = Joined(rows, wy_ref, wy_sc, low, high), Joined(rows, wz_ref, wz_sc, low, high)
-        inverse, base = [
-            Joined(rows, held_ref, full, low + 1, high - 1) for held_ref, full in ((inv_ref, inv_sc), (base_ref, base_sc))
+    def one_side(above):
+        halo = 0 if above else last_own
+        put_halo(halo)
+        faces = Faces(rows, land_sc[...], lands)
+        tables = lane_tables((kst_ref, alphat_ref, storet_ref), layers)
+        for row in range(halo, halo + HALO):
+            soil = rows.get(soil_sc, row).astype(jnp.int32)
+            for table, ref in zip(tables, (ks_sc, alpha_sc, store_sc)):
+                rows.put(ref, row, look_up(rows, table, soil))
+        first, ks, alpha, store = [
+            Joined(rows, held_ref, full, HALO, last_own)
+            for held_ref, full in ((first_ref, first_sc), (ks_ref, ks_sc), (alpha_ref, alpha_sc), (store_ref, store_sc))
         ]
-        here_before, wx_before, sums_before = None, None, None
-        for row in range(begin, stop):
-            at_end = row in (low, high - 1)
-            here, sums = None, None
-            if not wy_of.holds(row) or at_end:
-                here = faces.conduct(ks.get(row), alpha.get(row), now.get(row))
-            if at_end:
-                sums = rows.get(inv_ref, row - HALO), rows.get(base_ref, row - HALO)
-            elif not wy_of.holds(row) and begin < row < stop - 1:
-                wy, wz, diagonal, gravity = faces.in_row(row, here)
-                wy_of.put(row, wy)
-                wz_of.put(row, wz)
-                sums = store.get(row) + diagonal, store.get(row) * first.get(row) + gravity
-            if row > begin:
-                if wx_of.holds(row - 1):
-                    wx = wx_of.get(row - 1)
-                else:
-                    wx = faces.between_rows(row - 1, here_before, here)
-                    wx_of.put(row - 1, wx)
-                if sums_before is not None:
-                    diagonal = sums_before[0] + wx_before + wx + river_row(rows, dtop_sc, row - 1, top)
-                    inverse.put(row - 1, reciprocal(diagonal))
-                    base.put(row - 1, sums_before[1] + river_row(rows, rtop_sc, row - 1, top))
-                wx_before = wx
-            here_before, sums_before = here, sums
-        for _ in range(SWEEPS):
-            begin, stop = begin + 1, stop - 1
-            later = Joined(rows, staged_refs[done], (ping_sc, pong_sc)[done % 2], HALO + done + 1, last_own - done - 1)
-            done += 1
-            for row in range(begin, stop):
-                if not later.holds(row):
+        now, begin, stop, done = first, 0, window, 0
+        for wx_ref, wy_ref, wz_ref, inv_ref, base_ref in fields:
+            low, high = HALO + done, last_own - done
+            wx_of = Joined(rows, wx_ref, wx_sc, low, high - 1)
+            wy_of, wz_of = Joined(rows, wy_ref, wy_sc, low, high), Joined(rows, wz_ref, wz_sc, low, high)
+            inverse, base = [
+                Joined(rows, held_ref, full, low + 1, high - 1) for held_ref, full in ((inv_ref, inv_sc), (base_ref, base_sc))
+            ]
+            start, finish, last_staged = (begin, low + 2, low) if above else (high - 2, stop, high - 1)
+            here_before, wx_before, sums_before = None, None, None
+            for row in range(start, finish):
+                here, sums = None, None
+                if row == last_staged or not wy_of.holds(row):
+                    here = faces.conduct(ks.get(row), alpha.get(row), now.get(row))
+                if row == last_staged:
+                    sums = rows.get(inv_ref, row - HALO), rows.get(base_ref, row - HALO)
+                elif not wy_of.holds(row) and begin < row < stop - 1:
+                    wy, wz, diagonal, gravity = faces.in_row(row, here)
+                    wy_of.put(row, wy)
+                    wz_of.put(row, wz)
+                    sums = store.get(row) + diagonal, store.get(row) * first.get(row) + gravity
+                if row > start:
+                    if wx_of.holds(row - 1):
+                        wx = wx_of.get(row - 1)
+                    else:
+                        wx = faces.between_rows(row - 1, here_before, here)
+                        wx_of.put(row - 1, wx)
+                    if sums_before is not None:
+                        diagonal = sums_before[0] + wx_before + wx + river_row(rows, dtop_sc, row - 1, top)
+                        inverse.put(row - 1, reciprocal(diagonal))
+                        base.put(row - 1, sums_before[1] + river_row(rows, rtop_sc, row - 1, top))
+                    wx_before = wx
+                here_before, sums_before = here, sums
+            for _ in range(SWEEPS):
+                begin, stop = begin + 1, stop - 1
+                later = Joined(
+                    rows, staged_refs[done], (ping_sc, pong_sc)[done % 2], HALO + done + 1, last_own - done - 1
+                )
+                done += 1
+                for row in range(begin, later.first) if above else range(later.last, stop):
                     head = now.get(row - 1), now.get(row), now.get(row + 1)
                     value, _ = relax_row(rows, row, head, (wx_of, wy_of, wz_of), wx_of.get(row - 1), base, inverse)
                     later.put(row, value)
-            now = later
-    for row in range(now.first, now.last):
-        now.put(row, now.get(row))
-    for part in range(rows.per_row):
-        lanes = pl.ds(part * LANES, LANES)
-        top_ref[:, lanes] = now.full[part, pl.ds(HALO * layers, span, stride=layers), :]
-        for step, head_ref in enumerate(head_refs):
-            for held_layer in range(held):
-                layer = (own ^ step) * held + held_layer
-                head_ref[held_layer, :, lanes] = now.full[part, pl.ds(HALO * layers + layer, span, stride=layers), :]
+                now = later
+        mine = range(HALO, now.first) if above else range(now.last, last_own)
+        for row in mine:
+            rows.put(result_ref, row - HALO, now.get(row))
+        if is_far:
+            for row in range(HALO, last_own):
+                if row not in mine:
+                    other = staged_refs[-1] if now.holds(row) else near_ref
+                    rows.put(result_ref, row - HALO, rows.get(other, row - HALO))
+
+    odd = lax.rem(number, 2)
+    for above in (True, False):
+        @pl.when(odd == (1 if above != is_far else 0))
+        def _(above=above):
+            one_side(above)
+
+    if is_far:
+        for part in range(rows.per_row):
+            lanes = pl.ds(part * LANES, LANES)
+            top_ref[:, lanes] = result_ref[part, pl.ds(0, span, stride=layers), :]
+            for step, head_ref in enumerate(head_refs):
+                for held_layer in range(held):
+                    layer = (own ^ step) * held + held_layer
+                    head_ref[held_layer, :, lanes] = result_ref[part, pl.ds(layer, span, stride=layers), :]
 
 
 def inflow_kernel(reach_rows, stride, cells_ref, bed_ref, slot_section_ref, reach_ref, *refs):
@@ -710,16 +728,22 @@
         4,
     )(ks_table, alpha_table, store_table, land_mask, diag, rhs, *received)
     head_shape = jax.ShapeDtypeStruct((held, span, breadth), jnp.float32)
-    *heads, top = call(
-        flow_kernel,
-        (head_shape,) * groups + (jax.ShapeDtypeStruct((span, breadth), jnp.float32),),
-        [in_smem] * 3 + [in_vmem] * (5 + len(staged)),
+    flow_scratch = (
         [field] * 12
         + [pltpu.VMEM((window, breadth), jnp.float32)]
         + [pltpu.VMEM((window * per_row, LANES), jnp.float32)] * 2
-        + [pltpu.VMEM((window, breadth), jnp.float32)] * 3,
-        3,
-    )(ks_table, alpha_table, store_table, land_mask, far_halo, near_halo, diag, rhs, *staged)
+        + [pltpu.VMEM((window, breadth), jnp.float32)] * 3
+    )
+    known = diag, rhs, *staged
+    near_side = call(
+        functools.partial(flow_kernel, False), own_field, [in_smem] * 3 + [in_vmem] * (2 + len(known)), flow_scratch, 2,
+    )(ks_table, alpha_table, store_table, land_mask, near_halo, *known)
+    *heads, top = call(
+        functools.partial(flow_kernel, True),
+        (head_shape,) * groups + (jax.ShapeDtypeStruct((span, breadth), jnp.float32),),
+        [in_smem] * 3 + [in_vmem] * (3 + len(known)),
+        [pltpu.VMEM(own_field.shape, jnp.float32)] + flow_scratch, 2,
+    )(ks_table, alpha_table, store_table, land_mask, far_halo, *known, near_side)
     tops = exchange([top] * groups)
     backs = exchange(heads)
 

time: 50.9 us -> 50.5 us (level)
    ppermute x1, starting transfers between devices: 2.93 us -> 0.07 us  [on_device(): near_halo = lax.ppermute(near_edge, 'layer', near)]
    ppermute x9, starting transfers between devices: 5.73 us -> 8.36 us  [exchange(): lax.ppermute(parts[step], 'layer', [(i, i ^ step) for i in range(groups)])]
    pallas_call x1 -> x2, Pallas kernels: 3.67 us -> 3.6 us  [the longest x1 1.88 us: on_device(): call(functools.partial(flow_kernel, True), (head_shape,) * groups + (jax....]
  transfers between devices with their start and end apart: 13 -> 13, of which waited for: 4 -> 4; matrix products, arithmetic and copies ran while one was open for 0% -> 0% of each run, Pallas kernels for 28% -> 31%
where the time goes in v18:
time: 50.5 us; the launch traced here: 50.2 us
  starting transfers between devices  20.7 us (41%)
  Pallas kernels  19.7 us (39%)
  waiting for transfers between devices  8.86 us (18%)
  between operations  0.88 us (2%)
    ppermute x9, starting transfers between devices, exchange(): lax.ppermute(parts[step], 'layer', [(i, i ^ step) for i in range(groups)])  8.36 us
    all_to_all x1, starting transfers between devices, on_device(): lax.all_to_all(spread, 'tile', 0, 0).reshape(tiles * stride, node_count)  7.4 us
    all_to_all x1, waiting for transfers between devices, on_device(): lax.all_to_all(partial.reshape(tiles, fold, node_count), 'tile', 0, 0)  5.82 us
    all_to_all x1, starting transfers between devices, on_device(): lax.all_to_all(partial.reshape(tiles, fold, node_count), 'tile', 0, 0)  4.18 us
    pallas_call x1, Pallas kernels, on_device(): call(stage_kernel, (own_field,) * (4 + 5 * ITERS + HALO), [in_smem] * 3 +...  4.1 us
    pallas_call x1, Pallas kernels, on_device(): call(functools.partial(river_kernel, stride), (riv_shape, node_field, jax...  3.38 us
    pallas_call x1, Pallas kernels, on_device(): call(functools.partial(early_kernel, breadth, span), (node_field, node_fi...  3.14 us
    pallas_call x1, Pallas kernels, on_device(): call(functools.partial(inflow_kernel, reach_rows, stride), jax.ShapeDtype...  2.49 us
  transfers between devices with their start and end apart: 13, of which 4 were waited for; matrix products, arithmetic and copies ran while one was open for 0% of the time, Pallas kernels for 31%

profile of v18, /device:TPU:0, one launch (start us, length us, event | category | flops | bytes accessed | tf_op | source)
XLA Modules:
  0.0 50.2 jit_solution(1779051698399049771)
XLA Ops:
  0.7 1.4 %shard_map.122.after_ref = f32[8,24,128]{2,1,0:T(8,128)} custom-call(f32[16,128]{1,0:T(8,128)} %section_hbm.1, s32[1,256]{1,0:T(1,128)} %owner_hbm.1, s32[1,256]{1,0:T(1,128)} %local_hbm.1), custom_call_target="tpu_custom_call" | custom-call | flops 1150000000 | tf_op jit(solution)/shard_map/pallas_call | solution.py:683
  2.1 7.4 %all-to-all-start = ((f32[8,24,128]{2,1,0:T(8,128)}), f32[8,24,128]{2,1,0:T(8,128)S(1)}, u32[]{:S(2)}, u32[]{:S(2)}) async-start(f32[8,24,128]{2,1,0:T(8,128)} %shard_map.122.after_ref), calls=%async_computation | async-start | bytes 196608 | tf_op jit(solution)/shard_map/all_to_all | solution.py:693
  9.7 1.6 %collective-permute-start.1 = (f32[2,2,16,512]{3,2,1,0:T(8,128)S(1)}, f32[2,2,16,512]{3,2,1,0:T(8,128)S(1)}, u32[]{:S(2)}, u32[]{:S(2)}) collective-permute-start(f32[2,2,16,512]{3,2,1,0:T(8,128)S(1)} %get-tuple-element.51), channel_id=1, source_target_pairs={{0,2},{1,3},{2,0},{3,1},{4,6},{5,7},{6,4},{7,5},{8,10},{9,11},{10,... | collective-permute-start | bytes 393224 | tf_op jit(solution)/shard_map/ppermute | solution.py:679
  11.3 0.3 collective-permute-start.2
  11.6 3.1 %shard_map.123 = (f32[256,128]{1,0:T(8,128)S(1)}, f32[256,128]{1,0:T(8,128)S(1)}, f32[64,128]{1,0:T(8,128)S(1)}) custom-call(s32[256,128]{1,0:T(8,128)S(1)} %bitcast.5, f32[256,128]{1,0:T(8,128)S(1)} %bitcast.7), custom_call_target="tpu_custom_call" | custom-call | flops 3449999872 | tf_op jit(solution)/shard_map/pallas_call | solution.py:706
  14.7 1.9 %all-to-all-done = f32[8,24,128]{2,1,0:T(8,128)S(1)} async-done(((f32[8,24,128]{2,1,0:T(8,128)}), f32[8,24,128]{2,1,0:T(8,128)S(1)}, u32[]{:S(2)}, u32[]{:S(2)}) %all-to-all-start) | async-done | bytes 98336 | tf_op jit(solution)/shard_map/all_to_all | solution.py:693
  16.6 3.4 %shard_map.124 = (f32[64,128]{1,0:T(8,128)S(1)}, f32[256,128]{1,0:T(8,128)S(1)}, f32[1,256]{1,0:T(1,128)S(1)}) custom-call(f32[256,128]{1,0:T(8,128)S(1)} %bitcast.8, f32[192,128]{1,0:T(8,128)S(1)} %bitcast.4, f32[256,128]{1,0:T(8,128)S(1)} %get-tuple-element.43.block_ref, f32[256,128]{1,0:T(8,128)S(1)} %get-tuple-element.44.spot_ref), custom_call_target="tpu_custom_call" | custom-call | flops 5750000128 | tf_op jit(solution)/shard_map/pallas_call | solution.py:710
  20.3 0.7 %collective-permute-start.3 = (f32[120,512]{1,0:T(8,128)S(1)}, f32[120,512]{1,0:T(8,128)S(1)}, u32[]{:S(2)}, u32[]{:S(2)}) collective-permute-start(f32[120,512]{1,0:T(8,128)S(1)} %get-tuple-element.53), channel_id=1, source_target_pairs={{1,2},{2,1},{3,7},{7,3},{5,6},{6,5},{4,8},{8,4},{9,10},{10,9},{11,... | collective-permute-start | bytes 737288 | tf_op jit(solution)/shard_map/ppermute | solution.py:719
  21.0 4.1 %shard_map.127 = (f32[4,128,128]{2,1,0:T(8,128)S(1)}, f32[4,128,128]{2,1,0:T(8,128)S(1)}, f32[4,128,128]{2,1,0:T(8,128)S(1)}, f32[4,128,128]{2,1,0:T(8,128)S(1)}...) custom-call(f32[12]{0:T(128)S(1)} %copy-done.6, ...), custom_call_target="tpu_custom_call" | custom-call | flops 4600000000 | tf_op jit(solution)/shard_map/pallas_call | solution.py:725
  25.1 1.7 %shard_map.128.refs_20_ = f32[4,128,128]{2,1,0:T(8,128)S(1)} custom-call(f32[12]{0:T(128)S(1)} %copy-done.6, f32[12]{0:T(128)S(1)} %copy-done.7, f32[12]{0:T(128)S(1)} %copy-done.8, s32[64,512]{1,0:T(8,128)S(1)} %copy-done, f32[120,512]{1,0:T(8,128)S(1)} %collective-permute-done.4.halo_ref, f32[64,128]{1,0:T(8,128)S(1)} %get-tuple-element.47.diag_ref, ...), custom_call_target="tpu_custom_call" | custom-call | flops 2300000000 | tf_op jit(solution)/shard_map/pallas_call | solution.py:738
  26.9 1.9 %shard_map.129 = (f32[2,16,512]{2,1,0:T(8,128)S(1)}, f32[2,16,512]{2,1,0:T(8,128)S(1)}, f32[2,16,512]{2,1,0:T(8,128)S(1)}, f32[2,16,512]{2,1,0:T(8,128)S(1)}, f32[16,512]{1,0:T(8,128)S(1)}) custom-call(f32[12]{0:T(128)S(1)} %copy-done.6, f32[12]{0:T(128)S(1)} %copy-done.7, f32[12]{0:T(128)S(1)} %copy-done.8, s32[64,512]{1,0:T(8,128)S(1)} %copy-done, ...), custom_call_target="tpu_custom_call" | custom-call | flops 2300000000 | tf_op jit(solution)/shard_map/pallas_call | solution.py:741
  28.7 2.9 %collective-permute-start.5 = (f32[16,512]{1,0:T(8,128)S(1)}, f32[16,512]{1,0:T(8,128)S(1)}, u32[]{:S(2)}, u32[]{:S(2)}) collective-permute-start(f32[16,512]{1,0:T(8,128)S(1)} %get-tuple-element.75.refs_0_), channel_id=1, source_target_pairs={{0,1},{1,0},{2,3},{3,2},{4,5},{5,4},{6,7},{7,6},{8,9},{9,8},{10,11... | collective-permute-start | bytes 98312 | tf_op jit(solution)/shard_map/ppermute | solution.py:679
  31.7 0.6 %collective-permute-start.6 = (f32[16,512]{1,0:T(8,128)S(1)}, f32[16,512]{1,0:T(8,128)S(1)}, u32[]{:S(2)}, u32[]{:S(2)}) collective-permute-start(f32[16,512]{1,0:T(8,128)S(1)} %get-tuple-element.75.refs_0_), channel_id=1, source_target_pairs={{0,2},{1,3},{2,0},{3,1},{4,6},{5,7},{6,4},{7,5},{8,10},{9,11},{10,... | collective-permute-start | bytes 98312 | tf_op jit(solution)/shard_map/ppermute | solution.py:679
  32.2 0.9 %collective-permute-start.7 = (f32[16,512]{1,0:T(8,128)S(1)}, f32[16,512]{1,0:T(8,128)S(1)}, u32[]{:S(2)}, u32[]{:S(2)}) collective-permute-start(f32[16,512]{1,0:T(8,128)S(1)} %get-tuple-element.75.refs_0_), channel_id=1, source_target_pairs={{0,3},{1,2},{2,1},{3,0},{4,7},{5,6},{6,5},{7,4},{8,11},{9,10},{10,... | collective-permute-start | bytes 98312 | tf_op jit(solution)/shard_map/ppermute | solution.py:679
  33.1 0.7 %collective-permute-start.8 = (f32[2,16,512]{2,1,0:T(8,128)S(1)}, f32[2,16,512]{2,1,0:T(8,128)S(1)}, u32[]{:S(2)}, u32[]{:S(2)}) collective-permute-start(f32[2,16,512]{2,1,0:T(8,128)S(1)} %get-tuple-element.77), channel_id=1, source_target_pairs={{0,1},{1,0},{2,3},{3,2},{4,5},{5,4},{6,7},{7,6},{8,9},{9,8},{10,11... | collective-permute-start | bytes 196616 | tf_op jit(solution)/shard_map/ppermute | solution.py:679
  33.8 0.6 %collective-permute-start.9 = (f32[2,16,512]{2,1,0:T(8,128)S(1)}, f32[2,16,512]{2,1,0:T(8,128)S(1)}, u32[]{:S(2)}, u32[]{:S(2)}) collective-permute-start(f32[2,16,512]{2,1,0:T(8,128)S(1)} %get-tuple-element.78), channel_id=1, source_target_pairs={{0,2},{1,3},{2,0},{3,1},{4,6},{5,7},{6,4},{7,5},{8,10},{9,11},{10,... | collective-permute-start | bytes 196616 | tf_op jit(solution)/shard_map/ppermute | solution.py:679
  34.4 0.8 %collective-permute-start.10 = (f32[2,16,512]{2,1,0:T(8,128)S(1)}, f32[2,16,512]{2,1,0:T(8,128)S(1)}, u32[]{:S(2)}, u32[]{:S(2)}) collective-permute-start(f32[2,16,512]{2,1,0:T(8,128)S(1)} %get-tuple-element.82), channel_id=1, source_target_pairs={{0,3},{1,2},{2,1},{3,0},{4,7},{5,6},{6,5},{7,4},{8,11},{9,10},{10,... | collective-permute-start | bytes 196616 | tf_op jit(solution)/shard_map/ppermute | solution.py:679
  35.2 0.8 %collective-permute-done.6.refs_2_ = f32[16,512]{1,0:T(8,128)S(1)} collective-permute-done((f32[16,512]{1,0:T(8,128)S(1)}, f32[16,512]{1,0:T(8,128)S(1)}, u32[]{:S(2)}, u32[]{:S(2)}) %collective-permute-start.6) | collective-permute-done | bytes 32800 | tf_op jit(solution)/shard_map/ppermute | solution.py:679
  35.9 2.5 %shard_map.130 = f32[32,128]{1,0:T(8,128)} custom-call(s32[256,128]{1,0:T(8,128)S(1)} %bitcast.6, f32[256,128]{1,0:T(8,128)S(1)} %bitcast.9, f32[256,128]{1,0:T(8,128)S(1)} %get-tuple-element.45.slot_section_ref, f32[1,256]{1,0:T(1,128)S(1)} %get-tuple-element.46.reach_ref, f32[16,512]{1,0:T(8,128)S(1)} %get-tuple-element.75.refs_0_, ...), custom_call_target="tpu_custom_call" | custom-call | flops 3449999872 | tf_op jit(solution)/shard_map/pallas_call | solution.py:752
  38.4 0.3 collective-permute-done.9.refs_2_
  38.8 4.2 %all-to-all-start.1 = ((f32[8,4,128]{2,1,0:T(4,128)}), f32[8,4,128]{2,1,0:T(4,128)S(1)}, u32[]{:S(2)}, u32[]{:S(2)}) async-start(f32[8,4,128]{2,1,0:T(4,128)} %bitcast.3), calls=%async_computation.1 | async-start | bytes 32768 | tf_op jit(solution)/shard_map/all_to_all | solution.py:760
  43.0 0.7 %shard_map.131 = f32[2,64,512]{2,1,0:T(8,128)} custom-call(f32[2,16,512]{2,1,0:T(8,128)S(1)} %get-tuple-element.79.refs_0_, f32[2,16,512]{2,1,0:T(8,128)S(1)} %collective-permute-done.8.refs_1_, f32[2,16,512]{2,1,0:T(8,128)S(1)} %collective-permute-done.9.refs_2_, f32[2,16,512]{2,1,0:T(8,128)S(1)} %collective-permute-done.10.refs_3_), custom_call_target="tpu_custom_call" | custom-call | flops 805000000 | tf_op jit(solution)/shard_map/pallas_call | solution.py:761
  43.7 5.8 %all-to-all-done.1.terms_ref = f32[8,4,128]{2,1,0:T(4,128)S(1)} async-done(((f32[8,4,128]{2,1,0:T(4,128)}), f32[8,4,128]{2,1,0:T(4,128)S(1)}, u32[]{:S(2)}, u32[]{:S(2)}) %all-to-all-start.1) | async-done | bytes 16416 | tf_op jit(solution)/shard_map/all_to_all | solution.py:760
  49.5 0.7 %shard_map.132 = f32[16,32]{1,0:T(8,128)} custom-call(f32[8,4,128]{2,1,0:T(4,128)S(1)} %all-to-all-done.1.terms_ref), custom_call_target="tpu_custom_call" | custom-call | flops 115000000 | tf_op jit(solution)/shard_map/pallas_call | solution.py:766
  (31 shorter events, 0.4 us)
Async XLA Ops:
  0.6 8.9 %copy-start.2 = (f32[2,64,512]{2,1,0:T(8,128)S(1)}, f32[2,64,512]{2,1,0:T(8,128)}, u32[]{:S(2)}) copy-start(f32[2,64,512]{2,1,0:T(8,128)} %head_ref.1) | copy-start | bytes 786436
  0.6 8.9 %copy-start.3 = (s32[2,64,512]{2,1,0:T(8,128)S(1)}, s32[2,64,512]{2,1,0:T(8,128)}, u32[]{:S(2)}) copy-start(s32[2,64,512]{2,1,0:T(8,128)} %soil_ref.1) | copy-start | bytes 786436
  2.1 7.4 %copy-start.1 = (f32[8,24,128]{2,1,0:T(8,128)S(1)}, f32[8,24,128]{2,1,0:T(8,128)}, u32[]{:S(2)}) copy-start(f32[8,24,128]{2,1,0:T(8,128)} %shard_map.122.after_ref) | copy-start | bytes 294916
  2.1 14.5 %all-to-all-start = ((f32[8,24,128]{2,1,0:T(8,128)}), f32[8,24,128]{2,1,0:T(8,128)S(1)}, u32[]{:S(2)}, u32[]{:S(2)}) async-start(f32[8,24,128]{2,1,0:T(8,128)} %shard_map.122.after_ref), calls=%async_computation | async-start | bytes 196608 | tf_op jit(solution)/shard_map/all_to_all | solution.py:693
  9.5 2.0 %copy-start.4 = (s32[1,256,128]{2,1,0:T(8,128)S(1)}, s32[1,256,128]{2,1,0:T(8,128)}, u32[]{:S(2)}) copy-start(s32[1,256,128]{2,1,0:T(8,128)} %param.20) | copy-start | bytes 393220
  9.5 2.0 %copy-start.5 = (f32[1,256,128]{2,1,0:T(8,128)S(1)}, f32[1,256,128]{2,1,0:T(8,128)}, u32[]{:S(2)}) copy-start(f32[1,256,128]{2,1,0:T(8,128)} %param.21) | copy-start | bytes 393220
  9.6 10.4 %collective-permute-start = (f32[2,2,16,512]{3,2,1,0:T(8,128)S(1)}, f32[2,2,16,512]{3,2,1,0:T(8,128)S(1)}, u32[]{:S(2)}, u32[]{:S(2)}) collective-permute-start(f32[2,2,16,512]{3,2,1,0:T(8,128)S(1)} %get-tuple-element.50), channel_id=1, source_target_pairs={{0,1},{1,0},{2,3},{3,2},{4,5},{5,4},{6,7},{7,6},{8,9},{9,8},{10,11... | collective-permute-start | bytes 393224 | tf_op jit(solution)/shard_map/ppermute | solution.py:679
  9.7 10.3 %collective-permute-start.1 = (f32[2,2,16,512]{3,2,1,0:T(8,128)S(1)}, f32[2,2,16,512]{3,2,1,0:T(8,128)S(1)}, u32[]{:S(2)}, u32[]{:S(2)}) collective-permute-start(f32[2,2,16,512]{3,2,1,0:T(8,128)S(1)} %get-tuple-element.51), channel_id=1, source_target_pairs={{0,2},{1,3},{2,0},{3,1},{4,6},{5,7},{6,4},{7,5},{8,10},{9,11},{10,... | collective-permute-start | bytes 393224 | tf_op jit(solution)/shard_map/ppermute | solution.py:679
  11.3 8.8 %collective-permute-start.2 = (f32[2,2,16,512]{3,2,1,0:T(8,128)S(1)}, f32[2,2,16,512]{3,2,1,0:T(8,128)S(1)}, u32[]{:S(2)}, u32[]{:S(2)}) collective-permute-start(f32[2,2,16,512]{3,2,1,0:T(8,128)S(1)} %get-tuple-element.52), channel_id=1, source_target_pairs={{0,3},{1,2},{2,1},{3,0},{4,7},{5,6},{6,5},{7,4},{8,11},{9,10},{10,... | collective-permute-start | bytes 393224 | tf_op jit(solution)/shard_map/ppermute | solution.py:679
  16.6 3.4 %copy-start = (s32[64,512]{1,0:T(8,128)S(1)}, s32[64,512]{1,0:T(8,128)}, u32[]{:S(2)}) copy-start(s32[64,512]{1,0:T(8,128)} %land_ref.7) | copy-start | bytes 393220
  20.2 0.8 %copy-start.6 = (f32[12]{0:T(128)S(1)}, f32[12]{0:T(128)}, u32[]{:S(2)}) copy-start(f32[12]{0:T(128)} %kst_ref.3) | copy-start | bytes 148
  20.2 0.8 %copy-start.7 = (f32[12]{0:T(128)S(1)}, f32[12]{0:T(128)}, u32[]{:S(2)}) copy-start(f32[12]{0:T(128)} %alphat_ref.3) | copy-start | bytes 148
  20.2 0.8 %copy-start.8 = (f32[12]{0:T(128)S(1)}, f32[12]{0:T(128)}, u32[]{:S(2)}) copy-start(f32[12]{0:T(128)} %storet_ref.3) | copy-start | bytes 148
  20.2 4.9 %collective-permute-start.4 = (f32[120,512]{1,0:T(8,128)S(1)}, f32[120,512]{1,0:T(8,128)S(1)}, u32[]{:S(2)}, u32[]{:S(2)}) collective-permute-start(f32[120,512]{1,0:T(8,128)S(1)} %get-tuple-element.74), channel_id=1, source_target_pairs={{0,1},{1,0},{2,3},{3,2},{4,5},{5,4},{6,7},{7,6},{8,9},{9,8},{10,11... | collective-permute-start | bytes 737288 | tf_op jit(solution)/shard_map/ppermute | solution.py:720
  20.3 6.6 %collective-permute-start.3 = (f32[120,512]{1,0:T(8,128)S(1)}, f32[120,512]{1,0:T(8,128)S(1)}, u32[]{:S(2)}, u32[]{:S(2)}) collective-permute-start(f32[120,512]{1,0:T(8,128)S(1)} %get-tuple-element.53), channel_id=1, source_target_pairs={{1,2},{2,1},{3,7},{7,3},{5,6},{6,5},{4,8},{8,4},{9,10},{10,9},{11,... | collective-permute-start | bytes 737288 | tf_op jit(solution)/shard_map/ppermute | solution.py:719
  28.7 5.6 %collective-permute-start.5 = (f32[16,512]{1,0:T(8,128)S(1)}, f32[16,512]{1,0:T(8,128)S(1)}, u32[]{:S(2)}, u32[]{:S(2)}) collective-permute-start(f32[16,512]{1,0:T(8,128)S(1)} %get-tuple-element.75.refs_0_), channel_id=1, source_target_pairs={{0,1},{1,0},{2,3},{3,2},{4,5},{5,4},{6,7},{7,6},{8,9},{9,8},{10,11... | collective-permute-start | bytes 98312 | tf_op jit(solution)/shard_map/ppermute | solution.py:679
  31.7 4.3 %collective-permute-start.6 = (f32[16,512]{1,0:T(8,128)S(1)}, f32[16,512]{1,0:T(8,128)S(1)}, u32[]{:S(2)}, u32[]{:S(2)}) collective-permute-start(f32[16,512]{1,0:T(8,128)S(1)} %get-tuple-element.75.refs_0_), channel_id=1, source_target_pairs={{0,2},{1,3},{2,0},{3,1},{4,6},{5,7},{6,4},{7,5},{8,10},{9,11},{10,... | collective-permute-start | bytes 98312 | tf_op jit(solution)/shard_map/ppermute | solution.py:679
  32.2 3.7 %collective-permute-start.7 = (f32[16,512]{1,0:T(8,128)S(1)}, f32[16,512]{1,0:T(8,128)S(1)}, u32[]{:S(2)}, u32[]{:S(2)}) collective-permute-start(f32[16,512]{1,0:T(8,128)S(1)} %get-tuple-element.75.refs_0_), channel_id=1, source_target_pairs={{0,3},{1,2},{2,1},{3,0},{4,7},{5,6},{6,5},{7,4},{8,11},{9,10},{10,... | collective-permute-start | bytes 98312 | tf_op jit(solution)/shard_map/ppermute | solution.py:679
  33.1 5.3 %collective-permute-start.8 = (f32[2,16,512]{2,1,0:T(8,128)S(1)}, f32[2,16,512]{2,1,0:T(8,128)S(1)}, u32[]{:S(2)}, u32[]{:S(2)}) collective-permute-start(f32[2,16,512]{2,1,0:T(8,128)S(1)} %get-tuple-element.77), channel_id=1, source_target_pairs={{0,1},{1,0},{2,3},{3,2},{4,5},{5,4},{6,7},{7,6},{8,9},{9,8},{10,11... | collective-permute-start | bytes 196616 | tf_op jit(solution)/shard_map/ppermute | solution.py:679
  33.8 5.0 %collective-permute-start.9 = (f32[2,16,512]{2,1,0:T(8,128)S(1)}, f32[2,16,512]{2,1,0:T(8,128)S(1)}, u32[]{:S(2)}, u32[]{:S(2)}) collective-permute-start(f32[2,16,512]{2,1,0:T(8,128)S(1)} %get-tuple-element.78), channel_id=1, source_target_pairs={{0,2},{1,3},{2,0},{3,1},{4,6},{5,7},{6,4},{7,5},{8,10},{9,11},{10,... | collective-permute-start | bytes 196616 | tf_op jit(solution)/shard_map/ppermute | solution.py:679
  34.4 8.6 %collective-permute-start.10 = (f32[2,16,512]{2,1,0:T(8,128)S(1)}, f32[2,16,512]{2,1,0:T(8,128)S(1)}, u32[]{:S(2)}, u32[]{:S(2)}) collective-permute-start(f32[2,16,512]{2,1,0:T(8,128)S(1)} %get-tuple-element.82), channel_id=1, source_target_pairs={{0,3},{1,2},{2,1},{3,0},{4,7},{5,6},{6,5},{7,4},{8,11},{9,10},{10,... | collective-permute-start | bytes 196616 | tf_op jit(solution)/shard_map/ppermute | solution.py:679
  38.8 10.8 %all-to-all-start.1 = ((f32[8,4,128]{2,1,0:T(4,128)}), f32[8,4,128]{2,1,0:T(4,128)S(1)}, u32[]{:S(2)}, u32[]{:S(2)}) async-start(f32[8,4,128]{2,1,0:T(4,128)} %bitcast.3), calls=%async_computation.1 | async-start | bytes 32768 | tf_op jit(solution)/shard_map/all_to_all | solution.py:760

commit v19 on v18

--- a/solution.py
+++ b/solution.py
@@ -79,7 +79,7 @@
     return block.astype(jnp.float32), (local & (width - 1)).astype(jnp.float32)
 
 
-GROUP = 64
+GROUP = 128
 
 
 def scatter_sum(group, blocks, block_ref, spot_ref, value_refs):

time: 50.5 us -> 50.3 us (level)
  Pallas kernels: 19.7 us -> 19.1 us
  transfers between devices with their start and end apart: 13 -> 13, of which waited for: 4 -> 4; matrix products, arithmetic and copies ran while one was open for 0% -> 0% of each run, Pallas kernels for 31% -> 30%
where the time goes in v19:
time: 50.3 us; the launch traced here: 50 us
  starting transfers between devices  20.8 us (41%)
  Pallas kernels  19.1 us (38%)
  waiting for transfers between devices  9.18 us (18%)
  between operations  0.88 us (2%)
    ppermute x9, starting transfers between devices, exchange(): lax.ppermute(parts[step], 'layer', [(i, i ^ step) for i in range(groups)])  8.36 us
    all_to_all x1, starting transfers between devices, on_device(): lax.all_to_all(spread, 'tile', 0, 0).reshape(tiles * stride, node_count)  7.4 us
    all_to_all x1, waiting for transfers between devices, on_device(): lax.all_to_all(partial.reshape(tiles, fold, node_count), 'tile', 0, 0)  5.82 us
    all_to_all x1, starting transfers between devices, on_device(): lax.all_to_all(partial.reshape(tiles, fold, node_count), 'tile', 0, 0)  4.31 us
    pallas_call x1, Pallas kernels, on_device(): call(stage_kernel, (own_field,) * (4 + 5 * ITERS + HALO), [in_smem] * 3 +...  4.1 us
    pallas_call x1, Pallas kernels, on_device(): call(functools.partial(river_kernel, stride), (riv_shape, node_field, jax...  3.06 us
    pallas_call x1, Pallas kernels, on_device(): call(functools.partial(early_kernel, breadth, span), (node_field, node_fi...  2.83 us
    pallas_call x1, Pallas kernels, on_device(): call(functools.partial(inflow_kernel, reach_rows, stride), jax.ShapeDtype...  2.49 us
  transfers between devices with their start and end apart: 13, of which 4 were waited for; matrix products, arithmetic and copies ran while one was open for 0% of the time, Pallas kernels for 30%

profile of v19, /device:TPU:0, one launch (start us, length us, event | category | flops | bytes accessed | tf_op | source)
XLA Modules:
  0.0 50.0 jit_solution(5777067631288324337)
XLA Ops:
  0.7 1.4 %shard_map.122.after_ref = f32[8,24,128]{2,1,0:T(8,128)} custom-call(f32[16,128]{1,0:T(8,128)} %section_hbm.1, s32[1,256]{1,0:T(1,128)} %owner_hbm.1, s32[1,256]{1,0:T(1,128)} %local_hbm.1), custom_call_target="tpu_custom_call" | custom-call | flops 1150000000 | tf_op jit(solution)/shard_map/pallas_call | solution.py:683
  2.1 7.4 %all-to-all-start = ((f32[8,24,128]{2,1,0:T(8,128)}), f32[8,24,128]{2,1,0:T(8,128)S(1)}, u32[]{:S(2)}, u32[]{:S(2)}) async-start(f32[8,24,128]{2,1,0:T(8,128)} %shard_map.122.after_ref), calls=%async_computation | async-start | bytes 196608 | tf_op jit(solution)/shard_map/all_to_all | solution.py:693
  9.7 1.6 %collective-permute-start.1 = (f32[2,2,16,512]{3,2,1,0:T(8,128)S(1)}, f32[2,2,16,512]{3,2,1,0:T(8,128)S(1)}, u32[]{:S(2)}, u32[]{:S(2)}) collective-permute-start(f32[2,2,16,512]{3,2,1,0:T(8,128)S(1)} %get-tuple-element.51), channel_id=1, source_target_pairs={{0,2},{1,3},{2,0},{3,1},{4,6},{5,7},{6,4},{7,5},{8,10},{9,11},{10,... | collective-permute-start | bytes 393224 | tf_op jit(solution)/shard_map/ppermute | solution.py:679
  11.3 0.3 collective-permute-start.2
  11.6 2.8 %shard_map.123 = (f32[256,128]{1,0:T(8,128)S(1)}, f32[256,128]{1,0:T(8,128)S(1)}, f32[64,128]{1,0:T(8,128)S(1)}) custom-call(s32[256,128]{1,0:T(8,128)S(1)} %bitcast.5, f32[256,128]{1,0:T(8,128)S(1)} %bitcast.7), custom_call_target="tpu_custom_call" | custom-call | flops 3449999872 | tf_op jit(solution)/shard_map/pallas_call | solution.py:706
  14.4 2.2 %all-to-all-done = f32[8,24,128]{2,1,0:T(8,128)S(1)} async-done(((f32[8,24,128]{2,1,0:T(8,128)}), f32[8,24,128]{2,1,0:T(8,128)S(1)}, u32[]{:S(2)}, u32[]{:S(2)}) %all-to-all-start) | async-done | bytes 98336 | tf_op jit(solution)/shard_map/all_to_all | solution.py:693
  16.6 3.1 %shard_map.124 = (f32[64,128]{1,0:T(8,128)S(1)}, f32[256,128]{1,0:T(8,128)S(1)}, f32[1,256]{1,0:T(1,128)S(1)}) custom-call(f32[256,128]{1,0:T(8,128)S(1)} %bitcast.8, f32[192,128]{1,0:T(8,128)S(1)} %bitcast.4, f32[256,128]{1,0:T(8,128)S(1)} %get-tuple-element.43.block_ref, f32[256,128]{1,0:T(8,128)S(1)} %get-tuple-element.44.spot_ref), custom_call_target="tpu_custom_call" | custom-call | flops 5750000128 | tf_op jit(solution)/shard_map/pallas_call | solution.py:710
  20.0 0.7 %collective-permute-start.3 = (f32[120,512]{1,0:T(8,128)S(1)}, f32[120,512]{1,0:T(8,128)S(1)}, u32[]{:S(2)}, u32[]{:S(2)}) collective-permute-start(f32[120,512]{1,0:T(8,128)S(1)} %get-tuple-element.53), channel_id=1, source_target_pairs={{1,2},{2,1},{3,7},{7,3},{5,6},{6,5},{4,8},{8,4},{9,10},{10,9},{11,... | collective-permute-start | bytes 737288 | tf_op jit(solution)/shard_map/ppermute | solution.py:719
  20.7 4.1 %shard_map.127 = (f32[4,128,128]{2,1,0:T(8,128)S(1)}, f32[4,128,128]{2,1,0:T(8,128)S(1)}, f32[4,128,128]{2,1,0:T(8,128)S(1)}, f32[4,128,128]{2,1,0:T(8,128)S(1)}...) custom-call(f32[12]{0:T(128)S(1)} %copy-done.6, ...), custom_call_target="tpu_custom_call" | custom-call | flops 4600000000 | tf_op jit(solution)/shard_map/pallas_call | solution.py:725
  24.8 1.7 %shard_map.128.refs_20_ = f32[4,128,128]{2,1,0:T(8,128)S(1)} custom-call(f32[12]{0:T(128)S(1)} %copy-done.6, f32[12]{0:T(128)S(1)} %copy-done.7, f32[12]{0:T(128)S(1)} %copy-done.8, s32[64,512]{1,0:T(8,128)S(1)} %copy-done, f32[120,512]{1,0:T(8,128)S(1)} %collective-permute-done.4.halo_ref, f32[64,128]{1,0:T(8,128)S(1)} %get-tuple-element.47.diag_ref, ...), custom_call_target="tpu_custom_call" | custom-call | flops 2300000000 | tf_op jit(solution)/shard_map/pallas_call | solution.py:738
  26.5 1.9 %shard_map.129 = (f32[2,16,512]{2,1,0:T(8,128)S(1)}, f32[2,16,512]{2,1,0:T(8,128)S(1)}, f32[2,16,512]{2,1,0:T(8,128)S(1)}, f32[2,16,512]{2,1,0:T(8,128)S(1)}, f32[16,512]{1,0:T(8,128)S(1)}) custom-call(f32[12]{0:T(128)S(1)} %copy-done.6, f32[12]{0:T(128)S(1)} %copy-done.7, f32[12]{0:T(128)S(1)} %copy-done.8, s32[64,512]{1,0:T(8,128)S(1)} %copy-done, ...), custom_call_target="tpu_custom_call" | custom-call | flops 2300000000 | tf_op jit(solution)/shard_map/pallas_call | solution.py:741
  28.4 2.9 %collective-permute-start.5 = (f32[16,512]{1,0:T(8,128)S(1)}, f32[16,512]{1,0:T(8,128)S(1)}, u32[]{:S(2)}, u32[]{:S(2)}) collective-permute-start(f32[16,512]{1,0:T(8,128)S(1)} %get-tuple-element.75.refs_0_), channel_id=1, source_target_pairs={{0,1},{1,0},{2,3},{3,2},{4,5},{5,4},{6,7},{7,6},{8,9},{9,8},{10,11... | collective-permute-start | bytes 98312 | tf_op jit(solution)/shard_map/ppermute | solution.py:679
  31.3 0.6 %collective-permute-start.6 = (f32[16,512]{1,0:T(8,128)S(1)}, f32[16,512]{1,0:T(8,128)S(1)}, u32[]{:S(2)}, u32[]{:S(2)}) collective-permute-start(f32[16,512]{1,0:T(8,128)S(1)} %get-tuple-element.75.refs_0_), channel_id=1, source_target_pairs={{0,2},{1,3},{2,0},{3,1},{4,6},{5,7},{6,4},{7,5},{8,10},{9,11},{10,... | collective-permute-start | bytes 98312 | tf_op jit(solution)/shard_map/ppermute | solution.py:679
  31.9 0.9 %collective-permute-start.7 = (f32[16,512]{1,0:T(8,128)S(1)}, f32[16,512]{1,0:T(8,128)S(1)}, u32[]{:S(2)}, u32[]{:S(2)}) collective-permute-start(f32[16,512]{1,0:T(8,128)S(1)} %get-tuple-element.75.refs_0_), channel_id=1, source_target_pairs={{0,3},{1,2},{2,1},{3,0},{4,7},{5,6},{6,5},{7,4},{8,11},{9,10},{10,... | collective-permute-start | bytes 98312 | tf_op jit(solution)/shard_map/ppermute | solution.py:679
  32.8 0.7 %collective-permute-start.8 = (f32[2,16,512]{2,1,0:T(8,128)S(1)}, f32[2,16,512]{2,1,0:T(8,128)S(1)}, u32[]{:S(2)}, u32[]{:S(2)}) collective-permute-start(f32[2,16,512]{2,1,0:T(8,128)S(1)} %get-tuple-element.77), channel_id=1, source_target_pairs={{0,1},{1,0},{2,3},{3,2},{4,5},{5,4},{6,7},{7,6},{8,9},{9,8},{10,11... | collective-permute-start | bytes 196616 | tf_op jit(solution)/shard_map/ppermute | solution.py:679
  33.5 0.6 %collective-permute-start.9 = (f32[2,16,512]{2,1,0:T(8,128)S(1)}, f32[2,16,512]{2,1,0:T(8,128)S(1)}, u32[]{:S(2)}, u32[]{:S(2)}) collective-permute-start(f32[2,16,512]{2,1,0:T(8,128)S(1)} %get-tuple-element.78), channel_id=1, source_target_pairs={{0,2},{1,3},{2,0},{3,1},{4,6},{5,7},{6,4},{7,5},{8,10},{9,11},{10,... | collective-permute-start | bytes 196616 | tf_op jit(solution)/shard_map/ppermute | solution.py:679
  34.1 0.8 %collective-permute-start.10 = (f32[2,16,512]{2,1,0:T(8,128)S(1)}, f32[2,16,512]{2,1,0:T(8,128)S(1)}, u32[]{:S(2)}, u32[]{:S(2)}) collective-permute-start(f32[2,16,512]{2,1,0:T(8,128)S(1)} %get-tuple-element.82), channel_id=1, source_target_pairs={{0,3},{1,2},{2,1},{3,0},{4,7},{5,6},{6,5},{7,4},{8,11},{9,10},{10,... | collective-permute-start | bytes 196616 | tf_op jit(solution)/shard_map/ppermute | solution.py:679
  34.8 0.7 %collective-permute-done.6.refs_2_ = f32[16,512]{1,0:T(8,128)S(1)} collective-permute-done((f32[16,512]{1,0:T(8,128)S(1)}, f32[16,512]{1,0:T(8,128)S(1)}, u32[]{:S(2)}, u32[]{:S(2)}) %collective-permute-start.6) | collective-permute-done | bytes 32800 | tf_op jit(solution)/shard_map/ppermute | solution.py:679
  35.6 2.5 %shard_map.130 = f32[32,128]{1,0:T(8,128)} custom-call(s32[256,128]{1,0:T(8,128)S(1)} %bitcast.6, f32[256,128]{1,0:T(8,128)S(1)} %bitcast.9, f32[256,128]{1,0:T(8,128)S(1)} %get-tuple-element.45.slot_section_ref, f32[1,256]{1,0:T(1,128)S(1)} %get-tuple-element.46.reach_ref, f32[16,512]{1,0:T(8,128)S(1)} %get-tuple-element.75.refs_0_, ...), custom_call_target="tpu_custom_call" | custom-call | flops 3449999872 | tf_op jit(solution)/shard_map/pallas_call | solution.py:752
  38.1 0.4 collective-permute-done.9.refs_2_
  38.4 4.3 %all-to-all-start.1 = ((f32[8,4,128]{2,1,0:T(4,128)}), f32[8,4,128]{2,1,0:T(4,128)S(1)}, u32[]{:S(2)}, u32[]{:S(2)}) async-start(f32[8,4,128]{2,1,0:T(4,128)} %bitcast.3), calls=%async_computation.1 | async-start | bytes 32768 | tf_op jit(solution)/shard_map/all_to_all | solution.py:760
  42.8 0.7 %shard_map.131 = f32[2,64,512]{2,1,0:T(8,128)} custom-call(f32[2,16,512]{2,1,0:T(8,128)S(1)} %get-tuple-element.79.refs_0_, f32[2,16,512]{2,1,0:T(8,128)S(1)} %collective-permute-done.8.refs_1_, f32[2,16,512]{2,1,0:T(8,128)S(1)} %collective-permute-done.9.refs_2_, f32[2,16,512]{2,1,0:T(8,128)S(1)} %collective-permute-done.10.refs_3_), custom_call_target="tpu_custom_call" | custom-call | flops 805000000 | tf_op jit(solution)/shard_map/pallas_call | solution.py:761
  43.5 5.8 %all-to-all-done.1.terms_ref = f32[8,4,128]{2,1,0:T(4,128)S(1)} async-done(((f32[8,4,128]{2,1,0:T(4,128)}), f32[8,4,128]{2,1,0:T(4,128)S(1)}, u32[]{:S(2)}, u32[]{:S(2)}) %all-to-all-start.1) | async-done | bytes 16416 | tf_op jit(solution)/shard_map/all_to_all | solution.py:760
  49.3 0.7 %shard_map.132 = f32[16,32]{1,0:T(8,128)} custom-call(f32[8,4,128]{2,1,0:T(4,128)S(1)} %all-to-all-done.1.terms_ref), custom_call_target="tpu_custom_call" | custom-call | flops 115000000 | tf_op jit(solution)/shard_map/pallas_call | solution.py:766
  (31 shorter events, 0.4 us)
Async XLA Ops:
  0.6 8.9 %copy-start.2 = (f32[2,64,512]{2,1,0:T(8,128)S(1)}, f32[2,64,512]{2,1,0:T(8,128)}, u32[]{:S(2)}) copy-start(f32[2,64,512]{2,1,0:T(8,128)} %head_ref.1) | copy-start | bytes 786436
  0.6 8.9 %copy-start.3 = (s32[2,64,512]{2,1,0:T(8,128)S(1)}, s32[2,64,512]{2,1,0:T(8,128)}, u32[]{:S(2)}) copy-start(s32[2,64,512]{2,1,0:T(8,128)} %soil_ref.1) | copy-start | bytes 786436
  2.1 7.4 %copy-start.1 = (f32[8,24,128]{2,1,0:T(8,128)S(1)}, f32[8,24,128]{2,1,0:T(8,128)}, u32[]{:S(2)}) copy-start(f32[8,24,128]{2,1,0:T(8,128)} %shard_map.122.after_ref) | copy-start | bytes 294916
  2.1 14.5 %all-to-all-start = ((f32[8,24,128]{2,1,0:T(8,128)}), f32[8,24,128]{2,1,0:T(8,128)S(1)}, u32[]{:S(2)}, u32[]{:S(2)}) async-start(f32[8,24,128]{2,1,0:T(8,128)} %shard_map.122.after_ref), calls=%async_computation | async-start | bytes 196608 | tf_op jit(solution)/shard_map/all_to_all | solution.py:693
  9.5 2.0 %copy-start.4 = (s32[1,256,128]{2,1,0:T(8,128)S(1)}, s32[1,256,128]{2,1,0:T(8,128)}, u32[]{:S(2)}) copy-start(s32[1,256,128]{2,1,0:T(8,128)} %param.20) | copy-start | bytes 393220
  9.5 2.0 %copy-start.5 = (f32[1,256,128]{2,1,0:T(8,128)S(1)}, f32[1,256,128]{2,1,0:T(8,128)}, u32[]{:S(2)}) copy-start(f32[1,256,128]{2,1,0:T(8,128)} %param.21) | copy-start | bytes 393220
  9.6 10.1 %collective-permute-start = (f32[2,2,16,512]{3,2,1,0:T(8,128)S(1)}, f32[2,2,16,512]{3,2,1,0:T(8,128)S(1)}, u32[]{:S(2)}, u32[]{:S(2)}) collective-permute-start(f32[2,2,16,512]{3,2,1,0:T(8,128)S(1)} %get-tuple-element.50), channel_id=1, source_target_pairs={{0,1},{1,0},{2,3},{3,2},{4,5},{5,4},{6,7},{7,6},{8,9},{9,8},{10,11... | collective-permute-start | bytes 393224 | tf_op jit(solution)/shard_map/ppermute | solution.py:679
  9.7 10.0 %collective-permute-start.1 = (f32[2,2,16,512]{3,2,1,0:T(8,128)S(1)}, f32[2,2,16,512]{3,2,1,0:T(8,128)S(1)}, u32[]{:S(2)}, u32[]{:S(2)}) collective-permute-start(f32[2,2,16,512]{3,2,1,0:T(8,128)S(1)} %get-tuple-element.51), channel_id=1, source_target_pairs={{0,2},{1,3},{2,0},{3,1},{4,6},{5,7},{6,4},{7,5},{8,10},{9,11},{10,... | collective-permute-start | bytes 393224 | tf_op jit(solution)/shard_map/ppermute | solution.py:679
  11.3 8.4 %collective-permute-start.2 = (f32[2,2,16,512]{3,2,1,0:T(8,128)S(1)}, f32[2,2,16,512]{3,2,1,0:T(8,128)S(1)}, u32[]{:S(2)}, u32[]{:S(2)}) collective-permute-start(f32[2,2,16,512]{3,2,1,0:T(8,128)S(1)} %get-tuple-element.52), channel_id=1, source_target_pairs={{0,3},{1,2},{2,1},{3,0},{4,7},{5,6},{6,5},{7,4},{8,11},{9,10},{10,... | collective-permute-start | bytes 393224 | tf_op jit(solution)/shard_map/ppermute | solution.py:679
  16.6 3.1 %copy-start = (s32[64,512]{1,0:T(8,128)S(1)}, s32[64,512]{1,0:T(8,128)}, u32[]{:S(2)}) copy-start(s32[64,512]{1,0:T(8,128)} %land_ref.7) | copy-start | bytes 393220
  19.8 0.8 %copy-start.6 = (f32[12]{0:T(128)S(1)}, f32[12]{0:T(128)}, u32[]{:S(2)}) copy-start(f32[12]{0:T(128)} %kst_ref.3) | copy-start | bytes 148
  19.8 0.8 %copy-start.7 = (f32[12]{0:T(128)S(1)}, f32[12]{0:T(128)}, u32[]{:S(2)}) copy-start(f32[12]{0:T(128)} %alphat_ref.3) | copy-start | bytes 148
  19.9 0.8 %copy-start.8 = (f32[12]{0:T(128)S(1)}, f32[12]{0:T(128)}, u32[]{:S(2)}) copy-start(f32[12]{0:T(128)} %storet_ref.3) | copy-start | bytes 148
  19.9 4.9 %collective-permute-start.4 = (f32[120,512]{1,0:T(8,128)S(1)}, f32[120,512]{1,0:T(8,128)S(1)}, u32[]{:S(2)}, u32[]{:S(2)}) collective-permute-start(f32[120,512]{1,0:T(8,128)S(1)} %get-tuple-element.74), channel_id=1, source_target_pairs={{0,1},{1,0},{2,3},{3,2},{4,5},{5,4},{6,7},{7,6},{8,9},{9,8},{10,11... | collective-permute-start | bytes 737288 | tf_op jit(solution)/shard_map/ppermute | solution.py:720
  20.0 6.6 %collective-permute-start.3 = (f32[120,512]{1,0:T(8,128)S(1)}, f32[120,512]{1,0:T(8,128)S(1)}, u32[]{:S(2)}, u32[]{:S(2)}) collective-permute-start(f32[120,512]{1,0:T(8,128)S(1)} %get-tuple-element.53), channel_id=1, source_target_pairs={{1,2},{2,1},{3,7},{7,3},{5,6},{6,5},{4,8},{8,4},{9,10},{10,9},{11,... | collective-permute-start | bytes 737288 | tf_op jit(solution)/shard_map/ppermute | solution.py:719
  28.4 5.6 %collective-permute-start.5 = (f32[16,512]{1,0:T(8,128)S(1)}, f32[16,512]{1,0:T(8,128)S(1)}, u32[]{:S(2)}, u32[]{:S(2)}) collective-permute-start(f32[16,512]{1,0:T(8,128)S(1)} %get-tuple-element.75.refs_0_), channel_id=1, source_target_pairs={{0,1},{1,0},{2,3},{3,2},{4,5},{5,4},{6,7},{7,6},{8,9},{9,8},{10,11... | collective-permute-start | bytes 98312 | tf_op jit(solution)/shard_map/ppermute | solution.py:679
  31.3 4.2 %collective-permute-start.6 = (f32[16,512]{1,0:T(8,128)S(1)}, f32[16,512]{1,0:T(8,128)S(1)}, u32[]{:S(2)}, u32[]{:S(2)}) collective-permute-start(f32[16,512]{1,0:T(8,128)S(1)} %get-tuple-element.75.refs_0_), channel_id=1, source_target_pairs={{0,2},{1,3},{2,0},{3,1},{4,6},{5,7},{6,4},{7,5},{8,10},{9,11},{10,... | collective-permute-start | bytes 98312 | tf_op jit(solution)/shard_map/ppermute | solution.py:679
  31.9 3.7 %collective-permute-start.7 = (f32[16,512]{1,0:T(8,128)S(1)}, f32[16,512]{1,0:T(8,128)S(1)}, u32[]{:S(2)}, u32[]{:S(2)}) collective-permute-start(f32[16,512]{1,0:T(8,128)S(1)} %get-tuple-element.75.refs_0_), channel_id=1, source_target_pairs={{0,3},{1,2},{2,1},{3,0},{4,7},{5,6},{6,5},{7,4},{8,11},{9,10},{10,... | collective-permute-start | bytes 98312 | tf_op jit(solution)/shard_map/ppermute | solution.py:679
  32.8 5.3 %collective-permute-start.8 = (f32[2,16,512]{2,1,0:T(8,128)S(1)}, f32[2,16,512]{2,1,0:T(8,128)S(1)}, u32[]{:S(2)}, u32[]{:S(2)}) collective-permute-start(f32[2,16,512]{2,1,0:T(8,128)S(1)} %get-tuple-element.77), channel_id=1, source_target_pairs={{0,1},{1,0},{2,3},{3,2},{4,5},{5,4},{6,7},{7,6},{8,9},{9,8},{10,11... | collective-permute-start | bytes 196616 | tf_op jit(solution)/shard_map/ppermute | solution.py:679
  33.5 5.0 %collective-permute-start.9 = (f32[2,16,512]{2,1,0:T(8,128)S(1)}, f32[2,16,512]{2,1,0:T(8,128)S(1)}, u32[]{:S(2)}, u32[]{:S(2)}) collective-permute-start(f32[2,16,512]{2,1,0:T(8,128)S(1)} %get-tuple-element.78), channel_id=1, source_target_pairs={{0,2},{1,3},{2,0},{3,1},{4,6},{5,7},{6,4},{7,5},{8,10},{9,11},{10,... | collective-permute-start | bytes 196616 | tf_op jit(solution)/shard_map/ppermute | solution.py:679
  34.1 8.7 %collective-permute-start.10 = (f32[2,16,512]{2,1,0:T(8,128)S(1)}, f32[2,16,512]{2,1,0:T(8,128)S(1)}, u32[]{:S(2)}, u32[]{:S(2)}) collective-permute-start(f32[2,16,512]{2,1,0:T(8,128)S(1)} %get-tuple-element.82), channel_id=1, source_target_pairs={{0,3},{1,2},{2,1},{3,0},{4,7},{5,6},{6,5},{7,4},{8,11},{9,10},{10,... | collective-permute-start | bytes 196616 | tf_op jit(solution)/shard_map/ppermute | solution.py:679
  38.4 10.9 %all-to-all-start.1 = ((f32[8,4,128]{2,1,0:T(4,128)}), f32[8,4,128]{2,1,0:T(4,128)S(1)}, u32[]{:S(2)}, u32[]{:S(2)}) async-start(f32[8,4,128]{2,1,0:T(4,128)} %bitcast.3), calls=%async_computation.1 | async-start | bytes 32768 | tf_op jit(solution)/shard_map/all_to_all | solution.py:760
